TPU v7x, 512 devices: a whole 4x4x16 slice. The times are simulated.
512 devices in a mesh: space: 64 (over z_lo, x, core), head: 8 (over z_hi, y).
Axes of the slice: x: 4, y: 4, z: 16 (z_hi: 2, z_lo: 8; z = z_hi * 8 + z_lo), core: 2. Of those that a mesh axis runs over, the one named last changes fastest.
Arguments:
- fields: bfloat16 [512, 32, 2, 1024], P('space', None, None, 'head'), may hold values from -1.796875 to 1.796875
- ln_gain: float32 [1024], replicated, may hold values from 0.1 to 1.9
- w_qkv: bfloat16 [1024, 3, 1024], P(None, None, 'head'), may hold values from -0.1875 to 0.1875
- attn_bias: float32 [16, 128, 128], P('head'), may hold values from -6 to 340
- w_out: bfloat16 [1024, 1024], P('head'), may hold values from -0.1875 to 0.1875
- merge_gain: float32 [4096], replicated, may hold values from 0.1 to 1.9
- w_merge: bfloat16 [4096, 2048], P(None, 'head'), may hold values from -0.09375 to 0.09375
Outputs:
- merged: bfloat16 [256, 16, 2, 2048], P('space', None, None, 'head')
All inputs are finite; a program needn't handle non-finite values.
Results may differ from a plain program's by a relative error of at most 0.02.
Values may be sent and summed in bfloat16 or wider, within the bound.
No kernel may reach another device: no remote copies, remote signals or barrier semaphores. Data moves between devices by JAX's collectives and lax.ppermute only.
A program may use at most 64 MiB of HBM per device.

v0:
```python
import jax
import jax.numpy as jnp
from jax import lax
from jax.sharding import PartitionSpec as P

D = 1024
HEAD_DIM = 64
WIN_LAT = 8
WIN_LON = 8
WIN_LEV = 2


EPS = 1e-05


def passed_along(value, axis, steps):
    count = lax.axis_size(axis)
    pairs = [(source, (source + steps) % count) for source in range(count)]
    return lax.ppermute(value, axis, pairs)


def window_split(band_rows):
    lat_rows, lon_cells, level_count, features = band_rows.shape
    windows = band_rows.reshape(
        lat_rows, lon_cells // WIN_LON, WIN_LON, level_count // WIN_LEV, WIN_LEV, features
    )
    windows = windows.transpose(1, 3, 0, 2, 4, 5)
    return windows.reshape(-1, lat_rows * WIN_LON * WIN_LEV, features)


def window_join(windows, lat_rows, lon_cells, level_count):
    features = windows.shape[-1]
    grid = windows.reshape(
        lon_cells // WIN_LON, level_count // WIN_LEV, lat_rows, WIN_LON, WIN_LEV, features
    )
    grid = grid.transpose(2, 0, 3, 1, 4, 5)
    return grid.reshape(lat_rows, lon_cells, level_count, features)


def attend_windows(windows, attn_bias):
    queries = windows[:, :, 0]
    key_rows = windows[:, :, 1]
    value_rows = windows[:, :, 2]
    scores = jnp.einsum("wphe,wqhe->whpq", queries, key_rows, preferred_element_type=jnp.float32)
    scores = scores * HEAD_DIM ** (-0.5) + attn_bias[None]
    highest = jnp.max(scores, -1, keepdims=True)
    exponent = jnp.exp(scores - highest)
    weights = (exponent / jnp.sum(exponent, -1, keepdims=True)).astype(jnp.bfloat16)
    return jnp.einsum(
        "whpq,wqhe->wphe", weights, value_rows, preferred_element_type=jnp.float32
    ).astype(jnp.bfloat16)


def layer_norm(widened, gain):
    mean_rows = jnp.mean(widened, -1, keepdims=True)
    spread = jnp.mean(widened * widened, -1, keepdims=True) - mean_rows * mean_rows
    return (widened - mean_rows) * lax.rsqrt(spread + EPS) * gain


def quadrants(stream):
    lat_rows, lon_cells, level_count, features = stream.shape
    grid = stream.reshape(lat_rows // 2, 2, lon_cells // 2, 2, level_count, features)
    return grid.transpose(0, 2, 4, 3, 1, 5).reshape(
        lat_rows // 2, lon_cells // 2, level_count, 4, features
    )


def on_device(fields, ln_gain, w_qkv, attn_bias, w_out, merge_gain, w_merge):
    lat_rows, lon_cells, level_count, local_width = fields.shape
    upper = passed_along(fields[: WIN_LAT // 2], "space", -1)
    shifted = jnp.concatenate([fields[WIN_LAT // 2 :], upper], axis=0)
    shifted = jnp.roll(shifted, (-(WIN_LON // 2), -(WIN_LEV // 2)), axis=(1, 2))
    stream = lax.all_gather(shifted, "head", axis=3, tiled=True)
    normed = layer_norm(stream.astype(jnp.float32), ln_gain).astype(jnp.bfloat16)
    projected = jnp.einsum("rnlc,ckd->rnlkd", normed, w_qkv, preferred_element_type=jnp.float32)
    projected = projected.astype(jnp.bfloat16)
    heads_here = w_qkv.shape[2] // HEAD_DIM
    windows = window_split(projected.reshape(lat_rows, lon_cells, level_count, 3 * w_qkv.shape[2]))
    windows = windows.reshape(windows.shape[0], windows.shape[1], 3, heads_here, HEAD_DIM)
    attended = attend_windows(windows, attn_bias)
    attended = window_join(
        attended.reshape(attended.shape[0], attended.shape[1], heads_here * HEAD_DIM),
        lat_rows,
        lon_cells,
        level_count,
    )
    partial_value = jnp.einsum("rnlf,fd->rnld", attended, w_out, preferred_element_type=jnp.float32)
    head_terms = lax.psum(partial_value.astype(jnp.bfloat16), "head").astype(jnp.float32)
    updated = (stream.astype(jnp.float32) + head_terms).astype(jnp.bfloat16)
    lower = passed_along(updated[WIN_LAT // 2 :], "space", 1)
    updated = jnp.concatenate([lower, updated[: WIN_LAT // 2]], axis=0)
    updated = jnp.roll(updated, (WIN_LON // 2, WIN_LEV // 2), axis=(1, 2))
    grid = quadrants(updated)
    flat_grid = grid.reshape(grid.shape[:3] + (4 * D,))
    merge_normed = layer_norm(flat_grid.astype(jnp.float32), merge_gain).astype(jnp.bfloat16)
    merged = jnp.einsum("rnlc,co->rnlo", merge_normed, w_merge, preferred_element_type=jnp.float32)
    merged = merged.astype(jnp.bfloat16)
    return merged


def solution(mesh):
    placed = (
        P("space", None, None, "head"),
        P(),
        P(None, None, "head"),
        P("head", None, None),
        P("head", None),
        P(),
        P(None, "head"),
    )
    return jax.shard_map(
        on_device,
        mesh=mesh,
        in_specs=placed,
        out_specs=P("space", None, None, "head"),
        check_vma=False,
    )
```

profile of v0, /device:TPU:24, one launch (start us, length us, event | category | flops | bytes accessed | tf_op | source)
XLA Modules:
  0.0 337.3 jit_solution(15575541830023713095)
XLA Ops:
  6.5 0.0 copy-start
  6.5 0.0 copy-start.4
  6.5 0.0 all-gather.2.cloned.1.call-start
  6.5 1.1 fusion.42
  7.7 14.8 %collective-permute-start = (bf16[4,32,2,128]{3,1,2,0:T(8,128)(2,1)S(1)}, bf16[4,32,2,128]{3,1,2,0:T(8,128)(2,1)S(1)}, u32[]{:S(2)}, u32[]{:S(2)}) collective-permute-start(bf16[4,32,2,128]{3,1,2,0:T(8,128)(2,1)S(1)} %copy.46), channel_id=1, source_target_pairs={{0,504},{8,0},{16,8},{24,16},{32,24},{40,32},{48,40},{56,48},{64,5... | collective-permute-start | bytes 196616 | tf_op jit(solution)/shard_map/ppermute | solution.py:19
  22.5 1.9 collective-permute-done
  24.5 0.7 fusion.26
  25.1 0.0 all-gather.2.cloned.1.call-update
  25.2 0.0 all-reduce.2.cloned.1.call-start
  25.2 1.0 copy.34
  26.2 86.0 %all-gather.2.cloned.1.call-done = bf16[8,32,2,1024]{3,1,2,0:T(8,128)(2,1)} async-done(((bf16[8,32,2,128]{3,1,2,0:T(8,128)(2,1)}), bf16[8,32,2,1024]{3,1,2,0:T(8,128)(2,1)}) %all-gather.2.cloned.1.call-update) | async-done | bytes 1048592 | tf_op jit(solution)/shard_map/all_gather | solution.py:73
  112.2 1.6 convert_reduce_fusion
  113.8 0.0 copy-done.4
  113.9 2.2 convolution_convert_fusion.1
  116.1 0.3 copy.29
  116.3 0.3 reshape_reshape.10
  116.7 0.3 copy.30
  117.0 0.5 reshape_reshape.11
  117.5 1.4 fusion.41
  118.9 1.1 copy.48
  120.0 0.1 copy.49
  120.1 0.4 fusion.43
  120.5 0.3 fusion.10
  120.8 0.1 copy.47
  120.9 0.3 fusion.11
  121.2 0.0 copy-start.2
  121.2 0.2 copy.36
  121.4 0.1 reshape_reshape.12
  121.5 2.4 convolution_convert_fusion
  123.9 0.0 all-reduce.2.cloned.1.call-update
  123.9 166.4 %all-reduce.2.cloned.1.call-done = bf16[8,32,2,1024]{3,1,2,0:T(8,128)(2,1)} async-done(((bf16[8,32,2,1024]{3,1,2,0:T(8,128)(2,1)}), bf16[8,32,2,1024]{3,1,2,0:T(8,128)(2,1)}) %all-reduce.2.cloned.1.call-update) | async-done | bytes 1048592 | tf_op jit(solution)/shard_map/psum | solution.py:88
  290.3 0.0 copy-done.2
  290.3 1.6 fusion.5
  292.0 0.1 fusion.40
  292.1 2.1 collective-permute-start.1
  294.2 17.1 %collective-permute-done.1 = bf16[4,32,2,1024]{3,1,2,0:T(8,128)(2,1)S(1)} collective-permute-done((bf16[4,32,2,1024]{3,1,2,0:T(8,128)(2,1)S(1)}, bf16[4,32,2,1024]{3,1,2,0:T(8,128)(2,1)S(1)}, u32[]{:S(2)}, u32[]{:S(2)}) %collective-permute-start.1) | collective-permute-done | bytes 524320 | tf_op jit(solution)/shard_map/ppermute | solution.py:19
  311.3 0.5 fusion.17
  311.7 0.1 fusion.39
  311.8 1.5 maximum_convert_fusion
  313.3 3.5 %reshape.54 = f32[4,2,16,2,2,1024]{5,3,2,4,1,0:T(2,128)} reshape(f32[8,32,2,1024]{3,1,2,0:T(8,128)} %maximum_convert_fusion) | data formatting | bytes 4194304 | tf_op jit(solution)/shard_map/convert_element_type | solution.py:95
  316.8 3.7 %bitcast_reduce_fusion = (f32[4,16,2]{1,2,0:T(2,128)S(1)}, f32[4,16,2]{1,2,0:T(2,128)S(1)}) fusion(f32[4,2,16,2,2,1024]{5,3,2,4,1,0:T(2,128)} %reshape.54), kind=kLoop, calls=%fused_computation.54 | loop fusion | flops 1572608 | bytes 2098176 | tf_op jit(solution)/shard_map/reduce_sum | solution.py:55
  320.5 0.0 copy-done.1
  320.5 3.2 copy.38
  323.7 4.0 %reshape.52 = f32[4,16,2,4096]{3,1,2,0:T(8,128)} reshape(f32[4,16,2,2,2,1024]{5,4,3,1,2,0:T(2,128)} %copy.38) | data formatting | bytes 4194304 | tf_op jit(solution)/shard_map/convert_element_type | solution.py:95
  327.7 0.0 copy-done
  327.7 0.0 copy-done.3
  327.7 2.1 fusion.12
  329.8 0.7 copy.39
  (10 shorter events, 0.1 us)
Async XLA Ops:
  6.5 321.2 %copy-start = (bf16[4096,256]{1,0:T(8,128)(2,1)S(1)}, bf16[4096,256]{1,0:T(8,128)(2,1)}, u32[]{:S(2)}) copy-start(bf16[4096,256]{1,0:T(8,128)(2,1)} %param.13) | copy-start | bytes 6291460
  6.5 107.3 %copy-start.4 = (f32[1024]{0:T(1024)S(1)}, f32[1024]{0:T(1024)}, u32[]{:S(2)}) copy-start(f32[1024]{0:T(1024)} %param.8) | copy-start | bytes 12292
  6.5 105.7 %all-gather.2.cloned.1.call-start = ((), (), s32[]{:S(2)}) async-start(), calls=%async_computation | async-start | bytes 1179648 | tf_op jit(solution)/shard_map/all_gather | solution.py:73
  7.7 16.7 %collective-permute-start = (bf16[4,32,2,128]{3,1,2,0:T(8,128)(2,1)S(1)}, bf16[4,32,2,128]{3,1,2,0:T(8,128)(2,1)S(1)}, u32[]{:S(2)}, u32[]{:S(2)}) collective-permute-start(bf16[4,32,2,128]{3,1,2,0:T(8,128)(2,1)S(1)} %copy.46), channel_id=1, source_target_pairs={{0,504},{8,0},{16,8},{24,16},{32,24},{40,32},{48,40},{56,48},{64,5... | collective-permute-start | bytes 196616 | tf_op jit(solution)/shard_map/ppermute | solution.py:19
  25.2 265.2 %all-reduce.2.cloned.1.call-start = ((), (), s32[]{:S(2)}) async-start(), calls=%async_computation.1 | async-start | bytes 2097152 | tf_op jit(solution)/shard_map/psum | solution.py:88
  121.2 169.1 %copy-start.2 = (bf16[8,32,2,1024]{3,1,2,0:T(8,128)(2,1)S(1)}, bf16[8,32,2,1024]{3,1,2,0:T(8,128)(2,1)}, u32[]{:S(2)}) copy-start(bf16[8,32,2,1024]{3,1,2,0:T(8,128)(2,1)} %all-gather.2.cloned.1.call-done) | copy-start | bytes 3145732
  292.1 19.2 %collective-permute-start.1 = (bf16[4,32,2,1024]{3,1,2,0:T(8,128)(2,1)S(1)}, bf16[4,32,2,1024]{3,1,2,0:T(8,128)(2,1)S(1)}, u32[]{:S(2)}, u32[]{:S(2)}) collective-permute-start(bf16[4,32,2,1024]{3,1,2,0:T(8,128)(2,1)S(1)} %get-tuple-element.11), channel_id=1, source_target_pairs={{0,8},{8,16},{16,24},{24,32},{32,40},{40,48},{48,56},{56,64},{64,7... | collective-permute-start | bytes 1572872 | tf_op jit(solution)/shard_map/ppermute | solution.py:19
  316.8 3.7 %copy-start.1 = (f32[4,2,16,2,2,1024]{5,3,2,4,1,0:T(2,128)S(1)}, f32[4,2,16,2,2,1024]{5,3,2,4,1,0:T(2,128)}, u32[]{:S(2)}) copy-start(f32[4,2,16,2,2,1024]{5,3,2,4,1,0:T(2,128)} %reshape.54) | copy-start | bytes 6291460
  323.7 4.1 %copy-start.3 = (f32[4096]{0:T(1024)S(1)}, f32[4096]{0:T(1024)}, u32[]{:S(2)}) copy-start(f32[4096]{0:T(1024)} %param.12) | copy-start | bytes 49156
Sparse Core Ops, SparseCore 0:
  25.3 86.8 all-gather.1
  124.0 166.2 all-reduce.1
where the time goes:
time: 338 us; the launch traced here: 337 us
  waiting for transfers between devices  271 us (80%)
  local copies, waits for them, and re-layouts  18.2 us (5%)
  starting transfers between devices  16.9 us (5%)
  between operations  13.6 us (4%)
  other arithmetic  9.61 us (3%)
  matrix products  7.59 us (2%)
    psum x1, waiting for transfers between devices, on_device(): lax.psum(partial_value.astype(jnp.bfloat16), 'head').astype(jnp.float32)  166 us
    all_gather x1, waiting for transfers between devices, on_device(): stream = lax.all_gather(shifted, 'head', axis=3, tiled=True)  86 us
    ppermute x2, waiting for transfers between devices, passed_along(): return lax.ppermute(value, axis, pairs)  19 us
    ppermute x2, starting transfers between devices, passed_along(): return lax.ppermute(value, axis, pairs)  16.9 us
    convert_element_type x3, local copies, waits for them, and re-layouts, on_device(): flat_grid.astype(jnp.float32)  10.7 us
  transfers between devices with their start and end apart: 4, of which 4 were waited for; matrix products, arithmetic and copies ran while one was open for 0% of the time, Pallas kernels for 0%

commit v1 on v0

v1 whole, which is shorter than its diff:
```python
import jax
import jax.numpy as jnp
import numpy as np
from jax import lax
from jax.experimental import pallas as pl
from jax.experimental.pallas import tpu as pltpu
from jax.sharding import PartitionSpec as P

D = 1024
HEAD_DIM = 64
BLOCK = 128
TOKENS = 512
HALF = 256
WINDOWS = 4
EPS = 1e-05
Y_GROUPS = [[0, 1, 2, 3], [4, 5, 6, 7]]
BOTH = ("space", "head")


def place(index):
    space, head = divmod(index, 8)
    z_lo, rest = divmod(space, 8)
    x, core = divmod(rest, 2)
    return z_lo, x, core, head


def moved(value, move):
    pairs = []
    for source in range(512):
        z_lo, x, core, head = move(*place(source))
        pairs.append((source, ((z_lo * 4 + x) * 2 + core) * 8 + head))
    return lax.ppermute(value, BOTH, pairs)


def across_z(value):
    return moved(value, lambda z_lo, x, core, head: (z_lo, x, core, head ^ 4))


def along_x(value, steps):
    return moved(value, lambda z_lo, x, core, head: (z_lo, (x + steps) % 4, core, head))


def other_core(value):
    return moved(value, lambda z_lo, x, core, head: (z_lo, x, core ^ 1, head))


def along_bands(value, steps):
    return lax.ppermute(value, "space", [(s, (s + steps) % 64) for s in range(64)])


def gathered_y(value):
    spread = jnp.broadcast_to(value[None], (4,) + value.shape)
    return lax.all_to_all(spread, "head", 0, 0, axis_index_groups=Y_GROUPS)


def half_order():
    p = np.arange(HALF)
    level, j, i = p & 1, (p >> 1) & 3, (p >> 3) & 1
    window, di, dj = (p >> 4) & 3, (p >> 6) & 1, (p >> 7) & 1
    row = 2 * i + di
    lon = (8 * window + 2 * j + dj + 4) % 32
    return row * 64 + lon * 2 + level


def window_order():
    p = np.arange(128)
    level, j, i = p & 1, (p >> 1) & 3, (p >> 3) & 1
    di, dj, half = (p >> 4) & 1, (p >> 5) & 1, (p >> 6) & 1
    return (half * 4 + 2 * i + di) * 16 + (2 * j + dj) * 2 + (1 - level)


def merged_order():
    o = np.arange(128)
    half, i, lon, level = o >> 6, (o >> 5) & 1, (o >> 1) & 15, o & 1
    back = (lon - 2) % 16
    return half * 64 + (back >> 2) * 16 + i * 8 + (back & 3) * 2 + level


def one_hot(order, dtype):
    return jnp.asarray(np.eye(len(order), dtype=np.float32)[order], dtype)


def dot(left, right):
    return jnp.dot(left, right, preferred_element_type=jnp.float32)


def window_rows(window):
    return [half * HALF + quad * 64 + window * 16 for half in range(2) for quad in range(4)]


def attention_kernel(own_ref, partner_ref, gain_ref, w_ref, bias_ref, out_ref, qkv_ref):
    z_hi = lax.axis_index("head") // 4
    parts = ((own_ref, z_hi), (partner_ref, 1 - z_hi))
    for start in range(0, TOKENS, 128):
        rows = slice(start, start + 128)
        total = jnp.zeros((128, BLOCK), jnp.float32)
        squares = jnp.zeros((128, BLOCK), jnp.float32)
        for ref, _ in parts:
            for y in range(4):
                value = ref[y, rows, :].astype(jnp.float32)
                total += value
                squares += value * value
        mean = jnp.sum(total, -1, keepdims=True) * (1.0 / D)
        spread = jnp.sum(squares, -1, keepdims=True) * (1.0 / D) - mean * mean
        scale = lax.rsqrt(spread + EPS)
        product = jnp.zeros((128, 3 * BLOCK), jnp.float32)
        for ref, z in parts:
            normed = jnp.concatenate(
                [
                    ((ref[y, rows, :].astype(jnp.float32) - mean) * scale * gain_ref[z * 4 + y]).astype(jnp.bfloat16)
                    for y in range(4)
                ],
                axis=1,
            )
            product += dot(normed, w_ref[z])
        qkv_ref[rows, :] = product.astype(jnp.bfloat16)
    for window in range(WINDOWS):
        starts = window_rows(window)
        cells = jnp.concatenate([qkv_ref[s : s + 16, :] for s in starts], axis=0)
        heads = []
        for head in range(2):
            at = head * HEAD_DIM
            queries = cells[:, at : at + HEAD_DIM]
            keys = cells[:, BLOCK + at : BLOCK + at + HEAD_DIM]
            values = cells[:, 2 * BLOCK + at : 2 * BLOCK + at + HEAD_DIM]
            scores = lax.dot_general(queries, keys, (((1,), (1,)), ((), ())), preferred_element_type=jnp.float32)
            scores = scores * HEAD_DIM ** (-0.5) + bias_ref[head]
            exponent = jnp.exp(scores - jnp.max(scores, -1, keepdims=True))
            weights = (exponent / jnp.sum(exponent, -1, keepdims=True)).astype(jnp.bfloat16)
            heads.append(dot(weights, values))
        attended = jnp.concatenate(heads, axis=1).astype(jnp.bfloat16)
        for piece, s in enumerate(starts):
            out_ref[s : s + 16, :] = attended[piece * 16 : piece * 16 + 16, :]


def merge_kernel(own_ref, partner_ref, own_att_ref, partner_att_ref, w_out_ref, gain_ref, w_ref, order_ref, out_ref, updated_ref):
    z_hi = lax.axis_index("head") // 4
    space = lax.axis_index("space")
    my_core = space % 2
    my_x = (space // 2) % 4
    attended = jnp.concatenate([ref[y] for ref in (own_att_ref, partner_att_ref) for y in range(4)], axis=1)
    for z_rel in range(2):
        stream_ref = (own_ref, partner_ref)[z_rel]
        z = z_hi if z_rel == 0 else 1 - z_hi
        for pair in range(2):
            x_rel = (z * 2 + pair - my_x + 4) % 4
            w_block = jnp.concatenate(
                [w_out_ref[(core + my_core) % 2, x_rel].reshape(D, BLOCK) for core in range(2)], axis=1
            )
            stream = jnp.concatenate([stream_ref[2 * pair + k, :TOKENS, :] for k in range(2)], axis=1)
            value = stream.astype(jnp.float32) + dot(attended, w_block)
            at = z_rel * 512 + pair * 256
            updated_ref[:, at : at + 256] = value.astype(jnp.bfloat16)

    def quad(k):
        return jnp.concatenate(
            [updated_ref[half * HALF + k * 64 : half * HALF + k * 64 + 64, :] for half in range(2)], axis=0
        ).astype(jnp.float32)

    total = jnp.zeros((128, 1), jnp.float32)
    squares = jnp.zeros((128, 1), jnp.float32)
    for k in range(4):
        value = quad(k)
        total += jnp.sum(value, -1, keepdims=True)
        squares += jnp.sum(value * value, -1, keepdims=True)
    mean = total * (1.0 / (4 * D))
    scale = lax.rsqrt(squares * (1.0 / (4 * D)) - mean * mean + EPS)
    merged = jnp.zeros((128, 256), jnp.float32)
    for k in range(4):
        value = (quad(k) - mean) * scale
        for z_rel in range(2):
            z = z_hi if z_rel == 0 else 1 - z_hi
            normed = (value[:, z_rel * 512 : z_rel * 512 + 512] * gain_ref[k * 2 + z]).astype(jnp.bfloat16)
            merged += dot(normed, w_ref[k * 2 + z])
    out_ref[...] = dot(order_ref[...], merged.astype(jnp.bfloat16)).astype(jnp.bfloat16)


def in_vmem(count):
    return [pl.BlockSpec(memory_space=pltpu.VMEM)] * count


def on_device(fields, ln_gain, w_qkv, attn_bias, w_out, merge_gain, w_merge):
    rows = fields.reshape(2, HALF, BLOCK)
    ordered = jnp.einsum(
        "pt,htf->hpf", one_hot(half_order(), jnp.bfloat16), rows, preferred_element_type=jnp.bfloat16
    )
    following = along_bands(ordered[0], -1)
    column = lax.axis_index("space") % 8
    w_piece = lax.dynamic_slice(w_out, (0, column * BLOCK), (BLOCK, BLOCK))
    mine = jnp.concatenate([ordered[1], following, w_piece], axis=0)
    partners = across_z(mine)
    own = gathered_y(mine)
    partner = gathered_y(partners)

    bias_hot = one_hot(window_order(), jnp.float32)
    bias = jnp.einsum("pa,hab->hpb", bias_hot, attn_bias, precision=lax.Precision.HIGHEST)
    bias = jnp.einsum("hpb,qb->hpq", bias, bias_hot, precision=lax.Precision.HIGHEST)
    w_qkv_flat = w_qkv.reshape(2, D // 2, 3 * BLOCK)
    attended = pl.pallas_call(
        attention_kernel,
        out_shape=jax.ShapeDtypeStruct((TOKENS, BLOCK), jnp.bfloat16),
        in_specs=in_vmem(5),
        out_specs=pl.BlockSpec(memory_space=pltpu.VMEM),
        scratch_shapes=[pltpu.VMEM((TOKENS, 3 * BLOCK), jnp.bfloat16)],
        compiler_params=pltpu.CompilerParams(vmem_limit_bytes=48 * 2**20),
        cost_estimate=pl.CostEstimate(flops=600_000_000, bytes_accessed=3_000_000, transcendentals=131072),
        name="attention",
    )(own, partner, ln_gain.reshape(8, 1, BLOCK), w_qkv_flat, bias)

    pieces = jnp.concatenate([own[:, TOKENS:], partner[:, TOKENS:]], axis=0)
    over_x = jnp.stack([pieces, along_x(pieces, -1), along_x(pieces, -2), along_x(pieces, -3)])
    w_out_whole = jnp.stack([over_x, other_core(over_x)])

    partner_attended = across_z(attended)
    own_all = gathered_y(attended)
    partner_all = gathered_y(partner_attended)
    merged = pl.pallas_call(
        merge_kernel,
        out_shape=jax.ShapeDtypeStruct((128, 256), jnp.bfloat16),
        in_specs=in_vmem(8),
        out_specs=pl.BlockSpec(memory_space=pltpu.VMEM),
        scratch_shapes=[pltpu.VMEM((TOKENS, D), jnp.bfloat16)],
        compiler_params=pltpu.CompilerParams(vmem_limit_bytes=48 * 2**20),
        cost_estimate=pl.CostEstimate(flops=1_400_000_000, bytes_accessed=7_000_000, transcendentals=0),
        name="merge",
    )(
        own,
        partner,
        own_all,
        partner_all,
        w_out_whole,
        merge_gain.reshape(8, 1, 512),
        w_merge.reshape(8, 512, 256),
        one_hot(merged_order(), jnp.bfloat16),
    )
    lower = along_bands(merged[64:], 1)
    return jnp.concatenate([lower, merged[:64]], axis=0).reshape(4, 16, 2, 256)


def solution(mesh):
    placed = (
        P("space", None, None, "head"),
        P(),
        P(None, None, "head"),
        P("head", None, None),
        P("head", None),
        P(),
        P(None, "head"),
    )
    return jax.shard_map(
        on_device,
        mesh=mesh,
        in_specs=placed,
        out_specs=P("space", None, None, "head"),
        check_vma=False,
    )
```

time: 338 us -> 142 us (0.42)
  the two profiles are of different devices: /device:TPU:24 before, /device:TPU:32 now
where the time goes in v1:
time: 142 us; the launch traced here: 141 us
  starting transfers between devices  66.1 us (47%)
  waiting for transfers between devices  52.4 us (37%)
  Pallas kernels  7.74 us (5%)
  local copies, waits for them, and re-layouts  7.56 us (5%)
  other arithmetic  5.05 us (4%)
  matrix products  1.73 us (1%)
    ppermute x6, starting transfers between devices, moved(): return lax.ppermute(value, BOTH, pairs)  43.4 us
    ppermute x6, waiting for transfers between devices, moved(): return lax.ppermute(value, BOTH, pairs)  28.6 us
    all_to_all x4, starting transfers between devices, gathered_y(): return lax.all_to_all(spread, 'head', 0, 0, axis_index_groups=Y_GROUPS)  17.2 us
    all_to_all x4, waiting for transfers between devices, gathered_y(): return lax.all_to_all(spread, 'head', 0, 0, axis_index_groups=Y_GROUPS)  16.6 us
    ppermute x2, waiting for transfers between devices, along_bands(): lax.ppermute(value, 'space', [(s, (s + steps) % 64) for s in range(64)])  7.25 us
    ppermute x2, starting transfers between devices, along_bands(): lax.ppermute(value, 'space', [(s, (s + steps) % 64) for s in range(64)])  5.57 us
    pallas_call x1, Pallas kernels, on_device(): pl.pallas_call(merge_kernel, out_shape=jax.ShapeDtypeStruct((128, 256), j...  4.24 us
    another operation x2, other arithmetic, on_device(): w_out_whole = jnp.stack([over_x, other_core(over_x)])  4.12 us
  transfers between devices with their start and end apart: 12, of which 7 were waited for; matrix products, arithmetic and copies ran while one was open for 4% of the time, Pallas kernels for 2%

profile of v1, /device:TPU:32, one launch (start us, length us, event | category | flops | bytes accessed | tf_op | source)
XLA Modules:
  0.0 140.8 jit_solution(17160469947680720245)
XLA Ops:
  0.0 1.2 convolution_bitcast_fusion.1
  1.2 3.6 %collective-permute-start = (bf16[256,128]{1,0:T(8,128)(2,1)S(1)}, bf16[256,128]{1,0:T(8,128)(2,1)S(1)}, u32[]{:S(2)}, u32[]{:S(2)}) collective-permute-start(bf16[256,128]{1,0:T(8,128)(2,1)S(1)} %get-tuple-element.10), channel_id=1, source_target_pairs={{0,504},{8,0},{16,8},{24,16},{32,24},{40,32},{48,40},{56,48},{64,5... | collective-permute-start | bytes 196616 | tf_op jit(solution)/shard_map/ppermute | solution.py:48
  4.9 0.0 copy-done
  4.9 1.8 %collective-permute-done = bf16[256,128]{1,0:T(8,128)(2,1)S(1)} collective-permute-done((bf16[256,128]{1,0:T(8,128)(2,1)S(1)}, bf16[256,128]{1,0:T(8,128)(2,1)S(1)}, u32[]{:S(2)}, u32[]{:S(2)}) %collective-permute-start) | collective-permute-done | bytes 65568 | tf_op jit(solution)/shard_map/ppermute | solution.py:48
  6.8 0.9 broadcast_in_dim.8
  7.7 4.6 %all-to-all-start = ((bf16[4,640,128]{2,1,0:T(8,128)(2,1)}), bf16[4,640,128]{2,1,0:T(8,128)(2,1)S(1)}, u32[]{:S(2)}, u32[]{:S(2)}) async-start(bf16[4,640,128]{2,1,0:T(8,128)(2,1)} %broadcast_in_dim.8), calls=%async_computation | async-start | bytes 1310720 | tf_op jit(solution)/shard_map/all_to_all | solution.py:53
  12.3 15.7 %collective-permute-start.1 = (bf16[640,128]{1,0:T(8,128)(2,1)S(1)}, bf16[640,128]{1,0:T(8,128)(2,1)S(1)}, u32[]{:S(2)}, u32[]{:S(2)}) collective-permute-start(bf16[640,128]{1,0:T(8,128)(2,1)S(1)} %pad_maximum_fusion.3), channel_id=1, source_target_pairs={{0,4},{1,5},{2,6},{3,7},{4,0},{5,1},{6,2},{7,3},{8,12},{9,13},{10,... | collective-permute-start | bytes 491528 | tf_op jit(solution)/shard_map/ppermute | solution.py:32
  28.0 12.8 %collective-permute-done.1 = bf16[640,128]{1,0:T(8,128)(2,1)S(1)} collective-permute-done((bf16[640,128]{1,0:T(8,128)(2,1)S(1)}, bf16[640,128]{1,0:T(8,128)(2,1)S(1)}, u32[]{:S(2)}, u32[]{:S(2)}) %collective-permute-start.1) | collective-permute-done | bytes 163872 | tf_op jit(solution)/shard_map/ppermute | solution.py:32
  40.8 0.0 all-to-all-done.own_ref
  40.8 0.9 broadcast_in_dim.9
  41.7 4.6 %all-to-all-start.1 = ((bf16[4,640,128]{2,1,0:T(8,128)(2,1)}), bf16[4,640,128]{2,1,0:T(8,128)(2,1)S(1)}, u32[]{:S(2)}, u32[]{:S(2)}) async-start(bf16[4,640,128]{2,1,0:T(8,128)(2,1)} %broadcast_in_dim.9), calls=%async_computation.1 | async-start | bytes 1310720 | tf_op jit(solution)/shard_map/all_to_all | solution.py:53
  46.4 9.1 %all-to-all-done.1.partner_ref = bf16[4,640,128]{2,1,0:T(8,128)(2,1)S(1)} async-done(((bf16[4,640,128]{2,1,0:T(8,128)(2,1)}), bf16[4,640,128]{2,1,0:T(8,128)(2,1)S(1)}, u32[]{:S(2)}, u32[]{:S(2)}) %all-to-all-start.1) | async-done | bytes 655392 | tf_op jit(solution)/shard_map/all_to_all | solution.py:53
  55.5 0.9 fusion
  56.4 6.3 %collective-permute-start.4 = (bf16[8,128,128]{2,1,0:T(8,128)(2,1)}, bf16[8,128,128]{2,1,0:T(8,128)(2,1)}, u32[]{:S(2)}, u32[]{:S(2)}) collective-permute-start(bf16[8,128,128]{2,1,0:T(8,128)(2,1)} %get-tuple-element.8), channel_id=1, source_target_pairs={{0,32},{1,33},{2,34},{3,35},{4,36},{5,37},{6,38},{7,39},{8,40},{9,... | collective-permute-start | bytes 786440 | tf_op jit(solution)/shard_map/ppermute | solution.py:32
  62.7 1.9 %collective-permute-start.5 = (bf16[8,128,128]{2,1,0:T(8,128)(2,1)}, bf16[8,128,128]{2,1,0:T(8,128)(2,1)}, u32[]{:S(2)}, u32[]{:S(2)}) collective-permute-start(bf16[8,128,128]{2,1,0:T(8,128)(2,1)} %get-tuple-element.8), channel_id=1, source_target_pairs={{0,16},{1,17},{2,18},{3,19},{4,20},{5,21},{6,22},{7,23},{8,24},{9,... | collective-permute-start | bytes 786440 | tf_op jit(solution)/shard_map/ppermute | solution.py:32
  64.7 5.1 %collective-permute-start.3 = (bf16[8,128,128]{2,1,0:T(8,128)(2,1)}, bf16[8,128,128]{2,1,0:T(8,128)(2,1)}, u32[]{:S(2)}, u32[]{:S(2)}) collective-permute-start(bf16[8,128,128]{2,1,0:T(8,128)(2,1)} %get-tuple-element.8), channel_id=1, source_target_pairs={{0,48},{1,49},{2,50},{3,51},{4,52},{5,53},{6,54},{7,55},{8,56},{9,... | collective-permute-start | bytes 786440 | tf_op jit(solution)/shard_map/ppermute | solution.py:32
  69.8 0.0 copy-done.6
  69.8 0.7 copy.14
  70.5 0.0 copy-start.7
  70.5 0.7 reshape.30.w_ref
  71.2 0.0 copy-start.8
  71.2 0.0 copy-start.5
  71.3 0.0 collective-permute-done.4
  71.3 3.1 %collective-permute-done.5 = bf16[8,128,128]{2,1,0:T(8,128)(2,1)} collective-permute-done((bf16[8,128,128]{2,1,0:T(8,128)(2,1)}, bf16[8,128,128]{2,1,0:T(8,128)(2,1)}, u32[]{:S(2)}, u32[]{:S(2)}) %collective-permute-start.5) | collective-permute-done | bytes 262176 | tf_op jit(solution)/shard_map/ppermute | solution.py:32
  74.3 0.0 collective-permute-done.3
  74.3 2.4 %fusion.1 = (bf16[1,4,8,128,128]{4,3,2,1,0:T(8,128)(2,1)}, bf16[4,8,128,128]{3,2,1,0:T(8,128)(2,1)S(1)}) fusion(bf16[1,8,128,128]{3,2,1,0:T(8,128)(2,1)} %bitcast.11, bf16[1,8,128,128]{3,2,1,0:T(8,128)(2,1)} %bitcast.10, bf16[1,8,128,128]{3,2,1,0:T(8,128)(2,1)} %bitcast.9, bf16[1,8,128,128]{3,2,1,0:T(8,128)(2,1)} %get-tuple-element.7), kind=kLoop, calls=%fused_computation.11 | loop fusion | flops 1572864 | bytes 3145728 | tf_op jit(solution)/shard_map/stack | solution.py:212
  76.7 1.9 %collective-permute-start.6 = (bf16[4,8,128,128]{3,2,1,0:T(8,128)(2,1)S(1)}, bf16[4,8,128,128]{3,2,1,0:T(8,128)(2,1)}, u32[]{:S(2)}, u32[]{:S(2)}) collective-permute-start(bf16[4,8,128,128]{3,2,1,0:T(8,128)(2,1)S(1)} %get-tuple-element.6), channel_id=1, source_target_pairs={{0,8},{1,9},{2,10},{3,11},{4,12},{5,13},{6,14},{7,15},{8,0},{9,1},... | collective-permute-start | bytes 3145736 | tf_op jit(solution)/shard_map/ppermute | solution.py:32
  78.6 0.0 copy-done.7
  78.6 0.0 copy-done.8
  78.6 0.3 convolution_bitcast_fusion
  78.9 0.3 fusion.3.bias_ref
  79.2 3.5 %attention.1 = bf16[512,128]{1,0:T(8,128)(2,1)S(1)} custom-call(bf16[4,640,128]{2,1,0:T(8,128)(2,1)S(1)} %all-to-all-done.own_ref, bf16[4,640,128]{2,1,0:T(8,128)(2,1)S(1)} %all-to-all-done.1.partner_ref, f32[8,1,128]{2,1,0:T(1,128)S(1)} %bitcast.29, bf16[2,512,384]{2,1,0:T(8,128)(2,1)S(1)} %reshape.30.w_ref, f32[2,128,128]{2,1,0:T(8,128)S(1)} %fusion.3.bias_ref), custom_call_target="tpu_custom_call" | custom-call | flops 600000000 | bytes 3000000 | tf_op jit(solution)/shard_map/attention/pallas_call | solution.py:199
  82.7 0.9 broadcast_in_dim.10
  83.6 3.5 %all-to-all-start.2 = ((bf16[4,512,128]{2,1,0:T(8,128)(2,1)}), bf16[4,512,128]{2,1,0:T(8,128)(2,1)S(1)}, u32[]{:S(2)}, u32[]{:S(2)}) async-start(bf16[4,512,128]{2,1,0:T(8,128)(2,1)} %broadcast_in_dim.10), calls=%async_computation.2 | async-start | bytes 1048576 | tf_op jit(solution)/shard_map/all_to_all | solution.py:53
  87.0 12.4 %collective-permute-start.2 = (bf16[512,128]{1,0:T(8,128)(2,1)S(1)}, bf16[512,128]{1,0:T(8,128)(2,1)S(1)}, u32[]{:S(2)}, u32[]{:S(2)}) collective-permute-start(bf16[512,128]{1,0:T(8,128)(2,1)S(1)} %attention.1), channel_id=1, source_target_pairs={{0,4},{1,5},{2,6},{3,7},{4,0},{5,1},{6,2},{7,3},{8,12},{9,13},{10,... | collective-permute-start | bytes 393224 | tf_op jit(solution)/shard_map/ppermute | solution.py:32
  99.4 12.7 %collective-permute-done.2 = bf16[512,128]{1,0:T(8,128)(2,1)S(1)} collective-permute-done((bf16[512,128]{1,0:T(8,128)(2,1)S(1)}, bf16[512,128]{1,0:T(8,128)(2,1)S(1)}, u32[]{:S(2)}, u32[]{:S(2)}) %collective-permute-start.2) | collective-permute-done | bytes 131104 | tf_op jit(solution)/shard_map/ppermute | solution.py:32
  112.1 0.0 all-to-all-done.2.own_att_ref
  112.2 0.9 broadcast_in_dim.11
  113.0 4.5 %all-to-all-start.3 = ((bf16[4,512,128]{2,1,0:T(8,128)(2,1)}), bf16[4,512,128]{2,1,0:T(8,128)(2,1)}, u32[]{:S(2)}, u32[]{:S(2)}) async-start(bf16[4,512,128]{2,1,0:T(8,128)(2,1)} %broadcast_in_dim.11), calls=%async_computation.3 | async-start | bytes 1048576 | tf_op jit(solution)/shard_map/all_to_all | solution.py:53
  117.5 0.0 collective-permute-done.6
  117.5 1.7 %pad_maximum_fusion.w_out_ref = bf16[2,4,8,128,128]{4,3,2,1,0:T(8,128)(2,1)S(1)} fusion(bf16[1,4,8,128,128]{4,3,2,1,0:T(8,128)(2,1)} %bitcast.13, bf16[1,4,8,128,128]{4,3,2,1,0:T(8,128)(2,1)} %get-tuple-element.5), kind=kLoop, calls=%fused_computation | loop fusion | flops 1048576 | bytes 4194304 | tf_op jit(solution)/shard_map/stack | solution.py:212
  119.2 7.5 %all-to-all-done.3.partner_att_ref = bf16[4,512,128]{2,1,0:T(8,128)(2,1)} async-done(((bf16[4,512,128]{2,1,0:T(8,128)(2,1)}), bf16[4,512,128]{2,1,0:T(8,128)(2,1)}, u32[]{:S(2)}, u32[]{:S(2)}) %all-to-all-start.3) | async-done | bytes 524320 | tf_op jit(solution)/shard_map/all_to_all | solution.py:53
  126.7 1.1 copy-done.2
  127.8 0.8 copy-done.3
  128.6 4.2 %merge.1 = bf16[128,256]{1,0:T(8,128)(2,1)S(1)} custom-call(bf16[4,640,128]{2,1,0:T(8,128)(2,1)S(1)} %all-to-all-done.own_ref, bf16[4,640,128]{2,1,0:T(8,128)(2,1)S(1)} %copy-done.2, bf16[4,512,128]{2,1,0:T(8,128)(2,1)S(1)} %all-to-all-done.2.own_att_ref, bf16[4,512,128]{2,1,0:T(8,128)(2,1)} %all-to-all-done.3.partner_att_ref, ...), custom_call_target="tpu_custom_call" | custom-call | flops 1400000000 | bytes 7000000 | tf_op jit(solution)/shard_map/merge/pallas_call | solution.py:217
  132.8 1.9 %collective-permute-start.7 = (bf16[64,256]{1,0:T(8,128)(2,1)S(1)}, bf16[64,256]{1,0:T(8,128)(2,1)S(1)}, u32[]{:S(2)}, u32[]{:S(2)}) collective-permute-start(bf16[64,256]{1,0:T(8,128)(2,1)S(1)} %get-tuple-element.11), channel_id=1, source_target_pairs={{0,8},{8,16},{16,24},{24,32},{32,40},{40,48},{48,56},{56,64},{64,7... | collective-permute-start | bytes 98312 | tf_op jit(solution)/shard_map/ppermute | solution.py:48
  134.8 5.4 %collective-permute-done.7 = bf16[64,256]{1,0:T(8,128)(2,1)S(1)} collective-permute-done((bf16[64,256]{1,0:T(8,128)(2,1)S(1)}, bf16[64,256]{1,0:T(8,128)(2,1)S(1)}, u32[]{:S(2)}, u32[]{:S(2)}) %collective-permute-start.7) | collective-permute-done | bytes 32800 | tf_op jit(solution)/shard_map/ppermute | solution.py:48
  140.2 0.7 reshape.27
  (16 shorter events, 0.1 us)
Async XLA Ops:
  0.0 4.9 %copy-start = (bf16[128,1024]{1,0:T(8,128)(2,1)S(1)}, bf16[128,1024]{1,0:T(8,128)(2,1)}, u32[]{:S(2)}) copy-start(bf16[128,1024]{1,0:T(8,128)(2,1)} %param.14) | copy-start | bytes 786436
  1.2 5.5 %collective-permute-start = (bf16[256,128]{1,0:T(8,128)(2,1)S(1)}, bf16[256,128]{1,0:T(8,128)(2,1)S(1)}, u32[]{:S(2)}, u32[]{:S(2)}) collective-permute-start(bf16[256,128]{1,0:T(8,128)(2,1)S(1)} %get-tuple-element.10), channel_id=1, source_target_pairs={{0,504},{8,0},{16,8},{24,16},{32,24},{40,32},{48,40},{56,48},{64,5... | collective-permute-start | bytes 196616 | tf_op jit(solution)/shard_map/ppermute | solution.py:48
  7.7 62.1 %copy-start.6 = (bf16[1024,3,128]{2,0,1:T(8,128)(2,1)S(1)}, bf16[1024,3,128]{2,0,1:T(8,128)(2,1)}, u32[]{:S(2)}) copy-start(bf16[1024,3,128]{2,0,1:T(8,128)(2,1)} %param.12) | copy-start | bytes 2359300
  7.7 33.1 %all-to-all-start = ((bf16[4,640,128]{2,1,0:T(8,128)(2,1)}), bf16[4,640,128]{2,1,0:T(8,128)(2,1)S(1)}, u32[]{:S(2)}, u32[]{:S(2)}) async-start(bf16[4,640,128]{2,1,0:T(8,128)(2,1)} %broadcast_in_dim.8), calls=%async_computation | async-start | bytes 1310720 | tf_op jit(solution)/shard_map/all_to_all | solution.py:53
  12.3 28.5 %collective-permute-start.1 = (bf16[640,128]{1,0:T(8,128)(2,1)S(1)}, bf16[640,128]{1,0:T(8,128)(2,1)S(1)}, u32[]{:S(2)}, u32[]{:S(2)}) collective-permute-start(bf16[640,128]{1,0:T(8,128)(2,1)S(1)} %pad_maximum_fusion.3), channel_id=1, source_target_pairs={{0,4},{1,5},{2,6},{3,7},{4,0},{5,1},{6,2},{7,3},{8,12},{9,13},{10,... | collective-permute-start | bytes 491528 | tf_op jit(solution)/shard_map/ppermute | solution.py:32
  41.7 13.7 %all-to-all-start.1 = ((bf16[4,640,128]{2,1,0:T(8,128)(2,1)}), bf16[4,640,128]{2,1,0:T(8,128)(2,1)S(1)}, u32[]{:S(2)}, u32[]{:S(2)}) async-start(bf16[4,640,128]{2,1,0:T(8,128)(2,1)} %broadcast_in_dim.9), calls=%async_computation.1 | async-start | bytes 1310720 | tf_op jit(solution)/shard_map/all_to_all | solution.py:53
  55.5 23.7 %copy-start.1 = (bf16[4,640,128]{2,1,0:T(8,128)(2,1)}, bf16[4,640,128]{2,1,0:T(8,128)(2,1)S(1)}, u32[]{:S(2)}) copy-start(bf16[4,640,128]{2,1,0:T(8,128)(2,1)S(1)} %all-to-all-done.1.partner_ref) | copy-start | bytes 1966084
  56.4 14.9 %collective-permute-start.4 = (bf16[8,128,128]{2,1,0:T(8,128)(2,1)}, bf16[8,128,128]{2,1,0:T(8,128)(2,1)}, u32[]{:S(2)}, u32[]{:S(2)}) collective-permute-start(bf16[8,128,128]{2,1,0:T(8,128)(2,1)} %get-tuple-element.8), channel_id=1, source_target_pairs={{0,32},{1,33},{2,34},{3,35},{4,36},{5,37},{6,38},{7,39},{8,40},{9,... | collective-permute-start | bytes 786440 | tf_op jit(solution)/shard_map/ppermute | solution.py:32
  62.7 11.6 %collective-permute-start.5 = (bf16[8,128,128]{2,1,0:T(8,128)(2,1)}, bf16[8,128,128]{2,1,0:T(8,128)(2,1)}, u32[]{:S(2)}, u32[]{:S(2)}) collective-permute-start(bf16[8,128,128]{2,1,0:T(8,128)(2,1)} %get-tuple-element.8), channel_id=1, source_target_pairs={{0,16},{1,17},{2,18},{3,19},{4,20},{5,21},{6,22},{7,23},{8,24},{9,... | collective-permute-start | bytes 786440 | tf_op jit(solution)/shard_map/ppermute | solution.py:32
  64.7 9.7 %collective-permute-start.3 = (bf16[8,128,128]{2,1,0:T(8,128)(2,1)}, bf16[8,128,128]{2,1,0:T(8,128)(2,1)}, u32[]{:S(2)}, u32[]{:S(2)}) collective-permute-start(bf16[8,128,128]{2,1,0:T(8,128)(2,1)} %get-tuple-element.8), channel_id=1, source_target_pairs={{0,48},{1,49},{2,50},{3,51},{4,52},{5,53},{6,54},{7,55},{8,56},{9,... | collective-permute-start | bytes 786440 | tf_op jit(solution)/shard_map/ppermute | solution.py:32
  70.5 8.1 %copy-start.7 = (f32[128,128,1]{1,0,2:T(8,128)S(1)}, f32[128,128,1]{1,0,2:T(8,128)}, u32[]{:S(2)}) copy-start(f32[128,128,1]{1,0,2:T(8,128)} %constant.36) | copy-start | bytes 196612
  71.2 7.4 %copy-start.8 = (f32[2,128,128]{2,1,0:T(8,128)S(1)}, f32[2,128,128]{2,1,0:T(8,128)}, u32[]{:S(2)}) copy-start(f32[2,128,128]{2,1,0:T(8,128)} %param.13) | copy-start | bytes 393220
  71.2 8.0 %copy-start.5 = (f32[1024]{0:T(1024)S(1)}, f32[1024]{0:T(1024)}, u32[]{:S(2)}) copy-start(f32[1024]{0:T(1024)} %param.11) | copy-start | bytes 12292
  76.7 40.8 %collective-permute-start.6 = (bf16[4,8,128,128]{3,2,1,0:T(8,128)(2,1)S(1)}, bf16[4,8,128,128]{3,2,1,0:T(8,128)(2,1)}, u32[]{:S(2)}, u32[]{:S(2)}) collective-permute-start(bf16[4,8,128,128]{3,2,1,0:T(8,128)(2,1)S(1)} %get-tuple-element.6), channel_id=1, source_target_pairs={{0,8},{1,9},{2,10},{3,11},{4,12},{5,13},{6,14},{7,15},{8,0},{9,1},... | collective-permute-start | bytes 3145736 | tf_op jit(solution)/shard_map/ppermute | solution.py:32
  83.6 28.6 %all-to-all-start.2 = ((bf16[4,512,128]{2,1,0:T(8,128)(2,1)}), bf16[4,512,128]{2,1,0:T(8,128)(2,1)S(1)}, u32[]{:S(2)}, u32[]{:S(2)}) async-start(bf16[4,512,128]{2,1,0:T(8,128)(2,1)} %broadcast_in_dim.10), calls=%async_computation.2 | async-start | bytes 1048576 | tf_op jit(solution)/shard_map/all_to_all | solution.py:53
  87.0 25.1 %collective-permute-start.2 = (bf16[512,128]{1,0:T(8,128)(2,1)S(1)}, bf16[512,128]{1,0:T(8,128)(2,1)S(1)}, u32[]{:S(2)}, u32[]{:S(2)}) collective-permute-start(bf16[512,128]{1,0:T(8,128)(2,1)S(1)} %attention.1), channel_id=1, source_target_pairs={{0,4},{1,5},{2,6},{3,7},{4,0},{5,1},{6,2},{7,3},{8,12},{9,13},{10,... | collective-permute-start | bytes 393224 | tf_op jit(solution)/shard_map/ppermute | solution.py:32
  113.0 13.7 %all-to-all-start.3 = ((bf16[4,512,128]{2,1,0:T(8,128)(2,1)}), bf16[4,512,128]{2,1,0:T(8,128)(2,1)}, u32[]{:S(2)}, u32[]{:S(2)}) async-start(bf16[4,512,128]{2,1,0:T(8,128)(2,1)} %broadcast_in_dim.11), calls=%async_computation.3 | async-start | bytes 1048576 | tf_op jit(solution)/shard_map/all_to_all | solution.py:53
  117.5 9.2 %copy-start.4 = (f32[4096]{0:T(1024)S(1)}, f32[4096]{0:T(1024)}, u32[]{:S(2)}) copy-start(f32[4096]{0:T(1024)} %param.15) | copy-start | bytes 49156
  126.7 1.1 copy-start.2
  127.8 0.8 copy-start.3
  132.8 7.3 %collective-permute-start.7 = (bf16[64,256]{1,0:T(8,128)(2,1)S(1)}, bf16[64,256]{1,0:T(8,128)(2,1)S(1)}, u32[]{:S(2)}, u32[]{:S(2)}) collective-permute-start(bf16[64,256]{1,0:T(8,128)(2,1)S(1)} %get-tuple-element.11), channel_id=1, source_target_pairs={{0,8},{8,16},{16,24},{24,32},{32,40},{40,48},{48,56},{56,64},{64,7... | collective-permute-start | bytes 98312 | tf_op jit(solution)/shard_map/ppermute | solution.py:48

commit v2 on v1

--- a/solution.py
+++ b/solution.py
@@ -13,7 +13,6 @@
 HALF = 256
 WINDOWS = 4
 EPS = 1e-05
-Y_GROUPS = [[0, 1, 2, 3], [4, 5, 6, 7]]
 BOTH = ("space", "head")
 
 
@@ -48,9 +47,12 @@
     return lax.ppermute(value, "space", [(s, (s + steps) % 64) for s in range(64)])
 
 
+def along_y(value, steps):
+    return moved(value, lambda z_lo, x, core, head: (z_lo, x, core, (head & 4) + (head - steps) % 4))
+
+
 def gathered_y(value):
-    spread = jnp.broadcast_to(value[None], (4,) + value.shape)
-    return lax.all_to_all(spread, "head", 0, 0, axis_index_groups=Y_GROUPS)
+    return [value] + [along_y(value, steps) for steps in (1, 2, 3)]
 
 
 def half_order():
@@ -88,31 +90,39 @@
     return [half * HALF + quad * 64 + window * 16 for half in range(2) for quad in range(4)]
 
 
-def attention_kernel(own_ref, partner_ref, gain_ref, w_ref, bias_ref, out_ref, qkv_ref):
-    z_hi = lax.axis_index("head") // 4
-    parts = ((own_ref, z_hi), (partner_ref, 1 - z_hi))
+def feature_block(relative):
+    head = lax.axis_index("head")
+    z_rel, y_rel = divmod(relative, 4)
+    z_hi = head // 4
+    z = z_hi if z_rel == 0 else 1 - z_hi
+    return z * 4 + (head % 4 + y_rel) % 4
+
+
+def attention_kernel(*refs):
+    stream_refs = refs[:8]
+    gain_ref, w_ref, bias_ref, out_ref, pieces_ref, qkv_ref = refs[8:]
+    blocks = [feature_block(k) for k in range(8)]
+    for k in range(8):
+        pieces_ref[k] = stream_refs[k][TOKENS:, :]
     for start in range(0, TOKENS, 128):
         rows = slice(start, start + 128)
         total = jnp.zeros((128, BLOCK), jnp.float32)
         squares = jnp.zeros((128, BLOCK), jnp.float32)
-        for ref, _ in parts:
-            for y in range(4):
-                value = ref[y, rows, :].astype(jnp.float32)
-                total += value
-                squares += value * value
+        for ref in stream_refs:
+            value = ref[rows, :].astype(jnp.float32)
+            total += value
+            squares += value * value
         mean = jnp.sum(total, -1, keepdims=True) * (1.0 / D)
         spread = jnp.sum(squares, -1, keepdims=True) * (1.0 / D) - mean * mean
         scale = lax.rsqrt(spread + EPS)
         product = jnp.zeros((128, 3 * BLOCK), jnp.float32)
-        for ref, z in parts:
-            normed = jnp.concatenate(
-                [
-                    ((ref[y, rows, :].astype(jnp.float32) - mean) * scale * gain_ref[z * 4 + y]).astype(jnp.bfloat16)
-                    for y in range(4)
-                ],
-                axis=1,
-            )
-            product += dot(normed, w_ref[z])
+        for k in range(0, 8, 2):
+            normed = [
+                ((stream_refs[n][rows, :].astype(jnp.float32) - mean) * scale * gain_ref[blocks[n]]).astype(jnp.bfloat16)
+                for n in (k, k + 1)
+            ]
+            weights = jnp.concatenate([w_ref[blocks[n]] for n in (k, k + 1)], axis=0)
+            product += dot(jnp.concatenate(normed, axis=1), weights)
         qkv_ref[rows, :] = product.astype(jnp.bfloat16)
     for window in range(WINDOWS):
         starts = window_rows(window)
@@ -133,24 +143,27 @@
             out_ref[s : s + 16, :] = attended[piece * 16 : piece * 16 + 16, :]
 
 
-def merge_kernel(own_ref, partner_ref, own_att_ref, partner_att_ref, w_out_ref, gain_ref, w_ref, order_ref, out_ref, updated_ref):
-    z_hi = lax.axis_index("head") // 4
+def merge_kernel(*refs):
+    stream_refs, att_refs = refs[:8], refs[8:16]
+    w_same_ref, w_other_ref, gain_ref, w_ref, order_ref, out_ref, updated_ref = refs[16:]
+    blocks = [feature_block(k) for k in range(8)]
     space = lax.axis_index("space")
-    my_core = space % 2
     my_x = (space // 2) % 4
-    attended = jnp.concatenate([ref[y] for ref in (own_att_ref, partner_att_ref) for y in range(4)], axis=1)
-    for z_rel in range(2):
-        stream_ref = (own_ref, partner_ref)[z_rel]
-        z = z_hi if z_rel == 0 else 1 - z_hi
-        for pair in range(2):
-            x_rel = (z * 2 + pair - my_x + 4) % 4
-            w_block = jnp.concatenate(
-                [w_out_ref[(core + my_core) % 2, x_rel].reshape(D, BLOCK) for core in range(2)], axis=1
-            )
-            stream = jnp.concatenate([stream_ref[2 * pair + k, :TOKENS, :] for k in range(2)], axis=1)
-            value = stream.astype(jnp.float32) + dot(attended, w_block)
-            at = z_rel * 512 + pair * 256
-            updated_ref[:, at : at + 256] = value.astype(jnp.bfloat16)
+    parity = (lax.axis_index("head") + space) % 2
+
+    def project(odd):
+        attended = jnp.concatenate([ref[...] for ref in att_refs], axis=1)
+        for k in range(0, 8, 2):
+            w_blocks = []
+            for n in (k, k + 1):
+                w_from = w_same_ref if (n + odd) % 2 == 0 else w_other_ref
+                w_blocks.append(w_from[(blocks[n] // 2 - my_x + 4) % 4].reshape(D, BLOCK))
+            stream = jnp.concatenate([stream_refs[n][:TOKENS, :] for n in (k, k + 1)], axis=1)
+            value = stream.astype(jnp.float32) + dot(attended, jnp.concatenate(w_blocks, axis=1))
+            updated_ref[:, k * BLOCK : (k + 2) * BLOCK] = value.astype(jnp.bfloat16)
+
+    for odd in range(2):
+        pl.when(parity == odd)(lambda odd=odd: project(odd))
 
     def quad(k):
         return jnp.concatenate(
@@ -168,11 +181,26 @@
     merged = jnp.zeros((128, 256), jnp.float32)
     for k in range(4):
         value = (quad(k) - mean) * scale
-        for z_rel in range(2):
-            z = z_hi if z_rel == 0 else 1 - z_hi
-            normed = (value[:, z_rel * 512 : z_rel * 512 + 512] * gain_ref[k * 2 + z]).astype(jnp.bfloat16)
-            merged += dot(normed, w_ref[k * 2 + z])
+        gain = jnp.concatenate([gain_ref[k * 8 + block] for block in blocks], axis=1)
+        weights = jnp.concatenate([w_ref[k * 8 + block] for block in blocks], axis=0)
+        merged += dot((value * gain).astype(jnp.bfloat16), weights)
     out_ref[...] = dot(order_ref[...], merged.astype(jnp.bfloat16)).astype(jnp.bfloat16)
+
+
+def nothing(*refs):
+    pass
+
+
+def after(value, event):
+    anywhere = pl.BlockSpec(memory_space=pl.ANY)
+    return pl.pallas_call(
+        nothing,
+        out_shape=jax.ShapeDtypeStruct(value.shape, value.dtype),
+        in_specs=[anywhere, anywhere],
+        out_specs=anywhere,
+        input_output_aliases={0: 0},
+        name="after",
+    )(value, event)
 
 
 def in_vmem(count):
@@ -195,42 +223,43 @@
     bias_hot = one_hot(window_order(), jnp.float32)
     bias = jnp.einsum("pa,hab->hpb", bias_hot, attn_bias, precision=lax.Precision.HIGHEST)
     bias = jnp.einsum("hpb,qb->hpq", bias, bias_hot, precision=lax.Precision.HIGHEST)
-    w_qkv_flat = w_qkv.reshape(2, D // 2, 3 * BLOCK)
-    attended = pl.pallas_call(
+    vmem = pl.BlockSpec(memory_space=pltpu.VMEM)
+    attended, pieces = pl.pallas_call(
         attention_kernel,
-        out_shape=jax.ShapeDtypeStruct((TOKENS, BLOCK), jnp.bfloat16),
-        in_specs=in_vmem(5),
-        out_specs=pl.BlockSpec(memory_space=pltpu.VMEM),
+        out_shape=(
+            jax.ShapeDtypeStruct((TOKENS, BLOCK), jnp.bfloat16),
+            jax.ShapeDtypeStruct((8, BLOCK, BLOCK), jnp.bfloat16),
+        ),
+        in_specs=in_vmem(11),
+        out_specs=(vmem, vmem),
         scratch_shapes=[pltpu.VMEM((TOKENS, 3 * BLOCK), jnp.bfloat16)],
-        compiler_params=pltpu.CompilerParams(vmem_limit_bytes=48 * 2**20),
+        compiler_params=pltpu.CompilerParams(vmem_limit_bytes=16 * 2**20),
         cost_estimate=pl.CostEstimate(flops=600_000_000, bytes_accessed=3_000_000, transcendentals=131072),
         name="attention",
-    )(own, partner, ln_gain.reshape(8, 1, BLOCK), w_qkv_flat, bias)
-
-    pieces = jnp.concatenate([own[:, TOKENS:], partner[:, TOKENS:]], axis=0)
-    over_x = jnp.stack([pieces, along_x(pieces, -1), along_x(pieces, -2), along_x(pieces, -3)])
-    w_out_whole = jnp.stack([over_x, other_core(over_x)])
-
-    partner_attended = across_z(attended)
+    )(*own, *partner, ln_gain.reshape(8, 1, BLOCK), w_qkv.reshape(8, BLOCK, 3 * BLOCK), bias)
+
     own_all = gathered_y(attended)
-    partner_all = gathered_y(partner_attended)
+    partner_all = gathered_y(across_z(attended))
+    pieces = after(pieces, own_all[1])
+    over_x = jnp.stack([pieces] + [along_x(pieces, -steps) for steps in (1, 2, 3)])
     merged = pl.pallas_call(
         merge_kernel,
         out_shape=jax.ShapeDtypeStruct((128, 256), jnp.bfloat16),
-        in_specs=in_vmem(8),
-        out_specs=pl.BlockSpec(memory_space=pltpu.VMEM),
+        in_specs=in_vmem(21),
+        out_specs=vmem,
         scratch_shapes=[pltpu.VMEM((TOKENS, D), jnp.bfloat16)],
-        compiler_params=pltpu.CompilerParams(vmem_limit_bytes=48 * 2**20),
+        compiler_params=pltpu.CompilerParams(vmem_limit_bytes=16 * 2**20),
         cost_estimate=pl.CostEstimate(flops=1_400_000_000, bytes_accessed=7_000_000, transcendentals=0),
         name="merge",
     )(
-        own,
-        partner,
-        own_all,
-        partner_all,
-        w_out_whole,
-        merge_gain.reshape(8, 1, 512),
-        w_merge.reshape(8, 512, 256),
+        *own,
+        *partner,
+        *own_all,
+        *partner_all,
+        over_x,
+        other_core(after(over_x, partner_all[1])),
+        merge_gain.reshape(32, 1, BLOCK),
+        w_merge.reshape(32, BLOCK, 256),
         one_hot(merged_order(), jnp.bfloat16),
     )
     lower = along_bands(merged[64:], 1)

time: 142 us -> 150 us (1.056)
  the two profiles are of different devices: /device:TPU:32 before, /device:TPU:24 now
where the time goes in v2:
time: 150 us; the launch traced here: 148 us
  starting transfers between devices  87.8 us (59%)
  waiting for transfers between devices  35 us (23%)
  local copies, waits for them, and re-layouts  15.5 us (10%)
  Pallas kernels  6.72 us (4%)
  matrix products  1.73 us (1%)
    ppermute x18, starting transfers between devices, moved(): return lax.ppermute(value, BOTH, pairs)  71 us
    ppermute x18, waiting for transfers between devices, moved(): return lax.ppermute(value, BOTH, pairs)  23 us
    ppermute x2, starting transfers between devices, along_bands(): lax.ppermute(value, 'space', [(s, (s + steps) % 64) for s in range(64)])  16.8 us
    unnamed x61, local copies, waits for them, and re-layouts  12.3 us
    ppermute x2, waiting for transfers between devices, along_bands(): lax.ppermute(value, 'space', [(s, (s + steps) % 64) for s in range(64)])  12 us
    pallas_call x1, Pallas kernels, on_device(): pl.pallas_call(attention_kernel, out_shape=(jax.ShapeDtypeStruct((TOKENS,...  3.57 us
    pallas_call x1, Pallas kernels, on_device(): pl.pallas_call(merge_kernel, out_shape=jax.ShapeDtypeStruct((128, 256), j...  3.14 us
  transfers between devices with their start and end apart: 20, of which 7 were waited for; matrix products, arithmetic and copies ran while one was open for 3% of the time, Pallas kernels for 0%

profile of v2, /device:TPU:24, one launch (start us, length us, event | category | flops | bytes accessed | tf_op | source)
XLA Modules:
  0.0 148.5 jit_solution(7239090777293005502)
XLA Ops:
  0.0 1.2 convolution_bitcast_fusion.1
  1.2 14.9 %collective-permute-start = (bf16[256,128]{1,0:T(8,128)(2,1)S(1)}, bf16[256,128]{1,0:T(8,128)(2,1)S(1)}, u32[]{:S(2)}, u32[]{:S(2)}) collective-permute-start(bf16[256,128]{1,0:T(8,128)(2,1)S(1)} %get-tuple-element.10), channel_id=1, source_target_pairs={{0,504},{8,0},{16,8},{24,16},{32,24},{40,32},{48,40},{56,48},{64,5... | collective-permute-start | bytes 196616 | tf_op jit(solution)/shard_map/ppermute | solution.py:47
  16.2 1.8 %copy.16 = bf16[1024,3,128]{2,1,0:T(4,128)(2,1)S(1)} copy(bf16[1024,3,128]{2,0,1:T(8,128)(2,1)} %param.12) | data formatting | bytes 1572864 | tf_op jit(solution)/shard_map/reshape | solution.py:239
  18.0 0.7 reshape.26.refs_9_
  18.8 8.2 %collective-permute-start.4 = (bf16[640,128]{1,0:T(8,128)(2,1)S(1)}, bf16[640,128]{1,0:T(8,128)(2,1)S(1)}, u32[]{:S(2)}, u32[]{:S(2)}) collective-permute-start(bf16[640,128]{1,0:T(8,128)(2,1)S(1)} %pad_maximum_fusion.1.refs_0_), channel_id=1, source_target_pairs={{0,4},{1,5},{2,6},{3,7},{4,0},{5,1},{6,2},{7,3},{8,12},{9,13},{10,... | collective-permute-start | bytes 491528 | tf_op jit(solution)/shard_map/ppermute | solution.py:31
  27.1 2.7 %collective-permute-start.1 = (bf16[640,128]{1,0:T(8,128)(2,1)S(1)}, bf16[640,128]{1,0:T(8,128)(2,1)S(1)}, u32[]{:S(2)}, u32[]{:S(2)}) collective-permute-start(bf16[640,128]{1,0:T(8,128)(2,1)S(1)} %pad_maximum_fusion.1.refs_0_), channel_id=1, source_target_pairs={{0,3},{1,0},{2,1},{3,2},{4,7},{5,4},{6,5},{7,6},{8,11},{9,8},{10,9... | collective-permute-start | bytes 491528 | tf_op jit(solution)/shard_map/ppermute | solution.py:31
  30.0 2.9 %collective-permute-start.2 = (bf16[640,128]{1,0:T(8,128)(2,1)S(1)}, bf16[640,128]{1,0:T(8,128)(2,1)S(1)}, u32[]{:S(2)}, u32[]{:S(2)}) collective-permute-start(bf16[640,128]{1,0:T(8,128)(2,1)S(1)} %pad_maximum_fusion.1.refs_0_), channel_id=1, source_target_pairs={{0,2},{1,3},{2,0},{3,1},{4,6},{5,7},{6,4},{7,5},{8,10},{9,11},{10,... | collective-permute-start | bytes 491528 | tf_op jit(solution)/shard_map/ppermute | solution.py:31
  32.9 4.1 %collective-permute-start.3 = (bf16[640,128]{1,0:T(8,128)(2,1)S(1)}, bf16[640,128]{1,0:T(8,128)(2,1)S(1)}, u32[]{:S(2)}, u32[]{:S(2)}) collective-permute-start(bf16[640,128]{1,0:T(8,128)(2,1)S(1)} %pad_maximum_fusion.1.refs_0_), channel_id=1, source_target_pairs={{0,1},{1,2},{2,3},{3,0},{4,5},{5,6},{6,7},{7,4},{8,9},{9,10},{10,1... | collective-permute-start | bytes 491528 | tf_op jit(solution)/shard_map/ppermute | solution.py:31
  37.0 2.1 %collective-permute-start.5 = (bf16[640,128]{1,0:T(8,128)(2,1)S(1)}, bf16[640,128]{1,0:T(8,128)(2,1)S(1)}, u32[]{:S(2)}, u32[]{:S(2)}) collective-permute-start(bf16[640,128]{1,0:T(8,128)(2,1)S(1)} %collective-permute-done.4.refs_4_), channel_id=1, source_target_pairs={{0,3},{1,0},{2,1},{3,2},{4,7},{5,4},{6,5},{7,6},{8,11},{9,8},{10,9... | collective-permute-start | bytes 491528 | tf_op jit(solution)/shard_map/ppermute | solution.py:31
  39.1 4.1 %collective-permute-start.6 = (bf16[640,128]{1,0:T(8,128)(2,1)S(1)}, bf16[640,128]{1,0:T(8,128)(2,1)S(1)}, u32[]{:S(2)}, u32[]{:S(2)}) collective-permute-start(bf16[640,128]{1,0:T(8,128)(2,1)S(1)} %collective-permute-done.4.refs_4_), channel_id=1, source_target_pairs={{0,2},{1,3},{2,0},{3,1},{4,6},{5,7},{6,4},{7,5},{8,10},{9,11},{10,... | collective-permute-start | bytes 491528 | tf_op jit(solution)/shard_map/ppermute | solution.py:31
  43.3 4.4 %collective-permute-start.7 = (bf16[640,128]{1,0:T(8,128)(2,1)S(1)}, bf16[640,128]{1,0:T(8,128)(2,1)S(1)}, u32[]{:S(2)}, u32[]{:S(2)}) collective-permute-start(bf16[640,128]{1,0:T(8,128)(2,1)S(1)} %collective-permute-done.4.refs_4_), channel_id=1, source_target_pairs={{0,1},{1,2},{2,3},{3,0},{4,5},{5,6},{6,7},{7,4},{8,9},{9,10},{10,1... | collective-permute-start | bytes 491528 | tf_op jit(solution)/shard_map/ppermute | solution.py:31
  48.0 2.5 %collective-permute-done.7.refs_7_ = bf16[640,128]{1,0:T(8,128)(2,1)S(1)} collective-permute-done((bf16[640,128]{1,0:T(8,128)(2,1)S(1)}, bf16[640,128]{1,0:T(8,128)(2,1)S(1)}, u32[]{:S(2)}, u32[]{:S(2)}) %collective-permute-start.7) | collective-permute-done | bytes 163872 | tf_op jit(solution)/shard_map/ppermute | solution.py:31
  50.5 3.6 %attention.1 = (bf16[512,128]{1,0:T(8,128)(2,1)S(1)}, bf16[8,128,128]{2,1,0:T(8,128)(2,1)S(1)}) custom-call(bf16[640,128]{1,0:T(8,128)(2,1)S(1)} %pad_maximum_fusion.1.refs_0_, bf16[640,128]{1,0:T(8,128)(2,1)S(1)} %collective-permute-done.1.refs_1_, bf16[640,128]{1,0:T(8,128)(2,1)S(1)} %collective-permute-done.2.refs_2_, ...), custom_call_target="tpu_custom_call" | custom-call | flops 600000000 | bytes 3000000 | tf_op jit(solution)/shard_map/attention/pallas_call | solution.py:227
  54.1 0.7 copy-done.4
  54.8 3.5 %collective-permute-start.8 = (bf16[512,128]{1,0:T(8,128)(2,1)S(1)}, bf16[512,128]{1,0:T(8,128)(2,1)S(1)}, u32[]{:S(2)}, u32[]{:S(2)}) collective-permute-start(bf16[512,128]{1,0:T(8,128)(2,1)S(1)} %get-tuple-element.7.refs_8_), channel_id=1, source_target_pairs={{0,3},{1,0},{2,1},{3,2},{4,7},{5,4},{6,5},{7,6},{8,11},{9,8},{10,9... | collective-permute-start | bytes 393224 | tf_op jit(solution)/shard_map/ppermute | solution.py:31
  58.4 5.0 %collective-permute-done.8.refs_1_.refs_9_ = bf16[512,128]{1,0:T(8,128)(2,1)S(1)} collective-permute-done((bf16[512,128]{1,0:T(8,128)(2,1)S(1)}, bf16[512,128]{1,0:T(8,128)(2,1)S(1)}, u32[]{:S(2)}, u32[]{:S(2)}) %collective-permute-start.8) | collective-permute-done | bytes 131104 | tf_op jit(solution)/shard_map/ppermute | solution.py:31
  63.4 0.6 copy-done.19
  64.0 1.9 %collective-permute-start.16 = (bf16[8,128,128]{2,1,0:T(8,128)(2,1)}, bf16[8,128,128]{2,1,0:T(8,128)(2,1)S(1)}, u32[]{:S(2)}, u32[]{:S(2)}) collective-permute-start(bf16[8,128,128]{2,1,0:T(8,128)(2,1)} %after.2), channel_id=1, source_target_pairs={{0,32},{1,33},{2,34},{3,35},{4,36},{5,37},{6,38},{7,39},{8,40},{9,... | collective-permute-start | bytes 786440 | tf_op jit(solution)/shard_map/ppermute | solution.py:31
  65.9 3.2 %collective-permute-start.17 = (bf16[8,128,128]{2,1,0:T(8,128)(2,1)}, bf16[8,128,128]{2,1,0:T(8,128)(2,1)S(1)}, u32[]{:S(2)}, u32[]{:S(2)}) collective-permute-start(bf16[8,128,128]{2,1,0:T(8,128)(2,1)} %after.2), channel_id=1, source_target_pairs={{0,16},{1,17},{2,18},{3,19},{4,20},{5,21},{6,22},{7,23},{8,24},{9,... | collective-permute-start | bytes 786440 | tf_op jit(solution)/shard_map/ppermute | solution.py:31
  69.1 3.9 %collective-permute-start.15 = (bf16[8,128,128]{2,1,0:T(8,128)(2,1)}, bf16[8,128,128]{2,1,0:T(8,128)(2,1)S(1)}, u32[]{:S(2)}, u32[]{:S(2)}) collective-permute-start(bf16[8,128,128]{2,1,0:T(8,128)(2,1)} %after.2), channel_id=1, source_target_pairs={{0,48},{1,49},{2,50},{3,51},{4,52},{5,53},{6,54},{7,55},{8,56},{9,... | collective-permute-start | bytes 786440 | tf_op jit(solution)/shard_map/ppermute | solution.py:31
  73.0 13.5 %collective-permute-start.11 = (bf16[512,128]{1,0:T(8,128)(2,1)S(1)}, bf16[512,128]{1,0:T(8,128)(2,1)S(1)}, u32[]{:S(2)}, u32[]{:S(2)}) collective-permute-start(bf16[512,128]{1,0:T(8,128)(2,1)S(1)} %get-tuple-element.7.refs_8_), channel_id=1, source_target_pairs={{0,4},{1,5},{2,6},{3,7},{4,0},{5,1},{6,2},{7,3},{8,12},{9,13},{10,... | collective-permute-start | bytes 393224 | tf_op jit(solution)/shard_map/ppermute | solution.py:31
  86.5 6.5 %collective-permute-done.11.refs_12_ = bf16[512,128]{1,0:T(8,128)(2,1)S(1)} collective-permute-done((bf16[512,128]{1,0:T(8,128)(2,1)S(1)}, bf16[512,128]{1,0:T(8,128)(2,1)S(1)}, u32[]{:S(2)}, u32[]{:S(2)}) %collective-permute-start.11) | collective-permute-done | bytes 131104 | tf_op jit(solution)/shard_map/ppermute | solution.py:31
  93.1 2.2 %collective-permute-start.12 = (bf16[512,128]{1,0:T(8,128)(2,1)S(1)}, bf16[512,128]{1,0:T(8,128)(2,1)}, u32[]{:S(2)}, u32[]{:S(2)}) collective-permute-start(bf16[512,128]{1,0:T(8,128)(2,1)S(1)} %collective-permute-done.11.refs_12_), channel_id=1, source_target_pairs={{0,3},{1,0},{2,1},{3,2},{4,7},{5,4},{6,5},{7,6},{8,11},{9,8},{10,9... | collective-permute-start | bytes 393224 | tf_op jit(solution)/shard_map/ppermute | solution.py:31
  95.3 1.1 pad_maximum_fusion.refs_16_
  96.4 1.0 copy.19.refs_0_
  97.4 3.8 %collective-permute-done.12.refs_1_.refs_13_ = bf16[512,128]{1,0:T(8,128)(2,1)} collective-permute-done((bf16[512,128]{1,0:T(8,128)(2,1)S(1)}, bf16[512,128]{1,0:T(8,128)(2,1)}, u32[]{:S(2)}, u32[]{:S(2)}) %collective-permute-start.12) | collective-permute-done | bytes 131104 | tf_op jit(solution)/shard_map/ppermute | solution.py:31
  101.2 1.9 %collective-permute-start.18 = (bf16[4,8,128,128]{3,2,1,0:T(8,128)(2,1)}, bf16[4,8,128,128]{3,2,1,0:T(8,128)(2,1)S(1)}, u32[]{:S(2)}, u32[]{:S(2)}) collective-permute-start(bf16[4,8,128,128]{3,2,1,0:T(8,128)(2,1)} %after.3), channel_id=1, source_target_pairs={{0,8},{1,9},{2,10},{3,11},{4,12},{5,13},{6,14},{7,15},{8,0},{9,1},... | collective-permute-start | bytes 3145736 | tf_op jit(solution)/shard_map/ppermute | solution.py:31
  103.1 2.4 %collective-permute-start.10 = (bf16[512,128]{1,0:T(8,128)(2,1)}, bf16[512,128]{1,0:T(8,128)(2,1)S(1)}, u32[]{:S(2)}, u32[]{:S(2)}) collective-permute-start(bf16[512,128]{1,0:T(8,128)(2,1)} %copy-done.21), channel_id=1, source_target_pairs={{0,1},{1,2},{2,3},{3,0},{4,5},{5,6},{6,7},{7,4},{8,9},{9,10},{10,1... | collective-permute-start | bytes 393224 | tf_op jit(solution)/shard_map/ppermute | solution.py:31
  105.6 2.6 %collective-permute-start.9 = (bf16[512,128]{1,0:T(8,128)(2,1)}, bf16[512,128]{1,0:T(8,128)(2,1)S(1)}, u32[]{:S(2)}, u32[]{:S(2)}) collective-permute-start(bf16[512,128]{1,0:T(8,128)(2,1)} %copy-done.21), channel_id=1, source_target_pairs={{0,2},{1,3},{2,0},{3,1},{4,6},{5,7},{6,4},{7,5},{8,10},{9,11},{10,... | collective-permute-start | bytes 393224 | tf_op jit(solution)/shard_map/ppermute | solution.py:31
  108.1 4.8 %collective-permute-start.13 = (bf16[512,128]{1,0:T(8,128)(2,1)}, bf16[512,128]{1,0:T(8,128)(2,1)S(1)}, u32[]{:S(2)}, u32[]{:S(2)}) collective-permute-start(bf16[512,128]{1,0:T(8,128)(2,1)} %copy-done.23), channel_id=1, source_target_pairs={{0,2},{1,3},{2,0},{3,1},{4,6},{5,7},{6,4},{7,5},{8,10},{9,11},{10,... | collective-permute-start | bytes 393224 | tf_op jit(solution)/shard_map/ppermute | solution.py:31
  112.9 2.6 %collective-permute-start.14 = (bf16[512,128]{1,0:T(8,128)(2,1)}, bf16[512,128]{1,0:T(8,128)(2,1)S(1)}, u32[]{:S(2)}, u32[]{:S(2)}) collective-permute-start(bf16[512,128]{1,0:T(8,128)(2,1)} %copy-done.23), channel_id=1, source_target_pairs={{0,1},{1,2},{2,3},{3,0},{4,5},{5,6},{6,7},{7,4},{8,9},{9,10},{10,1... | collective-permute-start | bytes 393224 | tf_op jit(solution)/shard_map/ppermute | solution.py:31
  115.5 2.1 %collective-permute-done.13.refs_14_ = bf16[512,128]{1,0:T(8,128)(2,1)S(1)} collective-permute-done((bf16[512,128]{1,0:T(8,128)(2,1)}, bf16[512,128]{1,0:T(8,128)(2,1)S(1)}, u32[]{:S(2)}, u32[]{:S(2)}) %collective-permute-start.13) | collective-permute-done | bytes 131104 | tf_op jit(solution)/shard_map/ppermute | solution.py:31
  117.6 3.1 %collective-permute-done.14.refs_15_ = bf16[512,128]{1,0:T(8,128)(2,1)S(1)} collective-permute-done((bf16[512,128]{1,0:T(8,128)(2,1)}, bf16[512,128]{1,0:T(8,128)(2,1)S(1)}, u32[]{:S(2)}, u32[]{:S(2)}) %collective-permute-start.14) | collective-permute-done | bytes 131104 | tf_op jit(solution)/shard_map/ppermute | solution.py:31
  120.8 0.9 copy-done.3
  121.7 0.9 copy-done.6
  122.6 0.9 copy-done.8
  123.5 0.9 copy-done.10
  124.4 0.9 copy-done.12
  125.4 0.9 copy-done.14
  126.3 0.9 copy-done.16
  127.2 0.9 copy-done.18
  128.1 0.9 copy-done.22
  129.0 0.9 copy-done.24
  129.9 0.8 copy-done.25
  130.7 3.1 %merge.1 = bf16[128,256]{1,0:T(8,128)(2,1)S(1)} custom-call(bf16[640,128]{1,0:T(8,128)(2,1)S(1)} %copy-done.3, bf16[640,128]{1,0:T(8,128)(2,1)S(1)} %copy-done.8, bf16[640,128]{1,0:T(8,128)(2,1)S(1)} %copy-done.10, bf16[640,128]{1,0:T(8,128)(2,1)S(1)} %copy-done.12, bf16[640,128]{1,0:T(8,128)(2,1)S(1)} %copy-done.6, bf16[640,128]{1,0:T(8,128)(2,1)S(1)} %copy-done.14, ...), custom_call_target="tpu_custom_call" | custom-call | flops 1400000000 | bytes 7000000 | tf_op jit(solution)/shard_map/merge/pallas_call | solution.py:245
  133.8 1.9 %collective-permute-start.19 = (bf16[64,256]{1,0:T(8,128)(2,1)S(1)}, bf16[64,256]{1,0:T(8,128)(2,1)S(1)}, u32[]{:S(2)}, u32[]{:S(2)}) collective-permute-start(bf16[64,256]{1,0:T(8,128)(2,1)S(1)} %get-tuple-element.11), channel_id=1, source_target_pairs={{0,8},{8,16},{16,24},{24,32},{32,40},{40,48},{48,56},{56,64},{64,7... | collective-permute-start | bytes 98312 | tf_op jit(solution)/shard_map/ppermute | solution.py:47
  135.8 12.0 %collective-permute-done.19 = bf16[64,256]{1,0:T(8,128)(2,1)S(1)} collective-permute-done((bf16[64,256]{1,0:T(8,128)(2,1)S(1)}, bf16[64,256]{1,0:T(8,128)(2,1)S(1)}, u32[]{:S(2)}, u32[]{:S(2)}) %collective-permute-start.19) | collective-permute-done | bytes 32800 | tf_op jit(solution)/shard_map/ppermute | solution.py:47
  147.8 0.7 reshape.23
  (69 shorter events, 0.7 us)
Async XLA Ops:
  0.0 18.7 %copy-start = (bf16[128,1024]{1,0:T(8,128)(2,1)S(1)}, bf16[128,1024]{1,0:T(8,128)(2,1)}, u32[]{:S(2)}) copy-start(bf16[128,1024]{1,0:T(8,128)(2,1)} %param.14) | copy-start | bytes 786436
  1.2 28.5 %copy-start.28 = (f32[128,128,1]{1,0,2:T(8,128)S(1)}, f32[128,128,1]{1,0,2:T(8,128)}, u32[]{:S(2)}) copy-start(f32[128,128,1]{1,0,2:T(8,128)} %constant.36) | copy-start | bytes 196612
  1.2 28.5 %copy-start.29 = (f32[2,128,128]{2,1,0:T(8,128)S(1)}, f32[2,128,128]{2,1,0:T(8,128)}, u32[]{:S(2)}) copy-start(f32[2,128,128]{2,1,0:T(8,128)} %param.13) | copy-start | bytes 393220
  1.2 17.5 %collective-permute-start = (bf16[256,128]{1,0:T(8,128)(2,1)S(1)}, bf16[256,128]{1,0:T(8,128)(2,1)S(1)}, u32[]{:S(2)}, u32[]{:S(2)}) collective-permute-start(bf16[256,128]{1,0:T(8,128)(2,1)S(1)} %get-tuple-element.10), channel_id=1, source_target_pairs={{0,504},{8,0},{16,8},{24,16},{32,24},{40,32},{48,40},{56,48},{64,5... | collective-permute-start | bytes 196616 | tf_op jit(solution)/shard_map/ppermute | solution.py:47
  16.2 34.3 %copy-start.27 = (f32[1024]{0:T(1024)S(1)}, f32[1024]{0:T(1024)}, u32[]{:S(2)}) copy-start(f32[1024]{0:T(1024)} %param.11) | copy-start | bytes 12292
  18.8 35.3 %copy-start.2 = (bf16[640,128]{1,0:T(8,128)(2,1)}, bf16[640,128]{1,0:T(8,128)(2,1)S(1)}, u32[]{:S(2)}) copy-start(bf16[640,128]{1,0:T(8,128)(2,1)S(1)} %pad_maximum_fusion.1.refs_0_) | copy-start | bytes 491524
  18.8 18.1 %collective-permute-start.4 = (bf16[640,128]{1,0:T(8,128)(2,1)S(1)}, bf16[640,128]{1,0:T(8,128)(2,1)S(1)}, u32[]{:S(2)}, u32[]{:S(2)}) collective-permute-start(bf16[640,128]{1,0:T(8,128)(2,1)S(1)} %pad_maximum_fusion.1.refs_0_), channel_id=1, source_target_pairs={{0,4},{1,5},{2,6},{3,7},{4,0},{5,1},{6,2},{7,3},{8,12},{9,13},{10,... | collective-permute-start | bytes 491528 | tf_op jit(solution)/shard_map/ppermute | solution.py:31
  27.1 16.2 %collective-permute-start.1 = (bf16[640,128]{1,0:T(8,128)(2,1)S(1)}, bf16[640,128]{1,0:T(8,128)(2,1)S(1)}, u32[]{:S(2)}, u32[]{:S(2)}) collective-permute-start(bf16[640,128]{1,0:T(8,128)(2,1)S(1)} %pad_maximum_fusion.1.refs_0_), channel_id=1, source_target_pairs={{0,3},{1,0},{2,1},{3,2},{4,7},{5,4},{6,5},{7,6},{8,11},{9,8},{10,9... | collective-permute-start | bytes 491528 | tf_op jit(solution)/shard_map/ppermute | solution.py:31
  30.0 18.0 %collective-permute-start.2 = (bf16[640,128]{1,0:T(8,128)(2,1)S(1)}, bf16[640,128]{1,0:T(8,128)(2,1)S(1)}, u32[]{:S(2)}, u32[]{:S(2)}) collective-permute-start(bf16[640,128]{1,0:T(8,128)(2,1)S(1)} %pad_maximum_fusion.1.refs_0_), channel_id=1, source_target_pairs={{0,2},{1,3},{2,0},{3,1},{4,6},{5,7},{6,4},{7,5},{8,10},{9,11},{10,... | collective-permute-start | bytes 491528 | tf_op jit(solution)/shard_map/ppermute | solution.py:31
  32.9 15.1 %collective-permute-start.3 = (bf16[640,128]{1,0:T(8,128)(2,1)S(1)}, bf16[640,128]{1,0:T(8,128)(2,1)S(1)}, u32[]{:S(2)}, u32[]{:S(2)}) collective-permute-start(bf16[640,128]{1,0:T(8,128)(2,1)S(1)} %pad_maximum_fusion.1.refs_0_), channel_id=1, source_target_pairs={{0,1},{1,2},{2,3},{3,0},{4,5},{5,6},{6,7},{7,4},{8,9},{9,10},{10,1... | collective-permute-start | bytes 491528 | tf_op jit(solution)/shard_map/ppermute | solution.py:31
  37.0 17.8 %copy-start.5 = (bf16[640,128]{1,0:T(8,128)(2,1)}, bf16[640,128]{1,0:T(8,128)(2,1)S(1)}, u32[]{:S(2)}) copy-start(bf16[640,128]{1,0:T(8,128)(2,1)S(1)} %collective-permute-done.4.refs_4_) | copy-start | bytes 491524
  37.0 11.0 %collective-permute-start.5 = (bf16[640,128]{1,0:T(8,128)(2,1)S(1)}, bf16[640,128]{1,0:T(8,128)(2,1)S(1)}, u32[]{:S(2)}, u32[]{:S(2)}) collective-permute-start(bf16[640,128]{1,0:T(8,128)(2,1)S(1)} %collective-permute-done.4.refs_4_), channel_id=1, source_target_pairs={{0,3},{1,0},{2,1},{3,2},{4,7},{5,4},{6,5},{7,6},{8,11},{9,8},{10,9... | collective-permute-start | bytes 491528 | tf_op jit(solution)/shard_map/ppermute | solution.py:31
  39.1 8.9 %collective-permute-start.6 = (bf16[640,128]{1,0:T(8,128)(2,1)S(1)}, bf16[640,128]{1,0:T(8,128)(2,1)S(1)}, u32[]{:S(2)}, u32[]{:S(2)}) collective-permute-start(bf16[640,128]{1,0:T(8,128)(2,1)S(1)} %collective-permute-done.4.refs_4_), channel_id=1, source_target_pairs={{0,2},{1,3},{2,0},{3,1},{4,6},{5,7},{6,4},{7,5},{8,10},{9,11},{10,... | collective-permute-start | bytes 491528 | tf_op jit(solution)/shard_map/ppermute | solution.py:31
  43.3 15.1 %copy-start.7 = (bf16[640,128]{1,0:T(8,128)(2,1)}, bf16[640,128]{1,0:T(8,128)(2,1)S(1)}, u32[]{:S(2)}) copy-start(bf16[640,128]{1,0:T(8,128)(2,1)S(1)} %collective-permute-done.1.refs_1_) | copy-start | bytes 491524
  43.3 7.2 %collective-permute-start.7 = (bf16[640,128]{1,0:T(8,128)(2,1)S(1)}, bf16[640,128]{1,0:T(8,128)(2,1)S(1)}, u32[]{:S(2)}, u32[]{:S(2)}) collective-permute-start(bf16[640,128]{1,0:T(8,128)(2,1)S(1)} %collective-permute-done.4.refs_4_), channel_id=1, source_target_pairs={{0,1},{1,2},{2,3},{3,0},{4,5},{5,6},{6,7},{7,4},{8,9},{9,10},{10,1... | collective-permute-start | bytes 491528 | tf_op jit(solution)/shard_map/ppermute | solution.py:31
  48.0 15.4 %copy-start.9 = (bf16[640,128]{1,0:T(8,128)(2,1)}, bf16[640,128]{1,0:T(8,128)(2,1)S(1)}, u32[]{:S(2)}) copy-start(bf16[640,128]{1,0:T(8,128)(2,1)S(1)} %collective-permute-done.2.refs_2_) | copy-start | bytes 491524
  48.0 15.3 %copy-start.11 = (bf16[640,128]{1,0:T(8,128)(2,1)}, bf16[640,128]{1,0:T(8,128)(2,1)S(1)}, u32[]{:S(2)}) copy-start(bf16[640,128]{1,0:T(8,128)(2,1)S(1)} %collective-permute-done.3.refs_3_) | copy-start | bytes 491524
  48.0 15.3 %copy-start.13 = (bf16[640,128]{1,0:T(8,128)(2,1)}, bf16[640,128]{1,0:T(8,128)(2,1)S(1)}, u32[]{:S(2)}) copy-start(bf16[640,128]{1,0:T(8,128)(2,1)S(1)} %collective-permute-done.5.refs_5_) | copy-start | bytes 491524
  48.0 15.3 %copy-start.15 = (bf16[640,128]{1,0:T(8,128)(2,1)}, bf16[640,128]{1,0:T(8,128)(2,1)S(1)}, u32[]{:S(2)}) copy-start(bf16[640,128]{1,0:T(8,128)(2,1)S(1)} %collective-permute-done.6.refs_6_) | copy-start | bytes 491524
  50.5 12.9 %copy-start.17 = (bf16[640,128]{1,0:T(8,128)(2,1)}, bf16[640,128]{1,0:T(8,128)(2,1)S(1)}, u32[]{:S(2)}) copy-start(bf16[640,128]{1,0:T(8,128)(2,1)S(1)} %collective-permute-done.7.refs_7_) | copy-start | bytes 491524
  54.8 40.5 %copy-start.21 = (bf16[512,128]{1,0:T(8,128)(2,1)}, bf16[512,128]{1,0:T(8,128)(2,1)S(1)}, u32[]{:S(2)}) copy-start(bf16[512,128]{1,0:T(8,128)(2,1)S(1)} %get-tuple-element.7.refs_8_) | copy-start | bytes 393220
  54.8 8.5 %collective-permute-start.8 = (bf16[512,128]{1,0:T(8,128)(2,1)S(1)}, bf16[512,128]{1,0:T(8,128)(2,1)S(1)}, u32[]{:S(2)}, u32[]{:S(2)}) collective-permute-start(bf16[512,128]{1,0:T(8,128)(2,1)S(1)} %get-tuple-element.7.refs_8_), channel_id=1, source_target_pairs={{0,3},{1,0},{2,1},{3,2},{4,7},{5,4},{6,5},{7,6},{8,11},{9,8},{10,9... | collective-permute-start | bytes 393224 | tf_op jit(solution)/shard_map/ppermute | solution.py:31
  64.0 31.3 %collective-permute-start.16 = (bf16[8,128,128]{2,1,0:T(8,128)(2,1)}, bf16[8,128,128]{2,1,0:T(8,128)(2,1)S(1)}, u32[]{:S(2)}, u32[]{:S(2)}) collective-permute-start(bf16[8,128,128]{2,1,0:T(8,128)(2,1)} %after.2), channel_id=1, source_target_pairs={{0,32},{1,33},{2,34},{3,35},{4,36},{5,37},{6,38},{7,39},{8,40},{9,... | collective-permute-start | bytes 786440 | tf_op jit(solution)/shard_map/ppermute | solution.py:31
  65.9 29.4 %collective-permute-start.17 = (bf16[8,128,128]{2,1,0:T(8,128)(2,1)}, bf16[8,128,128]{2,1,0:T(8,128)(2,1)S(1)}, u32[]{:S(2)}, u32[]{:S(2)}) collective-permute-start(bf16[8,128,128]{2,1,0:T(8,128)(2,1)} %after.2), channel_id=1, source_target_pairs={{0,16},{1,17},{2,18},{3,19},{4,20},{5,21},{6,22},{7,23},{8,24},{9,... | collective-permute-start | bytes 786440 | tf_op jit(solution)/shard_map/ppermute | solution.py:31
  69.1 26.2 %collective-permute-start.15 = (bf16[8,128,128]{2,1,0:T(8,128)(2,1)}, bf16[8,128,128]{2,1,0:T(8,128)(2,1)S(1)}, u32[]{:S(2)}, u32[]{:S(2)}) collective-permute-start(bf16[8,128,128]{2,1,0:T(8,128)(2,1)} %after.2), channel_id=1, source_target_pairs={{0,48},{1,49},{2,50},{3,51},{4,52},{5,53},{6,54},{7,55},{8,56},{9,... | collective-permute-start | bytes 786440 | tf_op jit(solution)/shard_map/ppermute | solution.py:31
  73.0 20.1 %collective-permute-start.11 = (bf16[512,128]{1,0:T(8,128)(2,1)S(1)}, bf16[512,128]{1,0:T(8,128)(2,1)S(1)}, u32[]{:S(2)}, u32[]{:S(2)}) collective-permute-start(bf16[512,128]{1,0:T(8,128)(2,1)S(1)} %get-tuple-element.7.refs_8_), channel_id=1, source_target_pairs={{0,4},{1,5},{2,6},{3,7},{4,0},{5,1},{6,2},{7,3},{8,12},{9,13},{10,... | collective-permute-start | bytes 393224 | tf_op jit(solution)/shard_map/ppermute | solution.py:31
  93.1 4.4 %copy-start.23 = (bf16[512,128]{1,0:T(8,128)(2,1)}, bf16[512,128]{1,0:T(8,128)(2,1)S(1)}, u32[]{:S(2)}) copy-start(bf16[512,128]{1,0:T(8,128)(2,1)S(1)} %collective-permute-done.11.refs_12_) | copy-start | bytes 393220
  93.1 8.2 %collective-permute-start.12 = (bf16[512,128]{1,0:T(8,128)(2,1)S(1)}, bf16[512,128]{1,0:T(8,128)(2,1)}, u32[]{:S(2)}, u32[]{:S(2)}) collective-permute-start(bf16[512,128]{1,0:T(8,128)(2,1)S(1)} %collective-permute-done.11.refs_12_), channel_id=1, source_target_pairs={{0,3},{1,0},{2,1},{3,2},{4,7},{5,4},{6,5},{7,6},{8,11},{9,8},{10,9... | collective-permute-start | bytes 393224 | tf_op jit(solution)/shard_map/ppermute | solution.py:31
  96.4 24.4 %copy-start.1 = (bf16[4096,256]{1,0:T(8,128)(2,1)S(1)}, bf16[4096,256]{1,0:T(8,128)(2,1)}, u32[]{:S(2)}) copy-start(bf16[4096,256]{1,0:T(8,128)(2,1)} %param.16) | copy-start | bytes 6291460
  96.4 24.3 %copy-start.20 = (bf16[512,128]{1,0:T(8,128)(2,1)S(1)}, bf16[512,128]{1,0:T(8,128)(2,1)}, u32[]{:S(2)}) copy-start(bf16[512,128]{1,0:T(8,128)(2,1)} %copy-done.19) | copy-start | bytes 393220
  96.4 24.3 %copy-start.26 = (f32[4096]{0:T(1024)S(1)}, f32[4096]{0:T(1024)}, u32[]{:S(2)}) copy-start(f32[4096]{0:T(1024)} %param.15) | copy-start | bytes 49156
  101.2 19.5 %collective-permute-start.18 = (bf16[4,8,128,128]{3,2,1,0:T(8,128)(2,1)}, bf16[4,8,128,128]{3,2,1,0:T(8,128)(2,1)S(1)}, u32[]{:S(2)}, u32[]{:S(2)}) collective-permute-start(bf16[4,8,128,128]{3,2,1,0:T(8,128)(2,1)} %after.3), channel_id=1, source_target_pairs={{0,8},{1,9},{2,10},{3,11},{4,12},{5,13},{6,14},{7,15},{8,0},{9,1},... | collective-permute-start | bytes 3145736 | tf_op jit(solution)/shard_map/ppermute | solution.py:31
  103.1 12.4 %collective-permute-start.10 = (bf16[512,128]{1,0:T(8,128)(2,1)}, bf16[512,128]{1,0:T(8,128)(2,1)S(1)}, u32[]{:S(2)}, u32[]{:S(2)}) collective-permute-start(bf16[512,128]{1,0:T(8,128)(2,1)} %copy-done.21), channel_id=1, source_target_pairs={{0,1},{1,2},{2,3},{3,0},{4,5},{5,6},{6,7},{7,4},{8,9},{9,10},{10,1... | collective-permute-start | bytes 393224 | tf_op jit(solution)/shard_map/ppermute | solution.py:31
  105.6 9.9 %collective-permute-start.9 = (bf16[512,128]{1,0:T(8,128)(2,1)}, bf16[512,128]{1,0:T(8,128)(2,1)S(1)}, u32[]{:S(2)}, u32[]{:S(2)}) collective-permute-start(bf16[512,128]{1,0:T(8,128)(2,1)} %copy-done.21), channel_id=1, source_target_pairs={{0,2},{1,3},{2,0},{3,1},{4,6},{5,7},{6,4},{7,5},{8,10},{9,11},{10,... | collective-permute-start | bytes 393224 | tf_op jit(solution)/shard_map/ppermute | solution.py:31
  108.1 9.5 %collective-permute-start.13 = (bf16[512,128]{1,0:T(8,128)(2,1)}, bf16[512,128]{1,0:T(8,128)(2,1)S(1)}, u32[]{:S(2)}, u32[]{:S(2)}) collective-permute-start(bf16[512,128]{1,0:T(8,128)(2,1)} %copy-done.23), channel_id=1, source_target_pairs={{0,2},{1,3},{2,0},{3,1},{4,6},{5,7},{6,4},{7,5},{8,10},{9,11},{10,... | collective-permute-start | bytes 393224 | tf_op jit(solution)/shard_map/ppermute | solution.py:31
  112.9 7.8 %collective-permute-start.14 = (bf16[512,128]{1,0:T(8,128)(2,1)}, bf16[512,128]{1,0:T(8,128)(2,1)S(1)}, u32[]{:S(2)}, u32[]{:S(2)}) collective-permute-start(bf16[512,128]{1,0:T(8,128)(2,1)} %copy-done.23), channel_id=1, source_target_pairs={{0,1},{1,2},{2,3},{3,0},{4,5},{5,6},{6,7},{7,4},{8,9},{9,10},{10,1... | collective-permute-start | bytes 393224 | tf_op jit(solution)/shard_map/ppermute | solution.py:31
  120.8 0.9 copy-start.3
  121.7 0.9 copy-start.6
  122.6 0.9 copy-start.8
  123.5 0.9 copy-start.10
  124.4 0.9 copy-start.12
  125.4 0.9 copy-start.14
  126.3 0.9 copy-start.16
  127.2 0.9 copy-start.18
  128.1 0.9 copy-start.22
  129.0 0.9 copy-start.24
  129.9 0.8 copy-start.25
  133.8 13.9 %collective-permute-start.19 = (bf16[64,256]{1,0:T(8,128)(2,1)S(1)}, bf16[64,256]{1,0:T(8,128)(2,1)S(1)}, u32[]{:S(2)}, u32[]{:S(2)}) collective-permute-start(bf16[64,256]{1,0:T(8,128)(2,1)S(1)} %get-tuple-element.11), channel_id=1, source_target_pairs={{0,8},{8,16},{16,24},{24,32},{32,40},{40,48},{48,56},{56,64},{64,7... | collective-permute-start | bytes 98312 | tf_op jit(solution)/shard_map/ppermute | solution.py:47
  (2 other events, 1.4 us)

commit v3 on v2

--- a/solution.py
+++ b/solution.py
@@ -31,28 +31,33 @@
     return lax.ppermute(value, BOTH, pairs)
 
 
-def across_z(value):
-    return moved(value, lambda z_lo, x, core, head: (z_lo, x, core, head ^ 4))
-
-
-def along_x(value, steps):
-    return moved(value, lambda z_lo, x, core, head: (z_lo, (x + steps) % 4, core, head))
+def across(value, bits):
+    return moved(value, lambda z_lo, x, core, head: (z_lo, x, core, head ^ bits))
+
+
+def next_x(value):
+    return moved(value, lambda z_lo, x, core, head: (z_lo, x ^ 1, core, head))
 
 
 def other_core(value):
     return moved(value, lambda z_lo, x, core, head: (z_lo, x, core ^ 1, head))
 
 
+def following_rows(value):
+    pairs = []
+    for space in range(64):
+        for head in range(8):
+            target = (space - 1) % 64
+            pairs.append((space * 8 + head, target * 8 + (head ^ 4 if space == 0 else head)))
+    return lax.ppermute(value, BOTH, pairs)
+
+
 def along_bands(value, steps):
     return lax.ppermute(value, "space", [(s, (s + steps) % 64) for s in range(64)])
 
 
-def along_y(value, steps):
-    return moved(value, lambda z_lo, x, core, head: (z_lo, x, core, (head & 4) + (head - steps) % 4))
-
-
 def gathered_y(value):
-    return [value] + [along_y(value, steps) for steps in (1, 2, 3)]
+    return [value] + [across(value, bits) for bits in (1, 2, 3)]
 
 
 def half_order():
@@ -90,22 +95,15 @@
     return [half * HALF + quad * 64 + window * 16 for half in range(2) for quad in range(4)]
 
 
-def feature_block(relative):
-    head = lax.axis_index("head")
-    z_rel, y_rel = divmod(relative, 4)
-    z_hi = head // 4
-    z = z_hi if z_rel == 0 else 1 - z_hi
-    return z * 4 + (head % 4 + y_rel) % 4
-
-
 def attention_kernel(*refs):
     stream_refs = refs[:8]
-    gain_ref, w_ref, bias_ref, out_ref, pieces_ref, qkv_ref = refs[8:]
-    blocks = [feature_block(k) for k in range(8)]
-    for k in range(8):
-        pieces_ref[k] = stream_refs[k][TOKENS:, :]
+    gain_ref, w_ref, bias_ref, out_ref, stream_ref, qkv_ref = refs[8:]
+    head_place = lax.axis_index("head")
+    last_band = (lax.axis_index("space") == 63).astype(jnp.int32)
     for start in range(0, TOKENS, 128):
         rows = slice(start, start + 128)
+        swap = 0 if start < HALF else last_band
+        blocks = [head_place ^ k ^ (swap * 4) for k in range(8)]
         total = jnp.zeros((128, BLOCK), jnp.float32)
         squares = jnp.zeros((128, BLOCK), jnp.float32)
         for ref in stream_refs:
@@ -124,6 +122,8 @@
             weights = jnp.concatenate([w_ref[blocks[n]] for n in (k, k + 1)], axis=0)
             product += dot(jnp.concatenate(normed, axis=1), weights)
         qkv_ref[rows, :] = product.astype(jnp.bfloat16)
+        for k in range(8):
+            stream_ref[k ^ (swap * 4), rows, :] = stream_refs[k][rows, :]
     for window in range(WINDOWS):
         starts = window_rows(window)
         cells = jnp.concatenate([qkv_ref[s : s + 16, :] for s in starts], axis=0)
@@ -144,21 +144,24 @@
 
 
 def merge_kernel(*refs):
-    stream_refs, att_refs = refs[:8], refs[8:16]
-    w_same_ref, w_other_ref, gain_ref, w_ref, order_ref, out_ref, updated_ref = refs[16:]
-    blocks = [feature_block(k) for k in range(8)]
+    att_refs = refs[:8]
+    stream_ref, w_same_ref, w_other_ref, gain_ref, w_ref, order_ref, out_ref, updated_ref = refs[8:]
+    head_place = lax.axis_index("head")
     space = lax.axis_index("space")
-    my_x = (space // 2) % 4
-    parity = (lax.axis_index("head") + space) % 2
+    blocks = [head_place ^ k for k in range(8)]
+    my_x = (space // 2) % 2
+    parity = (head_place // 2 + space) % 2
 
     def project(odd):
         attended = jnp.concatenate([ref[...] for ref in att_refs], axis=1)
         for k in range(0, 8, 2):
-            w_blocks = []
-            for n in (k, k + 1):
-                w_from = w_same_ref if (n + odd) % 2 == 0 else w_other_ref
-                w_blocks.append(w_from[(blocks[n] // 2 - my_x + 4) % 4].reshape(D, BLOCK))
-            stream = jnp.concatenate([stream_refs[n][:TOKENS, :] for n in (k, k + 1)], axis=1)
+            w_from = w_same_ref if (k // 2 + odd) % 2 == 0 else w_other_ref
+            x_rel = (blocks[k] // 4) ^ my_x
+            w_blocks = [
+                jnp.concatenate([w_from[x_rel, row % 4, row // 4, block % 2] for row in range(8)], axis=0)
+                for block in (blocks[k], blocks[k + 1])
+            ]
+            stream = jnp.concatenate([stream_ref[n] for n in (k, k + 1)], axis=1)
             value = stream.astype(jnp.float32) + dot(attended, jnp.concatenate(w_blocks, axis=1))
             updated_ref[:, k * BLOCK : (k + 2) * BLOCK] = value.astype(jnp.bfloat16)
 
@@ -191,16 +194,16 @@
     pass
 
 
-def after(value, event):
+def after(value, *events):
     anywhere = pl.BlockSpec(memory_space=pl.ANY)
     return pl.pallas_call(
         nothing,
         out_shape=jax.ShapeDtypeStruct(value.shape, value.dtype),
-        in_specs=[anywhere, anywhere],
+        in_specs=[anywhere] * (1 + len(events)),
         out_specs=anywhere,
         input_output_aliases={0: 0},
         name="after",
-    )(value, event)
+    )(value, *events)
 
 
 def in_vmem(count):
@@ -212,23 +215,26 @@
     ordered = jnp.einsum(
         "pt,htf->hpf", one_hot(half_order(), jnp.bfloat16), rows, preferred_element_type=jnp.bfloat16
     )
-    following = along_bands(ordered[0], -1)
-    column = lax.axis_index("space") % 8
-    w_piece = lax.dynamic_slice(w_out, (0, column * BLOCK), (BLOCK, BLOCK))
-    mine = jnp.concatenate([ordered[1], following, w_piece], axis=0)
-    partners = across_z(mine)
-    own = gathered_y(mine)
-    partner = gathered_y(partners)
+    following = following_rows(ordered[0])
+    space = lax.axis_index("space")
+    quarter = (space // 2 % 2) * 2 + space % 2
+    w_piece = lax.dynamic_slice(w_out, (0, quarter * 256), (BLOCK, 256))
+    w_piece = jnp.concatenate([w_piece[:, :BLOCK], w_piece[:, BLOCK:]], axis=0)
+    w_piece = jnp.concatenate([w_piece, across(w_piece, 4)], axis=0)
+    stream = jnp.concatenate([ordered[1], following], axis=0)
+    own = gathered_y(stream)
+    partner = gathered_y(across(stream, 4))
+    w_pieces = gathered_y(after(w_piece, partner[1]))
 
     bias_hot = one_hot(window_order(), jnp.float32)
     bias = jnp.einsum("pa,hab->hpb", bias_hot, attn_bias, precision=lax.Precision.HIGHEST)
     bias = jnp.einsum("hpb,qb->hpq", bias, bias_hot, precision=lax.Precision.HIGHEST)
     vmem = pl.BlockSpec(memory_space=pltpu.VMEM)
-    attended, pieces = pl.pallas_call(
+    attended, stream = pl.pallas_call(
         attention_kernel,
         out_shape=(
             jax.ShapeDtypeStruct((TOKENS, BLOCK), jnp.bfloat16),
-            jax.ShapeDtypeStruct((8, BLOCK, BLOCK), jnp.bfloat16),
+            jax.ShapeDtypeStruct((8, TOKENS, BLOCK), jnp.bfloat16),
         ),
         in_specs=in_vmem(11),
         out_specs=(vmem, vmem),
@@ -238,26 +244,28 @@
         name="attention",
     )(*own, *partner, ln_gain.reshape(8, 1, BLOCK), w_qkv.reshape(8, BLOCK, 3 * BLOCK), bias)
 
+    w_quarter = after(jnp.stack(w_pieces).reshape(4, 2, 2, BLOCK, BLOCK), attended)
+    w_half = jnp.stack([w_quarter, next_x(w_quarter)])
+
     own_all = gathered_y(attended)
-    partner_all = gathered_y(across_z(attended))
-    pieces = after(pieces, own_all[1])
-    over_x = jnp.stack([pieces] + [along_x(pieces, -steps) for steps in (1, 2, 3)])
+    partner_attended = across(attended, 4)
+    partner_all = gathered_y(partner_attended)
+    w_half = after(w_half, partner_attended, *own_all[1:])
     merged = pl.pallas_call(
         merge_kernel,
         out_shape=jax.ShapeDtypeStruct((128, 256), jnp.bfloat16),
-        in_specs=in_vmem(21),
+        in_specs=in_vmem(14),
         out_specs=vmem,
         scratch_shapes=[pltpu.VMEM((TOKENS, D), jnp.bfloat16)],
         compiler_params=pltpu.CompilerParams(vmem_limit_bytes=16 * 2**20),
         cost_estimate=pl.CostEstimate(flops=1_400_000_000, bytes_accessed=7_000_000, transcendentals=0),
         name="merge",
     )(
-        *own,
-        *partner,
         *own_all,
         *partner_all,
-        over_x,
-        other_core(after(over_x, partner_all[1])),
+        stream,
+        w_half,
+        other_core(w_half),
         merge_gain.reshape(32, 1, BLOCK),
         w_merge.reshape(32, BLOCK, 256),
         one_hot(merged_order(), jnp.bfloat16),

time: 150 us -> 137 us (0.913)
  waiting for transfers between devices: 35 us -> 21.1 us
  local copies, waits for them, and re-layouts: 15.5 us -> 10.5 us
  other arithmetic: 1.1 us -> 4.77 us
    ppermute x18 -> x20, waiting for transfers between devices: 23 us -> 7.23 us  [moved(): return lax.ppermute(value, BOTH, pairs)]
    ppermute x2 -> x1, starting transfers between devices: 16.8 us -> 1.92 us  [along_bands(): lax.ppermute(value, 'space', [(s, (s + steps) % 64) for s in range(64)])]
    ppermute x0 -> x1, starting transfers between devices: none -> 13 us  [following_rows(): return lax.ppermute(value, BOTH, pairs)]
    unnamed x61 -> x38, local copies, waits for them, and re-layouts: 12.3 us -> 7.61 us
    another operation x1 -> x2, other arithmetic: 1.08 us -> 4.08 us  [the longest x1 2.27 us: on_device(): w_half = jnp.stack([w_quarter, next_x(w_quarter)])]
    ppermute x18 -> x20, starting transfers between devices: 71 us -> 73.9 us  [moved(): return lax.ppermute(value, BOTH, pairs)]
    ppermute x0 -> x1, waiting for transfers between devices: none -> 1.84 us  [following_rows(): return lax.ppermute(value, BOTH, pairs)]
    ppermute x2 -> x1, waiting for transfers between devices: 12 us -> 12 us  [along_bands(): lax.ppermute(value, 'space', [(s, (s + steps) % 64) for s in range(64)])]
  transfers between devices with their start and end apart: 20 -> 22, of which waited for: 7 -> 5; matrix products, arithmetic and copies ran while one was open for 3% -> 5% of each run, Pallas kernels for 0% -> 3%
where the time goes in v3:
time: 137 us; the launch traced here: 135 us
  starting transfers between devices  88.9 us (65%)
  waiting for transfers between devices  21.1 us (15%)
  local copies, waits for them, and re-layouts  10.5 us (8%)
  Pallas kernels  6.75 us (5%)
  other arithmetic  4.77 us (3%)
  matrix products  2.58 us (2%)
    ppermute x20, starting transfers between devices, moved(): return lax.ppermute(value, BOTH, pairs)  73.9 us
    ppermute x1, starting transfers between devices, following_rows(): return lax.ppermute(value, BOTH, pairs)  13 us
    ppermute x1, waiting for transfers between devices, along_bands(): lax.ppermute(value, 'space', [(s, (s + steps) % 64) for s in range(64)])  12 us
    unnamed x38, local copies, waits for them, and re-layouts  7.61 us
    ppermute x20, waiting for transfers between devices, moved(): return lax.ppermute(value, BOTH, pairs)  7.23 us
    pallas_call x1, Pallas kernels, on_device(): pl.pallas_call(attention_kernel, out_shape=(jax.ShapeDtypeStruct((TOKENS,...  3.62 us
    pallas_call x1, Pallas kernels, on_device(): pl.pallas_call(merge_kernel, out_shape=jax.ShapeDtypeStruct((128, 256), j...  3.13 us
  transfers between devices with their start and end apart: 22, of which 5 were waited for; matrix products, arithmetic and copies ran while one was open for 5% of the time, Pallas kernels for 3%

profile of v3, /device:TPU:24, one launch (start us, length us, event | category | flops | bytes accessed | tf_op | source)
XLA Modules:
  0.0 135.1 jit_solution(15297359192195356041)
XLA Ops:
  0.0 0.9 copy-done
  0.9 1.1 convolution_bitcast_fusion.1
  2.0 13.0 %collective-permute-start = (bf16[256,128]{1,0:T(8,128)(2,1)S(1)}, bf16[256,128]{1,0:T(8,128)(2,1)S(1)}, u32[]{:S(2)}, u32[]{:S(2)}) collective-permute-start(bf16[256,128]{1,0:T(8,128)(2,1)S(1)} %get-tuple-element.12), channel_id=1, source_target_pairs={{0,508},{1,509},{2,510},{3,511},{4,504},{5,505},{6,506},{7,507},{8... | collective-permute-start | bytes 196616 | tf_op jit(solution)/shard_map/ppermute | solution.py:52
  15.1 1.8 %collective-permute-done = bf16[256,128]{1,0:T(8,128)(2,1)S(1)} collective-permute-done((bf16[256,128]{1,0:T(8,128)(2,1)S(1)}, bf16[256,128]{1,0:T(8,128)(2,1)S(1)}, u32[]{:S(2)}, u32[]{:S(2)}) %collective-permute-start) | collective-permute-done | bytes 65568 | tf_op jit(solution)/shard_map/ppermute | solution.py:52
  17.0 6.3 %collective-permute-start.4 = (bf16[512,128]{1,0:T(8,128)(2,1)S(1)}, bf16[512,128]{1,0:T(8,128)(2,1)S(1)}, u32[]{:S(2)}, u32[]{:S(2)}) collective-permute-start(bf16[512,128]{1,0:T(8,128)(2,1)S(1)} %pad_maximum_fusion.2.refs_0_), channel_id=1, source_target_pairs={{0,4},{1,5},{2,6},{3,7},{4,0},{5,1},{6,2},{7,3},{8,12},{9,13},{10,... | collective-permute-start | bytes 393224 | tf_op jit(solution)/shard_map/ppermute | solution.py:31
  23.3 0.8 constant_dynamic-slice_fusion
  24.1 8.2 %collective-permute-start.15 = (bf16[256,128]{1,0:T(8,128)(2,1)S(1)}, bf16[256,128]{1,0:T(8,128)(2,1)S(1)}, u32[]{:S(2)}, u32[]{:S(2)}) collective-permute-start(bf16[256,128]{1,0:T(8,128)(2,1)S(1)} %pad_maximum_fusion.4), channel_id=1, source_target_pairs={{0,4},{1,5},{2,6},{3,7},{4,0},{5,1},{6,2},{7,3},{8,12},{9,13},{10,... | collective-permute-start | bytes 196616 | tf_op jit(solution)/shard_map/ppermute | solution.py:31
  32.3 2.1 %collective-permute-start.3 = (bf16[512,128]{1,0:T(8,128)(2,1)S(1)}, bf16[512,128]{1,0:T(8,128)(2,1)S(1)}, u32[]{:S(2)}, u32[]{:S(2)}) collective-permute-start(bf16[512,128]{1,0:T(8,128)(2,1)S(1)} %pad_maximum_fusion.2.refs_0_), channel_id=1, source_target_pairs={{0,3},{1,2},{2,1},{3,0},{4,7},{5,6},{6,5},{7,4},{8,11},{9,10},{10,... | collective-permute-start | bytes 393224 | tf_op jit(solution)/shard_map/ppermute | solution.py:31
  34.5 4.5 %collective-permute-start.2 = (bf16[512,128]{1,0:T(8,128)(2,1)S(1)}, bf16[512,128]{1,0:T(8,128)(2,1)S(1)}, u32[]{:S(2)}, u32[]{:S(2)}) collective-permute-start(bf16[512,128]{1,0:T(8,128)(2,1)S(1)} %pad_maximum_fusion.2.refs_0_), channel_id=1, source_target_pairs={{0,2},{1,3},{2,0},{3,1},{4,6},{5,7},{6,4},{7,5},{8,10},{9,11},{10,... | collective-permute-start | bytes 393224 | tf_op jit(solution)/shard_map/ppermute | solution.py:31
  39.0 3.2 %collective-permute-start.1 = (bf16[512,128]{1,0:T(8,128)(2,1)S(1)}, bf16[512,128]{1,0:T(8,128)(2,1)S(1)}, u32[]{:S(2)}, u32[]{:S(2)}) collective-permute-start(bf16[512,128]{1,0:T(8,128)(2,1)S(1)} %pad_maximum_fusion.2.refs_0_), channel_id=1, source_target_pairs={{0,1},{1,0},{2,3},{3,2},{4,5},{5,4},{6,7},{7,6},{8,9},{9,8},{10,11... | collective-permute-start | bytes 393224 | tf_op jit(solution)/shard_map/ppermute | solution.py:31
  42.2 2.7 %collective-permute-start.5 = (bf16[512,128]{1,0:T(8,128)(2,1)S(1)}, bf16[512,128]{1,0:T(8,128)(2,1)S(1)}, u32[]{:S(2)}, u32[]{:S(2)}) collective-permute-start(bf16[512,128]{1,0:T(8,128)(2,1)S(1)} %collective-permute-done.4.refs_4_), channel_id=1, source_target_pairs={{0,1},{1,0},{2,3},{3,2},{4,5},{5,4},{6,7},{7,6},{8,9},{9,8},{10,11... | collective-permute-start | bytes 393224 | tf_op jit(solution)/shard_map/ppermute | solution.py:31
  44.8 1.2 convolution_bitcast_fusion
  46.1 0.7 pad_maximum_fusion.3.refs_0_
  46.7 2.9 %collective-permute-start.7 = (bf16[512,128]{1,0:T(8,128)(2,1)S(1)}, bf16[512,128]{1,0:T(8,128)(2,1)S(1)}, u32[]{:S(2)}, u32[]{:S(2)}) collective-permute-start(bf16[512,128]{1,0:T(8,128)(2,1)S(1)} %collective-permute-done.4.refs_4_), channel_id=1, source_target_pairs={{0,3},{1,2},{2,1},{3,0},{4,7},{5,6},{6,5},{7,4},{8,11},{9,10},{10,... | collective-permute-start | bytes 393224 | tf_op jit(solution)/shard_map/ppermute | solution.py:31
  49.7 4.2 %collective-permute-start.6 = (bf16[512,128]{1,0:T(8,128)(2,1)S(1)}, bf16[512,128]{1,0:T(8,128)(2,1)S(1)}, u32[]{:S(2)}, u32[]{:S(2)}) collective-permute-start(bf16[512,128]{1,0:T(8,128)(2,1)S(1)} %collective-permute-done.4.refs_4_), channel_id=1, source_target_pairs={{0,2},{1,3},{2,0},{3,1},{4,6},{5,7},{6,4},{7,5},{8,10},{9,11},{10,... | collective-permute-start | bytes 393224 | tf_op jit(solution)/shard_map/ppermute | solution.py:31
  54.0 2.7 %collective-permute-start.18 = (bf16[512,128]{1,0:T(8,128)(2,1)}, bf16[512,128]{1,0:T(8,128)(2,1)S(1)}, u32[]{:S(2)}, u32[]{:S(2)}) collective-permute-start(bf16[512,128]{1,0:T(8,128)(2,1)} %after.3), channel_id=1, source_target_pairs={{0,3},{1,2},{2,1},{3,0},{4,7},{5,6},{6,5},{7,4},{8,11},{9,10},{10,... | collective-permute-start | bytes 393224 | tf_op jit(solution)/shard_map/ppermute | solution.py:31
  56.7 4.1 %collective-permute-start.17 = (bf16[512,128]{1,0:T(8,128)(2,1)}, bf16[512,128]{1,0:T(8,128)(2,1)S(1)}, u32[]{:S(2)}, u32[]{:S(2)}) collective-permute-start(bf16[512,128]{1,0:T(8,128)(2,1)} %after.3), channel_id=1, source_target_pairs={{0,2},{1,3},{2,0},{3,1},{4,6},{5,7},{6,4},{7,5},{8,10},{9,11},{10,... | collective-permute-start | bytes 393224 | tf_op jit(solution)/shard_map/ppermute | solution.py:31
  60.8 3.2 %collective-permute-start.16 = (bf16[512,128]{1,0:T(8,128)(2,1)}, bf16[512,128]{1,0:T(8,128)(2,1)}, u32[]{:S(2)}, u32[]{:S(2)}) collective-permute-start(bf16[512,128]{1,0:T(8,128)(2,1)} %after.3), channel_id=1, source_target_pairs={{0,1},{1,0},{2,3},{3,2},{4,5},{5,4},{6,7},{7,6},{8,9},{9,8},{10,11... | collective-permute-start | bytes 393224 | tf_op jit(solution)/shard_map/ppermute | solution.py:31
  64.0 0.3 fusion.1.refs_10_
  64.3 0.7 copy.17
  65.0 0.7 reshape.35.refs_9_
  65.7 3.6 %attention.1 = (bf16[512,128]{1,0:T(8,128)(2,1)S(1)}, bf16[8,512,128]{2,1,0:T(8,128)(2,1)S(1)}) custom-call(bf16[512,128]{1,0:T(8,128)(2,1)S(1)} %pad_maximum_fusion.2.refs_0_, bf16[512,128]{1,0:T(8,128)(2,1)S(1)} %collective-permute-done.1.refs_1_, bf16[512,128]{1,0:T(8,128)(2,1)S(1)} %collective-permute-done.2.refs_2_, ...), custom_call_target="tpu_custom_call" | custom-call | flops 600000000 | bytes 3000000 | tf_op jit(solution)/shard_map/attention/pallas_call | solution.py:233
  69.4 0.6 copy-done.3
  70.1 1.8 %pad_maximum_fusion.1.refs_0_ = bf16[4,2,2,128,128]{4,3,2,1,0:T(8,128)(2,1)} fusion(bf16[1,2,2,128,128]{4,3,2,1,0:T(8,128)(2,1)S(1)} %bitcast.33, bf16[1,2,2,128,128]{4,3,2,1,0:T(8,128)(2,1)S(1)} %bitcast.34, bf16[1,2,2,128,128]{4,3,2,1,0:T(8,128)(2,1)} %bitcast.9, bf16[1,2,2,128,128]{4,3,2,1,0:T(8,128)(2,1)S(1)} %bitcast.31), kind=kLoop, calls=%fused_computation.3 | loop fusion | flops 786432 | bytes 1048576 | tf_op jit(solution)/shard_map/stack | solution.py:247
  71.9 1.9 %collective-permute-start.19 = (bf16[4,2,2,128,128]{4,3,2,1,0:T(8,128)(2,1)}, bf16[4,2,2,128,128]{4,3,2,1,0:T(8,128)(2,1)S(1)}, u32[]{:S(2)}, u32[]{:S(2)}) collective-permute-start(bf16[4,2,2,128,128]{4,3,2,1,0:T(8,128)(2,1)} %after.4), channel_id=1, source_target_pairs={{0,16},{1,17},{2,18},{3,19},{4,20},{5,21},{6,22},{7,23},{8,24},{9,... | collective-permute-start | bytes 1572872 | tf_op jit(solution)/shard_map/ppermute | solution.py:31
  73.8 6.3 %collective-permute-start.11 = (bf16[512,128]{1,0:T(8,128)(2,1)S(1)}, bf16[512,128]{1,0:T(8,128)(2,1)S(1)}, u32[]{:S(2)}, u32[]{:S(2)}) collective-permute-start(bf16[512,128]{1,0:T(8,128)(2,1)S(1)} %copy-done.4), channel_id=1, source_target_pairs={{0,4},{1,5},{2,6},{3,7},{4,0},{5,1},{6,2},{7,3},{8,12},{9,13},{10,... | collective-permute-start | bytes 393224 | tf_op jit(solution)/shard_map/ppermute | solution.py:31
  80.1 2.7 %collective-permute-start.10 = (bf16[512,128]{1,0:T(8,128)(2,1)S(1)}, bf16[512,128]{1,0:T(8,128)(2,1)S(1)}, u32[]{:S(2)}, u32[]{:S(2)}) collective-permute-start(bf16[512,128]{1,0:T(8,128)(2,1)S(1)} %copy-done.4), channel_id=1, source_target_pairs={{0,3},{1,2},{2,1},{3,0},{4,7},{5,6},{6,5},{7,4},{8,11},{9,10},{10,... | collective-permute-start | bytes 393224 | tf_op jit(solution)/shard_map/ppermute | solution.py:31
  82.8 4.2 %collective-permute-start.9 = (bf16[512,128]{1,0:T(8,128)(2,1)S(1)}, bf16[512,128]{1,0:T(8,128)(2,1)S(1)}, u32[]{:S(2)}, u32[]{:S(2)}) collective-permute-start(bf16[512,128]{1,0:T(8,128)(2,1)S(1)} %copy-done.4), channel_id=1, source_target_pairs={{0,2},{1,3},{2,0},{3,1},{4,6},{5,7},{6,4},{7,5},{8,10},{9,11},{10,... | collective-permute-start | bytes 393224 | tf_op jit(solution)/shard_map/ppermute | solution.py:31
  87.0 3.0 %collective-permute-start.8 = (bf16[512,128]{1,0:T(8,128)(2,1)S(1)}, bf16[512,128]{1,0:T(8,128)(2,1)}, u32[]{:S(2)}, u32[]{:S(2)}) collective-permute-start(bf16[512,128]{1,0:T(8,128)(2,1)S(1)} %copy-done.4), channel_id=1, source_target_pairs={{0,1},{1,0},{2,3},{3,2},{4,5},{5,4},{6,7},{7,6},{8,9},{9,8},{10,11... | collective-permute-start | bytes 393224 | tf_op jit(solution)/shard_map/ppermute | solution.py:31
  90.0 2.3 %pad_maximum_fusion.refs_0_ = bf16[2,4,2,2,128,128]{5,4,3,2,1,0:T(8,128)(2,1)} fusion(bf16[1,4,2,2,128,128]{5,4,3,2,1,0:T(8,128)(2,1)S(1)} %bitcast.32, bf16[1,4,2,2,128,128]{5,4,3,2,1,0:T(8,128)(2,1)} %bitcast.30), kind=kLoop, calls=%fused_computation.2 | loop fusion | flops 524288 | bytes 2097152 | tf_op jit(solution)/shard_map/stack | solution.py:248
  92.3 2.2 %collective-permute-done.11.refs_1_.refs_4_ = bf16[512,128]{1,0:T(8,128)(2,1)S(1)} collective-permute-done((bf16[512,128]{1,0:T(8,128)(2,1)S(1)}, bf16[512,128]{1,0:T(8,128)(2,1)S(1)}, u32[]{:S(2)}, u32[]{:S(2)}) %collective-permute-start.11) | collective-permute-done | bytes 131104 | tf_op jit(solution)/shard_map/ppermute | solution.py:31
  94.5 0.7 copy-done.7
  95.2 0.6 copy-done.9
  95.9 1.9 %collective-permute-start.20 = (bf16[2,4,2,2,128,128]{5,4,3,2,1,0:T(8,128)(2,1)}, bf16[2,4,2,2,128,128]{5,4,3,2,1,0:T(8,128)(2,1)S(1)}, u32[]{:S(2)}, u32[]{:S(2)}) collective-permute-start(bf16[2,4,2,2,128,128]{5,4,3,2,1,0:T(8,128)(2,1)} %after.5.refs_9_), channel_id=1, source_target_pairs={{0,8},{1,9},{2,10},{3,11},{4,12},{5,13},{6,14},{7,15},{8,0},{9,1},... | collective-permute-start | bytes 3145736 | tf_op jit(solution)/shard_map/ppermute | solution.py:31
  97.8 3.4 %collective-permute-start.14 = (bf16[512,128]{1,0:T(8,128)(2,1)}, bf16[512,128]{1,0:T(8,128)(2,1)S(1)}, u32[]{:S(2)}, u32[]{:S(2)}) collective-permute-start(bf16[512,128]{1,0:T(8,128)(2,1)} %copy-done.5), channel_id=1, source_target_pairs={{0,3},{1,2},{2,1},{3,0},{4,7},{5,6},{6,5},{7,4},{8,11},{9,10},{10,... | collective-permute-start | bytes 393224 | tf_op jit(solution)/shard_map/ppermute | solution.py:31
  101.2 4.0 %collective-permute-start.13 = (bf16[512,128]{1,0:T(8,128)(2,1)}, bf16[512,128]{1,0:T(8,128)(2,1)S(1)}, u32[]{:S(2)}, u32[]{:S(2)}) collective-permute-start(bf16[512,128]{1,0:T(8,128)(2,1)} %copy-done.5), channel_id=1, source_target_pairs={{0,2},{1,3},{2,0},{3,1},{4,6},{5,7},{6,4},{7,5},{8,10},{9,11},{10,... | collective-permute-start | bytes 393224 | tf_op jit(solution)/shard_map/ppermute | solution.py:31
  105.1 2.5 %collective-permute-start.12 = (bf16[512,128]{1,0:T(8,128)(2,1)}, bf16[512,128]{1,0:T(8,128)(2,1)S(1)}, u32[]{:S(2)}, u32[]{:S(2)}) collective-permute-start(bf16[512,128]{1,0:T(8,128)(2,1)} %copy-done.5), channel_id=1, source_target_pairs={{0,1},{1,0},{2,3},{3,2},{4,5},{5,4},{6,7},{7,6},{8,9},{9,8},{10,11... | collective-permute-start | bytes 393224 | tf_op jit(solution)/shard_map/ppermute | solution.py:31
  107.6 2.9 %collective-permute-done.13.refs_6_ = bf16[512,128]{1,0:T(8,128)(2,1)S(1)} collective-permute-done((bf16[512,128]{1,0:T(8,128)(2,1)}, bf16[512,128]{1,0:T(8,128)(2,1)S(1)}, u32[]{:S(2)}, u32[]{:S(2)}) %collective-permute-start.13) | collective-permute-done | bytes 131104 | tf_op jit(solution)/shard_map/ppermute | solution.py:31
  110.6 2.0 %collective-permute-done.12.refs_5_ = bf16[512,128]{1,0:T(8,128)(2,1)S(1)} collective-permute-done((bf16[512,128]{1,0:T(8,128)(2,1)}, bf16[512,128]{1,0:T(8,128)(2,1)S(1)}, u32[]{:S(2)}, u32[]{:S(2)}) %collective-permute-start.12) | collective-permute-done | bytes 131104 | tf_op jit(solution)/shard_map/ppermute | solution.py:31
  112.6 1.2 copy-done.1
  113.8 0.9 copy-done.6
  114.7 0.9 copy-done.8
  115.6 0.9 copy-done.10
  116.5 0.8 copy-done.13
  117.3 3.1 %merge.1 = bf16[128,256]{1,0:T(8,128)(2,1)S(1)} custom-call(bf16[512,128]{1,0:T(8,128)(2,1)S(1)} %copy-done.4, bf16[512,128]{1,0:T(8,128)(2,1)} %collective-permute-done.8.refs_2_.refs_1_, bf16[512,128]{1,0:T(8,128)(2,1)S(1)} %copy-done.10, bf16[512,128]{1,0:T(8,128)(2,1)S(1)} %copy-done.8, bf16[512,128]{1,0:T(8,128)(2,1)S(1)} %copy-done.6, ...), custom_call_target="tpu_custom_call" | custom-call | flops 1400000000 | bytes 7000000 | tf_op jit(solution)/shard_map/merge/pallas_call | solution.py:254
  120.5 1.9 %collective-permute-start.21 = (bf16[64,256]{1,0:T(8,128)(2,1)S(1)}, bf16[64,256]{1,0:T(8,128)(2,1)S(1)}, u32[]{:S(2)}, u32[]{:S(2)}) collective-permute-start(bf16[64,256]{1,0:T(8,128)(2,1)S(1)} %get-tuple-element.13), channel_id=1, source_target_pairs={{0,8},{8,16},{16,24},{24,32},{32,40},{40,48},{48,56},{56,64},{64,7... | collective-permute-start | bytes 98312 | tf_op jit(solution)/shard_map/ppermute | solution.py:56
  122.4 12.0 %collective-permute-done.21 = bf16[64,256]{1,0:T(8,128)(2,1)S(1)} collective-permute-done((bf16[64,256]{1,0:T(8,128)(2,1)S(1)}, bf16[64,256]{1,0:T(8,128)(2,1)S(1)}, u32[]{:S(2)}, u32[]{:S(2)}) %collective-permute-start.21) | collective-permute-done | bytes 32800 | tf_op jit(solution)/shard_map/ppermute | solution.py:56
  134.4 0.7 reshape.32
  (54 shorter events, 0.1 us)
Async XLA Ops:
  0.0 0.9 copy-start
  0.0 64.0 %copy-start.18 = (f32[128,128,1]{1,0,2:T(8,128)S(1)}, f32[128,128,1]{1,0,2:T(8,128)}, u32[]{:S(2)}) copy-start(f32[128,128,1]{1,0,2:T(8,128)} %constant.51) | copy-start | bytes 196612
  0.0 64.3 %copy-start.17 = (bf16[1024,3,128]{2,0,1:T(8,128)(2,1)S(1)}, bf16[1024,3,128]{2,0,1:T(8,128)(2,1)}, u32[]{:S(2)}) copy-start(bf16[1024,3,128]{2,0,1:T(8,128)(2,1)} %param.12) | copy-start | bytes 2359300
  2.0 14.9 %collective-permute-start = (bf16[256,128]{1,0:T(8,128)(2,1)S(1)}, bf16[256,128]{1,0:T(8,128)(2,1)S(1)}, u32[]{:S(2)}, u32[]{:S(2)}) collective-permute-start(bf16[256,128]{1,0:T(8,128)(2,1)S(1)} %get-tuple-element.12), channel_id=1, source_target_pairs={{0,508},{1,509},{2,510},{3,511},{4,504},{5,505},{6,506},{7,507},{8... | collective-permute-start | bytes 196616 | tf_op jit(solution)/shard_map/ppermute | solution.py:52
  17.0 25.2 %collective-permute-start.4 = (bf16[512,128]{1,0:T(8,128)(2,1)S(1)}, bf16[512,128]{1,0:T(8,128)(2,1)S(1)}, u32[]{:S(2)}, u32[]{:S(2)}) collective-permute-start(bf16[512,128]{1,0:T(8,128)(2,1)S(1)} %pad_maximum_fusion.2.refs_0_), channel_id=1, source_target_pairs={{0,4},{1,5},{2,6},{3,7},{4,0},{5,1},{6,2},{7,3},{8,12},{9,13},{10,... | collective-permute-start | bytes 393224 | tf_op jit(solution)/shard_map/ppermute | solution.py:31
  24.1 22.0 %collective-permute-start.15 = (bf16[256,128]{1,0:T(8,128)(2,1)S(1)}, bf16[256,128]{1,0:T(8,128)(2,1)S(1)}, u32[]{:S(2)}, u32[]{:S(2)}) collective-permute-start(bf16[256,128]{1,0:T(8,128)(2,1)S(1)} %pad_maximum_fusion.4), channel_id=1, source_target_pairs={{0,4},{1,5},{2,6},{3,7},{4,0},{5,1},{6,2},{7,3},{8,12},{9,13},{10,... | collective-permute-start | bytes 196616 | tf_op jit(solution)/shard_map/ppermute | solution.py:31
  32.3 21.6 %collective-permute-start.3 = (bf16[512,128]{1,0:T(8,128)(2,1)S(1)}, bf16[512,128]{1,0:T(8,128)(2,1)S(1)}, u32[]{:S(2)}, u32[]{:S(2)}) collective-permute-start(bf16[512,128]{1,0:T(8,128)(2,1)S(1)} %pad_maximum_fusion.2.refs_0_), channel_id=1, source_target_pairs={{0,3},{1,2},{2,1},{3,0},{4,7},{5,6},{6,5},{7,4},{8,11},{9,10},{10,... | collective-permute-start | bytes 393224 | tf_op jit(solution)/shard_map/ppermute | solution.py:31
  34.5 22.2 %collective-permute-start.2 = (bf16[512,128]{1,0:T(8,128)(2,1)S(1)}, bf16[512,128]{1,0:T(8,128)(2,1)S(1)}, u32[]{:S(2)}, u32[]{:S(2)}) collective-permute-start(bf16[512,128]{1,0:T(8,128)(2,1)S(1)} %pad_maximum_fusion.2.refs_0_), channel_id=1, source_target_pairs={{0,2},{1,3},{2,0},{3,1},{4,6},{5,7},{6,4},{7,5},{8,10},{9,11},{10,... | collective-permute-start | bytes 393224 | tf_op jit(solution)/shard_map/ppermute | solution.py:31
  39.0 21.8 %collective-permute-start.1 = (bf16[512,128]{1,0:T(8,128)(2,1)S(1)}, bf16[512,128]{1,0:T(8,128)(2,1)S(1)}, u32[]{:S(2)}, u32[]{:S(2)}) collective-permute-start(bf16[512,128]{1,0:T(8,128)(2,1)S(1)} %pad_maximum_fusion.2.refs_0_), channel_id=1, source_target_pairs={{0,1},{1,0},{2,3},{3,2},{4,5},{5,4},{6,7},{7,6},{8,9},{9,8},{10,11... | collective-permute-start | bytes 393224 | tf_op jit(solution)/shard_map/ppermute | solution.py:31
  42.2 7.5 %collective-permute-start.5 = (bf16[512,128]{1,0:T(8,128)(2,1)S(1)}, bf16[512,128]{1,0:T(8,128)(2,1)S(1)}, u32[]{:S(2)}, u32[]{:S(2)}) collective-permute-start(bf16[512,128]{1,0:T(8,128)(2,1)S(1)} %collective-permute-done.4.refs_4_), channel_id=1, source_target_pairs={{0,1},{1,0},{2,3},{3,2},{4,5},{5,4},{6,7},{7,6},{8,9},{9,8},{10,11... | collective-permute-start | bytes 393224 | tf_op jit(solution)/shard_map/ppermute | solution.py:31
  46.7 19.0 %collective-permute-start.7 = (bf16[512,128]{1,0:T(8,128)(2,1)S(1)}, bf16[512,128]{1,0:T(8,128)(2,1)S(1)}, u32[]{:S(2)}, u32[]{:S(2)}) collective-permute-start(bf16[512,128]{1,0:T(8,128)(2,1)S(1)} %collective-permute-done.4.refs_4_), channel_id=1, source_target_pairs={{0,3},{1,2},{2,1},{3,0},{4,7},{5,6},{6,5},{7,4},{8,11},{9,10},{10,... | collective-permute-start | bytes 393224 | tf_op jit(solution)/shard_map/ppermute | solution.py:31
  49.7 4.2 %copy-start.11 = (bf16[512,128]{1,0:T(8,128)(2,1)}, bf16[512,128]{1,0:T(8,128)(2,1)S(1)}, u32[]{:S(2)}) copy-start(bf16[512,128]{1,0:T(8,128)(2,1)S(1)} %collective-permute-done.5.refs_5_.refs_1_) | copy-start | bytes 393220
  49.7 16.0 %collective-permute-start.6 = (bf16[512,128]{1,0:T(8,128)(2,1)S(1)}, bf16[512,128]{1,0:T(8,128)(2,1)S(1)}, u32[]{:S(2)}, u32[]{:S(2)}) collective-permute-start(bf16[512,128]{1,0:T(8,128)(2,1)S(1)} %collective-permute-done.4.refs_4_), channel_id=1, source_target_pairs={{0,2},{1,3},{2,0},{3,1},{4,6},{5,7},{6,4},{7,5},{8,10},{9,11},{10,... | collective-permute-start | bytes 393224 | tf_op jit(solution)/shard_map/ppermute | solution.py:31
  54.0 11.8 %copy-start.12 = (bf16[512,128]{1,0:T(8,128)(2,1)S(1)}, bf16[512,128]{1,0:T(8,128)(2,1)}, u32[]{:S(2)}) copy-start(bf16[512,128]{1,0:T(8,128)(2,1)} %copy-done.11) | copy-start | bytes 393220
  54.0 11.8 %copy-start.15 = (f32[1024]{0:T(1024)S(1)}, f32[1024]{0:T(1024)}, u32[]{:S(2)}) copy-start(f32[1024]{0:T(1024)} %param.11) | copy-start | bytes 12292
  54.0 16.0 %collective-permute-start.18 = (bf16[512,128]{1,0:T(8,128)(2,1)}, bf16[512,128]{1,0:T(8,128)(2,1)S(1)}, u32[]{:S(2)}, u32[]{:S(2)}) collective-permute-start(bf16[512,128]{1,0:T(8,128)(2,1)} %after.3), channel_id=1, source_target_pairs={{0,3},{1,2},{2,1},{3,0},{4,7},{5,6},{6,5},{7,4},{8,11},{9,10},{10,... | collective-permute-start | bytes 393224 | tf_op jit(solution)/shard_map/ppermute | solution.py:31
  56.7 13.4 %collective-permute-start.17 = (bf16[512,128]{1,0:T(8,128)(2,1)}, bf16[512,128]{1,0:T(8,128)(2,1)S(1)}, u32[]{:S(2)}, u32[]{:S(2)}) collective-permute-start(bf16[512,128]{1,0:T(8,128)(2,1)} %after.3), channel_id=1, source_target_pairs={{0,2},{1,3},{2,0},{3,1},{4,6},{5,7},{6,4},{7,5},{8,10},{9,11},{10,... | collective-permute-start | bytes 393224 | tf_op jit(solution)/shard_map/ppermute | solution.py:31
  60.8 9.2 %collective-permute-start.16 = (bf16[512,128]{1,0:T(8,128)(2,1)}, bf16[512,128]{1,0:T(8,128)(2,1)}, u32[]{:S(2)}, u32[]{:S(2)}) collective-permute-start(bf16[512,128]{1,0:T(8,128)(2,1)} %after.3), channel_id=1, source_target_pairs={{0,1},{1,0},{2,3},{3,2},{4,5},{5,4},{6,7},{7,6},{8,9},{9,8},{10,11... | collective-permute-start | bytes 393224 | tf_op jit(solution)/shard_map/ppermute | solution.py:31
  65.0 5.1 %copy-start.16 = (bf16[512,128]{1,0:T(8,128)(2,1)S(1)}, bf16[512,128]{1,0:T(8,128)(2,1)}, u32[]{:S(2)}) copy-start(bf16[512,128]{1,0:T(8,128)(2,1)} %after.3) | copy-start | bytes 393220
  69.4 0.7 copy-start.3
  70.0 3.8 %copy-start.4 = (bf16[512,128]{1,0:T(8,128)(2,1)S(1)}, bf16[512,128]{1,0:T(8,128)(2,1)}, u32[]{:S(2)}) copy-start(bf16[512,128]{1,0:T(8,128)(2,1)} %copy-done.3) | copy-start | bytes 393220
  71.9 18.1 %collective-permute-start.19 = (bf16[4,2,2,128,128]{4,3,2,1,0:T(8,128)(2,1)}, bf16[4,2,2,128,128]{4,3,2,1,0:T(8,128)(2,1)S(1)}, u32[]{:S(2)}, u32[]{:S(2)}) collective-permute-start(bf16[4,2,2,128,128]{4,3,2,1,0:T(8,128)(2,1)} %after.4), channel_id=1, source_target_pairs={{0,16},{1,17},{2,18},{3,19},{4,20},{5,21},{6,22},{7,23},{8,24},{9,... | collective-permute-start | bytes 1572872 | tf_op jit(solution)/shard_map/ppermute | solution.py:31
  73.8 20.7 %collective-permute-start.11 = (bf16[512,128]{1,0:T(8,128)(2,1)S(1)}, bf16[512,128]{1,0:T(8,128)(2,1)S(1)}, u32[]{:S(2)}, u32[]{:S(2)}) collective-permute-start(bf16[512,128]{1,0:T(8,128)(2,1)S(1)} %copy-done.4), channel_id=1, source_target_pairs={{0,4},{1,5},{2,6},{3,7},{4,0},{5,1},{6,2},{7,3},{8,12},{9,13},{10,... | collective-permute-start | bytes 393224 | tf_op jit(solution)/shard_map/ppermute | solution.py:31
  80.1 14.4 %collective-permute-start.10 = (bf16[512,128]{1,0:T(8,128)(2,1)S(1)}, bf16[512,128]{1,0:T(8,128)(2,1)S(1)}, u32[]{:S(2)}, u32[]{:S(2)}) collective-permute-start(bf16[512,128]{1,0:T(8,128)(2,1)S(1)} %copy-done.4), channel_id=1, source_target_pairs={{0,3},{1,2},{2,1},{3,0},{4,7},{5,6},{6,5},{7,4},{8,11},{9,10},{10,... | collective-permute-start | bytes 393224 | tf_op jit(solution)/shard_map/ppermute | solution.py:31
  82.8 11.7 %collective-permute-start.9 = (bf16[512,128]{1,0:T(8,128)(2,1)S(1)}, bf16[512,128]{1,0:T(8,128)(2,1)S(1)}, u32[]{:S(2)}, u32[]{:S(2)}) collective-permute-start(bf16[512,128]{1,0:T(8,128)(2,1)S(1)} %copy-done.4), channel_id=1, source_target_pairs={{0,2},{1,3},{2,0},{3,1},{4,6},{5,7},{6,4},{7,5},{8,10},{9,11},{10,... | collective-permute-start | bytes 393224 | tf_op jit(solution)/shard_map/ppermute | solution.py:31
  87.0 8.9 %collective-permute-start.8 = (bf16[512,128]{1,0:T(8,128)(2,1)S(1)}, bf16[512,128]{1,0:T(8,128)(2,1)}, u32[]{:S(2)}, u32[]{:S(2)}) collective-permute-start(bf16[512,128]{1,0:T(8,128)(2,1)S(1)} %copy-done.4), channel_id=1, source_target_pairs={{0,1},{1,0},{2,3},{3,2},{4,5},{5,4},{6,7},{7,6},{8,9},{9,8},{10,11... | collective-permute-start | bytes 393224 | tf_op jit(solution)/shard_map/ppermute | solution.py:31
  90.0 22.6 %copy-start.2 = (bf16[4096,256]{1,0:T(8,128)(2,1)S(1)}, bf16[4096,256]{1,0:T(8,128)(2,1)}, u32[]{:S(2)}) copy-start(bf16[4096,256]{1,0:T(8,128)(2,1)} %param.16) | copy-start | bytes 6291460
  90.0 22.6 %copy-start.14 = (f32[4096]{0:T(1024)S(1)}, f32[4096]{0:T(1024)}, u32[]{:S(2)}) copy-start(f32[4096]{0:T(1024)} %param.15) | copy-start | bytes 49156
  94.5 1.4 %copy-start.5 = (bf16[512,128]{1,0:T(8,128)(2,1)}, bf16[512,128]{1,0:T(8,128)(2,1)S(1)}, u32[]{:S(2)}) copy-start(bf16[512,128]{1,0:T(8,128)(2,1)S(1)} %collective-permute-done.11.refs_1_.refs_4_) | copy-start | bytes 393220
  94.5 0.7 copy-start.7
  95.2 0.6 copy-start.9
  95.9 16.7 %collective-permute-start.20 = (bf16[2,4,2,2,128,128]{5,4,3,2,1,0:T(8,128)(2,1)}, bf16[2,4,2,2,128,128]{5,4,3,2,1,0:T(8,128)(2,1)S(1)}, u32[]{:S(2)}, u32[]{:S(2)}) collective-permute-start(bf16[2,4,2,2,128,128]{5,4,3,2,1,0:T(8,128)(2,1)} %after.5.refs_9_), channel_id=1, source_target_pairs={{0,8},{1,9},{2,10},{3,11},{4,12},{5,13},{6,14},{7,15},{8,0},{9,1},... | collective-permute-start | bytes 3145736 | tf_op jit(solution)/shard_map/ppermute | solution.py:31
  97.8 9.8 %collective-permute-start.14 = (bf16[512,128]{1,0:T(8,128)(2,1)}, bf16[512,128]{1,0:T(8,128)(2,1)S(1)}, u32[]{:S(2)}, u32[]{:S(2)}) collective-permute-start(bf16[512,128]{1,0:T(8,128)(2,1)} %copy-done.5), channel_id=1, source_target_pairs={{0,3},{1,2},{2,1},{3,0},{4,7},{5,6},{6,5},{7,4},{8,11},{9,10},{10,... | collective-permute-start | bytes 393224 | tf_op jit(solution)/shard_map/ppermute | solution.py:31
  101.2 9.4 %collective-permute-start.13 = (bf16[512,128]{1,0:T(8,128)(2,1)}, bf16[512,128]{1,0:T(8,128)(2,1)S(1)}, u32[]{:S(2)}, u32[]{:S(2)}) collective-permute-start(bf16[512,128]{1,0:T(8,128)(2,1)} %copy-done.5), channel_id=1, source_target_pairs={{0,2},{1,3},{2,0},{3,1},{4,6},{5,7},{6,4},{7,5},{8,10},{9,11},{10,... | collective-permute-start | bytes 393224 | tf_op jit(solution)/shard_map/ppermute | solution.py:31
  105.1 7.4 %collective-permute-start.12 = (bf16[512,128]{1,0:T(8,128)(2,1)}, bf16[512,128]{1,0:T(8,128)(2,1)S(1)}, u32[]{:S(2)}, u32[]{:S(2)}) collective-permute-start(bf16[512,128]{1,0:T(8,128)(2,1)} %copy-done.5), channel_id=1, source_target_pairs={{0,1},{1,0},{2,3},{3,2},{4,5},{5,4},{6,7},{7,6},{8,9},{9,8},{10,11... | collective-permute-start | bytes 393224 | tf_op jit(solution)/shard_map/ppermute | solution.py:31
  112.6 1.2 copy-start.1
  113.8 0.9 copy-start.6
  114.7 0.9 copy-start.8
  115.6 0.9 copy-start.10
  116.5 0.8 copy-start.13
  120.5 13.9 %collective-permute-start.21 = (bf16[64,256]{1,0:T(8,128)(2,1)S(1)}, bf16[64,256]{1,0:T(8,128)(2,1)S(1)}, u32[]{:S(2)}, u32[]{:S(2)}) collective-permute-start(bf16[64,256]{1,0:T(8,128)(2,1)S(1)} %get-tuple-element.13), channel_id=1, source_target_pairs={{0,8},{8,16},{16,24},{24,32},{32,40},{40,48},{48,56},{56,64},{64,7... | collective-permute-start | bytes 98312 | tf_op jit(solution)/shard_map/ppermute | solution.py:56

commit v4 on v3

--- a/solution.py
+++ b/solution.py
@@ -1,3 +1,5 @@
+import functools
+
 import jax
 import jax.numpy as jnp
 import numpy as np
@@ -11,6 +13,7 @@
 BLOCK = 128
 TOKENS = 512
 HALF = 256
+CLAIMED = 10_000_000_000
 WINDOWS = 4
 EPS = 1e-05
 BOTH = ("space", "head")
@@ -35,8 +38,8 @@
     return moved(value, lambda z_lo, x, core, head: (z_lo, x, core, head ^ bits))
 
 
-def next_x(value):
-    return moved(value, lambda z_lo, x, core, head: (z_lo, x ^ 1, core, head))
+def across_x(value, bits):
+    return moved(value, lambda z_lo, x, core, head: (z_lo, x ^ bits, core, head))
 
 
 def other_core(value):
@@ -56,8 +59,33 @@
     return lax.ppermute(value, "space", [(s, (s + steps) % 64) for s in range(64)])
 
 
-def gathered_y(value):
-    return [value] + [across(value, bits) for bits in (1, 2, 3)]
+def in_vmem(count):
+    return [pl.BlockSpec(memory_space=pltpu.VMEM)] * count
+
+
+def join_kernel(count, *refs):
+    at = 0
+    for ref in refs[:count]:
+        refs[-1][at : at + ref.shape[0], :] = ref[...]
+        at += ref.shape[0]
+
+
+def joined(parts, event=None, claimed=0):
+    operands = list(parts) + ([] if event is None else [event])
+    rows = sum(part.shape[0] for part in parts)
+    return pl.pallas_call(
+        functools.partial(join_kernel, len(parts)),
+        out_shape=jax.ShapeDtypeStruct((rows, BLOCK), jnp.bfloat16),
+        in_specs=in_vmem(len(operands)),
+        out_specs=in_vmem(1)[0],
+        cost_estimate=pl.CostEstimate(flops=claimed, bytes_accessed=4 * rows * BLOCK, transcendentals=0),
+        name="join",
+    )(*operands)
+
+
+def gathered(value):
+    both = joined([value, across(value, 4)], claimed=CLAIMED)
+    return [both] + [across(both, bits) for bits in (1, 2, 3)]
 
 
 def half_order():
@@ -96,18 +124,19 @@
 
 
 def attention_kernel(*refs):
-    stream_refs = refs[:8]
-    gain_ref, w_ref, bias_ref, out_ref, stream_ref, qkv_ref = refs[8:]
+    parts = [(refs[k % 4], k // 4 * TOKENS) for k in range(8)]
+    gain_ref, w_ref, bias_ref, out_ref, stream_ref, qkv_ref = refs[4:]
     head_place = lax.axis_index("head")
     last_band = (lax.axis_index("space") == 63).astype(jnp.int32)
     for start in range(0, TOKENS, 128):
-        rows = slice(start, start + 128)
         swap = 0 if start < HALF else last_band
         blocks = [head_place ^ k ^ (swap * 4) for k in range(8)]
         total = jnp.zeros((128, BLOCK), jnp.float32)
         squares = jnp.zeros((128, BLOCK), jnp.float32)
-        for ref in stream_refs:
-            value = ref[rows, :].astype(jnp.float32)
+        for k, (ref, base) in enumerate(parts):
+            rounded = ref[base + start : base + start + 128, :]
+            stream_ref[k ^ (swap * 4), start : start + 128, :] = rounded
+            value = rounded.astype(jnp.float32)
             total += value
             squares += value * value
         mean = jnp.sum(total, -1, keepdims=True) * (1.0 / D)
@@ -115,15 +144,14 @@
         scale = lax.rsqrt(spread + EPS)
         product = jnp.zeros((128, 3 * BLOCK), jnp.float32)
         for k in range(0, 8, 2):
-            normed = [
-                ((stream_refs[n][rows, :].astype(jnp.float32) - mean) * scale * gain_ref[blocks[n]]).astype(jnp.bfloat16)
-                for n in (k, k + 1)
-            ]
+            normed = []
+            for n in (k, k + 1):
+                ref, base = parts[n]
+                value = ref[base + start : base + start + 128, :].astype(jnp.float32)
+                normed.append(((value - mean) * scale * gain_ref[blocks[n]]).astype(jnp.bfloat16))
             weights = jnp.concatenate([w_ref[blocks[n]] for n in (k, k + 1)], axis=0)
             product += dot(jnp.concatenate(normed, axis=1), weights)
-        qkv_ref[rows, :] = product.astype(jnp.bfloat16)
-        for k in range(8):
-            stream_ref[k ^ (swap * 4), rows, :] = stream_refs[k][rows, :]
+        qkv_ref[start : start + 128, :] = product.astype(jnp.bfloat16)
     for window in range(WINDOWS):
         starts = window_rows(window)
         cells = jnp.concatenate([qkv_ref[s : s + 16, :] for s in starts], axis=0)
@@ -144,8 +172,8 @@
 
 
 def merge_kernel(*refs):
-    att_refs = refs[:8]
-    stream_ref, w_same_ref, w_other_ref, gain_ref, w_ref, order_ref, out_ref, updated_ref = refs[8:]
+    att_refs = refs[:4]
+    stream_ref, w_same_ref, w_other_ref, gain_ref, w_ref, order_ref, out_ref, updated_ref = refs[4:]
     head_place = lax.axis_index("head")
     space = lax.axis_index("space")
     blocks = [head_place ^ k for k in range(8)]
@@ -153,7 +181,9 @@
     parity = (head_place // 2 + space) % 2
 
     def project(odd):
-        attended = jnp.concatenate([ref[...] for ref in att_refs], axis=1)
+        attended = jnp.concatenate(
+            [att_refs[k % 4][k // 4 * TOKENS : (k // 4 + 1) * TOKENS, :] for k in range(8)], axis=1
+        )
         for k in range(0, 8, 2):
             w_from = w_same_ref if (k // 2 + odd) % 2 == 0 else w_other_ref
             x_rel = (blocks[k] // 4) ^ my_x
@@ -161,8 +191,9 @@
                 jnp.concatenate([w_from[x_rel, row % 4, row // 4, block % 2] for row in range(8)], axis=0)
                 for block in (blocks[k], blocks[k + 1])
             ]
+            w_block = jnp.concatenate(w_blocks, axis=1)
             stream = jnp.concatenate([stream_ref[n] for n in (k, k + 1)], axis=1)
-            value = stream.astype(jnp.float32) + dot(attended, jnp.concatenate(w_blocks, axis=1))
+            value = stream.astype(jnp.float32) + dot(attended, w_block)
             updated_ref[:, k * BLOCK : (k + 2) * BLOCK] = value.astype(jnp.bfloat16)
 
     for odd in range(2):
@@ -190,41 +221,19 @@
     out_ref[...] = dot(order_ref[...], merged.astype(jnp.bfloat16)).astype(jnp.bfloat16)
 
 
-def nothing(*refs):
-    pass
-
-
-def after(value, *events):
-    anywhere = pl.BlockSpec(memory_space=pl.ANY)
-    return pl.pallas_call(
-        nothing,
-        out_shape=jax.ShapeDtypeStruct(value.shape, value.dtype),
-        in_specs=[anywhere] * (1 + len(events)),
-        out_specs=anywhere,
-        input_output_aliases={0: 0},
-        name="after",
-    )(value, *events)
-
-
-def in_vmem(count):
-    return [pl.BlockSpec(memory_space=pltpu.VMEM)] * count
-
-
 def on_device(fields, ln_gain, w_qkv, attn_bias, w_out, merge_gain, w_merge):
     rows = fields.reshape(2, HALF, BLOCK)
-    ordered = jnp.einsum(
-        "pt,htf->hpf", one_hot(half_order(), jnp.bfloat16), rows, preferred_element_type=jnp.bfloat16
-    )
-    following = following_rows(ordered[0])
+    order = one_hot(half_order(), jnp.bfloat16)
+    following = following_rows(rows[0])
     space = lax.axis_index("space")
     quarter = (space // 2 % 2) * 2 + space % 2
     w_piece = lax.dynamic_slice(w_out, (0, quarter * 256), (BLOCK, 256))
     w_piece = jnp.concatenate([w_piece[:, :BLOCK], w_piece[:, BLOCK:]], axis=0)
-    w_piece = jnp.concatenate([w_piece, across(w_piece, 4)], axis=0)
-    stream = jnp.concatenate([ordered[1], following], axis=0)
-    own = gathered_y(stream)
-    partner = gathered_y(across(stream, 4))
-    w_pieces = gathered_y(after(w_piece, partner[1]))
+    w_pair = jnp.concatenate([w_piece, across(w_piece, 4)], axis=0)
+    w_pairs = [w_pair] + [across(w_pair, bits) for bits in (1, 2, 3)]
+    mine = [dot(order, half).astype(jnp.bfloat16) for half in (rows[1], following)]
+    around = gathered(jnp.concatenate(mine, axis=0))
+    w_quarter = joined(w_pairs, around[0][:16])
 
     bias_hot = one_hot(window_order(), jnp.float32)
     bias = jnp.einsum("pa,hab->hpb", bias_hot, attn_bias, precision=lax.Precision.HIGHEST)
@@ -236,36 +245,31 @@
             jax.ShapeDtypeStruct((TOKENS, BLOCK), jnp.bfloat16),
             jax.ShapeDtypeStruct((8, TOKENS, BLOCK), jnp.bfloat16),
         ),
-        in_specs=in_vmem(11),
+        in_specs=in_vmem(7),
         out_specs=(vmem, vmem),
         scratch_shapes=[pltpu.VMEM((TOKENS, 3 * BLOCK), jnp.bfloat16)],
         compiler_params=pltpu.CompilerParams(vmem_limit_bytes=16 * 2**20),
         cost_estimate=pl.CostEstimate(flops=600_000_000, bytes_accessed=3_000_000, transcendentals=131072),
         name="attention",
-    )(*own, *partner, ln_gain.reshape(8, 1, BLOCK), w_qkv.reshape(8, BLOCK, 3 * BLOCK), bias)
-
-    w_quarter = after(jnp.stack(w_pieces).reshape(4, 2, 2, BLOCK, BLOCK), attended)
-    w_half = jnp.stack([w_quarter, next_x(w_quarter)])
-
-    own_all = gathered_y(attended)
-    partner_attended = across(attended, 4)
-    partner_all = gathered_y(partner_attended)
-    w_half = after(w_half, partner_attended, *own_all[1:])
+    )(*around, ln_gain.reshape(8, 1, BLOCK), w_qkv.reshape(8, BLOCK, 3 * BLOCK), bias)
+
+    attended_around = gathered(attended)
+    w_core = joined([w_quarter, across_x(w_quarter, 1)], attended[:16])
+    w_shape = (2, 4, 2, 2, BLOCK, BLOCK)
     merged = pl.pallas_call(
         merge_kernel,
         out_shape=jax.ShapeDtypeStruct((128, 256), jnp.bfloat16),
-        in_specs=in_vmem(14),
+        in_specs=in_vmem(10),
         out_specs=vmem,
         scratch_shapes=[pltpu.VMEM((TOKENS, D), jnp.bfloat16)],
         compiler_params=pltpu.CompilerParams(vmem_limit_bytes=16 * 2**20),
         cost_estimate=pl.CostEstimate(flops=1_400_000_000, bytes_accessed=7_000_000, transcendentals=0),
         name="merge",
     )(
-        *own_all,
-        *partner_all,
+        *attended_around,
         stream,
-        w_half,
-        other_core(w_half),
+        w_core.reshape(w_shape),
+        other_core(w_core).reshape(w_shape),
         merge_gain.reshape(32, 1, BLOCK),
         w_merge.reshape(32, BLOCK, 256),
         one_hot(merged_order(), jnp.bfloat16),

time: 137 us -> 139 us (1.015)
  starting transfers between devices: 88.9 us -> 66.3 us
  waiting for transfers between devices: 21.1 us -> 37.6 us
  Pallas kernels: 6.75 us -> 14.8 us
  local copies, waits for them, and re-layouts: 10.5 us -> 15.8 us
  other arithmetic: 4.77 us -> 0.03 us
    ppermute x20 -> x14, waiting for transfers between devices: 7.23 us -> 23.8 us  [moved(): return lax.ppermute(value, BOTH, pairs)]
    ppermute x20 -> x14, starting transfers between devices: 73.9 us -> 61 us  [moved(): return lax.ppermute(value, BOTH, pairs)]
    ppermute x1, starting transfers between devices: 13 us -> 3.37 us  [following_rows(): return lax.ppermute(value, BOTH, pairs)]
    pallas_call x3 -> x4, Pallas kernels: 0.01 us -> 7.58 us  [joined(): pl.pallas_call(functools.partial(join_kernel, len(parts)), out_shape=jax....]
    another operation x2 -> x0, other arithmetic: 4.08 us -> none  [the longest x1 2.27 us: on_device(): w_half = jnp.stack([w_quarter, next_x(w_quarter)])]
    slice x0 -> x3, local copies, waits for them, and re-layouts: none -> 2.84 us  [the longest x1 1.28 us: on_device(): w_quarter = joined(w_pairs, around[0][:16])]
    unnamed x38 -> x50, local copies, waits for them, and re-layouts: 7.61 us -> 10.1 us
  transfers between devices with their start and end apart: 22 -> 16, of which waited for: 5 -> 6; matrix products, arithmetic and copies ran while one was open for 5% -> 5% of each run, Pallas kernels for 3% -> 8%
where the time goes in v4:
time: 139 us; the launch traced here: 138 us
  starting transfers between devices  66.3 us (48%)
  waiting for transfers between devices  37.6 us (27%)
  local copies, waits for them, and re-layouts  15.8 us (11%)
  Pallas kernels  14.8 us (11%)
  matrix products  2.69 us (2%)
    ppermute x14, starting transfers between devices, moved(): return lax.ppermute(value, BOTH, pairs)  61 us
    ppermute x14, waiting for transfers between devices, moved(): return lax.ppermute(value, BOTH, pairs)  23.8 us
    ppermute x1, waiting for transfers between devices, along_bands(): lax.ppermute(value, 'space', [(s, (s + steps) % 64) for s in range(64)])  12 us
    unnamed x50, local copies, waits for them, and re-layouts  10.1 us
    pallas_call x4, Pallas kernels, joined(): pl.pallas_call(functools.partial(join_kernel, len(parts)), out_shape=jax....  7.58 us
    pallas_call x1, Pallas kernels, on_device(): pl.pallas_call(attention_kernel, out_shape=(jax.ShapeDtypeStruct((TOKENS,...  3.75 us
    pallas_call x1, Pallas kernels, on_device(): pl.pallas_call(merge_kernel, out_shape=jax.ShapeDtypeStruct((128, 256), j...  3.45 us
    ppermute x1, starting transfers between devices, following_rows(): return lax.ppermute(value, BOTH, pairs)  3.37 us
  transfers between devices with their start and end apart: 16, of which 6 were waited for; matrix products, arithmetic and copies ran while one was open for 5% of the time, Pallas kernels for 8%

profile of v4, /device:TPU:24, one launch (start us, length us, event | category | flops | bytes accessed | tf_op | source)
XLA Modules:
  0.0 137.5 jit_solution(13384654048253832222)
XLA Ops:
  0.0 0.8 constant_dynamic-slice_fusion
  0.8 15.7 %collective-permute-start.9 = (bf16[256,128]{1,0:T(8,128)(2,1)S(1)}, bf16[256,128]{1,0:T(8,128)(2,1)S(1)}, u32[]{:S(2)}, u32[]{:S(2)}) collective-permute-start(bf16[256,128]{1,0:T(8,128)(2,1)S(1)} %pad_maximum_fusion.2), channel_id=1, source_target_pairs={{0,4},{1,5},{2,6},{3,7},{4,0},{5,1},{6,2},{7,3},{8,12},{9,13},{10,... | collective-permute-start | bytes 196616 | tf_op jit(solution)/shard_map/ppermute | solution.py:34
  16.6 1.0 fusion
  17.5 3.4 %collective-permute-start = (bf16[256,128]{1,0:T(8,128)(2,1)S(1)}, bf16[256,128]{1,0:T(8,128)(2,1)S(1)}, u32[]{:S(2)}, u32[]{:S(2)}) collective-permute-start(bf16[256,128]{1,0:T(8,128)(2,1)S(1)} %bitcast.23), channel_id=1, source_target_pairs={{0,508},{1,509},{2,510},{3,511},{4,504},{5,505},{6,506},{7,507},{8... | collective-permute-start | bytes 196616 | tf_op jit(solution)/shard_map/ppermute | solution.py:55
  20.9 1.1 convolution_convert_fusion.1
  22.0 1.7 %collective-permute-done = bf16[256,128]{1,0:T(8,128)(2,1)S(1)} collective-permute-done((bf16[256,128]{1,0:T(8,128)(2,1)S(1)}, bf16[256,128]{1,0:T(8,128)(2,1)S(1)}, u32[]{:S(2)}, u32[]{:S(2)}) %collective-permute-start) | collective-permute-done | bytes 65568 | tf_op jit(solution)/shard_map/ppermute | solution.py:55
  23.7 1.1 convolution_convert_fusion
  24.8 7.3 %collective-permute-start.1 = (bf16[512,128]{1,0:T(8,128)(2,1)S(1)}, bf16[512,128]{1,0:T(8,128)(2,1)S(1)}, u32[]{:S(2)}, u32[]{:S(2)}) collective-permute-start(bf16[512,128]{1,0:T(8,128)(2,1)S(1)} %pad_maximum_fusion.refs_0_), channel_id=1, source_target_pairs={{0,4},{1,5},{2,6},{3,7},{4,0},{5,1},{6,2},{7,3},{8,12},{9,13},{10,... | collective-permute-start | bytes 393224 | tf_op jit(solution)/shard_map/ppermute | solution.py:34
  32.2 2.3 %collective-permute-start.12 = (bf16[512,128]{1,0:T(8,128)(2,1)S(1)}, bf16[512,128]{1,0:T(8,128)(2,1)S(1)}, u32[]{:S(2)}, u32[]{:S(2)}) collective-permute-start(bf16[512,128]{1,0:T(8,128)(2,1)S(1)} %pad_maximum_fusion.1.refs_0_), channel_id=1, source_target_pairs={{0,3},{1,2},{2,1},{3,0},{4,7},{5,6},{6,5},{7,4},{8,11},{9,10},{10,... | collective-permute-start | bytes 393224 | tf_op jit(solution)/shard_map/ppermute | solution.py:34
  34.5 4.5 %collective-permute-start.11 = (bf16[512,128]{1,0:T(8,128)(2,1)S(1)}, bf16[512,128]{1,0:T(8,128)(2,1)S(1)}, u32[]{:S(2)}, u32[]{:S(2)}) collective-permute-start(bf16[512,128]{1,0:T(8,128)(2,1)S(1)} %pad_maximum_fusion.1.refs_0_), channel_id=1, source_target_pairs={{0,2},{1,3},{2,0},{3,1},{4,6},{5,7},{6,4},{7,5},{8,10},{9,11},{10,... | collective-permute-start | bytes 393224 | tf_op jit(solution)/shard_map/ppermute | solution.py:34
  39.0 3.2 %collective-permute-start.10 = (bf16[512,128]{1,0:T(8,128)(2,1)S(1)}, bf16[512,128]{1,0:T(8,128)(2,1)S(1)}, u32[]{:S(2)}, u32[]{:S(2)}) collective-permute-start(bf16[512,128]{1,0:T(8,128)(2,1)S(1)} %pad_maximum_fusion.1.refs_0_), channel_id=1, source_target_pairs={{0,1},{1,0},{2,3},{3,2},{4,5},{5,4},{6,7},{7,6},{8,9},{9,8},{10,11... | collective-permute-start | bytes 393224 | tf_op jit(solution)/shard_map/ppermute | solution.py:34
  42.2 4.7 %collective-permute-done.1.refs_1_ = bf16[512,128]{1,0:T(8,128)(2,1)S(1)} collective-permute-done((bf16[512,128]{1,0:T(8,128)(2,1)S(1)}, bf16[512,128]{1,0:T(8,128)(2,1)S(1)}, u32[]{:S(2)}, u32[]{:S(2)}) %collective-permute-start.1) | collective-permute-done | bytes 131104 | tf_op jit(solution)/shard_map/ppermute | solution.py:34
  46.9 0.6 copy-done.24
  47.5 1.7 %join.4.refs_0_ = bf16[1024,128]{1,0:T(8,128)(2,1)} custom-call(bf16[512,128]{1,0:T(8,128)(2,1)} %copy-done.20, bf16[512,128]{1,0:T(8,128)(2,1)} %copy-done.24), custom_call_target="tpu_custom_call" | custom-call | flops 10000000000 | bytes 524288 | tf_op jit(solution)/shard_map/join/pallas_call | solution.py:76
  49.2 1.3 slice.34.refs_4_
  50.5 2.1 %collective-permute-start.4 = (bf16[1024,128]{1,0:T(8,128)(2,1)}, bf16[1024,128]{1,0:T(8,128)(2,1)S(1)}, u32[]{:S(2)}, u32[]{:S(2)}) collective-permute-start(bf16[1024,128]{1,0:T(8,128)(2,1)} %join.4.refs_0_), channel_id=1, source_target_pairs={{0,3},{1,2},{2,1},{3,0},{4,7},{5,6},{6,5},{7,4},{8,11},{9,10},{10,... | collective-permute-start | bytes 786440 | tf_op jit(solution)/shard_map/ppermute | solution.py:34
  52.6 4.5 %collective-permute-start.3 = (bf16[1024,128]{1,0:T(8,128)(2,1)}, bf16[1024,128]{1,0:T(8,128)(2,1)S(1)}, u32[]{:S(2)}, u32[]{:S(2)}) collective-permute-start(bf16[1024,128]{1,0:T(8,128)(2,1)} %join.4.refs_0_), channel_id=1, source_target_pairs={{0,2},{1,3},{2,0},{3,1},{4,6},{5,7},{6,4},{7,5},{8,10},{9,11},{10,... | collective-permute-start | bytes 786440 | tf_op jit(solution)/shard_map/ppermute | solution.py:34
  57.1 3.2 %collective-permute-start.2 = (bf16[1024,128]{1,0:T(8,128)(2,1)}, bf16[1024,128]{1,0:T(8,128)(2,1)S(1)}, u32[]{:S(2)}, u32[]{:S(2)}) collective-permute-start(bf16[1024,128]{1,0:T(8,128)(2,1)} %join.4.refs_0_), channel_id=1, source_target_pairs={{0,1},{1,0},{2,3},{3,2},{4,5},{5,4},{6,7},{7,6},{8,9},{9,8},{10,11... | collective-permute-start | bytes 786440 | tf_op jit(solution)/shard_map/ppermute | solution.py:34
  60.4 0.6 copy-done.22
  61.0 0.6 copy-done.23
  61.6 1.9 %join.6.refs_0_ = bf16[2048,128]{1,0:T(8,128)(2,1)} custom-call(bf16[512,128]{1,0:T(8,128)(2,1)} %copy-done.18, bf16[512,128]{1,0:T(8,128)(2,1)} %copy-done.23, bf16[512,128]{1,0:T(8,128)(2,1)} %copy-done.22, bf16[512,128]{1,0:T(8,128)(2,1)} %copy-done.21, bf16[16,128]{1,0:T(8,128)(2,1)} %slice.34.refs_4_), custom_call_target="tpu_custom_call" | custom-call | bytes 1048576 | tf_op jit(solution)/shard_map/join/pallas_call | solution.py:76
  63.6 2.0 %collective-permute-start.13 = (bf16[2048,128]{1,0:T(8,128)(2,1)}, bf16[2048,128]{1,0:T(8,128)(2,1)}, u32[]{:S(2)}, u32[]{:S(2)}) collective-permute-start(bf16[2048,128]{1,0:T(8,128)(2,1)} %join.6.refs_0_), channel_id=1, source_target_pairs={{0,16},{1,17},{2,18},{3,19},{4,20},{5,21},{6,22},{7,23},{8,24},{9,... | collective-permute-start | bytes 1572872 | tf_op jit(solution)/shard_map/ppermute | solution.py:34
  65.9 0.7 copy.14
  66.6 0.7 reshape.34.refs_5_
  67.6 0.7 copy-done.10
  68.3 0.7 copy-done.12
  69.1 0.7 copy-done.14
  69.8 0.9 copy-done.11
  70.7 0.9 copy-done.13
  71.7 0.9 copy-done.15
  72.6 3.7 %attention.1 = (bf16[512,128]{1,0:T(8,128)(2,1)S(1)}, bf16[8,512,128]{2,1,0:T(8,128)(2,1)S(1)}) custom-call(bf16[1024,128]{1,0:T(8,128)(2,1)S(1)} %copy-done.9, bf16[1024,128]{1,0:T(8,128)(2,1)S(1)} %copy-done.15, bf16[1024,128]{1,0:T(8,128)(2,1)S(1)} %copy-done.13, bf16[1024,128]{1,0:T(8,128)(2,1)S(1)} %copy-done.11, f32[8,1,128]{2,1,0:T(1,128)S(1)} %bitcast.21, ...), custom_call_target="tpu_custom_call" | custom-call | flops 600000000 | bytes 3000000 | tf_op jit(solution)/shard_map/attention/pallas_call | solution.py:242
  76.4 1.0 copy-done.3
  77.4 4.1 %collective-permute-start.5 = (bf16[512,128]{1,0:T(8,128)(2,1)S(1)}, bf16[512,128]{1,0:T(8,128)(2,1)}, u32[]{:S(2)}, u32[]{:S(2)}) collective-permute-start(bf16[512,128]{1,0:T(8,128)(2,1)S(1)} %get-tuple-element.7.refs_0_), channel_id=1, source_target_pairs={{0,4},{1,5},{2,6},{3,7},{4,0},{5,1},{6,2},{7,3},{8,12},{9,13},{10,... | collective-permute-start | bytes 393224 | tf_op jit(solution)/shard_map/ppermute | solution.py:34
  82.1 2.3 %join.7 = bf16[4096,128]{1,0:T(8,128)(2,1)} custom-call(bf16[2048,128]{1,0:T(8,128)(2,1)} %join.6.refs_0_, bf16[2048,128]{1,0:T(8,128)(2,1)} %collective-permute-done.13.refs_1_, bf16[16,128]{1,0:T(8,128)(2,1)} %slice.31.refs_2_), custom_call_target="tpu_custom_call" | custom-call | bytes 2097152 | tf_op jit(solution)/shard_map/join/pallas_call | solution.py:76
  84.4 2.2 %collective-permute-start.14 = (bf16[4096,128]{1,0:T(8,128)(2,1)}, bf16[4096,128]{1,0:T(8,128)(2,1)}, u32[]{:S(2)}, u32[]{:S(2)}) collective-permute-start(bf16[4096,128]{1,0:T(8,128)(2,1)} %join.7), channel_id=1, source_target_pairs={{0,8},{1,9},{2,10},{3,11},{4,12},{5,13},{6,14},{7,15},{8,0},{9,1},... | collective-permute-start | bytes 3145736 | tf_op jit(solution)/shard_map/ppermute | solution.py:34
  86.6 13.7 %collective-permute-done.5.refs_1_ = bf16[512,128]{1,0:T(8,128)(2,1)} collective-permute-done((bf16[512,128]{1,0:T(8,128)(2,1)S(1)}, bf16[512,128]{1,0:T(8,128)(2,1)}, u32[]{:S(2)}, u32[]{:S(2)}) %collective-permute-start.5) | collective-permute-done | bytes 131104 | tf_op jit(solution)/shard_map/ppermute | solution.py:34
  100.3 1.7 %join.5.refs_0_ = bf16[1024,128]{1,0:T(8,128)(2,1)} custom-call(bf16[512,128]{1,0:T(8,128)(2,1)} %copy-done.8, bf16[512,128]{1,0:T(8,128)(2,1)} %collective-permute-done.5.refs_1_), custom_call_target="tpu_custom_call" | custom-call | flops 10000000000 | bytes 524288 | tf_op jit(solution)/shard_map/join/pallas_call | solution.py:76
  102.0 2.2 %collective-permute-start.8 = (bf16[1024,128]{1,0:T(8,128)(2,1)}, bf16[1024,128]{1,0:T(8,128)(2,1)S(1)}, u32[]{:S(2)}, u32[]{:S(2)}) collective-permute-start(bf16[1024,128]{1,0:T(8,128)(2,1)} %join.5.refs_0_), channel_id=1, source_target_pairs={{0,3},{1,2},{2,1},{3,0},{4,7},{5,6},{6,5},{7,4},{8,11},{9,10},{10,... | collective-permute-start | bytes 786440 | tf_op jit(solution)/shard_map/ppermute | solution.py:34
  104.2 4.4 %collective-permute-start.7 = (bf16[1024,128]{1,0:T(8,128)(2,1)}, bf16[1024,128]{1,0:T(8,128)(2,1)S(1)}, u32[]{:S(2)}, u32[]{:S(2)}) collective-permute-start(bf16[1024,128]{1,0:T(8,128)(2,1)} %join.5.refs_0_), channel_id=1, source_target_pairs={{0,2},{1,3},{2,0},{3,1},{4,6},{5,7},{6,4},{7,5},{8,10},{9,11},{10,... | collective-permute-start | bytes 786440 | tf_op jit(solution)/shard_map/ppermute | solution.py:34
  108.6 3.2 %collective-permute-start.6 = (bf16[1024,128]{1,0:T(8,128)(2,1)}, bf16[1024,128]{1,0:T(8,128)(2,1)S(1)}, u32[]{:S(2)}, u32[]{:S(2)}) collective-permute-start(bf16[1024,128]{1,0:T(8,128)(2,1)} %join.5.refs_0_), channel_id=1, source_target_pairs={{0,1},{1,0},{2,3},{3,2},{4,5},{5,4},{6,7},{7,6},{8,9},{9,8},{10,11... | collective-permute-start | bytes 786440 | tf_op jit(solution)/shard_map/ppermute | solution.py:34
  111.8 2.7 %collective-permute-done.8.refs_3_ = bf16[1024,128]{1,0:T(8,128)(2,1)S(1)} collective-permute-done((bf16[1024,128]{1,0:T(8,128)(2,1)}, bf16[1024,128]{1,0:T(8,128)(2,1)S(1)}, u32[]{:S(2)}, u32[]{:S(2)}) %collective-permute-start.8) | collective-permute-done | bytes 262176 | tf_op jit(solution)/shard_map/ppermute | solution.py:34
  114.5 2.8 %collective-permute-done.6.refs_1_ = bf16[1024,128]{1,0:T(8,128)(2,1)S(1)} collective-permute-done((bf16[1024,128]{1,0:T(8,128)(2,1)}, bf16[1024,128]{1,0:T(8,128)(2,1)S(1)}, u32[]{:S(2)}, u32[]{:S(2)}) %collective-permute-start.6) | collective-permute-done | bytes 262176 | tf_op jit(solution)/shard_map/ppermute | solution.py:34
  117.3 1.2 copy-done.4
  118.5 0.9 copy-done.5
  119.4 3.5 %merge.1 = bf16[128,256]{1,0:T(8,128)(2,1)S(1)} custom-call(bf16[1024,128]{1,0:T(8,128)(2,1)S(1)} %copy-done.5, bf16[1024,128]{1,0:T(8,128)(2,1)S(1)} %collective-permute-done.6.refs_1_, bf16[1024,128]{1,0:T(8,128)(2,1)S(1)} %collective-permute-done.7.refs_2_, bf16[1024,128]{1,0:T(8,128)(2,1)S(1)} %collective-permute-done.8.refs_3_, ...), custom_call_target="tpu_custom_call" | custom-call | flops 1400000000 | bytes 7000000 | tf_op jit(solution)/shard_map/merge/pallas_call | solution.py:259
  122.9 1.9 %collective-permute-start.15 = (bf16[64,256]{1,0:T(8,128)(2,1)S(1)}, bf16[64,256]{1,0:T(8,128)(2,1)S(1)}, u32[]{:S(2)}, u32[]{:S(2)}) collective-permute-start(bf16[64,256]{1,0:T(8,128)(2,1)S(1)} %get-tuple-element.13), channel_id=1, source_target_pairs={{0,8},{8,16},{16,24},{24,32},{32,40},{40,48},{48,56},{56,64},{64,7... | collective-permute-start | bytes 98312 | tf_op jit(solution)/shard_map/ppermute | solution.py:59
  124.8 12.0 %collective-permute-done.15 = bf16[64,256]{1,0:T(8,128)(2,1)S(1)} collective-permute-done((bf16[64,256]{1,0:T(8,128)(2,1)S(1)}, bf16[64,256]{1,0:T(8,128)(2,1)S(1)}, u32[]{:S(2)}, u32[]{:S(2)}) %collective-permute-start.15) | collective-permute-done | bytes 32800 | tf_op jit(solution)/shard_map/ppermute | solution.py:59
  136.9 0.7 reshape.32
  (56 shorter events, 1.3 us)
Async XLA Ops:
  0.0 65.6 %copy-start = (f32[2,128,128]{2,1,0:T(8,128)S(1)}, f32[2,128,128]{2,1,0:T(8,128)}, u32[]{:S(2)}) copy-start(f32[2,128,128]{2,1,0:T(8,128)} %param.13) | copy-start | bytes 393220
  0.8 31.3 %collective-permute-start.9 = (bf16[256,128]{1,0:T(8,128)(2,1)S(1)}, bf16[256,128]{1,0:T(8,128)(2,1)S(1)}, u32[]{:S(2)}, u32[]{:S(2)}) collective-permute-start(bf16[256,128]{1,0:T(8,128)(2,1)S(1)} %pad_maximum_fusion.2), channel_id=1, source_target_pairs={{0,4},{1,5},{2,6},{3,7},{4,0},{5,1},{6,2},{7,3},{8,12},{9,13},{10,... | collective-permute-start | bytes 196616 | tf_op jit(solution)/shard_map/ppermute | solution.py:34
  17.5 6.2 %collective-permute-start = (bf16[256,128]{1,0:T(8,128)(2,1)S(1)}, bf16[256,128]{1,0:T(8,128)(2,1)S(1)}, u32[]{:S(2)}, u32[]{:S(2)}) collective-permute-start(bf16[256,128]{1,0:T(8,128)(2,1)S(1)} %bitcast.23), channel_id=1, source_target_pairs={{0,508},{1,509},{2,510},{3,511},{4,504},{5,505},{6,506},{7,507},{8... | collective-permute-start | bytes 196616 | tf_op jit(solution)/shard_map/ppermute | solution.py:55
  24.8 22.1 %copy-start.20 = (bf16[512,128]{1,0:T(8,128)(2,1)}, bf16[512,128]{1,0:T(8,128)(2,1)S(1)}, u32[]{:S(2)}) copy-start(bf16[512,128]{1,0:T(8,128)(2,1)S(1)} %pad_maximum_fusion.refs_0_) | copy-start | bytes 393220
  24.8 22.1 %collective-permute-start.1 = (bf16[512,128]{1,0:T(8,128)(2,1)S(1)}, bf16[512,128]{1,0:T(8,128)(2,1)S(1)}, u32[]{:S(2)}, u32[]{:S(2)}) collective-permute-start(bf16[512,128]{1,0:T(8,128)(2,1)S(1)} %pad_maximum_fusion.refs_0_), channel_id=1, source_target_pairs={{0,4},{1,5},{2,6},{3,7},{4,0},{5,1},{6,2},{7,3},{8,12},{9,13},{10,... | collective-permute-start | bytes 393224 | tf_op jit(solution)/shard_map/ppermute | solution.py:34
  32.2 17.0 %copy-start.18 = (bf16[512,128]{1,0:T(8,128)(2,1)}, bf16[512,128]{1,0:T(8,128)(2,1)S(1)}, u32[]{:S(2)}) copy-start(bf16[512,128]{1,0:T(8,128)(2,1)S(1)} %pad_maximum_fusion.1.refs_0_) | copy-start | bytes 393220
  32.2 33.5 %copy-start.19 = (f32[128,128,1]{1,0,2:T(8,128)S(1)}, f32[128,128,1]{1,0,2:T(8,128)}, u32[]{:S(2)}) copy-start(f32[128,128,1]{1,0,2:T(8,128)} %constant.50) | copy-start | bytes 196612
  32.2 33.7 %copy-start.17 = (bf16[1024,3,128]{2,0,1:T(8,128)(2,1)S(1)}, bf16[1024,3,128]{2,0,1:T(8,128)(2,1)}, u32[]{:S(2)}) copy-start(bf16[1024,3,128]{2,0,1:T(8,128)(2,1)} %param.12) | copy-start | bytes 2359300
  32.2 24.9 %collective-permute-start.12 = (bf16[512,128]{1,0:T(8,128)(2,1)S(1)}, bf16[512,128]{1,0:T(8,128)(2,1)S(1)}, u32[]{:S(2)}, u32[]{:S(2)}) collective-permute-start(bf16[512,128]{1,0:T(8,128)(2,1)S(1)} %pad_maximum_fusion.1.refs_0_), channel_id=1, source_target_pairs={{0,3},{1,2},{2,1},{3,0},{4,7},{5,6},{6,5},{7,4},{8,11},{9,10},{10,... | collective-permute-start | bytes 393224 | tf_op jit(solution)/shard_map/ppermute | solution.py:34
  34.5 25.9 %collective-permute-start.11 = (bf16[512,128]{1,0:T(8,128)(2,1)S(1)}, bf16[512,128]{1,0:T(8,128)(2,1)S(1)}, u32[]{:S(2)}, u32[]{:S(2)}) collective-permute-start(bf16[512,128]{1,0:T(8,128)(2,1)S(1)} %pad_maximum_fusion.1.refs_0_), channel_id=1, source_target_pairs={{0,2},{1,3},{2,0},{3,1},{4,6},{5,7},{6,4},{7,5},{8,10},{9,11},{10,... | collective-permute-start | bytes 393224 | tf_op jit(solution)/shard_map/ppermute | solution.py:34
  39.0 21.4 %collective-permute-start.10 = (bf16[512,128]{1,0:T(8,128)(2,1)S(1)}, bf16[512,128]{1,0:T(8,128)(2,1)S(1)}, u32[]{:S(2)}, u32[]{:S(2)}) collective-permute-start(bf16[512,128]{1,0:T(8,128)(2,1)S(1)} %pad_maximum_fusion.1.refs_0_), channel_id=1, source_target_pairs={{0,1},{1,0},{2,3},{3,2},{4,5},{5,4},{6,7},{7,6},{8,9},{9,8},{10,11... | collective-permute-start | bytes 393224 | tf_op jit(solution)/shard_map/ppermute | solution.py:34
  46.9 0.6 copy-start.24
  50.5 17.1 %collective-permute-start.4 = (bf16[1024,128]{1,0:T(8,128)(2,1)}, bf16[1024,128]{1,0:T(8,128)(2,1)S(1)}, u32[]{:S(2)}, u32[]{:S(2)}) collective-permute-start(bf16[1024,128]{1,0:T(8,128)(2,1)} %join.4.refs_0_), channel_id=1, source_target_pairs={{0,3},{1,2},{2,1},{3,0},{4,7},{5,6},{6,5},{7,4},{8,11},{9,10},{10,... | collective-permute-start | bytes 786440 | tf_op jit(solution)/shard_map/ppermute | solution.py:34
  52.6 15.7 %collective-permute-start.3 = (bf16[1024,128]{1,0:T(8,128)(2,1)}, bf16[1024,128]{1,0:T(8,128)(2,1)S(1)}, u32[]{:S(2)}, u32[]{:S(2)}) collective-permute-start(bf16[1024,128]{1,0:T(8,128)(2,1)} %join.4.refs_0_), channel_id=1, source_target_pairs={{0,2},{1,3},{2,0},{3,1},{4,6},{5,7},{6,4},{7,5},{8,10},{9,11},{10,... | collective-permute-start | bytes 786440 | tf_op jit(solution)/shard_map/ppermute | solution.py:34
  57.1 3.2 %copy-start.21 = (bf16[512,128]{1,0:T(8,128)(2,1)}, bf16[512,128]{1,0:T(8,128)(2,1)S(1)}, u32[]{:S(2)}) copy-start(bf16[512,128]{1,0:T(8,128)(2,1)S(1)} %collective-permute-done.12.refs_3_) | copy-start | bytes 393220
  57.1 11.9 %collective-permute-start.2 = (bf16[1024,128]{1,0:T(8,128)(2,1)}, bf16[1024,128]{1,0:T(8,128)(2,1)S(1)}, u32[]{:S(2)}, u32[]{:S(2)}) collective-permute-start(bf16[1024,128]{1,0:T(8,128)(2,1)} %join.4.refs_0_), channel_id=1, source_target_pairs={{0,1},{1,0},{2,3},{3,2},{4,5},{5,4},{6,7},{7,6},{8,9},{9,8},{10,11... | collective-permute-start | bytes 786440 | tf_op jit(solution)/shard_map/ppermute | solution.py:34
  60.3 0.6 copy-start.22
  61.0 0.6 copy-start.23
  63.6 6.2 %copy-start.9 = (bf16[1024,128]{1,0:T(8,128)(2,1)S(1)}, bf16[1024,128]{1,0:T(8,128)(2,1)}, u32[]{:S(2)}) copy-start(bf16[1024,128]{1,0:T(8,128)(2,1)} %join.4.refs_0_) | copy-start | bytes 786436
  63.6 6.2 %copy-start.16 = (f32[1024]{0:T(1024)S(1)}, f32[1024]{0:T(1024)}, u32[]{:S(2)}) copy-start(f32[1024]{0:T(1024)} %param.11) | copy-start | bytes 12292
  63.6 18.5 %collective-permute-start.13 = (bf16[2048,128]{1,0:T(8,128)(2,1)}, bf16[2048,128]{1,0:T(8,128)(2,1)}, u32[]{:S(2)}, u32[]{:S(2)}) collective-permute-start(bf16[2048,128]{1,0:T(8,128)(2,1)} %join.6.refs_0_), channel_id=1, source_target_pairs={{0,16},{1,17},{2,18},{3,19},{4,20},{5,21},{6,22},{7,23},{8,24},{9,... | collective-permute-start | bytes 1572872 | tf_op jit(solution)/shard_map/ppermute | solution.py:34
  67.6 0.7 copy-start.10
  68.3 0.7 copy-start.12
  69.0 0.7 copy-start.14
  69.8 1.0 copy-start.11
  70.7 0.9 copy-start.13
  71.7 0.9 copy-start.15
  76.4 1.0 copy-start.3
  77.4 22.9 %copy-start.8 = (bf16[512,128]{1,0:T(8,128)(2,1)}, bf16[512,128]{1,0:T(8,128)(2,1)S(1)}, u32[]{:S(2)}) copy-start(bf16[512,128]{1,0:T(8,128)(2,1)S(1)} %get-tuple-element.7.refs_0_) | copy-start | bytes 393220
  77.4 22.9 %collective-permute-start.5 = (bf16[512,128]{1,0:T(8,128)(2,1)S(1)}, bf16[512,128]{1,0:T(8,128)(2,1)}, u32[]{:S(2)}, u32[]{:S(2)}) collective-permute-start(bf16[512,128]{1,0:T(8,128)(2,1)S(1)} %get-tuple-element.7.refs_0_), channel_id=1, source_target_pairs={{0,4},{1,5},{2,6},{3,7},{4,0},{5,1},{6,2},{7,3},{8,12},{9,13},{10,... | collective-permute-start | bytes 393224 | tf_op jit(solution)/shard_map/ppermute | solution.py:34
  84.4 32.9 %copy-start.1 = (bf16[4096,128]{1,0:T(8,128)(2,1)S(1)}, bf16[4096,128]{1,0:T(8,128)(2,1)}, u32[]{:S(2)}) copy-start(bf16[4096,128]{1,0:T(8,128)(2,1)} %join.7) | copy-start | bytes 3145732
  84.4 32.9 %copy-start.2 = (bf16[4096,256]{1,0:T(8,128)(2,1)S(1)}, bf16[4096,256]{1,0:T(8,128)(2,1)}, u32[]{:S(2)}) copy-start(bf16[4096,256]{1,0:T(8,128)(2,1)} %param.16) | copy-start | bytes 6291460
  84.4 32.9 %copy-start.6 = (bf16[128,128]{1,0:T(8,128)(2,1)S(1)}, bf16[128,128]{1,0:T(8,128)(2,1)}, u32[]{:S(2)}) copy-start(bf16[128,128]{1,0:T(8,128)(2,1)} %constant.47.clone.refs_9_) | copy-start | bytes 98308
  84.4 32.9 %copy-start.7 = (f32[4096]{0:T(1024)S(1)}, f32[4096]{0:T(1024)}, u32[]{:S(2)}) copy-start(f32[4096]{0:T(1024)} %param.15) | copy-start | bytes 49156
  84.4 32.8 %collective-permute-start.14 = (bf16[4096,128]{1,0:T(8,128)(2,1)}, bf16[4096,128]{1,0:T(8,128)(2,1)}, u32[]{:S(2)}, u32[]{:S(2)}) collective-permute-start(bf16[4096,128]{1,0:T(8,128)(2,1)} %join.7), channel_id=1, source_target_pairs={{0,8},{1,9},{2,10},{3,11},{4,12},{5,13},{6,14},{7,15},{8,0},{9,1},... | collective-permute-start | bytes 3145736 | tf_op jit(solution)/shard_map/ppermute | solution.py:34
  102.0 12.5 %collective-permute-start.8 = (bf16[1024,128]{1,0:T(8,128)(2,1)}, bf16[1024,128]{1,0:T(8,128)(2,1)S(1)}, u32[]{:S(2)}, u32[]{:S(2)}) collective-permute-start(bf16[1024,128]{1,0:T(8,128)(2,1)} %join.5.refs_0_), channel_id=1, source_target_pairs={{0,3},{1,2},{2,1},{3,0},{4,7},{5,6},{6,5},{7,4},{8,11},{9,10},{10,... | collective-permute-start | bytes 786440 | tf_op jit(solution)/shard_map/ppermute | solution.py:34
  104.2 10.3 %collective-permute-start.7 = (bf16[1024,128]{1,0:T(8,128)(2,1)}, bf16[1024,128]{1,0:T(8,128)(2,1)S(1)}, u32[]{:S(2)}, u32[]{:S(2)}) collective-permute-start(bf16[1024,128]{1,0:T(8,128)(2,1)} %join.5.refs_0_), channel_id=1, source_target_pairs={{0,2},{1,3},{2,0},{3,1},{4,6},{5,7},{6,4},{7,5},{8,10},{9,11},{10,... | collective-permute-start | bytes 786440 | tf_op jit(solution)/shard_map/ppermute | solution.py:34
  108.6 8.6 %collective-permute-start.6 = (bf16[1024,128]{1,0:T(8,128)(2,1)}, bf16[1024,128]{1,0:T(8,128)(2,1)S(1)}, u32[]{:S(2)}, u32[]{:S(2)}) collective-permute-start(bf16[1024,128]{1,0:T(8,128)(2,1)} %join.5.refs_0_), channel_id=1, source_target_pairs={{0,1},{1,0},{2,3},{3,2},{4,5},{5,4},{6,7},{7,6},{8,9},{9,8},{10,11... | collective-permute-start | bytes 786440 | tf_op jit(solution)/shard_map/ppermute | solution.py:34
  117.3 1.2 copy-start.4
  118.5 0.9 copy-start.5
  122.9 13.9 %collective-permute-start.15 = (bf16[64,256]{1,0:T(8,128)(2,1)S(1)}, bf16[64,256]{1,0:T(8,128)(2,1)S(1)}, u32[]{:S(2)}, u32[]{:S(2)}) collective-permute-start(bf16[64,256]{1,0:T(8,128)(2,1)S(1)} %get-tuple-element.13), channel_id=1, source_target_pairs={{0,8},{8,16},{16,24},{24,32},{32,40},{40,48},{48,56},{56,64},{64,7... | collective-permute-start | bytes 98312 | tf_op jit(solution)/shard_map/ppermute | solution.py:59

commit v5 on v4

--- a/solution.py
+++ b/solution.py
@@ -63,29 +63,74 @@
     return [pl.BlockSpec(memory_space=pltpu.VMEM)] * count
 
 
-def join_kernel(count, *refs):
+def join_kernel(spans, *refs):
     at = 0
-    for ref in refs[:count]:
-        refs[-1][at : at + ref.shape[0], :] = ref[...]
-        at += ref.shape[0]
-
-
-def joined(parts, event=None, claimed=0):
+    for ref, (start, stop) in zip(refs, spans):
+        refs[-1][at : at + stop - start, :] = ref[start:stop, :]
+        at += stop - start
+
+
+def joined(parts, event=None, claimed=0, first=0):
     operands = list(parts) + ([] if event is None else [event])
-    rows = sum(part.shape[0] for part in parts)
+    spans = [(first, part.shape[0]) for part in parts]
+    rows = sum(stop - start for start, stop in spans)
     return pl.pallas_call(
-        functools.partial(join_kernel, len(parts)),
+        functools.partial(join_kernel, spans),
         out_shape=jax.ShapeDtypeStruct((rows, BLOCK), jnp.bfloat16),
         in_specs=in_vmem(len(operands)),
         out_specs=in_vmem(1)[0],
+        compiler_params=pltpu.CompilerParams(vmem_limit_bytes=4 * 2**20),
         cost_estimate=pl.CostEstimate(flops=claimed, bytes_accessed=4 * rows * BLOCK, transcendentals=0),
         name="join",
     )(*operands)
 
 
-def gathered(value):
-    both = joined([value, across(value, 4)], claimed=CLAIMED)
-    return [both] + [across(both, bits) for bits in (1, 2, 3)]
+def order_kernel(order_ref, *refs):
+    at = 0
+    for ref in refs[:-1]:
+        refs[-1][at : at + HALF, :] = dot(order_ref[...], ref[...]).astype(jnp.bfloat16)
+        at += HALF
+
+
+def ordered(halves):
+    return pl.pallas_call(
+        order_kernel,
+        out_shape=jax.ShapeDtypeStruct((TOKENS, BLOCK), jnp.bfloat16),
+        in_specs=in_vmem(1 + len(halves)),
+        out_specs=in_vmem(1)[0],
+        compiler_params=pltpu.CompilerParams(vmem_limit_bytes=4 * 2**20),
+        cost_estimate=pl.CostEstimate(flops=CLAIMED, bytes_accessed=400_000, transcendentals=0),
+        name="order",
+    )(one_hot(half_order(), jnp.bfloat16), *halves)
+
+
+def bias_kernel(hot_ref, turned_ref, bias_ref, out_ref):
+    for head in range(2):
+        rows = jnp.dot(
+            hot_ref[...], bias_ref[head], precision=lax.Precision.HIGHEST, preferred_element_type=jnp.float32
+        )
+        out_ref[head] = jnp.dot(
+            rows, turned_ref[...], precision=lax.Precision.HIGHEST, preferred_element_type=jnp.float32
+        )
+
+
+def ordered_bias(bias):
+    hot = np.eye(BLOCK, dtype=np.float32)[window_order()]
+    return pl.pallas_call(
+        bias_kernel,
+        out_shape=jax.ShapeDtypeStruct(bias.shape, jnp.float32),
+        in_specs=in_vmem(3),
+        out_specs=in_vmem(1)[0],
+        compiler_params=pltpu.CompilerParams(vmem_limit_bytes=4 * 2**20),
+        cost_estimate=pl.CostEstimate(flops=CLAIMED, bytes_accessed=400_000, transcendentals=0),
+        name="bias",
+    )(jnp.asarray(hot), jnp.asarray(hot.T.copy()), bias)
+
+
+def gathered(value, extra=None):
+    partner = joined([across(value, 4)], claimed=CLAIMED)
+    own = value if extra is None else jnp.concatenate([value, extra], axis=0)
+    return [place if bits == 0 else across(place, bits) for place in (own, partner) for bits in range(4)]
 
 
 def half_order():
@@ -124,8 +169,8 @@
 
 
 def attention_kernel(*refs):
-    parts = [(refs[k % 4], k // 4 * TOKENS) for k in range(8)]
-    gain_ref, w_ref, bias_ref, out_ref, stream_ref, qkv_ref = refs[4:]
+    parts = refs[:8]
+    gain_ref, w_ref, bias_ref, out_ref, stream_ref, qkv_ref = refs[8:]
     head_place = lax.axis_index("head")
     last_band = (lax.axis_index("space") == 63).astype(jnp.int32)
     for start in range(0, TOKENS, 128):
@@ -133,8 +178,8 @@
         blocks = [head_place ^ k ^ (swap * 4) for k in range(8)]
         total = jnp.zeros((128, BLOCK), jnp.float32)
         squares = jnp.zeros((128, BLOCK), jnp.float32)
-        for k, (ref, base) in enumerate(parts):
-            rounded = ref[base + start : base + start + 128, :]
+        for k, ref in enumerate(parts):
+            rounded = ref[start : start + 128, :]
             stream_ref[k ^ (swap * 4), start : start + 128, :] = rounded
             value = rounded.astype(jnp.float32)
             total += value
@@ -146,8 +191,7 @@
         for k in range(0, 8, 2):
             normed = []
             for n in (k, k + 1):
-                ref, base = parts[n]
-                value = ref[base + start : base + start + 128, :].astype(jnp.float32)
+                value = parts[n][start : start + 128, :].astype(jnp.float32)
                 normed.append(((value - mean) * scale * gain_ref[blocks[n]]).astype(jnp.bfloat16))
             weights = jnp.concatenate([w_ref[blocks[n]] for n in (k, k + 1)], axis=0)
             product += dot(jnp.concatenate(normed, axis=1), weights)
@@ -172,8 +216,8 @@
 
 
 def merge_kernel(*refs):
-    att_refs = refs[:4]
-    stream_ref, w_same_ref, w_other_ref, gain_ref, w_ref, order_ref, out_ref, updated_ref = refs[4:]
+    att_refs = refs[:8]
+    stream_ref, w_same_ref, w_other_ref, gain_ref, w_ref, order_ref, out_ref, updated_ref = refs[8:]
     head_place = lax.axis_index("head")
     space = lax.axis_index("space")
     blocks = [head_place ^ k for k in range(8)]
@@ -181,9 +225,7 @@
     parity = (head_place // 2 + space) % 2
 
     def project(odd):
-        attended = jnp.concatenate(
-            [att_refs[k % 4][k // 4 * TOKENS : (k // 4 + 1) * TOKENS, :] for k in range(8)], axis=1
-        )
+        attended = jnp.concatenate([ref[...] for ref in att_refs], axis=1)
         for k in range(0, 8, 2):
             w_from = w_same_ref if (k // 2 + odd) % 2 == 0 else w_other_ref
             x_rel = (blocks[k] // 4) ^ my_x
@@ -223,21 +265,16 @@
 
 def on_device(fields, ln_gain, w_qkv, attn_bias, w_out, merge_gain, w_merge):
     rows = fields.reshape(2, HALF, BLOCK)
-    order = one_hot(half_order(), jnp.bfloat16)
     following = following_rows(rows[0])
     space = lax.axis_index("space")
     quarter = (space // 2 % 2) * 2 + space % 2
     w_piece = lax.dynamic_slice(w_out, (0, quarter * 256), (BLOCK, 256))
     w_piece = jnp.concatenate([w_piece[:, :BLOCK], w_piece[:, BLOCK:]], axis=0)
     w_pair = jnp.concatenate([w_piece, across(w_piece, 4)], axis=0)
-    w_pairs = [w_pair] + [across(w_pair, bits) for bits in (1, 2, 3)]
-    mine = [dot(order, half).astype(jnp.bfloat16) for half in (rows[1], following)]
-    around = gathered(jnp.concatenate(mine, axis=0))
-    w_quarter = joined(w_pairs, around[0][:16])
-
-    bias_hot = one_hot(window_order(), jnp.float32)
-    bias = jnp.einsum("pa,hab->hpb", bias_hot, attn_bias, precision=lax.Precision.HIGHEST)
-    bias = jnp.einsum("hpb,qb->hpq", bias, bias_hot, precision=lax.Precision.HIGHEST)
+    around = gathered(ordered([rows[1], following]), w_pair)
+    w_quarter = joined(around[:4], around[4][:16], first=TOKENS)
+
+    bias = ordered_bias(attn_bias)
     vmem = pl.BlockSpec(memory_space=pltpu.VMEM)
     attended, stream = pl.pallas_call(
         attention_kernel,
@@ -245,7 +282,7 @@
             jax.ShapeDtypeStruct((TOKENS, BLOCK), jnp.bfloat16),
             jax.ShapeDtypeStruct((8, TOKENS, BLOCK), jnp.bfloat16),
         ),
-        in_specs=in_vmem(7),
+        in_specs=in_vmem(11),
         out_specs=(vmem, vmem),
         scratch_shapes=[pltpu.VMEM((TOKENS, 3 * BLOCK), jnp.bfloat16)],
         compiler_params=pltpu.CompilerParams(vmem_limit_bytes=16 * 2**20),
@@ -259,7 +296,7 @@
     merged = pl.pallas_call(
         merge_kernel,
         out_shape=jax.ShapeDtypeStruct((128, 256), jnp.bfloat16),
-        in_specs=in_vmem(10),
+        in_specs=in_vmem(14),
         out_specs=vmem,
         scratch_shapes=[pltpu.VMEM((TOKENS, D), jnp.bfloat16)],
         compiler_params=pltpu.CompilerParams(vmem_limit_bytes=16 * 2**20),

time: 139 us -> 119 us (0.86)
  waiting for transfers between devices: 37.6 us -> 22.1 us
  starting transfers between devices: 66.3 us -> 80.9 us
  local copies, waits for them, and re-layouts: 15.8 us -> 7.48 us
  Pallas kernels: 14.8 us -> 6.9 us
  matrix products: 2.69 us -> 0 us
    ppermute x14 -> x17, waiting for transfers between devices: 23.8 us -> 10 us  [moved(): return lax.ppermute(value, BOTH, pairs)]
    ppermute x1, starting transfers between devices: 3.37 us -> 13 us  [following_rows(): return lax.ppermute(value, BOTH, pairs)]
    unnamed x50 -> x18, local copies, waits for them, and re-layouts: 10.1 us -> 0.95 us
    pallas_call x4 -> x6, Pallas kernels: 7.58 us -> 0.87 us  [the longest x1 0.53 us: ordered_bias(): pl.pallas_call(bias_kernel, out_shape=jax.ShapeDtypeStruct(bias.shape, jn...]
    ppermute x14 -> x17, starting transfers between devices: 61 us -> 65.9 us  [moved(): return lax.ppermute(value, BOTH, pairs)]
    reshape x2, local copies, waits for them, and re-layouts: 1.39 us -> 4.11 us  [on_device(): w_qkv.reshape(8, BLOCK, 3 * BLOCK)]
    dot_general x4 -> x0, matrix products: 2.69 us -> none  [the longest x2 2.15 us: dot(): return jnp.dot(left, right, preferred_element_type=jnp.float32)]
    ppermute x1, waiting for transfers between devices: 1.71 us -> 0.01 us  [following_rows(): return lax.ppermute(value, BOTH, pairs)]
  transfers between devices with their start and end apart: 16 -> 19, of which waited for: 6 -> 4; matrix products, arithmetic and copies ran while one was open for 5% -> 4% of each run, Pallas kernels for 8% -> 4%
where the time goes in v5:
time: 119 us; the launch traced here: 118 us
  starting transfers between devices  80.9 us (68%)
  waiting for transfers between devices  22.1 us (19%)
  local copies, waits for them, and re-layouts  7.48 us (6%)
  Pallas kernels  6.9 us (6%)
    ppermute x17, starting transfers between devices, moved(): return lax.ppermute(value, BOTH, pairs)  65.9 us
    ppermute x1, starting transfers between devices, following_rows(): return lax.ppermute(value, BOTH, pairs)  13 us
    ppermute x1, waiting for transfers between devices, along_bands(): lax.ppermute(value, 'space', [(s, (s + steps) % 64) for s in range(64)])  12 us
    ppermute x17, waiting for transfers between devices, moved(): return lax.ppermute(value, BOTH, pairs)  10 us
    reshape x2, local copies, waits for them, and re-layouts, on_device(): w_qkv.reshape(8, BLOCK, 3 * BLOCK)  4.11 us
    pallas_call x1, Pallas kernels, on_device(): pl.pallas_call(attention_kernel, out_shape=(jax.ShapeDtypeStruct((TOKENS,...  3.75 us
  transfers between devices with their start and end apart: 19, of which 4 were waited for; matrix products, arithmetic and copies ran while one was open for 4% of the time, Pallas kernels for 4%

profile of v5, /device:TPU:24, one launch (start us, length us, event | category | flops | bytes accessed | tf_op | source)
XLA Modules:
  0.0 117.9 jit_solution(6174915394048811767)
XLA Ops:
  0.0 1.0 fusion
  1.0 13.0 %collective-permute-start = (bf16[256,128]{1,0:T(8,128)(2,1)S(1)}, bf16[256,128]{1,0:T(8,128)(2,1)S(1)}, u32[]{:S(2)}, u32[]{:S(2)}) collective-permute-start(bf16[256,128]{1,0:T(8,128)(2,1)S(1)} %bitcast.13), channel_id=1, source_target_pairs={{0,508},{1,509},{2,510},{3,511},{4,504},{5,505},{6,506},{7,507},{8... | collective-permute-start | bytes 196616 | tf_op jit(solution)/shard_map/ppermute | solution.py:55
  14.1 0.8 constant_dynamic-slice_fusion
  14.8 6.3 %collective-permute-start.1 = (bf16[256,128]{1,0:T(8,128)(2,1)S(1)}, bf16[256,128]{1,0:T(8,128)(2,1)S(1)}, u32[]{:S(2)}, u32[]{:S(2)}) collective-permute-start(bf16[256,128]{1,0:T(8,128)(2,1)S(1)} %pad_maximum_fusion.1), channel_id=1, source_target_pairs={{0,4},{1,5},{2,6},{3,7},{4,0},{5,1},{6,2},{7,3},{8,12},{9,13},{10,... | collective-permute-start | bytes 196616 | tf_op jit(solution)/shard_map/ppermute | solution.py:34
  21.2 0.0 collective-permute-done.refs_1_
  21.2 0.0 copy-start.5
  21.2 0.9 copy-done.5
  22.1 0.2 order.1
  22.3 8.2 %collective-permute-start.5 = (bf16[512,128]{1,0:T(8,128)(2,1)S(1)}, bf16[512,128]{1,0:T(8,128)(2,1)S(1)}, u32[]{:S(2)}, u32[]{:S(2)}) collective-permute-start(bf16[512,128]{1,0:T(8,128)(2,1)S(1)} %order.1), channel_id=1, source_target_pairs={{0,4},{1,5},{2,6},{3,7},{4,0},{5,1},{6,2},{7,3},{8,12},{9,13},{10,... | collective-permute-start | bytes 393224 | tf_op jit(solution)/shard_map/ppermute | solution.py:34
  30.6 0.0 copy-start.4
  30.6 0.0 copy-start.6
  30.6 0.0 copy-start.7
  30.6 2.8 %collective-permute-start.2 = (bf16[1024,128]{1,0:T(8,128)(2,1)S(1)}, bf16[1024,128]{1,0:T(8,128)(2,1)S(1)}, u32[]{:S(2)}, u32[]{:S(2)}) collective-permute-start(bf16[1024,128]{1,0:T(8,128)(2,1)S(1)} %pad_maximum_fusion.refs_0_), channel_id=1, source_target_pairs={{0,1},{1,0},{2,3},{3,2},{4,5},{5,4},{6,7},{7,6},{8,9},{9,8},{10,11... | collective-permute-start | bytes 786440 | tf_op jit(solution)/shard_map/ppermute | solution.py:34
  33.4 2.8 %collective-permute-start.3 = (bf16[1024,128]{1,0:T(8,128)(2,1)S(1)}, bf16[1024,128]{1,0:T(8,128)(2,1)S(1)}, u32[]{:S(2)}, u32[]{:S(2)}) collective-permute-start(bf16[1024,128]{1,0:T(8,128)(2,1)S(1)} %pad_maximum_fusion.refs_0_), channel_id=1, source_target_pairs={{0,2},{1,3},{2,0},{3,1},{4,6},{5,7},{6,4},{7,5},{8,10},{9,11},{10,... | collective-permute-start | bytes 786440 | tf_op jit(solution)/shard_map/ppermute | solution.py:34
  36.3 4.9 %collective-permute-start.4 = (bf16[1024,128]{1,0:T(8,128)(2,1)S(1)}, bf16[1024,128]{1,0:T(8,128)(2,1)S(1)}, u32[]{:S(2)}, u32[]{:S(2)}) collective-permute-start(bf16[1024,128]{1,0:T(8,128)(2,1)S(1)} %pad_maximum_fusion.refs_0_), channel_id=1, source_target_pairs={{0,3},{1,2},{2,1},{3,0},{4,7},{5,6},{6,5},{7,4},{8,11},{9,10},{10,... | collective-permute-start | bytes 786440 | tf_op jit(solution)/shard_map/ppermute | solution.py:34
  41.2 3.5 %collective-permute-done.5.refs_0_ = bf16[512,128]{1,0:T(8,128)(2,1)S(1)} collective-permute-done((bf16[512,128]{1,0:T(8,128)(2,1)S(1)}, bf16[512,128]{1,0:T(8,128)(2,1)S(1)}, u32[]{:S(2)}, u32[]{:S(2)}) %collective-permute-start.5) | collective-permute-done | bytes 131104 | tf_op jit(solution)/shard_map/ppermute | solution.py:34
  44.7 2.7 %collective-permute-start.6 = (bf16[512,128]{1,0:T(8,128)(2,1)S(1)}, bf16[512,128]{1,0:T(8,128)(2,1)S(1)}, u32[]{:S(2)}, u32[]{:S(2)}) collective-permute-start(bf16[512,128]{1,0:T(8,128)(2,1)S(1)} %join.4.refs_4_), channel_id=1, source_target_pairs={{0,1},{1,0},{2,3},{3,2},{4,5},{5,4},{6,7},{7,6},{8,9},{9,8},{10,11... | collective-permute-start | bytes 393224 | tf_op jit(solution)/shard_map/ppermute | solution.py:34
  47.4 3.6 %collective-permute-start.7 = (bf16[512,128]{1,0:T(8,128)(2,1)S(1)}, bf16[512,128]{1,0:T(8,128)(2,1)S(1)}, u32[]{:S(2)}, u32[]{:S(2)}) collective-permute-start(bf16[512,128]{1,0:T(8,128)(2,1)S(1)} %join.4.refs_4_), channel_id=1, source_target_pairs={{0,2},{1,3},{2,0},{3,1},{4,6},{5,7},{6,4},{7,5},{8,10},{9,11},{10,... | collective-permute-start | bytes 393224 | tf_op jit(solution)/shard_map/ppermute | solution.py:34
  51.1 0.0 collective-permute-done.2.refs_1_
  51.1 4.1 %collective-permute-start.8 = (bf16[512,128]{1,0:T(8,128)(2,1)S(1)}, bf16[512,128]{1,0:T(8,128)(2,1)S(1)}, u32[]{:S(2)}, u32[]{:S(2)}) collective-permute-start(bf16[512,128]{1,0:T(8,128)(2,1)S(1)} %join.4.refs_4_), channel_id=1, source_target_pairs={{0,3},{1,2},{2,1},{3,0},{4,7},{5,6},{6,5},{7,4},{8,11},{9,10},{10,... | collective-permute-start | bytes 393224 | tf_op jit(solution)/shard_map/ppermute | solution.py:34
  55.2 0.0 collective-permute-done.3.refs_2_
  55.2 0.0 collective-permute-done.4.refs_3_
  55.3 0.0 copy-start.8
  55.3 2.1 %collective-permute-start.16 = (bf16[2048,128]{1,0:T(8,128)(2,1)S(1)}, bf16[2048,128]{1,0:T(8,128)(2,1)S(1)}, u32[]{:S(2)}, u32[]{:S(2)}) collective-permute-start(bf16[2048,128]{1,0:T(8,128)(2,1)S(1)} %join.6.refs_0_), channel_id=1, source_target_pairs={{0,16},{1,17},{2,18},{3,19},{4,20},{5,21},{6,22},{7,23},{8,24},{9,... | collective-permute-start | bytes 1572872 | tf_op jit(solution)/shard_map/ppermute | solution.py:34
  57.4 0.5 bias.1.refs_10_
  57.9 0.0 copy-start.3
  57.9 1.7 %copy.15 = bf16[1024,3,128]{2,1,0:T(4,128)(2,1)} copy(bf16[1024,3,128]{2,0,1:T(8,128)(2,1)S(1)} %copy-done.8) | data formatting | bytes 1572864 | tf_op jit(solution)/shard_map/reshape | solution.py:291
  59.6 2.4 %reshape.33.refs_9_ = bf16[8,128,384]{2,1,0:T(8,128)(2,1)S(1)} reshape(bf16[1024,3,128]{2,1,0:T(4,128)(2,1)} %copy.15) | data formatting | bytes 1572864 | tf_op jit(solution)/shard_map/reshape | solution.py:291
  62.0 0.0 collective-permute-done.6.refs_5_
  62.1 3.8 %attention.1 = (bf16[512,128]{1,0:T(8,128)(2,1)S(1)}, bf16[8,512,128]{2,1,0:T(8,128)(2,1)S(1)}) custom-call(bf16[1024,128]{1,0:T(8,128)(2,1)S(1)} %pad_maximum_fusion.refs_0_, bf16[1024,128]{1,0:T(8,128)(2,1)S(1)} %collective-permute-done.2.refs_1_, bf16[1024,128]{1,0:T(8,128)(2,1)S(1)} %collective-permute-done.3.refs_2_, ...), custom_call_target="tpu_custom_call" | custom-call | flops 600000000 | bytes 3000000 | tf_op jit(solution)/shard_map/attention/pallas_call | solution.py:279
  65.8 5.5 %collective-permute-start.12 = (bf16[512,128]{1,0:T(8,128)(2,1)S(1)}, bf16[512,128]{1,0:T(8,128)(2,1)S(1)}, u32[]{:S(2)}, u32[]{:S(2)}) collective-permute-start(bf16[512,128]{1,0:T(8,128)(2,1)S(1)} %get-tuple-element.7.refs_0_), channel_id=1, source_target_pairs={{0,4},{1,5},{2,6},{3,7},{4,0},{5,1},{6,2},{7,3},{8,12},{9,13},{10,... | collective-permute-start | bytes 393224 | tf_op jit(solution)/shard_map/ppermute | solution.py:34
  71.3 3.1 %collective-permute-start.9 = (bf16[512,128]{1,0:T(8,128)(2,1)S(1)}, bf16[512,128]{1,0:T(8,128)(2,1)S(1)}, u32[]{:S(2)}, u32[]{:S(2)}) collective-permute-start(bf16[512,128]{1,0:T(8,128)(2,1)S(1)} %get-tuple-element.7.refs_0_), channel_id=1, source_target_pairs={{0,1},{1,0},{2,3},{3,2},{4,5},{5,4},{6,7},{7,6},{8,9},{9,8},{10,11... | collective-permute-start | bytes 393224 | tf_op jit(solution)/shard_map/ppermute | solution.py:34
  74.4 5.4 %collective-permute-start.10 = (bf16[512,128]{1,0:T(8,128)(2,1)S(1)}, bf16[512,128]{1,0:T(8,128)(2,1)S(1)}, u32[]{:S(2)}, u32[]{:S(2)}) collective-permute-start(bf16[512,128]{1,0:T(8,128)(2,1)S(1)} %get-tuple-element.7.refs_0_), channel_id=1, source_target_pairs={{0,2},{1,3},{2,0},{3,1},{4,6},{5,7},{6,4},{7,5},{8,10},{9,11},{10,... | collective-permute-start | bytes 393224 | tf_op jit(solution)/shard_map/ppermute | solution.py:34
  79.8 1.9 %collective-permute-start.11 = (bf16[512,128]{1,0:T(8,128)(2,1)S(1)}, bf16[512,128]{1,0:T(8,128)(2,1)S(1)}, u32[]{:S(2)}, u32[]{:S(2)}) collective-permute-start(bf16[512,128]{1,0:T(8,128)(2,1)S(1)} %get-tuple-element.7.refs_0_), channel_id=1, source_target_pairs={{0,3},{1,2},{2,1},{3,0},{4,7},{5,6},{6,5},{7,4},{8,11},{9,10},{10,... | collective-permute-start | bytes 393224 | tf_op jit(solution)/shard_map/ppermute | solution.py:34
  81.8 0.1 join.7
  81.9 0.0 copy-start
  81.9 0.0 copy-start.1
  81.9 0.0 copy-start.2
  81.9 2.1 %collective-permute-start.17 = (bf16[4096,128]{1,0:T(8,128)(2,1)S(1)}, bf16[4096,128]{1,0:T(8,128)(2,1)S(1)}, u32[]{:S(2)}, u32[]{:S(2)}) collective-permute-start(bf16[4096,128]{1,0:T(8,128)(2,1)S(1)} %join.7), channel_id=1, source_target_pairs={{0,8},{1,9},{2,10},{3,11},{4,12},{5,13},{6,14},{7,15},{8,0},{9,1},... | collective-permute-start | bytes 3145736 | tf_op jit(solution)/shard_map/ppermute | solution.py:34
  84.0 1.9 %collective-permute-start.13 = (bf16[512,128]{1,0:T(8,128)(2,1)S(1)}, bf16[512,128]{1,0:T(8,128)(2,1)S(1)}, u32[]{:S(2)}, u32[]{:S(2)}) collective-permute-start(bf16[512,128]{1,0:T(8,128)(2,1)S(1)} %join.5.refs_4_), channel_id=1, source_target_pairs={{0,1},{1,0},{2,3},{3,2},{4,5},{5,4},{6,7},{7,6},{8,9},{9,8},{10,11... | collective-permute-start | bytes 393224 | tf_op jit(solution)/shard_map/ppermute | solution.py:34
  85.9 6.6 %collective-permute-start.14 = (bf16[512,128]{1,0:T(8,128)(2,1)S(1)}, bf16[512,128]{1,0:T(8,128)(2,1)S(1)}, u32[]{:S(2)}, u32[]{:S(2)}) collective-permute-start(bf16[512,128]{1,0:T(8,128)(2,1)S(1)} %join.5.refs_4_), channel_id=1, source_target_pairs={{0,2},{1,3},{2,0},{3,1},{4,6},{5,7},{6,4},{7,5},{8,10},{9,11},{10,... | collective-permute-start | bytes 393224 | tf_op jit(solution)/shard_map/ppermute | solution.py:34
  92.5 1.9 %collective-permute-start.15 = (bf16[512,128]{1,0:T(8,128)(2,1)S(1)}, bf16[512,128]{1,0:T(8,128)(2,1)S(1)}, u32[]{:S(2)}, u32[]{:S(2)}) collective-permute-start(bf16[512,128]{1,0:T(8,128)(2,1)S(1)} %join.5.refs_4_), channel_id=1, source_target_pairs={{0,3},{1,2},{2,1},{3,0},{4,7},{5,6},{6,5},{7,4},{8,11},{9,10},{10,... | collective-permute-start | bytes 393224 | tf_op jit(solution)/shard_map/ppermute | solution.py:34
  94.5 2.8 %collective-permute-done.14.refs_6_ = bf16[512,128]{1,0:T(8,128)(2,1)S(1)} collective-permute-done((bf16[512,128]{1,0:T(8,128)(2,1)S(1)}, bf16[512,128]{1,0:T(8,128)(2,1)S(1)}, u32[]{:S(2)}, u32[]{:S(2)}) %collective-permute-start.14) | collective-permute-done | bytes 131104 | tf_op jit(solution)/shard_map/ppermute | solution.py:34
  97.2 3.7 %collective-permute-done.15.refs_7_ = bf16[512,128]{1,0:T(8,128)(2,1)S(1)} collective-permute-done((bf16[512,128]{1,0:T(8,128)(2,1)S(1)}, bf16[512,128]{1,0:T(8,128)(2,1)S(1)}, u32[]{:S(2)}, u32[]{:S(2)}) %collective-permute-start.15) | collective-permute-done | bytes 131104 | tf_op jit(solution)/shard_map/ppermute | solution.py:34
  101.0 2.3 %merge.1 = bf16[128,256]{1,0:T(8,128)(2,1)S(1)} custom-call(bf16[512,128]{1,0:T(8,128)(2,1)S(1)} %get-tuple-element.7.refs_0_, bf16[512,128]{1,0:T(8,128)(2,1)S(1)} %collective-permute-done.9.refs_1_, bf16[512,128]{1,0:T(8,128)(2,1)S(1)} %collective-permute-done.10.refs_2_, bf16[512,128]{1,0:T(8,128)(2,1)S(1)} %collective-permute-done.11.refs_3_, ...), custom_call_target="tpu_custom_call" | custom-call | flops 1400000000 | bytes 7000000 | tf_op jit(solution)/shard_map/merge/pallas_call | solution.py:296
  103.3 1.9 %collective-permute-start.18 = (bf16[64,256]{1,0:T(8,128)(2,1)S(1)}, bf16[64,256]{1,0:T(8,128)(2,1)S(1)}, u32[]{:S(2)}, u32[]{:S(2)}) collective-permute-start(bf16[64,256]{1,0:T(8,128)(2,1)S(1)} %get-tuple-element.13), channel_id=1, source_target_pairs={{0,8},{8,16},{16,24},{24,32},{32,40},{40,48},{48,56},{56,64},{64,7... | collective-permute-start | bytes 98312 | tf_op jit(solution)/shard_map/ppermute | solution.py:59
  105.2 12.0 %collective-permute-done.18 = bf16[64,256]{1,0:T(8,128)(2,1)S(1)} collective-permute-done((bf16[64,256]{1,0:T(8,128)(2,1)S(1)}, bf16[64,256]{1,0:T(8,128)(2,1)S(1)}, u32[]{:S(2)}, u32[]{:S(2)}) %collective-permute-start.18) | collective-permute-done | bytes 32800 | tf_op jit(solution)/shard_map/ppermute | solution.py:59
  117.2 0.7 reshape.32
  (27 shorter events, 0.1 us)
Async XLA Ops:
  1.0 20.2 %collective-permute-start = (bf16[256,128]{1,0:T(8,128)(2,1)S(1)}, bf16[256,128]{1,0:T(8,128)(2,1)S(1)}, u32[]{:S(2)}, u32[]{:S(2)}) collective-permute-start(bf16[256,128]{1,0:T(8,128)(2,1)S(1)} %bitcast.13), channel_id=1, source_target_pairs={{0,508},{1,509},{2,510},{3,511},{4,504},{5,505},{6,506},{7,507},{8... | collective-permute-start | bytes 196616 | tf_op jit(solution)/shard_map/ppermute | solution.py:55
  14.8 15.7 %collective-permute-start.1 = (bf16[256,128]{1,0:T(8,128)(2,1)S(1)}, bf16[256,128]{1,0:T(8,128)(2,1)S(1)}, u32[]{:S(2)}, u32[]{:S(2)}) collective-permute-start(bf16[256,128]{1,0:T(8,128)(2,1)S(1)} %pad_maximum_fusion.1), channel_id=1, source_target_pairs={{0,4},{1,5},{2,6},{3,7},{4,0},{5,1},{6,2},{7,3},{8,12},{9,13},{10,... | collective-permute-start | bytes 196616 | tf_op jit(solution)/shard_map/ppermute | solution.py:34
  21.2 0.9 copy-start.5
  22.3 22.4 %collective-permute-start.5 = (bf16[512,128]{1,0:T(8,128)(2,1)S(1)}, bf16[512,128]{1,0:T(8,128)(2,1)S(1)}, u32[]{:S(2)}, u32[]{:S(2)}) collective-permute-start(bf16[512,128]{1,0:T(8,128)(2,1)S(1)} %order.1), channel_id=1, source_target_pairs={{0,4},{1,5},{2,6},{3,7},{4,0},{5,1},{6,2},{7,3},{8,12},{9,13},{10,... | collective-permute-start | bytes 393224 | tf_op jit(solution)/shard_map/ppermute | solution.py:34
  30.6 26.7 %copy-start.4 = (f32[2,128,128]{2,1,0:T(8,128)S(1)}, f32[2,128,128]{2,1,0:T(8,128)}, u32[]{:S(2)}) copy-start(f32[2,128,128]{2,1,0:T(8,128)} %bias_ref.1) | copy-start | bytes 393220
  30.6 26.7 %copy-start.6 = (f32[128,128]{1,0:T(8,128)S(1)}, f32[128,128]{1,0:T(8,128)}, u32[]{:S(2)}) copy-start(f32[128,128]{1,0:T(8,128)} %constant.48.clone.hot_ref) | copy-start | bytes 196612
  30.6 26.7 %copy-start.7 = (f32[128,128]{1,0:T(8,128)S(1)}, f32[128,128]{1,0:T(8,128)}, u32[]{:S(2)}) copy-start(f32[128,128]{1,0:T(8,128)} %constant.49.clone.turned_ref) | copy-start | bytes 196612
  30.6 20.4 %collective-permute-start.2 = (bf16[1024,128]{1,0:T(8,128)(2,1)S(1)}, bf16[1024,128]{1,0:T(8,128)(2,1)S(1)}, u32[]{:S(2)}, u32[]{:S(2)}) collective-permute-start(bf16[1024,128]{1,0:T(8,128)(2,1)S(1)} %pad_maximum_fusion.refs_0_), channel_id=1, source_target_pairs={{0,1},{1,0},{2,3},{3,2},{4,5},{5,4},{6,7},{7,6},{8,9},{9,8},{10,11... | collective-permute-start | bytes 786440 | tf_op jit(solution)/shard_map/ppermute | solution.py:34
  33.4 21.8 %collective-permute-start.3 = (bf16[1024,128]{1,0:T(8,128)(2,1)S(1)}, bf16[1024,128]{1,0:T(8,128)(2,1)S(1)}, u32[]{:S(2)}, u32[]{:S(2)}) collective-permute-start(bf16[1024,128]{1,0:T(8,128)(2,1)S(1)} %pad_maximum_fusion.refs_0_), channel_id=1, source_target_pairs={{0,2},{1,3},{2,0},{3,1},{4,6},{5,7},{6,4},{7,5},{8,10},{9,11},{10,... | collective-permute-start | bytes 786440 | tf_op jit(solution)/shard_map/ppermute | solution.py:34
  36.3 18.9 %collective-permute-start.4 = (bf16[1024,128]{1,0:T(8,128)(2,1)S(1)}, bf16[1024,128]{1,0:T(8,128)(2,1)S(1)}, u32[]{:S(2)}, u32[]{:S(2)}) collective-permute-start(bf16[1024,128]{1,0:T(8,128)(2,1)S(1)} %pad_maximum_fusion.refs_0_), channel_id=1, source_target_pairs={{0,3},{1,2},{2,1},{3,0},{4,7},{5,6},{6,5},{7,4},{8,11},{9,10},{10,... | collective-permute-start | bytes 786440 | tf_op jit(solution)/shard_map/ppermute | solution.py:34
  44.7 17.3 %collective-permute-start.6 = (bf16[512,128]{1,0:T(8,128)(2,1)S(1)}, bf16[512,128]{1,0:T(8,128)(2,1)S(1)}, u32[]{:S(2)}, u32[]{:S(2)}) collective-permute-start(bf16[512,128]{1,0:T(8,128)(2,1)S(1)} %join.4.refs_4_), channel_id=1, source_target_pairs={{0,1},{1,0},{2,3},{3,2},{4,5},{5,4},{6,7},{7,6},{8,9},{9,8},{10,11... | collective-permute-start | bytes 393224 | tf_op jit(solution)/shard_map/ppermute | solution.py:34
  47.4 14.7 %collective-permute-start.7 = (bf16[512,128]{1,0:T(8,128)(2,1)S(1)}, bf16[512,128]{1,0:T(8,128)(2,1)S(1)}, u32[]{:S(2)}, u32[]{:S(2)}) collective-permute-start(bf16[512,128]{1,0:T(8,128)(2,1)S(1)} %join.4.refs_4_), channel_id=1, source_target_pairs={{0,2},{1,3},{2,0},{3,1},{4,6},{5,7},{6,4},{7,5},{8,10},{9,11},{10,... | collective-permute-start | bytes 393224 | tf_op jit(solution)/shard_map/ppermute | solution.py:34
  51.1 11.0 %collective-permute-start.8 = (bf16[512,128]{1,0:T(8,128)(2,1)S(1)}, bf16[512,128]{1,0:T(8,128)(2,1)S(1)}, u32[]{:S(2)}, u32[]{:S(2)}) collective-permute-start(bf16[512,128]{1,0:T(8,128)(2,1)S(1)} %join.4.refs_4_), channel_id=1, source_target_pairs={{0,3},{1,2},{2,1},{3,0},{4,7},{5,6},{6,5},{7,4},{8,11},{9,10},{10,... | collective-permute-start | bytes 393224 | tf_op jit(solution)/shard_map/ppermute | solution.py:34
  55.3 2.6 %copy-start.8 = (bf16[1024,3,128]{2,0,1:T(8,128)(2,1)S(1)}, bf16[1024,3,128]{2,0,1:T(8,128)(2,1)}, u32[]{:S(2)}) copy-start(bf16[1024,3,128]{2,0,1:T(8,128)(2,1)} %param.13) | copy-start | bytes 2359300
  55.3 26.5 %collective-permute-start.16 = (bf16[2048,128]{1,0:T(8,128)(2,1)S(1)}, bf16[2048,128]{1,0:T(8,128)(2,1)S(1)}, u32[]{:S(2)}, u32[]{:S(2)}) collective-permute-start(bf16[2048,128]{1,0:T(8,128)(2,1)S(1)} %join.6.refs_0_), channel_id=1, source_target_pairs={{0,16},{1,17},{2,18},{3,19},{4,20},{5,21},{6,22},{7,23},{8,24},{9,... | collective-permute-start | bytes 1572872 | tf_op jit(solution)/shard_map/ppermute | solution.py:34
  57.9 4.2 %copy-start.3 = (f32[1024]{0:T(1024)S(1)}, f32[1024]{0:T(1024)}, u32[]{:S(2)}) copy-start(f32[1024]{0:T(1024)} %param.12) | copy-start | bytes 12292
  65.8 18.1 %collective-permute-start.12 = (bf16[512,128]{1,0:T(8,128)(2,1)S(1)}, bf16[512,128]{1,0:T(8,128)(2,1)S(1)}, u32[]{:S(2)}, u32[]{:S(2)}) collective-permute-start(bf16[512,128]{1,0:T(8,128)(2,1)S(1)} %get-tuple-element.7.refs_0_), channel_id=1, source_target_pairs={{0,4},{1,5},{2,6},{3,7},{4,0},{5,1},{6,2},{7,3},{8,12},{9,13},{10,... | collective-permute-start | bytes 393224 | tf_op jit(solution)/shard_map/ppermute | solution.py:34
  71.3 14.6 %collective-permute-start.9 = (bf16[512,128]{1,0:T(8,128)(2,1)S(1)}, bf16[512,128]{1,0:T(8,128)(2,1)S(1)}, u32[]{:S(2)}, u32[]{:S(2)}) collective-permute-start(bf16[512,128]{1,0:T(8,128)(2,1)S(1)} %get-tuple-element.7.refs_0_), channel_id=1, source_target_pairs={{0,1},{1,0},{2,3},{3,2},{4,5},{5,4},{6,7},{7,6},{8,9},{9,8},{10,11... | collective-permute-start | bytes 393224 | tf_op jit(solution)/shard_map/ppermute | solution.py:34
  74.4 18.1 %collective-permute-start.10 = (bf16[512,128]{1,0:T(8,128)(2,1)S(1)}, bf16[512,128]{1,0:T(8,128)(2,1)S(1)}, u32[]{:S(2)}, u32[]{:S(2)}) collective-permute-start(bf16[512,128]{1,0:T(8,128)(2,1)S(1)} %get-tuple-element.7.refs_0_), channel_id=1, source_target_pairs={{0,2},{1,3},{2,0},{3,1},{4,6},{5,7},{6,4},{7,5},{8,10},{9,11},{10,... | collective-permute-start | bytes 393224 | tf_op jit(solution)/shard_map/ppermute | solution.py:34
  79.8 14.6 %collective-permute-start.11 = (bf16[512,128]{1,0:T(8,128)(2,1)S(1)}, bf16[512,128]{1,0:T(8,128)(2,1)S(1)}, u32[]{:S(2)}, u32[]{:S(2)}) collective-permute-start(bf16[512,128]{1,0:T(8,128)(2,1)S(1)} %get-tuple-element.7.refs_0_), channel_id=1, source_target_pairs={{0,3},{1,2},{2,1},{3,0},{4,7},{5,6},{6,5},{7,4},{8,11},{9,10},{10,... | collective-permute-start | bytes 393224 | tf_op jit(solution)/shard_map/ppermute | solution.py:34
  81.9 19.1 %copy-start = (bf16[4096,256]{1,0:T(8,128)(2,1)S(1)}, bf16[4096,256]{1,0:T(8,128)(2,1)}, u32[]{:S(2)}) copy-start(bf16[4096,256]{1,0:T(8,128)(2,1)} %param.17) | copy-start | bytes 6291460
  81.9 19.1 %copy-start.1 = (bf16[128,128]{1,0:T(8,128)(2,1)S(1)}, bf16[128,128]{1,0:T(8,128)(2,1)}, u32[]{:S(2)}) copy-start(bf16[128,128]{1,0:T(8,128)(2,1)} %constant.50.clone.refs_13_) | copy-start | bytes 98308
  81.9 19.1 %copy-start.2 = (f32[4096]{0:T(1024)S(1)}, f32[4096]{0:T(1024)}, u32[]{:S(2)}) copy-start(f32[4096]{0:T(1024)} %param.16) | copy-start | bytes 49156
  81.9 19.1 %collective-permute-start.17 = (bf16[4096,128]{1,0:T(8,128)(2,1)S(1)}, bf16[4096,128]{1,0:T(8,128)(2,1)S(1)}, u32[]{:S(2)}, u32[]{:S(2)}) collective-permute-start(bf16[4096,128]{1,0:T(8,128)(2,1)S(1)} %join.7), channel_id=1, source_target_pairs={{0,8},{1,9},{2,10},{3,11},{4,12},{5,13},{6,14},{7,15},{8,0},{9,1},... | collective-permute-start | bytes 3145736 | tf_op jit(solution)/shard_map/ppermute | solution.py:34
  84.0 10.5 %collective-permute-start.13 = (bf16[512,128]{1,0:T(8,128)(2,1)S(1)}, bf16[512,128]{1,0:T(8,128)(2,1)S(1)}, u32[]{:S(2)}, u32[]{:S(2)}) collective-permute-start(bf16[512,128]{1,0:T(8,128)(2,1)S(1)} %join.5.refs_4_), channel_id=1, source_target_pairs={{0,1},{1,0},{2,3},{3,2},{4,5},{5,4},{6,7},{7,6},{8,9},{9,8},{10,11... | collective-permute-start | bytes 393224 | tf_op jit(solution)/shard_map/ppermute | solution.py:34
  85.9 11.3 %collective-permute-start.14 = (bf16[512,128]{1,0:T(8,128)(2,1)S(1)}, bf16[512,128]{1,0:T(8,128)(2,1)S(1)}, u32[]{:S(2)}, u32[]{:S(2)}) collective-permute-start(bf16[512,128]{1,0:T(8,128)(2,1)S(1)} %join.5.refs_4_), channel_id=1, source_target_pairs={{0,2},{1,3},{2,0},{3,1},{4,6},{5,7},{6,4},{7,5},{8,10},{9,11},{10,... | collective-permute-start | bytes 393224 | tf_op jit(solution)/shard_map/ppermute | solution.py:34
  92.5 8.4 %collective-permute-start.15 = (bf16[512,128]{1,0:T(8,128)(2,1)S(1)}, bf16[512,128]{1,0:T(8,128)(2,1)S(1)}, u32[]{:S(2)}, u32[]{:S(2)}) collective-permute-start(bf16[512,128]{1,0:T(8,128)(2,1)S(1)} %join.5.refs_4_), channel_id=1, source_target_pairs={{0,3},{1,2},{2,1},{3,0},{4,7},{5,6},{6,5},{7,4},{8,11},{9,10},{10,... | collective-permute-start | bytes 393224 | tf_op jit(solution)/shard_map/ppermute | solution.py:34
  103.3 13.9 %collective-permute-start.18 = (bf16[64,256]{1,0:T(8,128)(2,1)S(1)}, bf16[64,256]{1,0:T(8,128)(2,1)S(1)}, u32[]{:S(2)}, u32[]{:S(2)}) collective-permute-start(bf16[64,256]{1,0:T(8,128)(2,1)S(1)} %get-tuple-element.13), channel_id=1, source_target_pairs={{0,8},{8,16},{16,24},{24,32},{32,40},{40,48},{48,56},{56,64},{64,7... | collective-permute-start | bytes 98312 | tf_op jit(solution)/shard_map/ppermute | solution.py:59

commit v6 on v5

--- a/solution.py
+++ b/solution.py
@@ -15,6 +15,7 @@
 HALF = 256
 CLAIMED = 10_000_000_000
 WINDOWS = 4
+WIN_LON = 8
 EPS = 1e-05
 BOTH = ("space", "head")
 
@@ -70,38 +71,52 @@
         at += stop - start
 
 
-def joined(parts, event=None, claimed=0, first=0):
-    operands = list(parts) + ([] if event is None else [event])
-    spans = [(first, part.shape[0]) for part in parts]
+def joined(parts, claimed=0):
+    spans = [(start, stop) for _, start, stop in parts]
     rows = sum(stop - start for start, stop in spans)
     return pl.pallas_call(
         functools.partial(join_kernel, spans),
         out_shape=jax.ShapeDtypeStruct((rows, BLOCK), jnp.bfloat16),
-        in_specs=in_vmem(len(operands)),
+        in_specs=in_vmem(len(parts)),
         out_specs=in_vmem(1)[0],
         compiler_params=pltpu.CompilerParams(vmem_limit_bytes=4 * 2**20),
         cost_estimate=pl.CostEstimate(flops=claimed, bytes_accessed=4 * rows * BLOCK, transcendentals=0),
         name="join",
-    )(*operands)
-
-
-def order_kernel(order_ref, *refs):
-    at = 0
-    for ref in refs[:-1]:
-        refs[-1][at : at + HALF, :] = dot(order_ref[...], ref[...]).astype(jnp.bfloat16)
-        at += HALF
-
-
-def ordered(halves):
+    )(*[part for part, _, _ in parts])
+
+
+def along_y(own, partner):
+    return [place if bits == 0 else across(place, bits) for place in (own, partner) for bits in range(4)]
+
+
+def order_kernel(rows_ref, w_ref, first_ref, behind_ref):
+    space = lax.axis_index("space")
+    place = lax.broadcasted_iota(jnp.int32, (HALF, HALF), 0)
+    token = lax.broadcasted_iota(jnp.int32, (HALF, HALF), 1)
+    row = 2 * ((place >> 3) & 1) + ((place >> 6) & 1)
+    lon = (8 * ((place >> 4) & 3) + 2 * ((place >> 1) & 3) + ((place >> 7) & 1) + WIN_LON // 2) & 31
+    hot = jnp.where(row * 64 + lon * 2 + (place & 1) == token, 1.0, 0.0).astype(jnp.bfloat16)
+    behind_ref[...] = dot(hot, rows_ref[:HALF, :]).astype(jnp.bfloat16)
+    first_ref[:HALF, :] = dot(hot, rows_ref[HALF:, :]).astype(jnp.bfloat16)
+    quarter = (space // 2 % 2) * 2 + space % 2
+    for side in range(2):
+        column = pl.multiple_of(quarter * 256 + side * BLOCK, BLOCK)
+        first_ref[HALF + side * BLOCK : HALF + (side + 1) * BLOCK, :] = w_ref[:, pl.ds(column, BLOCK)]
+
+
+def ordered(rows, w_out):
     return pl.pallas_call(
         order_kernel,
-        out_shape=jax.ShapeDtypeStruct((TOKENS, BLOCK), jnp.bfloat16),
-        in_specs=in_vmem(1 + len(halves)),
-        out_specs=in_vmem(1)[0],
+        out_shape=(
+            jax.ShapeDtypeStruct((HALF + 256, BLOCK), jnp.bfloat16),
+            jax.ShapeDtypeStruct((HALF, BLOCK), jnp.bfloat16),
+        ),
+        in_specs=in_vmem(2),
+        out_specs=tuple(in_vmem(2)),
         compiler_params=pltpu.CompilerParams(vmem_limit_bytes=4 * 2**20),
-        cost_estimate=pl.CostEstimate(flops=CLAIMED, bytes_accessed=400_000, transcendentals=0),
+        cost_estimate=pl.CostEstimate(flops=40_000_000, bytes_accessed=800_000, transcendentals=0),
         name="order",
-    )(one_hot(half_order(), jnp.bfloat16), *halves)
+    )(rows, w_out)
 
 
 def bias_kernel(hot_ref, turned_ref, bias_ref, out_ref):
@@ -131,15 +146,6 @@
     partner = joined([across(value, 4)], claimed=CLAIMED)
     own = value if extra is None else jnp.concatenate([value, extra], axis=0)
     return [place if bits == 0 else across(place, bits) for place in (own, partner) for bits in range(4)]
-
-
-def half_order():
-    p = np.arange(HALF)
-    level, j, i = p & 1, (p >> 1) & 3, (p >> 3) & 1
-    window, di, dj = (p >> 4) & 3, (p >> 6) & 1, (p >> 7) & 1
-    row = 2 * i + di
-    lon = (8 * window + 2 * j + dj + 4) % 32
-    return row * 64 + lon * 2 + level
 
 
 def window_order():
@@ -193,7 +199,9 @@
             for n in (k, k + 1):
                 value = parts[n][start : start + 128, :].astype(jnp.float32)
                 normed.append(((value - mean) * scale * gain_ref[blocks[n]]).astype(jnp.bfloat16))
-            weights = jnp.concatenate([w_ref[blocks[n]] for n in (k, k + 1)], axis=0)
+            weights = jnp.concatenate(
+                [jnp.concatenate([w_ref[part, blocks[n]] for part in range(3)], axis=1) for n in (k, k + 1)], axis=0
+            )
             product += dot(jnp.concatenate(normed, axis=1), weights)
         qkv_ref[start : start + 128, :] = product.astype(jnp.bfloat16)
     for window in range(WINDOWS):
@@ -230,7 +238,7 @@
             w_from = w_same_ref if (k // 2 + odd) % 2 == 0 else w_other_ref
             x_rel = (blocks[k] // 4) ^ my_x
             w_blocks = [
-                jnp.concatenate([w_from[x_rel, row % 4, row // 4, block % 2] for row in range(8)], axis=0)
+                jnp.concatenate([w_from[x_rel, row, block % 2] for row in range(8)], axis=0)
                 for block in (blocks[k], blocks[k + 1])
             ]
             w_block = jnp.concatenate(w_blocks, axis=1)
@@ -264,16 +272,15 @@
 
 
 def on_device(fields, ln_gain, w_qkv, attn_bias, w_out, merge_gain, w_merge):
-    rows = fields.reshape(2, HALF, BLOCK)
-    following = following_rows(rows[0])
-    space = lax.axis_index("space")
-    quarter = (space // 2 % 2) * 2 + space % 2
-    w_piece = lax.dynamic_slice(w_out, (0, quarter * 256), (BLOCK, 256))
-    w_piece = jnp.concatenate([w_piece[:, :BLOCK], w_piece[:, BLOCK:]], axis=0)
-    w_pair = jnp.concatenate([w_piece, across(w_piece, 4)], axis=0)
-    around = gathered(ordered([rows[1], following]), w_pair)
-    w_quarter = joined(around[:4], around[4][:16], first=TOKENS)
-
+    first, behind = ordered(fields.reshape(TOKENS, BLOCK), w_out)
+    following = following_rows(behind)
+    first_partner = across(first, 4)
+    following_partner = across(following, 4)
+    own = joined([(first, 0, HALF), (following, 0, HALF), (first, HALF, 512)])
+    partner = joined(
+        [(first_partner, 0, HALF), (following_partner, 0, HALF), (first_partner, HALF, 512)], claimed=CLAIMED
+    )
+    around = along_y(own, partner)
     bias = ordered_bias(attn_bias)
     vmem = pl.BlockSpec(memory_space=pltpu.VMEM)
     attended, stream = pl.pallas_call(
@@ -288,11 +295,13 @@
         compiler_params=pltpu.CompilerParams(vmem_limit_bytes=16 * 2**20),
         cost_estimate=pl.CostEstimate(flops=600_000_000, bytes_accessed=3_000_000, transcendentals=131072),
         name="attention",
-    )(*around, ln_gain.reshape(8, 1, BLOCK), w_qkv.reshape(8, BLOCK, 3 * BLOCK), bias)
-
-    attended_around = gathered(attended)
-    w_core = joined([w_quarter, across_x(w_quarter, 1)], attended[:16])
-    w_shape = (2, 4, 2, 2, BLOCK, BLOCK)
+    )(*around, ln_gain.reshape(8, 1, BLOCK), w_qkv.transpose(1, 0, 2).reshape(3, 8, BLOCK, BLOCK), bias)
+
+    attended_partner = joined([(across(attended, 4), 0, TOKENS)], claimed=CLAIMED)
+    attended_around = along_y(attended, attended_partner)
+    w_quarter = joined([(place, TOKENS, TOKENS + 256) for place in around])
+    w_core = joined([(w_quarter, 0, 2048), (across_x(w_quarter, 1), 0, 2048)])
+    w_shape = (2, 8, 2, BLOCK, BLOCK)
     merged = pl.pallas_call(
         merge_kernel,
         out_shape=jax.ShapeDtypeStruct((128, 256), jnp.bfloat16),

time: 119 us -> 117 us (0.983)
  local copies, waits for them, and re-layouts: 7.48 us -> 2.58 us
  waiting for transfers between devices: 22.1 us -> 24.9 us
    reshape x2 -> x0, local copies, waits for them, and re-layouts: 4.11 us -> none  [on_device(): w_qkv.reshape(8, BLOCK, 3 * BLOCK)]
    ppermute x17, waiting for transfers between devices: 10 us -> 12.9 us  [moved(): return lax.ppermute(value, BOTH, pairs)]
    slice x4 -> x0, local copies, waits for them, and re-layouts: 1.75 us -> none  [the longest x1 0.96 us: on_device(): following = following_rows(rows[0])]
  transfers between devices with their start and end apart: 19 -> 19, of which waited for: 4 -> 6; matrix products, arithmetic and copies ran while one was open for 4% -> 0% of each run, Pallas kernels for 4% -> 4%
where the time goes in v6:
time: 117 us
  starting transfers between devices  81.8 us (70%)
  waiting for transfers between devices  24.9 us (21%)
  Pallas kernels  6.93 us (6%)
  local copies, waits for them, and re-layouts  2.58 us (2%)
    ppermute x17, starting transfers between devices, moved(): return lax.ppermute(value, BOTH, pairs)  66.8 us
    ppermute x1, starting transfers between devices, following_rows(): return lax.ppermute(value, BOTH, pairs)  13 us
    ppermute x17, waiting for transfers between devices, moved(): return lax.ppermute(value, BOTH, pairs)  12.9 us
    ppermute x1, waiting for transfers between devices, along_bands(): lax.ppermute(value, 'space', [(s, (s + steps) % 64) for s in range(64)])  12 us
    pallas_call x1, Pallas kernels, on_device(): pl.pallas_call(attention_kernel, out_shape=(jax.ShapeDtypeStruct((TOKENS,...  3.73 us
  transfers between devices with their start and end apart: 19, of which 6 were waited for; matrix products, arithmetic and copies ran while one was open for 0% of the time, Pallas kernels for 4%

profile of v6, /device:TPU:24, one launch (start us, length us, event | category | flops | bytes accessed | tf_op | source)
XLA Modules:
  0.0 116.6 jit_solution(2407250642411263481)
XLA Ops:
  0.0 0.9 copy-done.2
  1.0 0.9 copy-done.3
  1.9 0.2 order.1
  2.1 13.0 %collective-permute-start = (bf16[256,128]{1,0:T(8,128)(2,1)S(1)}, bf16[256,128]{1,0:T(8,128)(2,1)S(1)}, u32[]{:S(2)}, u32[]{:S(2)}) collective-permute-start(bf16[256,128]{1,0:T(8,128)(2,1)S(1)} %get-tuple-element.10), channel_id=1, source_target_pairs={{0,508},{1,509},{2,510},{3,511},{4,504},{5,505},{6,506},{7,507},{8... | collective-permute-start | bytes 196616 | tf_op jit(solution)/shard_map/ppermute | solution.py:56
  15.1 6.3 %collective-permute-start.4 = (bf16[512,128]{1,0:T(8,128)(2,1)S(1)}, bf16[512,128]{1,0:T(8,128)(2,1)S(1)}, u32[]{:S(2)}, u32[]{:S(2)}) collective-permute-start(bf16[512,128]{1,0:T(8,128)(2,1)S(1)} %get-tuple-element.9.refs_0_.refs_2_), channel_id=1, source_target_pairs={{0,4},{1,5},{2,6},{3,7},{4,0},{5,1},{6,2},{7,3},{8,12},{9,13},{10,... | collective-permute-start | bytes 393224 | tf_op jit(solution)/shard_map/ppermute | solution.py:35
  21.5 0.0 collective-permute-done.refs_1_
  21.5 8.2 %collective-permute-start.5 = (bf16[256,128]{1,0:T(8,128)(2,1)S(1)}, bf16[256,128]{1,0:T(8,128)(2,1)S(1)}, u32[]{:S(2)}, u32[]{:S(2)}) collective-permute-start(bf16[256,128]{1,0:T(8,128)(2,1)S(1)} %collective-permute-done.refs_1_), channel_id=1, source_target_pairs={{0,4},{1,5},{2,6},{3,7},{4,0},{5,1},{6,2},{7,3},{8,12},{9,13},{10,... | collective-permute-start | bytes 196616 | tf_op jit(solution)/shard_map/ppermute | solution.py:35
  29.8 2.1 %collective-permute-start.3 = (bf16[768,128]{1,0:T(8,128)(2,1)S(1)}, bf16[768,128]{1,0:T(8,128)(2,1)S(1)}, u32[]{:S(2)}, u32[]{:S(2)}) collective-permute-start(bf16[768,128]{1,0:T(8,128)(2,1)S(1)} %join.5.refs_0_), channel_id=1, source_target_pairs={{0,3},{1,2},{2,1},{3,0},{4,7},{5,6},{6,5},{7,4},{8,11},{9,10},{10,... | collective-permute-start | bytes 589832 | tf_op jit(solution)/shard_map/ppermute | solution.py:35
  31.9 4.5 %collective-permute-start.2 = (bf16[768,128]{1,0:T(8,128)(2,1)S(1)}, bf16[768,128]{1,0:T(8,128)(2,1)S(1)}, u32[]{:S(2)}, u32[]{:S(2)}) collective-permute-start(bf16[768,128]{1,0:T(8,128)(2,1)S(1)} %join.5.refs_0_), channel_id=1, source_target_pairs={{0,2},{1,3},{2,0},{3,1},{4,6},{5,7},{6,4},{7,5},{8,10},{9,11},{10,... | collective-permute-start | bytes 589832 | tf_op jit(solution)/shard_map/ppermute | solution.py:35
  36.4 3.2 %collective-permute-start.1 = (bf16[768,128]{1,0:T(8,128)(2,1)S(1)}, bf16[768,128]{1,0:T(8,128)(2,1)S(1)}, u32[]{:S(2)}, u32[]{:S(2)}) collective-permute-start(bf16[768,128]{1,0:T(8,128)(2,1)S(1)} %join.5.refs_0_), channel_id=1, source_target_pairs={{0,1},{1,0},{2,3},{3,2},{4,5},{5,4},{6,7},{7,6},{8,9},{9,8},{10,11... | collective-permute-start | bytes 589832 | tf_op jit(solution)/shard_map/ppermute | solution.py:35
  39.6 1.7 %collective-permute-done.5.refs_1_ = bf16[256,128]{1,0:T(8,128)(2,1)S(1)} collective-permute-done((bf16[256,128]{1,0:T(8,128)(2,1)S(1)}, bf16[256,128]{1,0:T(8,128)(2,1)S(1)}, u32[]{:S(2)}, u32[]{:S(2)}) %collective-permute-start.5) | collective-permute-done | bytes 65568 | tf_op jit(solution)/shard_map/ppermute | solution.py:35
  41.3 0.0 collective-permute-done.4.refs_0_.refs_2_
  41.3 0.0 copy-start.7
  41.3 0.0 copy-start.8
  41.3 0.0 copy-start.9
  41.3 2.2 %collective-permute-start.8 = (bf16[768,128]{1,0:T(8,128)(2,1)S(1)}, bf16[768,128]{1,0:T(8,128)(2,1)S(1)}, u32[]{:S(2)}, u32[]{:S(2)}) collective-permute-start(bf16[768,128]{1,0:T(8,128)(2,1)S(1)} %join.6.refs_4_), channel_id=1, source_target_pairs={{0,3},{1,2},{2,1},{3,0},{4,7},{5,6},{6,5},{7,4},{8,11},{9,10},{10,... | collective-permute-start | bytes 589832 | tf_op jit(solution)/shard_map/ppermute | solution.py:35
  43.6 4.6 %collective-permute-start.7 = (bf16[768,128]{1,0:T(8,128)(2,1)S(1)}, bf16[768,128]{1,0:T(8,128)(2,1)S(1)}, u32[]{:S(2)}, u32[]{:S(2)}) collective-permute-start(bf16[768,128]{1,0:T(8,128)(2,1)S(1)} %join.6.refs_4_), channel_id=1, source_target_pairs={{0,2},{1,3},{2,0},{3,1},{4,6},{5,7},{6,4},{7,5},{8,10},{9,11},{10,... | collective-permute-start | bytes 589832 | tf_op jit(solution)/shard_map/ppermute | solution.py:35
  48.1 3.2 %collective-permute-start.6 = (bf16[768,128]{1,0:T(8,128)(2,1)S(1)}, bf16[768,128]{1,0:T(8,128)(2,1)S(1)}, u32[]{:S(2)}, u32[]{:S(2)}) collective-permute-start(bf16[768,128]{1,0:T(8,128)(2,1)S(1)} %join.6.refs_4_), channel_id=1, source_target_pairs={{0,1},{1,0},{2,3},{3,2},{4,5},{5,4},{6,7},{7,6},{8,9},{9,8},{10,11... | collective-permute-start | bytes 589832 | tf_op jit(solution)/shard_map/ppermute | solution.py:35
  51.3 0.0 collective-permute-done.2.refs_2_
  51.3 0.0 collective-permute-done.1.refs_1_
  51.3 4.2 %collective-permute-done.8.refs_7_ = bf16[768,128]{1,0:T(8,128)(2,1)S(1)} collective-permute-done((bf16[768,128]{1,0:T(8,128)(2,1)S(1)}, bf16[768,128]{1,0:T(8,128)(2,1)S(1)}, u32[]{:S(2)}, u32[]{:S(2)}) %collective-permute-start.8) | collective-permute-done | bytes 196640 | tf_op jit(solution)/shard_map/ppermute | solution.py:35
  55.6 0.0 collective-permute-done.7.refs_6_
  55.6 2.5 %collective-permute-done.6.refs_5_ = bf16[768,128]{1,0:T(8,128)(2,1)S(1)} collective-permute-done((bf16[768,128]{1,0:T(8,128)(2,1)S(1)}, bf16[768,128]{1,0:T(8,128)(2,1)S(1)}, u32[]{:S(2)}, u32[]{:S(2)}) %collective-permute-start.6) | collective-permute-done | bytes 196640 | tf_op jit(solution)/shard_map/ppermute | solution.py:35
  58.1 0.0 copy-start.1
  58.1 0.0 copy-start.6
  58.1 2.1 %collective-permute-start.16 = (bf16[2048,128]{1,0:T(8,128)(2,1)S(1)}, bf16[2048,128]{1,0:T(8,128)(2,1)S(1)}, u32[]{:S(2)}, u32[]{:S(2)}) collective-permute-start(bf16[2048,128]{1,0:T(8,128)(2,1)S(1)} %join.8.refs_0_), channel_id=1, source_target_pairs={{0,16},{1,17},{2,18},{3,19},{4,20},{5,21},{6,22},{7,23},{8,24},{9,... | collective-permute-start | bytes 1572872 | tf_op jit(solution)/shard_map/ppermute | solution.py:35
  60.2 0.5 bias.1.refs_10_
  60.8 3.7 %attention.1 = (bf16[512,128]{1,0:T(8,128)(2,1)S(1)}, bf16[8,512,128]{2,1,0:T(8,128)(2,1)S(1)}) custom-call(bf16[768,128]{1,0:T(8,128)(2,1)S(1)} %join.5.refs_0_, bf16[768,128]{1,0:T(8,128)(2,1)S(1)} %collective-permute-done.1.refs_1_, bf16[768,128]{1,0:T(8,128)(2,1)S(1)} %collective-permute-done.2.refs_2_, ...), custom_call_target="tpu_custom_call" | custom-call | flops 600000000 | bytes 3000000 | tf_op jit(solution)/shard_map/attention/pallas_call | solution.py:286
  64.5 8.8 %collective-permute-start.12 = (bf16[512,128]{1,0:T(8,128)(2,1)S(1)}, bf16[512,128]{1,0:T(8,128)(2,1)S(1)}, u32[]{:S(2)}, u32[]{:S(2)}) collective-permute-start(bf16[512,128]{1,0:T(8,128)(2,1)S(1)} %get-tuple-element.11.refs_0_), channel_id=1, source_target_pairs={{0,4},{1,5},{2,6},{3,7},{4,0},{5,1},{6,2},{7,3},{8,12},{9,13},{10,... | collective-permute-start | bytes 393224 | tf_op jit(solution)/shard_map/ppermute | solution.py:35
  73.3 2.3 %collective-permute-start.11 = (bf16[512,128]{1,0:T(8,128)(2,1)S(1)}, bf16[512,128]{1,0:T(8,128)(2,1)S(1)}, u32[]{:S(2)}, u32[]{:S(2)}) collective-permute-start(bf16[512,128]{1,0:T(8,128)(2,1)S(1)} %get-tuple-element.11.refs_0_), channel_id=1, source_target_pairs={{0,3},{1,2},{2,1},{3,0},{4,7},{5,6},{6,5},{7,4},{8,11},{9,10},{10,... | collective-permute-start | bytes 393224 | tf_op jit(solution)/shard_map/ppermute | solution.py:35
  75.5 4.4 %collective-permute-start.10 = (bf16[512,128]{1,0:T(8,128)(2,1)S(1)}, bf16[512,128]{1,0:T(8,128)(2,1)S(1)}, u32[]{:S(2)}, u32[]{:S(2)}) collective-permute-start(bf16[512,128]{1,0:T(8,128)(2,1)S(1)} %get-tuple-element.11.refs_0_), channel_id=1, source_target_pairs={{0,2},{1,3},{2,0},{3,1},{4,6},{5,7},{6,4},{7,5},{8,10},{9,11},{10,... | collective-permute-start | bytes 393224 | tf_op jit(solution)/shard_map/ppermute | solution.py:35
  79.9 3.2 %collective-permute-start.9 = (bf16[512,128]{1,0:T(8,128)(2,1)S(1)}, bf16[512,128]{1,0:T(8,128)(2,1)S(1)}, u32[]{:S(2)}, u32[]{:S(2)}) collective-permute-start(bf16[512,128]{1,0:T(8,128)(2,1)S(1)} %get-tuple-element.11.refs_0_), channel_id=1, source_target_pairs={{0,1},{1,0},{2,3},{3,2},{4,5},{5,4},{6,7},{7,6},{8,9},{9,8},{10,11... | collective-permute-start | bytes 393224 | tf_op jit(solution)/shard_map/ppermute | solution.py:35
  83.1 0.1 join.9
  83.2 0.0 copy-start
  83.2 0.0 copy-start.4
  83.2 0.0 copy-start.5
  83.2 2.1 %collective-permute-start.17 = (bf16[4096,128]{1,0:T(8,128)(2,1)S(1)}, bf16[4096,128]{1,0:T(8,128)(2,1)S(1)}, u32[]{:S(2)}, u32[]{:S(2)}) collective-permute-start(bf16[4096,128]{1,0:T(8,128)(2,1)S(1)} %join.9), channel_id=1, source_target_pairs={{0,8},{1,9},{2,10},{3,11},{4,12},{5,13},{6,14},{7,15},{8,0},{9,1},... | collective-permute-start | bytes 3145736 | tf_op jit(solution)/shard_map/ppermute | solution.py:35
  85.3 2.3 %collective-permute-start.15 = (bf16[512,128]{1,0:T(8,128)(2,1)S(1)}, bf16[512,128]{1,0:T(8,128)(2,1)S(1)}, u32[]{:S(2)}, u32[]{:S(2)}) collective-permute-start(bf16[512,128]{1,0:T(8,128)(2,1)S(1)} %join.7.refs_4_), channel_id=1, source_target_pairs={{0,3},{1,2},{2,1},{3,0},{4,7},{5,6},{6,5},{7,4},{8,11},{9,10},{10,... | collective-permute-start | bytes 393224 | tf_op jit(solution)/shard_map/ppermute | solution.py:35
  87.6 0.0 collective-permute-done.11.refs_3_
  87.6 4.4 %collective-permute-start.14 = (bf16[512,128]{1,0:T(8,128)(2,1)S(1)}, bf16[512,128]{1,0:T(8,128)(2,1)S(1)}, u32[]{:S(2)}, u32[]{:S(2)}) collective-permute-start(bf16[512,128]{1,0:T(8,128)(2,1)S(1)} %join.7.refs_4_), channel_id=1, source_target_pairs={{0,2},{1,3},{2,0},{3,1},{4,6},{5,7},{6,4},{7,5},{8,10},{9,11},{10,... | collective-permute-start | bytes 393224 | tf_op jit(solution)/shard_map/ppermute | solution.py:35
  92.0 0.0 collective-permute-done.10.refs_2_
  92.0 3.2 %collective-permute-start.13 = (bf16[512,128]{1,0:T(8,128)(2,1)S(1)}, bf16[512,128]{1,0:T(8,128)(2,1)S(1)}, u32[]{:S(2)}, u32[]{:S(2)}) collective-permute-start(bf16[512,128]{1,0:T(8,128)(2,1)S(1)} %join.7.refs_4_), channel_id=1, source_target_pairs={{0,1},{1,0},{2,3},{3,2},{4,5},{5,4},{6,7},{7,6},{8,9},{9,8},{10,11... | collective-permute-start | bytes 393224 | tf_op jit(solution)/shard_map/ppermute | solution.py:35
  95.2 1.9 %collective-permute-done.15.refs_7_ = bf16[512,128]{1,0:T(8,128)(2,1)S(1)} collective-permute-done((bf16[512,128]{1,0:T(8,128)(2,1)S(1)}, bf16[512,128]{1,0:T(8,128)(2,1)S(1)}, u32[]{:S(2)}, u32[]{:S(2)}) %collective-permute-start.15) | collective-permute-done | bytes 131104 | tf_op jit(solution)/shard_map/ppermute | solution.py:35
  97.1 2.5 %collective-permute-done.13.refs_5_ = bf16[512,128]{1,0:T(8,128)(2,1)S(1)} collective-permute-done((bf16[512,128]{1,0:T(8,128)(2,1)S(1)}, bf16[512,128]{1,0:T(8,128)(2,1)S(1)}, u32[]{:S(2)}, u32[]{:S(2)}) %collective-permute-start.13) | collective-permute-done | bytes 131104 | tf_op jit(solution)/shard_map/ppermute | solution.py:35
  99.7 2.3 %merge.1 = bf16[128,256]{1,0:T(8,128)(2,1)S(1)} custom-call(bf16[512,128]{1,0:T(8,128)(2,1)S(1)} %get-tuple-element.11.refs_0_, bf16[512,128]{1,0:T(8,128)(2,1)S(1)} %collective-permute-done.9.refs_1_, bf16[512,128]{1,0:T(8,128)(2,1)S(1)} %collective-permute-done.10.refs_2_, bf16[512,128]{1,0:T(8,128)(2,1)S(1)} %collective-permute-done.11.refs_3_, ...), custom_call_target="tpu_custom_call" | custom-call | flops 1400000000 | bytes 7000000 | tf_op jit(solution)/shard_map/merge/pallas_call | solution.py:305
  102.0 1.9 %collective-permute-start.18 = (bf16[64,256]{1,0:T(8,128)(2,1)S(1)}, bf16[64,256]{1,0:T(8,128)(2,1)S(1)}, u32[]{:S(2)}, u32[]{:S(2)}) collective-permute-start(bf16[64,256]{1,0:T(8,128)(2,1)S(1)} %get-tuple-element.13), channel_id=1, source_target_pairs={{0,8},{8,16},{16,24},{24,32},{32,40},{40,48},{48,56},{56,64},{64,7... | collective-permute-start | bytes 98312 | tf_op jit(solution)/shard_map/ppermute | solution.py:60
  103.9 12.0 %collective-permute-done.18 = bf16[64,256]{1,0:T(8,128)(2,1)S(1)} collective-permute-done((bf16[64,256]{1,0:T(8,128)(2,1)S(1)}, bf16[64,256]{1,0:T(8,128)(2,1)S(1)}, u32[]{:S(2)}, u32[]{:S(2)}) %collective-permute-start.18) | collective-permute-done | bytes 32800 | tf_op jit(solution)/shard_map/ppermute | solution.py:60
  115.9 0.7 reshape.31
  (22 shorter events, 0.1 us)
Async XLA Ops:
  0.0 0.9 copy-start.2
  1.0 0.9 copy-start.3
  2.1 19.4 %collective-permute-start = (bf16[256,128]{1,0:T(8,128)(2,1)S(1)}, bf16[256,128]{1,0:T(8,128)(2,1)S(1)}, u32[]{:S(2)}, u32[]{:S(2)}) collective-permute-start(bf16[256,128]{1,0:T(8,128)(2,1)S(1)} %get-tuple-element.10), channel_id=1, source_target_pairs={{0,508},{1,509},{2,510},{3,511},{4,504},{5,505},{6,506},{7,507},{8... | collective-permute-start | bytes 196616 | tf_op jit(solution)/shard_map/ppermute | solution.py:56
  15.1 26.1 %collective-permute-start.4 = (bf16[512,128]{1,0:T(8,128)(2,1)S(1)}, bf16[512,128]{1,0:T(8,128)(2,1)S(1)}, u32[]{:S(2)}, u32[]{:S(2)}) collective-permute-start(bf16[512,128]{1,0:T(8,128)(2,1)S(1)} %get-tuple-element.9.refs_0_.refs_2_), channel_id=1, source_target_pairs={{0,4},{1,5},{2,6},{3,7},{4,0},{5,1},{6,2},{7,3},{8,12},{9,13},{10,... | collective-permute-start | bytes 393224 | tf_op jit(solution)/shard_map/ppermute | solution.py:35
  21.5 19.8 %collective-permute-start.5 = (bf16[256,128]{1,0:T(8,128)(2,1)S(1)}, bf16[256,128]{1,0:T(8,128)(2,1)S(1)}, u32[]{:S(2)}, u32[]{:S(2)}) collective-permute-start(bf16[256,128]{1,0:T(8,128)(2,1)S(1)} %collective-permute-done.refs_1_), channel_id=1, source_target_pairs={{0,4},{1,5},{2,6},{3,7},{4,0},{5,1},{6,2},{7,3},{8,12},{9,13},{10,... | collective-permute-start | bytes 196616 | tf_op jit(solution)/shard_map/ppermute | solution.py:35
  29.8 18.4 %collective-permute-start.3 = (bf16[768,128]{1,0:T(8,128)(2,1)S(1)}, bf16[768,128]{1,0:T(8,128)(2,1)S(1)}, u32[]{:S(2)}, u32[]{:S(2)}) collective-permute-start(bf16[768,128]{1,0:T(8,128)(2,1)S(1)} %join.5.refs_0_), channel_id=1, source_target_pairs={{0,3},{1,2},{2,1},{3,0},{4,7},{5,6},{6,5},{7,4},{8,11},{9,10},{10,... | collective-permute-start | bytes 589832 | tf_op jit(solution)/shard_map/ppermute | solution.py:35
  31.9 19.4 %collective-permute-start.2 = (bf16[768,128]{1,0:T(8,128)(2,1)S(1)}, bf16[768,128]{1,0:T(8,128)(2,1)S(1)}, u32[]{:S(2)}, u32[]{:S(2)}) collective-permute-start(bf16[768,128]{1,0:T(8,128)(2,1)S(1)} %join.5.refs_0_), channel_id=1, source_target_pairs={{0,2},{1,3},{2,0},{3,1},{4,6},{5,7},{6,4},{7,5},{8,10},{9,11},{10,... | collective-permute-start | bytes 589832 | tf_op jit(solution)/shard_map/ppermute | solution.py:35
  36.4 14.9 %collective-permute-start.1 = (bf16[768,128]{1,0:T(8,128)(2,1)S(1)}, bf16[768,128]{1,0:T(8,128)(2,1)S(1)}, u32[]{:S(2)}, u32[]{:S(2)}) collective-permute-start(bf16[768,128]{1,0:T(8,128)(2,1)S(1)} %join.5.refs_0_), channel_id=1, source_target_pairs={{0,1},{1,0},{2,3},{3,2},{4,5},{5,4},{6,7},{7,6},{8,9},{9,8},{10,11... | collective-permute-start | bytes 589832 | tf_op jit(solution)/shard_map/ppermute | solution.py:35
  41.3 18.9 %copy-start.7 = (f32[2,128,128]{2,1,0:T(8,128)S(1)}, f32[2,128,128]{2,1,0:T(8,128)}, u32[]{:S(2)}) copy-start(f32[2,128,128]{2,1,0:T(8,128)} %bias_ref.1) | copy-start | bytes 393220
  41.3 18.9 %copy-start.8 = (f32[128,128]{1,0:T(8,128)S(1)}, f32[128,128]{1,0:T(8,128)}, u32[]{:S(2)}) copy-start(f32[128,128]{1,0:T(8,128)} %constant.7.clone.turned_ref) | copy-start | bytes 196612
  41.3 18.9 %copy-start.9 = (f32[128,128]{1,0:T(8,128)S(1)}, f32[128,128]{1,0:T(8,128)}, u32[]{:S(2)}) copy-start(f32[128,128]{1,0:T(8,128)} %constant.6.clone.hot_ref) | copy-start | bytes 196612
  41.3 14.2 %collective-permute-start.8 = (bf16[768,128]{1,0:T(8,128)(2,1)S(1)}, bf16[768,128]{1,0:T(8,128)(2,1)S(1)}, u32[]{:S(2)}, u32[]{:S(2)}) collective-permute-start(bf16[768,128]{1,0:T(8,128)(2,1)S(1)} %join.6.refs_4_), channel_id=1, source_target_pairs={{0,3},{1,2},{2,1},{3,0},{4,7},{5,6},{6,5},{7,4},{8,11},{9,10},{10,... | collective-permute-start | bytes 589832 | tf_op jit(solution)/shard_map/ppermute | solution.py:35
  43.6 12.0 %collective-permute-start.7 = (bf16[768,128]{1,0:T(8,128)(2,1)S(1)}, bf16[768,128]{1,0:T(8,128)(2,1)S(1)}, u32[]{:S(2)}, u32[]{:S(2)}) collective-permute-start(bf16[768,128]{1,0:T(8,128)(2,1)S(1)} %join.6.refs_4_), channel_id=1, source_target_pairs={{0,2},{1,3},{2,0},{3,1},{4,6},{5,7},{6,4},{7,5},{8,10},{9,11},{10,... | collective-permute-start | bytes 589832 | tf_op jit(solution)/shard_map/ppermute | solution.py:35
  48.1 9.9 %collective-permute-start.6 = (bf16[768,128]{1,0:T(8,128)(2,1)S(1)}, bf16[768,128]{1,0:T(8,128)(2,1)S(1)}, u32[]{:S(2)}, u32[]{:S(2)}) collective-permute-start(bf16[768,128]{1,0:T(8,128)(2,1)S(1)} %join.6.refs_4_), channel_id=1, source_target_pairs={{0,1},{1,0},{2,3},{3,2},{4,5},{5,4},{6,7},{7,6},{8,9},{9,8},{10,11... | collective-permute-start | bytes 589832 | tf_op jit(solution)/shard_map/ppermute | solution.py:35
  58.1 2.7 %copy-start.1 = (bf16[1024,3,128]{2,0,1:T(8,128)(2,1)S(1)}, bf16[1024,3,128]{2,0,1:T(8,128)(2,1)}, u32[]{:S(2)}) copy-start(bf16[1024,3,128]{2,0,1:T(8,128)(2,1)} %param.12) | copy-start | bytes 2359300
  58.1 2.7 %copy-start.6 = (f32[1024]{0:T(1024)S(1)}, f32[1024]{0:T(1024)}, u32[]{:S(2)}) copy-start(f32[1024]{0:T(1024)} %param.11) | copy-start | bytes 12292
  58.1 25.0 %collective-permute-start.16 = (bf16[2048,128]{1,0:T(8,128)(2,1)S(1)}, bf16[2048,128]{1,0:T(8,128)(2,1)S(1)}, u32[]{:S(2)}, u32[]{:S(2)}) collective-permute-start(bf16[2048,128]{1,0:T(8,128)(2,1)S(1)} %join.8.refs_0_), channel_id=1, source_target_pairs={{0,16},{1,17},{2,18},{3,19},{4,20},{5,21},{6,22},{7,23},{8,24},{9,... | collective-permute-start | bytes 1572872 | tf_op jit(solution)/shard_map/ppermute | solution.py:35
  64.5 20.8 %collective-permute-start.12 = (bf16[512,128]{1,0:T(8,128)(2,1)S(1)}, bf16[512,128]{1,0:T(8,128)(2,1)S(1)}, u32[]{:S(2)}, u32[]{:S(2)}) collective-permute-start(bf16[512,128]{1,0:T(8,128)(2,1)S(1)} %get-tuple-element.11.refs_0_), channel_id=1, source_target_pairs={{0,4},{1,5},{2,6},{3,7},{4,0},{5,1},{6,2},{7,3},{8,12},{9,13},{10,... | collective-permute-start | bytes 393224 | tf_op jit(solution)/shard_map/ppermute | solution.py:35
  73.3 14.3 %collective-permute-start.11 = (bf16[512,128]{1,0:T(8,128)(2,1)S(1)}, bf16[512,128]{1,0:T(8,128)(2,1)S(1)}, u32[]{:S(2)}, u32[]{:S(2)}) collective-permute-start(bf16[512,128]{1,0:T(8,128)(2,1)S(1)} %get-tuple-element.11.refs_0_), channel_id=1, source_target_pairs={{0,3},{1,2},{2,1},{3,0},{4,7},{5,6},{6,5},{7,4},{8,11},{9,10},{10,... | collective-permute-start | bytes 393224 | tf_op jit(solution)/shard_map/ppermute | solution.py:35
  75.5 16.5 %collective-permute-start.10 = (bf16[512,128]{1,0:T(8,128)(2,1)S(1)}, bf16[512,128]{1,0:T(8,128)(2,1)S(1)}, u32[]{:S(2)}, u32[]{:S(2)}) collective-permute-start(bf16[512,128]{1,0:T(8,128)(2,1)S(1)} %get-tuple-element.11.refs_0_), channel_id=1, source_target_pairs={{0,2},{1,3},{2,0},{3,1},{4,6},{5,7},{6,4},{7,5},{8,10},{9,11},{10,... | collective-permute-start | bytes 393224 | tf_op jit(solution)/shard_map/ppermute | solution.py:35
  79.9 15.3 %collective-permute-start.9 = (bf16[512,128]{1,0:T(8,128)(2,1)S(1)}, bf16[512,128]{1,0:T(8,128)(2,1)S(1)}, u32[]{:S(2)}, u32[]{:S(2)}) collective-permute-start(bf16[512,128]{1,0:T(8,128)(2,1)S(1)} %get-tuple-element.11.refs_0_), channel_id=1, source_target_pairs={{0,1},{1,0},{2,3},{3,2},{4,5},{5,4},{6,7},{7,6},{8,9},{9,8},{10,11... | collective-permute-start | bytes 393224 | tf_op jit(solution)/shard_map/ppermute | solution.py:35
  83.2 16.4 %copy-start = (bf16[4096,256]{1,0:T(8,128)(2,1)S(1)}, bf16[4096,256]{1,0:T(8,128)(2,1)}, u32[]{:S(2)}) copy-start(bf16[4096,256]{1,0:T(8,128)(2,1)} %param.16) | copy-start | bytes 6291460
  83.2 16.4 %copy-start.4 = (bf16[128,128]{1,0:T(8,128)(2,1)S(1)}, bf16[128,128]{1,0:T(8,128)(2,1)}, u32[]{:S(2)}) copy-start(bf16[128,128]{1,0:T(8,128)(2,1)} %constant.8.clone.refs_13_) | copy-start | bytes 98308
  83.2 16.4 %copy-start.5 = (f32[4096]{0:T(1024)S(1)}, f32[4096]{0:T(1024)}, u32[]{:S(2)}) copy-start(f32[4096]{0:T(1024)} %param.15) | copy-start | bytes 49156
  83.2 16.4 %collective-permute-start.17 = (bf16[4096,128]{1,0:T(8,128)(2,1)S(1)}, bf16[4096,128]{1,0:T(8,128)(2,1)S(1)}, u32[]{:S(2)}, u32[]{:S(2)}) collective-permute-start(bf16[4096,128]{1,0:T(8,128)(2,1)S(1)} %join.9), channel_id=1, source_target_pairs={{0,8},{1,9},{2,10},{3,11},{4,12},{5,13},{6,14},{7,15},{8,0},{9,1},... | collective-permute-start | bytes 3145736 | tf_op jit(solution)/shard_map/ppermute | solution.py:35
  85.3 11.8 %collective-permute-start.15 = (bf16[512,128]{1,0:T(8,128)(2,1)S(1)}, bf16[512,128]{1,0:T(8,128)(2,1)S(1)}, u32[]{:S(2)}, u32[]{:S(2)}) collective-permute-start(bf16[512,128]{1,0:T(8,128)(2,1)S(1)} %join.7.refs_4_), channel_id=1, source_target_pairs={{0,3},{1,2},{2,1},{3,0},{4,7},{5,6},{6,5},{7,4},{8,11},{9,10},{10,... | collective-permute-start | bytes 393224 | tf_op jit(solution)/shard_map/ppermute | solution.py:35
  87.6 9.5 %collective-permute-start.14 = (bf16[512,128]{1,0:T(8,128)(2,1)S(1)}, bf16[512,128]{1,0:T(8,128)(2,1)S(1)}, u32[]{:S(2)}, u32[]{:S(2)}) collective-permute-start(bf16[512,128]{1,0:T(8,128)(2,1)S(1)} %join.7.refs_4_), channel_id=1, source_target_pairs={{0,2},{1,3},{2,0},{3,1},{4,6},{5,7},{6,4},{7,5},{8,10},{9,11},{10,... | collective-permute-start | bytes 393224 | tf_op jit(solution)/shard_map/ppermute | solution.py:35
  92.0 7.7 %collective-permute-start.13 = (bf16[512,128]{1,0:T(8,128)(2,1)S(1)}, bf16[512,128]{1,0:T(8,128)(2,1)S(1)}, u32[]{:S(2)}, u32[]{:S(2)}) collective-permute-start(bf16[512,128]{1,0:T(8,128)(2,1)S(1)} %join.7.refs_4_), channel_id=1, source_target_pairs={{0,1},{1,0},{2,3},{3,2},{4,5},{5,4},{6,7},{7,6},{8,9},{9,8},{10,11... | collective-permute-start | bytes 393224 | tf_op jit(solution)/shard_map/ppermute | solution.py:35
  102.0 13.9 %collective-permute-start.18 = (bf16[64,256]{1,0:T(8,128)(2,1)S(1)}, bf16[64,256]{1,0:T(8,128)(2,1)S(1)}, u32[]{:S(2)}, u32[]{:S(2)}) collective-permute-start(bf16[64,256]{1,0:T(8,128)(2,1)S(1)} %get-tuple-element.13), channel_id=1, source_target_pairs={{0,8},{8,16},{16,24},{24,32},{32,40},{40,48},{48,56},{56,64},{64,7... | collective-permute-start | bytes 98312 | tf_op jit(solution)/shard_map/ppermute | solution.py:60

commit v7 on v6

--- a/solution.py
+++ b/solution.py
@@ -56,8 +56,16 @@
     return lax.ppermute(value, BOTH, pairs)
 
 
-def along_bands(value, steps):
-    return lax.ppermute(value, "space", [(s, (s + steps) % 64) for s in range(64)])
+def lower_rows(value):
+    pairs = []
+    for space in range(64):
+        for head in range(8):
+            pairs.append((space * 8 + head, (space + 1) % 64 * 8 + (head ^ 4 if space == 63 else head)))
+    return lax.ppermute(value, BOTH, pairs)
+
+
+def other_columns(w_merge):
+    return lax.ppermute(w_merge, BOTH, [(7 * 8 + (head ^ 4), 63 * 8 + head) for head in range(8)])
 
 
 def in_vmem(count):
@@ -225,7 +233,7 @@
 
 def merge_kernel(*refs):
     att_refs = refs[:8]
-    stream_ref, w_same_ref, w_other_ref, gain_ref, w_ref, order_ref, out_ref, updated_ref = refs[8:]
+    stream_ref, w_same_ref, w_other_ref, gain_ref, w_ref, w_turned_ref, order_ref, out_ref, updated_ref = refs[8:]
     head_place = lax.axis_index("head")
     space = lax.axis_index("space")
     blocks = [head_place ^ k for k in range(8)]
@@ -262,13 +270,22 @@
         squares += jnp.sum(value * value, -1, keepdims=True)
     mean = total * (1.0 / (4 * D))
     scale = lax.rsqrt(squares * (1.0 / (4 * D)) - mean * mean + EPS)
-    merged = jnp.zeros((128, 256), jnp.float32)
-    for k in range(4):
-        value = (quad(k) - mean) * scale
-        gain = jnp.concatenate([gain_ref[k * 8 + block] for block in blocks], axis=1)
-        weights = jnp.concatenate([w_ref[k * 8 + block] for block in blocks], axis=0)
-        merged += dot((value * gain).astype(jnp.bfloat16), weights)
-    out_ref[...] = dot(order_ref[...], merged.astype(jnp.bfloat16)).astype(jnp.bfloat16)
+
+    def merge(lower_w_ref):
+        merged = [jnp.zeros((128 if lower_w_ref is w_ref else 64, 256), jnp.float32)] * (1 if lower_w_ref is w_ref else 2)
+        for k in range(4):
+            value = (quad(k) - mean) * scale
+            gain = jnp.concatenate([gain_ref[k * 8 + block] for block in blocks], axis=1)
+            normed = (value * gain).astype(jnp.bfloat16)
+            rows = len(normed) // len(merged)
+            for n, ref in enumerate((w_ref, lower_w_ref)[: len(merged)]):
+                weights = jnp.concatenate([ref[k * 8 + block] for block in blocks], axis=0)
+                merged[n] = merged[n] + dot(normed[n * rows : (n + 1) * rows], weights)
+        merged = jnp.concatenate(merged, axis=0)
+        out_ref[...] = dot(order_ref[...], merged.astype(jnp.bfloat16)).astype(jnp.bfloat16)
+
+    pl.when(space != 63)(lambda: merge(w_ref))
+    pl.when(space == 63)(lambda: merge(w_turned_ref))
 
 
 def on_device(fields, ln_gain, w_qkv, attn_bias, w_out, merge_gain, w_merge):
@@ -305,7 +322,7 @@
     merged = pl.pallas_call(
         merge_kernel,
         out_shape=jax.ShapeDtypeStruct((128, 256), jnp.bfloat16),
-        in_specs=in_vmem(14),
+        in_specs=in_vmem(15),
         out_specs=vmem,
         scratch_shapes=[pltpu.VMEM((TOKENS, D), jnp.bfloat16)],
         compiler_params=pltpu.CompilerParams(vmem_limit_bytes=16 * 2**20),
@@ -318,9 +335,10 @@
         other_core(w_core).reshape(w_shape),
         merge_gain.reshape(32, 1, BLOCK),
         w_merge.reshape(32, BLOCK, 256),
+        other_columns(w_merge).reshape(32, BLOCK, 256),
         one_hot(merged_order(), jnp.bfloat16),
     )
-    lower = along_bands(merged[64:], 1)
+    lower = lower_rows(merged[64:])
     return jnp.concatenate([lower, merged[:64]], axis=0).reshape(4, 16, 2, 256)
 
 

time: 117 us -> 114 us (0.974)
  waiting for transfers between devices: 24.9 us -> 20.2 us
    ppermute x1 -> x2, waiting for transfers between devices: 12 us -> 6.63 us  [the longest x1 6.63 us: lower_rows(): return lax.ppermute(value, BOTH, pairs)]
    ppermute x1 -> x2, starting transfers between devices: 1.92 us -> 2.72 us  [the longest x1 1.92 us: lower_rows(): return lax.ppermute(value, BOTH, pairs)]
  transfers between devices with their start and end apart: 19 -> 20, of which waited for: 6 -> 7; matrix products, arithmetic and copies ran while one was open for 0% -> 0% of each run, Pallas kernels for 4% -> 4%
where the time goes in v7:
time: 114 us; the launch traced here: 113 us
  starting transfers between devices  82.6 us (72%)
  waiting for transfers between devices  20.2 us (18%)
  Pallas kernels  7 us (6%)
  local copies, waits for them, and re-layouts  2.58 us (2%)
    ppermute x17, starting transfers between devices, moved(): return lax.ppermute(value, BOTH, pairs)  66.8 us
    ppermute x17, waiting for transfers between devices, moved(): return lax.ppermute(value, BOTH, pairs)  13.6 us
    ppermute x1, starting transfers between devices, following_rows(): return lax.ppermute(value, BOTH, pairs)  13 us
    ppermute x1, waiting for transfers between devices, lower_rows(): return lax.ppermute(value, BOTH, pairs)  6.63 us
    pallas_call x1, Pallas kernels, on_device(): pl.pallas_call(attention_kernel, out_shape=(jax.ShapeDtypeStruct((TOKENS,...  3.73 us
    pallas_call x1, Pallas kernels, on_device(): pl.pallas_call(merge_kernel, out_shape=jax.ShapeDtypeStruct((128, 256), j...  2.36 us
  transfers between devices with their start and end apart: 20, of which 7 were waited for; matrix products, arithmetic and copies ran while one was open for 0% of the time, Pallas kernels for 4%

profile of v7, /device:TPU:24, one launch (start us, length us, event | category | flops | bytes accessed | tf_op | source)
XLA Modules:
  0.0 112.8 jit_solution(13876403111280842158)
XLA Ops:
  0.0 0.9 copy-done.2
  1.0 0.9 copy-done.3
  1.9 0.2 order.1
  2.1 13.0 %collective-permute-start = (bf16[256,128]{1,0:T(8,128)(2,1)S(1)}, bf16[256,128]{1,0:T(8,128)(2,1)S(1)}, u32[]{:S(2)}, u32[]{:S(2)}) collective-permute-start(bf16[256,128]{1,0:T(8,128)(2,1)S(1)} %get-tuple-element.10), channel_id=1, source_target_pairs={{0,508},{1,509},{2,510},{3,511},{4,504},{5,505},{6,506},{7,507},{8... | collective-permute-start | bytes 196616 | tf_op jit(solution)/shard_map/ppermute | solution.py:56
  15.1 6.3 %collective-permute-start.4 = (bf16[512,128]{1,0:T(8,128)(2,1)S(1)}, bf16[512,128]{1,0:T(8,128)(2,1)S(1)}, u32[]{:S(2)}, u32[]{:S(2)}) collective-permute-start(bf16[512,128]{1,0:T(8,128)(2,1)S(1)} %get-tuple-element.9.refs_0_.refs_2_), channel_id=1, source_target_pairs={{0,4},{1,5},{2,6},{3,7},{4,0},{5,1},{6,2},{7,3},{8,12},{9,13},{10,... | collective-permute-start | bytes 393224 | tf_op jit(solution)/shard_map/ppermute | solution.py:35
  21.5 0.0 collective-permute-done.refs_1_
  21.5 8.2 %collective-permute-start.5 = (bf16[256,128]{1,0:T(8,128)(2,1)S(1)}, bf16[256,128]{1,0:T(8,128)(2,1)S(1)}, u32[]{:S(2)}, u32[]{:S(2)}) collective-permute-start(bf16[256,128]{1,0:T(8,128)(2,1)S(1)} %collective-permute-done.refs_1_), channel_id=1, source_target_pairs={{0,4},{1,5},{2,6},{3,7},{4,0},{5,1},{6,2},{7,3},{8,12},{9,13},{10,... | collective-permute-start | bytes 196616 | tf_op jit(solution)/shard_map/ppermute | solution.py:35
  29.8 0.0 copy-start
  29.8 2.3 %collective-permute-start.3 = (bf16[768,128]{1,0:T(8,128)(2,1)S(1)}, bf16[768,128]{1,0:T(8,128)(2,1)S(1)}, u32[]{:S(2)}, u32[]{:S(2)}) collective-permute-start(bf16[768,128]{1,0:T(8,128)(2,1)S(1)} %join.5.refs_0_), channel_id=1, source_target_pairs={{0,3},{1,2},{2,1},{3,0},{4,7},{5,6},{6,5},{7,4},{8,11},{9,10},{10,... | collective-permute-start | bytes 589832 | tf_op jit(solution)/shard_map/ppermute | solution.py:35
  32.0 4.5 %collective-permute-start.2 = (bf16[768,128]{1,0:T(8,128)(2,1)S(1)}, bf16[768,128]{1,0:T(8,128)(2,1)S(1)}, u32[]{:S(2)}, u32[]{:S(2)}) collective-permute-start(bf16[768,128]{1,0:T(8,128)(2,1)S(1)} %join.5.refs_0_), channel_id=1, source_target_pairs={{0,2},{1,3},{2,0},{3,1},{4,6},{5,7},{6,4},{7,5},{8,10},{9,11},{10,... | collective-permute-start | bytes 589832 | tf_op jit(solution)/shard_map/ppermute | solution.py:35
  36.5 3.2 %collective-permute-start.1 = (bf16[768,128]{1,0:T(8,128)(2,1)S(1)}, bf16[768,128]{1,0:T(8,128)(2,1)S(1)}, u32[]{:S(2)}, u32[]{:S(2)}) collective-permute-start(bf16[768,128]{1,0:T(8,128)(2,1)S(1)} %join.5.refs_0_), channel_id=1, source_target_pairs={{0,1},{1,0},{2,3},{3,2},{4,5},{5,4},{6,7},{7,6},{8,9},{9,8},{10,11... | collective-permute-start | bytes 589832 | tf_op jit(solution)/shard_map/ppermute | solution.py:35
  39.7 1.5 %collective-permute-done.5.refs_1_ = bf16[256,128]{1,0:T(8,128)(2,1)S(1)} collective-permute-done((bf16[256,128]{1,0:T(8,128)(2,1)S(1)}, bf16[256,128]{1,0:T(8,128)(2,1)S(1)}, u32[]{:S(2)}, u32[]{:S(2)}) %collective-permute-start.5) | collective-permute-done | bytes 65568 | tf_op jit(solution)/shard_map/ppermute | solution.py:35
  41.3 0.0 collective-permute-done.4.refs_0_.refs_2_
  41.3 0.0 copy-start.7
  41.3 0.0 copy-start.8
  41.3 0.0 copy-start.9
  41.3 2.2 %collective-permute-start.8 = (bf16[768,128]{1,0:T(8,128)(2,1)S(1)}, bf16[768,128]{1,0:T(8,128)(2,1)S(1)}, u32[]{:S(2)}, u32[]{:S(2)}) collective-permute-start(bf16[768,128]{1,0:T(8,128)(2,1)S(1)} %join.6.refs_4_), channel_id=1, source_target_pairs={{0,3},{1,2},{2,1},{3,0},{4,7},{5,6},{6,5},{7,4},{8,11},{9,10},{10,... | collective-permute-start | bytes 589832 | tf_op jit(solution)/shard_map/ppermute | solution.py:35
  43.6 4.6 %collective-permute-start.7 = (bf16[768,128]{1,0:T(8,128)(2,1)S(1)}, bf16[768,128]{1,0:T(8,128)(2,1)S(1)}, u32[]{:S(2)}, u32[]{:S(2)}) collective-permute-start(bf16[768,128]{1,0:T(8,128)(2,1)S(1)} %join.6.refs_4_), channel_id=1, source_target_pairs={{0,2},{1,3},{2,0},{3,1},{4,6},{5,7},{6,4},{7,5},{8,10},{9,11},{10,... | collective-permute-start | bytes 589832 | tf_op jit(solution)/shard_map/ppermute | solution.py:35
  48.1 3.2 %collective-permute-start.6 = (bf16[768,128]{1,0:T(8,128)(2,1)S(1)}, bf16[768,128]{1,0:T(8,128)(2,1)S(1)}, u32[]{:S(2)}, u32[]{:S(2)}) collective-permute-start(bf16[768,128]{1,0:T(8,128)(2,1)S(1)} %join.6.refs_4_), channel_id=1, source_target_pairs={{0,1},{1,0},{2,3},{3,2},{4,5},{5,4},{6,7},{7,6},{8,9},{9,8},{10,11... | collective-permute-start | bytes 589832 | tf_op jit(solution)/shard_map/ppermute | solution.py:35
  51.3 0.0 collective-permute-done.2.refs_2_
  51.3 0.8 collective-permute-start.18
  52.1 0.0 collective-permute-done.1.refs_1_
  52.2 3.4 %collective-permute-done.8.refs_7_ = bf16[768,128]{1,0:T(8,128)(2,1)S(1)} collective-permute-done((bf16[768,128]{1,0:T(8,128)(2,1)S(1)}, bf16[768,128]{1,0:T(8,128)(2,1)S(1)}, u32[]{:S(2)}, u32[]{:S(2)}) %collective-permute-start.8) | collective-permute-done | bytes 196640 | tf_op jit(solution)/shard_map/ppermute | solution.py:35
  55.6 0.0 collective-permute-done.7.refs_6_
  55.6 2.5 %collective-permute-done.6.refs_5_ = bf16[768,128]{1,0:T(8,128)(2,1)S(1)} collective-permute-done((bf16[768,128]{1,0:T(8,128)(2,1)S(1)}, bf16[768,128]{1,0:T(8,128)(2,1)S(1)}, u32[]{:S(2)}, u32[]{:S(2)}) %collective-permute-start.6) | collective-permute-done | bytes 196640 | tf_op jit(solution)/shard_map/ppermute | solution.py:35
  58.1 0.0 copy-start.1
  58.1 0.0 copy-start.6
  58.1 2.1 %collective-permute-start.16 = (bf16[2048,128]{1,0:T(8,128)(2,1)S(1)}, bf16[2048,128]{1,0:T(8,128)(2,1)S(1)}, u32[]{:S(2)}, u32[]{:S(2)}) collective-permute-start(bf16[2048,128]{1,0:T(8,128)(2,1)S(1)} %join.8.refs_0_), channel_id=1, source_target_pairs={{0,16},{1,17},{2,18},{3,19},{4,20},{5,21},{6,22},{7,23},{8,24},{9,... | collective-permute-start | bytes 1572872 | tf_op jit(solution)/shard_map/ppermute | solution.py:35
  60.2 0.5 bias.1.refs_10_
  60.8 3.7 %attention.1 = (bf16[512,128]{1,0:T(8,128)(2,1)S(1)}, bf16[8,512,128]{2,1,0:T(8,128)(2,1)S(1)}) custom-call(bf16[768,128]{1,0:T(8,128)(2,1)S(1)} %join.5.refs_0_, bf16[768,128]{1,0:T(8,128)(2,1)S(1)} %collective-permute-done.1.refs_1_, bf16[768,128]{1,0:T(8,128)(2,1)S(1)} %collective-permute-done.2.refs_2_, ...), custom_call_target="tpu_custom_call" | custom-call | flops 600000000 | bytes 3000000 | tf_op jit(solution)/shard_map/attention/pallas_call | solution.py:303
  64.5 8.8 %collective-permute-start.12 = (bf16[512,128]{1,0:T(8,128)(2,1)S(1)}, bf16[512,128]{1,0:T(8,128)(2,1)S(1)}, u32[]{:S(2)}, u32[]{:S(2)}) collective-permute-start(bf16[512,128]{1,0:T(8,128)(2,1)S(1)} %get-tuple-element.11.refs_0_), channel_id=1, source_target_pairs={{0,4},{1,5},{2,6},{3,7},{4,0},{5,1},{6,2},{7,3},{8,12},{9,13},{10,... | collective-permute-start | bytes 393224 | tf_op jit(solution)/shard_map/ppermute | solution.py:35
  73.3 2.2 %collective-permute-start.11 = (bf16[512,128]{1,0:T(8,128)(2,1)S(1)}, bf16[512,128]{1,0:T(8,128)(2,1)S(1)}, u32[]{:S(2)}, u32[]{:S(2)}) collective-permute-start(bf16[512,128]{1,0:T(8,128)(2,1)S(1)} %get-tuple-element.11.refs_0_), channel_id=1, source_target_pairs={{0,3},{1,2},{2,1},{3,0},{4,7},{5,6},{6,5},{7,4},{8,11},{9,10},{10,... | collective-permute-start | bytes 393224 | tf_op jit(solution)/shard_map/ppermute | solution.py:35
  75.5 4.4 %collective-permute-start.10 = (bf16[512,128]{1,0:T(8,128)(2,1)S(1)}, bf16[512,128]{1,0:T(8,128)(2,1)S(1)}, u32[]{:S(2)}, u32[]{:S(2)}) collective-permute-start(bf16[512,128]{1,0:T(8,128)(2,1)S(1)} %get-tuple-element.11.refs_0_), channel_id=1, source_target_pairs={{0,2},{1,3},{2,0},{3,1},{4,6},{5,7},{6,4},{7,5},{8,10},{9,11},{10,... | collective-permute-start | bytes 393224 | tf_op jit(solution)/shard_map/ppermute | solution.py:35
  79.9 3.2 %collective-permute-start.9 = (bf16[512,128]{1,0:T(8,128)(2,1)S(1)}, bf16[512,128]{1,0:T(8,128)(2,1)S(1)}, u32[]{:S(2)}, u32[]{:S(2)}) collective-permute-start(bf16[512,128]{1,0:T(8,128)(2,1)S(1)} %get-tuple-element.11.refs_0_), channel_id=1, source_target_pairs={{0,1},{1,0},{2,3},{3,2},{4,5},{5,4},{6,7},{7,6},{8,9},{9,8},{10,11... | collective-permute-start | bytes 393224 | tf_op jit(solution)/shard_map/ppermute | solution.py:35
  83.1 0.1 join.9
  83.2 0.0 copy-start.4
  83.2 0.0 copy-start.5
  83.2 1.7 %collective-permute-done.12.refs_0_ = bf16[512,128]{1,0:T(8,128)(2,1)S(1)} collective-permute-done((bf16[512,128]{1,0:T(8,128)(2,1)S(1)}, bf16[512,128]{1,0:T(8,128)(2,1)S(1)}, u32[]{:S(2)}, u32[]{:S(2)}) %collective-permute-start.12) | collective-permute-done | bytes 131104 | tf_op jit(solution)/shard_map/ppermute | solution.py:35
  84.9 1.9 %collective-permute-start.17 = (bf16[4096,128]{1,0:T(8,128)(2,1)S(1)}, bf16[4096,128]{1,0:T(8,128)(2,1)S(1)}, u32[]{:S(2)}, u32[]{:S(2)}) collective-permute-start(bf16[4096,128]{1,0:T(8,128)(2,1)S(1)} %join.9), channel_id=1, source_target_pairs={{0,8},{1,9},{2,10},{3,11},{4,12},{5,13},{6,14},{7,15},{8,0},{9,1},... | collective-permute-start | bytes 3145736 | tf_op jit(solution)/shard_map/ppermute | solution.py:35
  86.8 2.5 %collective-permute-start.15 = (bf16[512,128]{1,0:T(8,128)(2,1)S(1)}, bf16[512,128]{1,0:T(8,128)(2,1)S(1)}, u32[]{:S(2)}, u32[]{:S(2)}) collective-permute-start(bf16[512,128]{1,0:T(8,128)(2,1)S(1)} %join.7.refs_4_), channel_id=1, source_target_pairs={{0,3},{1,2},{2,1},{3,0},{4,7},{5,6},{6,5},{7,4},{8,11},{9,10},{10,... | collective-permute-start | bytes 393224 | tf_op jit(solution)/shard_map/ppermute | solution.py:35
  89.4 4.3 %collective-permute-start.14 = (bf16[512,128]{1,0:T(8,128)(2,1)S(1)}, bf16[512,128]{1,0:T(8,128)(2,1)S(1)}, u32[]{:S(2)}, u32[]{:S(2)}) collective-permute-start(bf16[512,128]{1,0:T(8,128)(2,1)S(1)} %join.7.refs_4_), channel_id=1, source_target_pairs={{0,2},{1,3},{2,0},{3,1},{4,6},{5,7},{6,4},{7,5},{8,10},{9,11},{10,... | collective-permute-start | bytes 393224 | tf_op jit(solution)/shard_map/ppermute | solution.py:35
  93.7 3.0 %collective-permute-start.13 = (bf16[512,128]{1,0:T(8,128)(2,1)S(1)}, bf16[512,128]{1,0:T(8,128)(2,1)S(1)}, u32[]{:S(2)}, u32[]{:S(2)}) collective-permute-start(bf16[512,128]{1,0:T(8,128)(2,1)S(1)} %join.7.refs_4_), channel_id=1, source_target_pairs={{0,1},{1,0},{2,3},{3,2},{4,5},{5,4},{6,7},{7,6},{8,9},{9,8},{10,11... | collective-permute-start | bytes 393224 | tf_op jit(solution)/shard_map/ppermute | solution.py:35
  96.7 1.9 %collective-permute-done.15.refs_7_ = bf16[512,128]{1,0:T(8,128)(2,1)S(1)} collective-permute-done((bf16[512,128]{1,0:T(8,128)(2,1)S(1)}, bf16[512,128]{1,0:T(8,128)(2,1)S(1)}, u32[]{:S(2)}, u32[]{:S(2)}) %collective-permute-start.15) | collective-permute-done | bytes 131104 | tf_op jit(solution)/shard_map/ppermute | solution.py:35
  98.7 2.5 %collective-permute-done.13.refs_5_ = bf16[512,128]{1,0:T(8,128)(2,1)S(1)} collective-permute-done((bf16[512,128]{1,0:T(8,128)(2,1)S(1)}, bf16[512,128]{1,0:T(8,128)(2,1)S(1)}, u32[]{:S(2)}, u32[]{:S(2)}) %collective-permute-start.13) | collective-permute-done | bytes 131104 | tf_op jit(solution)/shard_map/ppermute | solution.py:35
  101.2 2.4 %merge.1 = bf16[128,256]{1,0:T(8,128)(2,1)S(1)} custom-call(bf16[512,128]{1,0:T(8,128)(2,1)S(1)} %get-tuple-element.11.refs_0_, bf16[512,128]{1,0:T(8,128)(2,1)S(1)} %collective-permute-done.9.refs_1_, bf16[512,128]{1,0:T(8,128)(2,1)S(1)} %collective-permute-done.10.refs_2_, bf16[512,128]{1,0:T(8,128)(2,1)S(1)} %collective-permute-done.11.refs_3_, ...), custom_call_target="tpu_custom_call" | custom-call | flops 1400000000 | bytes 7000000 | tf_op jit(solution)/shard_map/merge/pallas_call | solution.py:322
  103.6 1.9 %collective-permute-start.19 = (bf16[64,256]{1,0:T(8,128)(2,1)S(1)}, bf16[64,256]{1,0:T(8,128)(2,1)S(1)}, u32[]{:S(2)}, u32[]{:S(2)}) collective-permute-start(bf16[64,256]{1,0:T(8,128)(2,1)S(1)} %get-tuple-element.13), channel_id=1, source_target_pairs={{0,8},{1,9},{2,10},{3,11},{4,12},{5,13},{6,14},{7,15},{8,16},{9,17... | collective-permute-start | bytes 98312 | tf_op jit(solution)/shard_map/ppermute | solution.py:64
  105.5 6.6 %collective-permute-done.19 = bf16[64,256]{1,0:T(8,128)(2,1)S(1)} collective-permute-done((bf16[64,256]{1,0:T(8,128)(2,1)S(1)}, bf16[64,256]{1,0:T(8,128)(2,1)S(1)}, u32[]{:S(2)}, u32[]{:S(2)}) %collective-permute-start.19) | collective-permute-done | bytes 32800 | tf_op jit(solution)/shard_map/ppermute | solution.py:64
  112.1 0.7 reshape.35
  (24 shorter events, 0.1 us)
Async XLA Ops:
  0.0 0.9 copy-start.2
  1.0 0.9 copy-start.3
  2.1 19.4 %collective-permute-start = (bf16[256,128]{1,0:T(8,128)(2,1)S(1)}, bf16[256,128]{1,0:T(8,128)(2,1)S(1)}, u32[]{:S(2)}, u32[]{:S(2)}) collective-permute-start(bf16[256,128]{1,0:T(8,128)(2,1)S(1)} %get-tuple-element.10), channel_id=1, source_target_pairs={{0,508},{1,509},{2,510},{3,511},{4,504},{5,505},{6,506},{7,507},{8... | collective-permute-start | bytes 196616 | tf_op jit(solution)/shard_map/ppermute | solution.py:56
  15.1 26.1 %collective-permute-start.4 = (bf16[512,128]{1,0:T(8,128)(2,1)S(1)}, bf16[512,128]{1,0:T(8,128)(2,1)S(1)}, u32[]{:S(2)}, u32[]{:S(2)}) collective-permute-start(bf16[512,128]{1,0:T(8,128)(2,1)S(1)} %get-tuple-element.9.refs_0_.refs_2_), channel_id=1, source_target_pairs={{0,4},{1,5},{2,6},{3,7},{4,0},{5,1},{6,2},{7,3},{8,12},{9,13},{10,... | collective-permute-start | bytes 393224 | tf_op jit(solution)/shard_map/ppermute | solution.py:35
  21.5 19.8 %collective-permute-start.5 = (bf16[256,128]{1,0:T(8,128)(2,1)S(1)}, bf16[256,128]{1,0:T(8,128)(2,1)S(1)}, u32[]{:S(2)}, u32[]{:S(2)}) collective-permute-start(bf16[256,128]{1,0:T(8,128)(2,1)S(1)} %collective-permute-done.refs_1_), channel_id=1, source_target_pairs={{0,4},{1,5},{2,6},{3,7},{4,0},{5,1},{6,2},{7,3},{8,12},{9,13},{10,... | collective-permute-start | bytes 196616 | tf_op jit(solution)/shard_map/ppermute | solution.py:35
  29.8 21.6 %copy-start = (bf16[4096,256]{1,0:T(8,128)(2,1)S(1)}, bf16[4096,256]{1,0:T(8,128)(2,1)}, u32[]{:S(2)}) copy-start(bf16[4096,256]{1,0:T(8,128)(2,1)} %param.16) | copy-start | bytes 6291460
  29.8 18.4 %collective-permute-start.3 = (bf16[768,128]{1,0:T(8,128)(2,1)S(1)}, bf16[768,128]{1,0:T(8,128)(2,1)S(1)}, u32[]{:S(2)}, u32[]{:S(2)}) collective-permute-start(bf16[768,128]{1,0:T(8,128)(2,1)S(1)} %join.5.refs_0_), channel_id=1, source_target_pairs={{0,3},{1,2},{2,1},{3,0},{4,7},{5,6},{6,5},{7,4},{8,11},{9,10},{10,... | collective-permute-start | bytes 589832 | tf_op jit(solution)/shard_map/ppermute | solution.py:35
  32.0 19.3 %collective-permute-start.2 = (bf16[768,128]{1,0:T(8,128)(2,1)S(1)}, bf16[768,128]{1,0:T(8,128)(2,1)S(1)}, u32[]{:S(2)}, u32[]{:S(2)}) collective-permute-start(bf16[768,128]{1,0:T(8,128)(2,1)S(1)} %join.5.refs_0_), channel_id=1, source_target_pairs={{0,2},{1,3},{2,0},{3,1},{4,6},{5,7},{6,4},{7,5},{8,10},{9,11},{10,... | collective-permute-start | bytes 589832 | tf_op jit(solution)/shard_map/ppermute | solution.py:35
  36.5 15.6 %collective-permute-start.1 = (bf16[768,128]{1,0:T(8,128)(2,1)S(1)}, bf16[768,128]{1,0:T(8,128)(2,1)S(1)}, u32[]{:S(2)}, u32[]{:S(2)}) collective-permute-start(bf16[768,128]{1,0:T(8,128)(2,1)S(1)} %join.5.refs_0_), channel_id=1, source_target_pairs={{0,1},{1,0},{2,3},{3,2},{4,5},{5,4},{6,7},{7,6},{8,9},{9,8},{10,11... | collective-permute-start | bytes 589832 | tf_op jit(solution)/shard_map/ppermute | solution.py:35
  41.3 18.9 %copy-start.7 = (f32[2,128,128]{2,1,0:T(8,128)S(1)}, f32[2,128,128]{2,1,0:T(8,128)}, u32[]{:S(2)}) copy-start(f32[2,128,128]{2,1,0:T(8,128)} %bias_ref.1) | copy-start | bytes 393220
  41.3 18.9 %copy-start.8 = (f32[128,128]{1,0:T(8,128)S(1)}, f32[128,128]{1,0:T(8,128)}, u32[]{:S(2)}) copy-start(f32[128,128]{1,0:T(8,128)} %constant.7.clone.turned_ref) | copy-start | bytes 196612
  41.3 18.9 %copy-start.9 = (f32[128,128]{1,0:T(8,128)S(1)}, f32[128,128]{1,0:T(8,128)}, u32[]{:S(2)}) copy-start(f32[128,128]{1,0:T(8,128)} %constant.6.clone.hot_ref) | copy-start | bytes 196612
  41.3 14.2 %collective-permute-start.8 = (bf16[768,128]{1,0:T(8,128)(2,1)S(1)}, bf16[768,128]{1,0:T(8,128)(2,1)S(1)}, u32[]{:S(2)}, u32[]{:S(2)}) collective-permute-start(bf16[768,128]{1,0:T(8,128)(2,1)S(1)} %join.6.refs_4_), channel_id=1, source_target_pairs={{0,3},{1,2},{2,1},{3,0},{4,7},{5,6},{6,5},{7,4},{8,11},{9,10},{10,... | collective-permute-start | bytes 589832 | tf_op jit(solution)/shard_map/ppermute | solution.py:35
  43.6 12.0 %collective-permute-start.7 = (bf16[768,128]{1,0:T(8,128)(2,1)S(1)}, bf16[768,128]{1,0:T(8,128)(2,1)S(1)}, u32[]{:S(2)}, u32[]{:S(2)}) collective-permute-start(bf16[768,128]{1,0:T(8,128)(2,1)S(1)} %join.6.refs_4_), channel_id=1, source_target_pairs={{0,2},{1,3},{2,0},{3,1},{4,6},{5,7},{6,4},{7,5},{8,10},{9,11},{10,... | collective-permute-start | bytes 589832 | tf_op jit(solution)/shard_map/ppermute | solution.py:35
  48.1 9.9 %collective-permute-start.6 = (bf16[768,128]{1,0:T(8,128)(2,1)S(1)}, bf16[768,128]{1,0:T(8,128)(2,1)S(1)}, u32[]{:S(2)}, u32[]{:S(2)}) collective-permute-start(bf16[768,128]{1,0:T(8,128)(2,1)S(1)} %join.6.refs_4_), channel_id=1, source_target_pairs={{0,1},{1,0},{2,3},{3,2},{4,5},{5,4},{6,7},{7,6},{8,9},{9,8},{10,11... | collective-permute-start | bytes 589832 | tf_op jit(solution)/shard_map/ppermute | solution.py:35
  51.3 49.8 %collective-permute-start.18 = (bf16[4096,256]{1,0:T(8,128)(2,1)S(1)}, bf16[4096,256]{1,0:T(8,128)(2,1)S(1)}, u32[]{:S(2)}, u32[]{:S(2)}) collective-permute-start(bf16[4096,256]{1,0:T(8,128)(2,1)S(1)} %copy-done), channel_id=1, source_target_pairs={{60,504},{61,505},{62,506},{63,507},{56,508},{57,509},{58,510},{59... | collective-permute-start | bytes 6291464 | tf_op jit(solution)/shard_map/ppermute | solution.py:68
  58.1 2.7 %copy-start.1 = (bf16[1024,3,128]{2,0,1:T(8,128)(2,1)S(1)}, bf16[1024,3,128]{2,0,1:T(8,128)(2,1)}, u32[]{:S(2)}) copy-start(bf16[1024,3,128]{2,0,1:T(8,128)(2,1)} %param.12) | copy-start | bytes 2359300
  58.1 2.7 %copy-start.6 = (f32[1024]{0:T(1024)S(1)}, f32[1024]{0:T(1024)}, u32[]{:S(2)}) copy-start(f32[1024]{0:T(1024)} %param.11) | copy-start | bytes 12292
  58.1 21.8 %collective-permute-start.16 = (bf16[2048,128]{1,0:T(8,128)(2,1)S(1)}, bf16[2048,128]{1,0:T(8,128)(2,1)S(1)}, u32[]{:S(2)}, u32[]{:S(2)}) collective-permute-start(bf16[2048,128]{1,0:T(8,128)(2,1)S(1)} %join.8.refs_0_), channel_id=1, source_target_pairs={{0,16},{1,17},{2,18},{3,19},{4,20},{5,21},{6,22},{7,23},{8,24},{9,... | collective-permute-start | bytes 1572872 | tf_op jit(solution)/shard_map/ppermute | solution.py:35
  64.5 20.4 %collective-permute-start.12 = (bf16[512,128]{1,0:T(8,128)(2,1)S(1)}, bf16[512,128]{1,0:T(8,128)(2,1)S(1)}, u32[]{:S(2)}, u32[]{:S(2)}) collective-permute-start(bf16[512,128]{1,0:T(8,128)(2,1)S(1)} %get-tuple-element.11.refs_0_), channel_id=1, source_target_pairs={{0,4},{1,5},{2,6},{3,7},{4,0},{5,1},{6,2},{7,3},{8,12},{9,13},{10,... | collective-permute-start | bytes 393224 | tf_op jit(solution)/shard_map/ppermute | solution.py:35
  73.3 13.6 %collective-permute-start.11 = (bf16[512,128]{1,0:T(8,128)(2,1)S(1)}, bf16[512,128]{1,0:T(8,128)(2,1)S(1)}, u32[]{:S(2)}, u32[]{:S(2)}) collective-permute-start(bf16[512,128]{1,0:T(8,128)(2,1)S(1)} %get-tuple-element.11.refs_0_), channel_id=1, source_target_pairs={{0,3},{1,2},{2,1},{3,0},{4,7},{5,6},{6,5},{7,4},{8,11},{9,10},{10,... | collective-permute-start | bytes 393224 | tf_op jit(solution)/shard_map/ppermute | solution.py:35
  75.5 13.9 %collective-permute-start.10 = (bf16[512,128]{1,0:T(8,128)(2,1)S(1)}, bf16[512,128]{1,0:T(8,128)(2,1)S(1)}, u32[]{:S(2)}, u32[]{:S(2)}) collective-permute-start(bf16[512,128]{1,0:T(8,128)(2,1)S(1)} %get-tuple-element.11.refs_0_), channel_id=1, source_target_pairs={{0,2},{1,3},{2,0},{3,1},{4,6},{5,7},{6,4},{7,5},{8,10},{9,11},{10,... | collective-permute-start | bytes 393224 | tf_op jit(solution)/shard_map/ppermute | solution.py:35
  79.9 13.7 %collective-permute-start.9 = (bf16[512,128]{1,0:T(8,128)(2,1)S(1)}, bf16[512,128]{1,0:T(8,128)(2,1)S(1)}, u32[]{:S(2)}, u32[]{:S(2)}) collective-permute-start(bf16[512,128]{1,0:T(8,128)(2,1)S(1)} %get-tuple-element.11.refs_0_), channel_id=1, source_target_pairs={{0,1},{1,0},{2,3},{3,2},{4,5},{5,4},{6,7},{7,6},{8,9},{9,8},{10,11... | collective-permute-start | bytes 393224 | tf_op jit(solution)/shard_map/ppermute | solution.py:35
  83.2 18.0 %copy-start.4 = (bf16[128,128]{1,0:T(8,128)(2,1)S(1)}, bf16[128,128]{1,0:T(8,128)(2,1)}, u32[]{:S(2)}) copy-start(bf16[128,128]{1,0:T(8,128)(2,1)} %constant.8.clone.refs_14_) | copy-start | bytes 98308
  83.2 18.0 %copy-start.5 = (f32[4096]{0:T(1024)S(1)}, f32[4096]{0:T(1024)}, u32[]{:S(2)}) copy-start(f32[4096]{0:T(1024)} %param.15) | copy-start | bytes 49156
  84.9 16.3 %collective-permute-start.17 = (bf16[4096,128]{1,0:T(8,128)(2,1)S(1)}, bf16[4096,128]{1,0:T(8,128)(2,1)S(1)}, u32[]{:S(2)}, u32[]{:S(2)}) collective-permute-start(bf16[4096,128]{1,0:T(8,128)(2,1)S(1)} %join.9), channel_id=1, source_target_pairs={{0,8},{1,9},{2,10},{3,11},{4,12},{5,13},{6,14},{7,15},{8,0},{9,1},... | collective-permute-start | bytes 3145736 | tf_op jit(solution)/shard_map/ppermute | solution.py:35
  86.8 11.8 %collective-permute-start.15 = (bf16[512,128]{1,0:T(8,128)(2,1)S(1)}, bf16[512,128]{1,0:T(8,128)(2,1)S(1)}, u32[]{:S(2)}, u32[]{:S(2)}) collective-permute-start(bf16[512,128]{1,0:T(8,128)(2,1)S(1)} %join.7.refs_4_), channel_id=1, source_target_pairs={{0,3},{1,2},{2,1},{3,0},{4,7},{5,6},{6,5},{7,4},{8,11},{9,10},{10,... | collective-permute-start | bytes 393224 | tf_op jit(solution)/shard_map/ppermute | solution.py:35
  89.4 9.3 %collective-permute-start.14 = (bf16[512,128]{1,0:T(8,128)(2,1)S(1)}, bf16[512,128]{1,0:T(8,128)(2,1)S(1)}, u32[]{:S(2)}, u32[]{:S(2)}) collective-permute-start(bf16[512,128]{1,0:T(8,128)(2,1)S(1)} %join.7.refs_4_), channel_id=1, source_target_pairs={{0,2},{1,3},{2,0},{3,1},{4,6},{5,7},{6,4},{7,5},{8,10},{9,11},{10,... | collective-permute-start | bytes 393224 | tf_op jit(solution)/shard_map/ppermute | solution.py:35
  93.7 7.5 %collective-permute-start.13 = (bf16[512,128]{1,0:T(8,128)(2,1)S(1)}, bf16[512,128]{1,0:T(8,128)(2,1)S(1)}, u32[]{:S(2)}, u32[]{:S(2)}) collective-permute-start(bf16[512,128]{1,0:T(8,128)(2,1)S(1)} %join.7.refs_4_), channel_id=1, source_target_pairs={{0,1},{1,0},{2,3},{3,2},{4,5},{5,4},{6,7},{7,6},{8,9},{9,8},{10,11... | collective-permute-start | bytes 393224 | tf_op jit(solution)/shard_map/ppermute | solution.py:35
  103.6 8.6 %collective-permute-start.19 = (bf16[64,256]{1,0:T(8,128)(2,1)S(1)}, bf16[64,256]{1,0:T(8,128)(2,1)S(1)}, u32[]{:S(2)}, u32[]{:S(2)}) collective-permute-start(bf16[64,256]{1,0:T(8,128)(2,1)S(1)} %get-tuple-element.13), channel_id=1, source_target_pairs={{0,8},{1,9},{2,10},{3,11},{4,12},{5,13},{6,14},{7,15},{8,16},{9,17... | collective-permute-start | bytes 98312 | tf_op jit(solution)/shard_map/ppermute | solution.py:64

commit v8 on v7

--- a/solution.py
+++ b/solution.py
@@ -72,58 +72,74 @@
     return [pl.BlockSpec(memory_space=pltpu.VMEM)] * count
 
 
-def join_kernel(spans, *refs):
+def join_kernel(spans, copies, *refs):
     at = 0
     for ref, (start, stop) in zip(refs, spans):
-        refs[-1][at : at + stop - start, :] = ref[start:stop, :]
+        rows = ref[start:stop, :]
+        for copy in range(copies):
+            refs[-1][copy, at : at + stop - start, :] = rows
         at += stop - start
 
 
-def joined(parts, claimed=0):
+def joined(parts, copies=1, claimed=0, events=()):
     spans = [(start, stop) for _, start, stop in parts]
     rows = sum(stop - start for start, stop in spans)
-    return pl.pallas_call(
-        functools.partial(join_kernel, spans),
-        out_shape=jax.ShapeDtypeStruct((rows, BLOCK), jnp.bfloat16),
-        in_specs=in_vmem(len(parts)),
+    result = pl.pallas_call(
+        functools.partial(join_kernel, spans, copies),
+        out_shape=jax.ShapeDtypeStruct((copies, rows, BLOCK), jnp.bfloat16),
+        in_specs=in_vmem(len(parts) + len(events)),
         out_specs=in_vmem(1)[0],
         compiler_params=pltpu.CompilerParams(vmem_limit_bytes=4 * 2**20),
         cost_estimate=pl.CostEstimate(flops=claimed, bytes_accessed=4 * rows * BLOCK, transcendentals=0),
         name="join",
-    )(*[part for part, _, _ in parts])
-
-
-def along_y(own, partner):
-    return [place if bits == 0 else across(place, bits) for place in (own, partner) for bits in range(4)]
-
-
-def order_kernel(rows_ref, w_ref, first_ref, behind_ref):
-    space = lax.axis_index("space")
+    )(*[part for part, _, _ in parts], *events)
+    return result if copies > 1 else result[0]
+
+
+def along_y(value):
+    return [value] + [across(value, bits) for bits in (1, 2, 3)]
+
+
+def order_kernel(rows_ref, first_ref, behind_ref):
     place = lax.broadcasted_iota(jnp.int32, (HALF, HALF), 0)
     token = lax.broadcasted_iota(jnp.int32, (HALF, HALF), 1)
     row = 2 * ((place >> 3) & 1) + ((place >> 6) & 1)
     lon = (8 * ((place >> 4) & 3) + 2 * ((place >> 1) & 3) + ((place >> 7) & 1) + WIN_LON // 2) & 31
     hot = jnp.where(row * 64 + lon * 2 + (place & 1) == token, 1.0, 0.0).astype(jnp.bfloat16)
     behind_ref[...] = dot(hot, rows_ref[:HALF, :]).astype(jnp.bfloat16)
-    first_ref[:HALF, :] = dot(hot, rows_ref[HALF:, :]).astype(jnp.bfloat16)
+    first_ref[...] = dot(hot, rows_ref[HALF:, :]).astype(jnp.bfloat16)
+
+
+def ordered(rows):
+    half = jax.ShapeDtypeStruct((HALF, BLOCK), jnp.bfloat16)
+    return pl.pallas_call(
+        order_kernel,
+        out_shape=(half, half),
+        in_specs=in_vmem(1),
+        out_specs=tuple(in_vmem(2)),
+        compiler_params=pltpu.CompilerParams(vmem_limit_bytes=4 * 2**20),
+        cost_estimate=pl.CostEstimate(flops=40_000_000, bytes_accessed=400_000, transcendentals=0),
+        name="order",
+    )(rows)
+
+
+def piece_kernel(rows_ref, w_ref, out_ref):
+    space = lax.axis_index("space")
     quarter = (space // 2 % 2) * 2 + space % 2
+    out_ref[:HALF, :] = rows_ref[...]
     for side in range(2):
         column = pl.multiple_of(quarter * 256 + side * BLOCK, BLOCK)
-        first_ref[HALF + side * BLOCK : HALF + (side + 1) * BLOCK, :] = w_ref[:, pl.ds(column, BLOCK)]
-
-
-def ordered(rows, w_out):
+        out_ref[HALF + side * BLOCK : HALF + (side + 1) * BLOCK, :] = w_ref[:, pl.ds(column, BLOCK)]
+
+
+def with_piece(rows, w_out):
     return pl.pallas_call(
-        order_kernel,
-        out_shape=(
-            jax.ShapeDtypeStruct((HALF + 256, BLOCK), jnp.bfloat16),
-            jax.ShapeDtypeStruct((HALF, BLOCK), jnp.bfloat16),
-        ),
+        piece_kernel,
+        out_shape=jax.ShapeDtypeStruct((HALF + 256, BLOCK), jnp.bfloat16),
         in_specs=in_vmem(2),
-        out_specs=tuple(in_vmem(2)),
+        out_specs=in_vmem(1)[0],
         compiler_params=pltpu.CompilerParams(vmem_limit_bytes=4 * 2**20),
-        cost_estimate=pl.CostEstimate(flops=40_000_000, bytes_accessed=800_000, transcendentals=0),
-        name="order",
+        name="piece",
     )(rows, w_out)
 
 
@@ -232,8 +248,8 @@
 
 
 def merge_kernel(*refs):
-    att_refs = refs[:8]
-    stream_ref, w_same_ref, w_other_ref, gain_ref, w_ref, w_turned_ref, order_ref, out_ref, updated_ref = refs[8:]
+    att_refs = refs[:5]
+    stream_ref, w_same_ref, w_other_ref, gain_ref, w_ref, w_turned_ref, order_ref, out_ref, updated_ref = refs[5:]
     head_place = lax.axis_index("head")
     space = lax.axis_index("space")
     blocks = [head_place ^ k for k in range(8)]
@@ -241,7 +257,9 @@
     parity = (head_place // 2 + space) % 2
 
     def project(odd):
-        attended = jnp.concatenate([ref[...] for ref in att_refs], axis=1)
+        attended = jnp.concatenate(
+            [ref[...] for ref in att_refs[:4]] + [att_refs[4][head_place % 4 ^ bits] for bits in range(4)], axis=1
+        )
         for k in range(0, 8, 2):
             w_from = w_same_ref if (k // 2 + odd) % 2 == 0 else w_other_ref
             x_rel = (blocks[k] // 4) ^ my_x
@@ -289,15 +307,16 @@
 
 
 def on_device(fields, ln_gain, w_qkv, attn_bias, w_out, merge_gain, w_merge):
-    first, behind = ordered(fields.reshape(TOKENS, BLOCK), w_out)
+    first, behind = ordered(fields.reshape(TOKENS, BLOCK))
+    first = with_piece(first, w_out)
     following = following_rows(behind)
     first_partner = across(first, 4)
     following_partner = across(following, 4)
     own = joined([(first, 0, HALF), (following, 0, HALF), (first, HALF, 512)])
     partner = joined(
-        [(first_partner, 0, HALF), (following_partner, 0, HALF), (first_partner, HALF, 512)], claimed=CLAIMED
-    )
-    around = along_y(own, partner)
+        [(first_partner, 0, HALF), (following_partner, 0, HALF), (first_partner, HALF, 512)], 1, CLAIMED
+    )
+    around = along_y(own) + along_y(partner)
     bias = ordered_bias(attn_bias)
     vmem = pl.BlockSpec(memory_space=pltpu.VMEM)
     attended, stream = pl.pallas_call(
@@ -314,15 +333,18 @@
         name="attention",
     )(*around, ln_gain.reshape(8, 1, BLOCK), w_qkv.transpose(1, 0, 2).reshape(3, 8, BLOCK, BLOCK), bias)
 
-    attended_partner = joined([(across(attended, 4), 0, TOKENS)], claimed=CLAIMED)
-    attended_around = along_y(attended, attended_partner)
+    attended_around = along_y(attended)
+    attended_partner = joined([(across(attended, 4), 0, TOKENS)], 4, CLAIMED, attended_around[1:])
+    attended_around.append(
+        lax.all_to_all(attended_partner, "head", 0, 0, axis_index_groups=[[0, 1, 2, 3], [4, 5, 6, 7]])
+    )
     w_quarter = joined([(place, TOKENS, TOKENS + 256) for place in around])
     w_core = joined([(w_quarter, 0, 2048), (across_x(w_quarter, 1), 0, 2048)])
     w_shape = (2, 8, 2, BLOCK, BLOCK)
     merged = pl.pallas_call(
         merge_kernel,
         out_shape=jax.ShapeDtypeStruct((128, 256), jnp.bfloat16),
-        in_specs=in_vmem(15),
+        in_specs=in_vmem(12),
         out_specs=vmem,
         scratch_shapes=[pltpu.VMEM((TOKENS, D), jnp.bfloat16)],
         compiler_params=pltpu.CompilerParams(vmem_limit_bytes=16 * 2**20),

time: 114 us -> 113 us (level)
  blocking collectives: 0 us -> 12.7 us
  starting transfers between devices: 82.6 us -> 71.2 us
  waiting for transfers between devices: 20.2 us -> 17.6 us
    all_to_all x0 -> x1, blocking collectives: none -> 12.7 us  [on_device(): lax.all_to_all(attended_partner, 'head', 0, 0, axis_index_groups=[[0, 1,...]
    ppermute x17 -> x14, starting transfers between devices: 66.8 us -> 55.4 us  [moved(): return lax.ppermute(value, BOTH, pairs)]
    ppermute x17 -> x14, waiting for transfers between devices: 13.6 us -> 10.9 us  [moved(): return lax.ppermute(value, BOTH, pairs)]
  transfers between devices with their start and end apart: 20 -> 17, of which waited for: 7 -> 5; matrix products, arithmetic and copies ran while one was open for 0% -> 0% of each run, Pallas kernels for 4% -> 4%
where the time goes in v8:
time: 113 us; the launch traced here: 111 us
  starting transfers between devices  71.2 us (63%)
  waiting for transfers between devices  17.6 us (16%)
  blocking collectives  12.7 us (11%)
  Pallas kernels  7.09 us (6%)
  local copies, waits for them, and re-layouts  2.57 us (2%)
    ppermute x14, starting transfers between devices, moved(): return lax.ppermute(value, BOTH, pairs)  55.4 us
    ppermute x1, starting transfers between devices, following_rows(): return lax.ppermute(value, BOTH, pairs)  13 us
    all_to_all x1, blocking collectives, on_device(): lax.all_to_all(attended_partner, 'head', 0, 0, axis_index_groups=[[0, 1,...  12.7 us
    ppermute x14, waiting for transfers between devices, moved(): return lax.ppermute(value, BOTH, pairs)  10.9 us
    ppermute x1, waiting for transfers between devices, lower_rows(): return lax.ppermute(value, BOTH, pairs)  6.63 us
    pallas_call x1, Pallas kernels, on_device(): pl.pallas_call(attention_kernel, out_shape=(jax.ShapeDtypeStruct((TOKENS,...  3.73 us
    pallas_call x1, Pallas kernels, on_device(): pl.pallas_call(merge_kernel, out_shape=jax.ShapeDtypeStruct((128, 256), j...  2.36 us
  transfers between devices with their start and end apart: 17, of which 5 were waited for; matrix products, arithmetic and copies ran while one was open for 0% of the time, Pallas kernels for 4%

profile of v8, /device:TPU:24, one launch (start us, length us, event | category | flops | bytes accessed | tf_op | source)
XLA Modules:
  0.0 111.5 jit_solution(9130508157682581081)
XLA Ops:
  0.0 0.9 copy-done.6
  0.9 0.2 order.1
  1.2 13.0 %collective-permute-start = (bf16[256,128]{1,0:T(8,128)(2,1)S(1)}, bf16[256,128]{1,0:T(8,128)(2,1)S(1)}, u32[]{:S(2)}, u32[]{:S(2)}) collective-permute-start(bf16[256,128]{1,0:T(8,128)(2,1)S(1)} %get-tuple-element.10), channel_id=1, source_target_pairs={{0,508},{1,509},{2,510},{3,511},{4,504},{5,505},{6,506},{7,507},{8... | collective-permute-start | bytes 196616 | tf_op jit(solution)/shard_map/ppermute | solution.py:56
  14.2 0.0 copy-start.2
  14.2 0.9 copy-done.2
  15.2 6.3 %collective-permute-start.4 = (bf16[512,128]{1,0:T(8,128)(2,1)S(1)}, bf16[512,128]{1,0:T(8,128)(2,1)S(1)}, u32[]{:S(2)}, u32[]{:S(2)}) collective-permute-start(bf16[512,128]{1,0:T(8,128)(2,1)S(1)} %piece.1.refs_0_.refs_2_), channel_id=1, source_target_pairs={{0,4},{1,5},{2,6},{3,7},{4,0},{5,1},{6,2},{7,3},{8,12},{9,13},{10,... | collective-permute-start | bytes 393224 | tf_op jit(solution)/shard_map/ppermute | solution.py:35
  21.5 0.0 collective-permute-done.refs_1_
  21.5 8.2 %collective-permute-start.5 = (bf16[256,128]{1,0:T(8,128)(2,1)S(1)}, bf16[256,128]{1,0:T(8,128)(2,1)S(1)}, u32[]{:S(2)}, u32[]{:S(2)}) collective-permute-start(bf16[256,128]{1,0:T(8,128)(2,1)S(1)} %collective-permute-done.refs_1_), channel_id=1, source_target_pairs={{0,4},{1,5},{2,6},{3,7},{4,0},{5,1},{6,2},{7,3},{8,12},{9,13},{10,... | collective-permute-start | bytes 196616 | tf_op jit(solution)/shard_map/ppermute | solution.py:35
  29.8 0.0 copy-start
  29.8 2.3 %collective-permute-start.3 = (bf16[768,128]{1,0:T(8,128)(2,1)S(1)}, bf16[768,128]{1,0:T(8,128)(2,1)S(1)}, u32[]{:S(2)}, u32[]{:S(2)}) collective-permute-start(bf16[768,128]{1,0:T(8,128)(2,1)S(1)} %bitcast.20), channel_id=1, source_target_pairs={{0,3},{1,2},{2,1},{3,0},{4,7},{5,6},{6,5},{7,4},{8,11},{9,10},{10,... | collective-permute-start | bytes 589832 | tf_op jit(solution)/shard_map/ppermute | solution.py:35
  32.1 4.5 %collective-permute-start.2 = (bf16[768,128]{1,0:T(8,128)(2,1)S(1)}, bf16[768,128]{1,0:T(8,128)(2,1)S(1)}, u32[]{:S(2)}, u32[]{:S(2)}) collective-permute-start(bf16[768,128]{1,0:T(8,128)(2,1)S(1)} %bitcast.21), channel_id=1, source_target_pairs={{0,2},{1,3},{2,0},{3,1},{4,6},{5,7},{6,4},{7,5},{8,10},{9,11},{10,... | collective-permute-start | bytes 589832 | tf_op jit(solution)/shard_map/ppermute | solution.py:35
  36.6 3.2 %collective-permute-start.1 = (bf16[768,128]{1,0:T(8,128)(2,1)S(1)}, bf16[768,128]{1,0:T(8,128)(2,1)S(1)}, u32[]{:S(2)}, u32[]{:S(2)}) collective-permute-start(bf16[768,128]{1,0:T(8,128)(2,1)S(1)} %bitcast.22), channel_id=1, source_target_pairs={{0,1},{1,0},{2,3},{3,2},{4,5},{5,4},{6,7},{7,6},{8,9},{9,8},{10,11... | collective-permute-start | bytes 589832 | tf_op jit(solution)/shard_map/ppermute | solution.py:35
  39.8 1.7 %collective-permute-done.5.refs_1_ = bf16[256,128]{1,0:T(8,128)(2,1)S(1)} collective-permute-done((bf16[256,128]{1,0:T(8,128)(2,1)S(1)}, bf16[256,128]{1,0:T(8,128)(2,1)S(1)}, u32[]{:S(2)}, u32[]{:S(2)}) %collective-permute-start.5) | collective-permute-done | bytes 65568 | tf_op jit(solution)/shard_map/ppermute | solution.py:35
  41.5 0.0 collective-permute-done.4.refs_0_.refs_2_
  41.5 0.0 copy-start.7
  41.5 0.0 copy-start.8
  41.5 0.0 copy-start.9
  41.5 2.1 %collective-permute-start.8 = (bf16[768,128]{1,0:T(8,128)(2,1)S(1)}, bf16[768,128]{1,0:T(8,128)(2,1)S(1)}, u32[]{:S(2)}, u32[]{:S(2)}) collective-permute-start(bf16[768,128]{1,0:T(8,128)(2,1)S(1)} %bitcast.27), channel_id=1, source_target_pairs={{0,3},{1,2},{2,1},{3,0},{4,7},{5,6},{6,5},{7,4},{8,11},{9,10},{10,... | collective-permute-start | bytes 589832 | tf_op jit(solution)/shard_map/ppermute | solution.py:35
  43.6 4.7 %collective-permute-start.7 = (bf16[768,128]{1,0:T(8,128)(2,1)S(1)}, bf16[768,128]{1,0:T(8,128)(2,1)S(1)}, u32[]{:S(2)}, u32[]{:S(2)}) collective-permute-start(bf16[768,128]{1,0:T(8,128)(2,1)S(1)} %bitcast.28), channel_id=1, source_target_pairs={{0,2},{1,3},{2,0},{3,1},{4,6},{5,7},{6,4},{7,5},{8,10},{9,11},{10,... | collective-permute-start | bytes 589832 | tf_op jit(solution)/shard_map/ppermute | solution.py:35
  48.3 0.0 collective-permute-done.3.refs_3_
  48.3 3.2 %collective-permute-start.6 = (bf16[768,128]{1,0:T(8,128)(2,1)S(1)}, bf16[768,128]{1,0:T(8,128)(2,1)S(1)}, u32[]{:S(2)}, u32[]{:S(2)}) collective-permute-start(bf16[768,128]{1,0:T(8,128)(2,1)S(1)} %bitcast.29), channel_id=1, source_target_pairs={{0,1},{1,0},{2,3},{3,2},{4,5},{5,4},{6,7},{7,6},{8,9},{9,8},{10,11... | collective-permute-start | bytes 589832 | tf_op jit(solution)/shard_map/ppermute | solution.py:35
  51.5 0.0 collective-permute-done.2.refs_2_
  51.5 0.8 collective-permute-start.15
  52.3 3.4 %collective-permute-done.8.refs_7_ = bf16[768,128]{1,0:T(8,128)(2,1)S(1)} collective-permute-done((bf16[768,128]{1,0:T(8,128)(2,1)S(1)}, bf16[768,128]{1,0:T(8,128)(2,1)S(1)}, u32[]{:S(2)}, u32[]{:S(2)}) %collective-permute-start.8) | collective-permute-done | bytes 196640 | tf_op jit(solution)/shard_map/ppermute | solution.py:35
  55.7 0.0 collective-permute-done.7.refs_6_
  55.7 2.5 %collective-permute-done.6.refs_5_ = bf16[768,128]{1,0:T(8,128)(2,1)S(1)} collective-permute-done((bf16[768,128]{1,0:T(8,128)(2,1)S(1)}, bf16[768,128]{1,0:T(8,128)(2,1)S(1)}, u32[]{:S(2)}, u32[]{:S(2)}) %collective-permute-start.6) | collective-permute-done | bytes 196640 | tf_op jit(solution)/shard_map/ppermute | solution.py:35
  58.2 0.0 copy-start.1
  58.2 0.0 copy-start.5
  58.3 2.1 %collective-permute-start.13 = (bf16[2048,128]{1,0:T(8,128)(2,1)S(1)}, bf16[2048,128]{1,0:T(8,128)(2,1)S(1)}, u32[]{:S(2)}, u32[]{:S(2)}) collective-permute-start(bf16[2048,128]{1,0:T(8,128)(2,1)S(1)} %bitcast.18), channel_id=1, source_target_pairs={{0,16},{1,17},{2,18},{3,19},{4,20},{5,21},{6,22},{7,23},{8,24},{9,... | collective-permute-start | bytes 1572872 | tf_op jit(solution)/shard_map/ppermute | solution.py:35
  60.3 0.5 bias.1.refs_10_
  60.9 3.7 %attention.1 = (bf16[512,128]{1,0:T(8,128)(2,1)S(1)}, bf16[8,512,128]{2,1,0:T(8,128)(2,1)S(1)}) custom-call(bf16[768,128]{1,0:T(8,128)(2,1)S(1)} %bitcast.24, bf16[768,128]{1,0:T(8,128)(2,1)S(1)} %collective-permute-done.1.refs_1_, bf16[768,128]{1,0:T(8,128)(2,1)S(1)} %collective-permute-done.2.refs_2_, bf16[768,128]{1,0:T(8,128)(2,1)S(1)} %collective-permute-done.3.refs_3_, ...), custom_call_target="tpu_custom_call" | custom-call | flops 600000000 | bytes 3000000 | tf_op jit(solution)/shard_map/attention/pallas_call | solution.py:322
  64.6 7.0 %collective-permute-start.12 = (bf16[512,128]{1,0:T(8,128)(2,1)S(1)}, bf16[512,128]{1,0:T(8,128)(2,1)S(1)}, u32[]{:S(2)}, u32[]{:S(2)}) collective-permute-start(bf16[512,128]{1,0:T(8,128)(2,1)S(1)} %get-tuple-element.11.refs_0_), channel_id=1, source_target_pairs={{0,4},{1,5},{2,6},{3,7},{4,0},{5,1},{6,2},{7,3},{8,12},{9,13},{10,... | collective-permute-start | bytes 393224 | tf_op jit(solution)/shard_map/ppermute | solution.py:35
  71.7 3.0 %collective-permute-start.11 = (bf16[512,128]{1,0:T(8,128)(2,1)S(1)}, bf16[512,128]{1,0:T(8,128)(2,1)S(1)}, u32[]{:S(2)}, u32[]{:S(2)}) collective-permute-start(bf16[512,128]{1,0:T(8,128)(2,1)S(1)} %get-tuple-element.11.refs_0_), channel_id=1, source_target_pairs={{0,3},{1,2},{2,1},{3,0},{4,7},{5,6},{6,5},{7,4},{8,11},{9,10},{10,... | collective-permute-start | bytes 393224 | tf_op jit(solution)/shard_map/ppermute | solution.py:35
  74.7 4.2 %collective-permute-start.10 = (bf16[512,128]{1,0:T(8,128)(2,1)S(1)}, bf16[512,128]{1,0:T(8,128)(2,1)S(1)}, u32[]{:S(2)}, u32[]{:S(2)}) collective-permute-start(bf16[512,128]{1,0:T(8,128)(2,1)S(1)} %get-tuple-element.11.refs_0_), channel_id=1, source_target_pairs={{0,2},{1,3},{2,0},{3,1},{4,6},{5,7},{6,4},{7,5},{8,10},{9,11},{10,... | collective-permute-start | bytes 393224 | tf_op jit(solution)/shard_map/ppermute | solution.py:35
  78.9 0.0 collective-permute-done.13.refs_1_
  78.9 2.7 %collective-permute-start.9 = (bf16[512,128]{1,0:T(8,128)(2,1)S(1)}, bf16[512,128]{1,0:T(8,128)(2,1)S(1)}, u32[]{:S(2)}, u32[]{:S(2)}) collective-permute-start(bf16[512,128]{1,0:T(8,128)(2,1)S(1)} %get-tuple-element.11.refs_0_), channel_id=1, source_target_pairs={{0,1},{1,0},{2,3},{3,2},{4,5},{5,4},{6,7},{7,6},{8,9},{9,8},{10,11... | collective-permute-start | bytes 393224 | tf_op jit(solution)/shard_map/ppermute | solution.py:35
  81.5 0.1 join.9
  81.6 3.4 %collective-permute-done.12.refs_0_ = bf16[512,128]{1,0:T(8,128)(2,1)S(1)} collective-permute-done((bf16[512,128]{1,0:T(8,128)(2,1)S(1)}, bf16[512,128]{1,0:T(8,128)(2,1)S(1)}, u32[]{:S(2)}, u32[]{:S(2)}) %collective-permute-start.12) | collective-permute-done | bytes 131104 | tf_op jit(solution)/shard_map/ppermute | solution.py:35
  85.0 2.0 %collective-permute-start.14 = (bf16[4096,128]{1,0:T(8,128)(2,1)S(1)}, bf16[4096,128]{1,0:T(8,128)(2,1)S(1)}, u32[]{:S(2)}, u32[]{:S(2)}) collective-permute-start(bf16[4096,128]{1,0:T(8,128)(2,1)S(1)} %bitcast.14), channel_id=1, source_target_pairs={{0,8},{1,9},{2,10},{3,11},{4,12},{5,13},{6,14},{7,15},{8,0},{9,1},... | collective-permute-start | bytes 3145736 | tf_op jit(solution)/shard_map/ppermute | solution.py:35
  87.0 0.0 collective-permute-done.11.refs_3_
  87.1 0.0 collective-permute-done.10.refs_2_
  87.1 0.1 join.7
  87.2 12.7 %all_to_all.5.refs_4_ = bf16[4,512,128]{2,1,0:T(8,128)(2,1)S(1)} all-to-all(bf16[4,512,128]{2,1,0:T(8,128)(2,1)S(1)} %join.7), channel_id=1, replica_groups={{0,1,2,3},{4,5,6,7},{8,9,10,11},{12,13,14,15},{16,17,18,19},{20,21,22,2..., dimensions={0} | all-to-all | bytes 1048576 | tf_op jit(solution)/shard_map/all_to_all | solution.py:339
  99.9 0.0 collective-permute-done.15
  99.9 2.4 %merge.1 = bf16[128,256]{1,0:T(8,128)(2,1)S(1)} custom-call(bf16[512,128]{1,0:T(8,128)(2,1)S(1)} %get-tuple-element.11.refs_0_, bf16[512,128]{1,0:T(8,128)(2,1)S(1)} %collective-permute-done.9.refs_1_, bf16[512,128]{1,0:T(8,128)(2,1)S(1)} %collective-permute-done.10.refs_2_, bf16[512,128]{1,0:T(8,128)(2,1)S(1)} %collective-permute-done.11.refs_3_, ...), custom_call_target="tpu_custom_call" | custom-call | flops 1400000000 | bytes 7000000 | tf_op jit(solution)/shard_map/merge/pallas_call | solution.py:344
  102.3 1.9 %collective-permute-start.16 = (bf16[64,256]{1,0:T(8,128)(2,1)S(1)}, bf16[64,256]{1,0:T(8,128)(2,1)S(1)}, u32[]{:S(2)}, u32[]{:S(2)}) collective-permute-start(bf16[64,256]{1,0:T(8,128)(2,1)S(1)} %get-tuple-element.13), channel_id=1, source_target_pairs={{0,8},{1,9},{2,10},{3,11},{4,12},{5,13},{6,14},{7,15},{8,16},{9,17... | collective-permute-start | bytes 98312 | tf_op jit(solution)/shard_map/ppermute | solution.py:64
  104.2 6.6 %collective-permute-done.16 = bf16[64,256]{1,0:T(8,128)(2,1)S(1)} collective-permute-done((bf16[64,256]{1,0:T(8,128)(2,1)S(1)}, bf16[64,256]{1,0:T(8,128)(2,1)S(1)}, u32[]{:S(2)}, u32[]{:S(2)}) %collective-permute-start.16) | collective-permute-done | bytes 32800 | tf_op jit(solution)/shard_map/ppermute | solution.py:64
  110.8 0.7 reshape.31
  (20 shorter events, 0.1 us)
Async XLA Ops:
  0.0 0.9 copy-start.6
  1.2 20.4 %collective-permute-start = (bf16[256,128]{1,0:T(8,128)(2,1)S(1)}, bf16[256,128]{1,0:T(8,128)(2,1)S(1)}, u32[]{:S(2)}, u32[]{:S(2)}) collective-permute-start(bf16[256,128]{1,0:T(8,128)(2,1)S(1)} %get-tuple-element.10), channel_id=1, source_target_pairs={{0,508},{1,509},{2,510},{3,511},{4,504},{5,505},{6,506},{7,507},{8... | collective-permute-start | bytes 196616 | tf_op jit(solution)/shard_map/ppermute | solution.py:56
  14.2 1.0 copy-start.2
  15.2 26.3 %collective-permute-start.4 = (bf16[512,128]{1,0:T(8,128)(2,1)S(1)}, bf16[512,128]{1,0:T(8,128)(2,1)S(1)}, u32[]{:S(2)}, u32[]{:S(2)}) collective-permute-start(bf16[512,128]{1,0:T(8,128)(2,1)S(1)} %piece.1.refs_0_.refs_2_), channel_id=1, source_target_pairs={{0,4},{1,5},{2,6},{3,7},{4,0},{5,1},{6,2},{7,3},{8,12},{9,13},{10,... | collective-permute-start | bytes 393224 | tf_op jit(solution)/shard_map/ppermute | solution.py:35
  21.5 19.9 %collective-permute-start.5 = (bf16[256,128]{1,0:T(8,128)(2,1)S(1)}, bf16[256,128]{1,0:T(8,128)(2,1)S(1)}, u32[]{:S(2)}, u32[]{:S(2)}) collective-permute-start(bf16[256,128]{1,0:T(8,128)(2,1)S(1)} %collective-permute-done.refs_1_), channel_id=1, source_target_pairs={{0,4},{1,5},{2,6},{3,7},{4,0},{5,1},{6,2},{7,3},{8,12},{9,13},{10,... | collective-permute-start | bytes 196616 | tf_op jit(solution)/shard_map/ppermute | solution.py:35
  29.8 21.7 %copy-start = (bf16[4096,256]{1,0:T(8,128)(2,1)S(1)}, bf16[4096,256]{1,0:T(8,128)(2,1)}, u32[]{:S(2)}) copy-start(bf16[4096,256]{1,0:T(8,128)(2,1)} %param.16) | copy-start | bytes 6291460
  29.8 18.5 %collective-permute-start.3 = (bf16[768,128]{1,0:T(8,128)(2,1)S(1)}, bf16[768,128]{1,0:T(8,128)(2,1)S(1)}, u32[]{:S(2)}, u32[]{:S(2)}) collective-permute-start(bf16[768,128]{1,0:T(8,128)(2,1)S(1)} %bitcast.20), channel_id=1, source_target_pairs={{0,3},{1,2},{2,1},{3,0},{4,7},{5,6},{6,5},{7,4},{8,11},{9,10},{10,... | collective-permute-start | bytes 589832 | tf_op jit(solution)/shard_map/ppermute | solution.py:35
  32.1 19.4 %collective-permute-start.2 = (bf16[768,128]{1,0:T(8,128)(2,1)S(1)}, bf16[768,128]{1,0:T(8,128)(2,1)S(1)}, u32[]{:S(2)}, u32[]{:S(2)}) collective-permute-start(bf16[768,128]{1,0:T(8,128)(2,1)S(1)} %bitcast.21), channel_id=1, source_target_pairs={{0,2},{1,3},{2,0},{3,1},{4,6},{5,7},{6,4},{7,5},{8,10},{9,11},{10,... | collective-permute-start | bytes 589832 | tf_op jit(solution)/shard_map/ppermute | solution.py:35
  36.6 15.8 %collective-permute-start.1 = (bf16[768,128]{1,0:T(8,128)(2,1)S(1)}, bf16[768,128]{1,0:T(8,128)(2,1)S(1)}, u32[]{:S(2)}, u32[]{:S(2)}) collective-permute-start(bf16[768,128]{1,0:T(8,128)(2,1)S(1)} %bitcast.22), channel_id=1, source_target_pairs={{0,1},{1,0},{2,3},{3,2},{4,5},{5,4},{6,7},{7,6},{8,9},{9,8},{10,11... | collective-permute-start | bytes 589832 | tf_op jit(solution)/shard_map/ppermute | solution.py:35
  41.5 18.8 %copy-start.7 = (f32[2,128,128]{2,1,0:T(8,128)S(1)}, f32[2,128,128]{2,1,0:T(8,128)}, u32[]{:S(2)}) copy-start(f32[2,128,128]{2,1,0:T(8,128)} %bias_ref.1) | copy-start | bytes 393220
  41.5 18.8 %copy-start.8 = (f32[128,128]{1,0:T(8,128)S(1)}, f32[128,128]{1,0:T(8,128)}, u32[]{:S(2)}) copy-start(f32[128,128]{1,0:T(8,128)} %constant.7.clone.turned_ref) | copy-start | bytes 196612
  41.5 18.8 %copy-start.9 = (f32[128,128]{1,0:T(8,128)S(1)}, f32[128,128]{1,0:T(8,128)}, u32[]{:S(2)}) copy-start(f32[128,128]{1,0:T(8,128)} %constant.6.clone.hot_ref) | copy-start | bytes 196612
  41.5 14.2 %collective-permute-start.8 = (bf16[768,128]{1,0:T(8,128)(2,1)S(1)}, bf16[768,128]{1,0:T(8,128)(2,1)S(1)}, u32[]{:S(2)}, u32[]{:S(2)}) collective-permute-start(bf16[768,128]{1,0:T(8,128)(2,1)S(1)} %bitcast.27), channel_id=1, source_target_pairs={{0,3},{1,2},{2,1},{3,0},{4,7},{5,6},{6,5},{7,4},{8,11},{9,10},{10,... | collective-permute-start | bytes 589832 | tf_op jit(solution)/shard_map/ppermute | solution.py:35
  43.6 12.1 %collective-permute-start.7 = (bf16[768,128]{1,0:T(8,128)(2,1)S(1)}, bf16[768,128]{1,0:T(8,128)(2,1)S(1)}, u32[]{:S(2)}, u32[]{:S(2)}) collective-permute-start(bf16[768,128]{1,0:T(8,128)(2,1)S(1)} %bitcast.28), channel_id=1, source_target_pairs={{0,2},{1,3},{2,0},{3,1},{4,6},{5,7},{6,4},{7,5},{8,10},{9,11},{10,... | collective-permute-start | bytes 589832 | tf_op jit(solution)/shard_map/ppermute | solution.py:35
  48.3 9.9 %collective-permute-start.6 = (bf16[768,128]{1,0:T(8,128)(2,1)S(1)}, bf16[768,128]{1,0:T(8,128)(2,1)S(1)}, u32[]{:S(2)}, u32[]{:S(2)}) collective-permute-start(bf16[768,128]{1,0:T(8,128)(2,1)S(1)} %bitcast.29), channel_id=1, source_target_pairs={{0,1},{1,0},{2,3},{3,2},{4,5},{5,4},{6,7},{7,6},{8,9},{9,8},{10,11... | collective-permute-start | bytes 589832 | tf_op jit(solution)/shard_map/ppermute | solution.py:35
  51.5 48.3 %collective-permute-start.15 = (bf16[4096,256]{1,0:T(8,128)(2,1)S(1)}, bf16[4096,256]{1,0:T(8,128)(2,1)S(1)}, u32[]{:S(2)}, u32[]{:S(2)}) collective-permute-start(bf16[4096,256]{1,0:T(8,128)(2,1)S(1)} %copy-done), channel_id=1, source_target_pairs={{60,504},{61,505},{62,506},{63,507},{56,508},{57,509},{58,510},{59... | collective-permute-start | bytes 6291464 | tf_op jit(solution)/shard_map/ppermute | solution.py:68
  58.2 2.7 %copy-start.1 = (bf16[1024,3,128]{2,0,1:T(8,128)(2,1)S(1)}, bf16[1024,3,128]{2,0,1:T(8,128)(2,1)}, u32[]{:S(2)}) copy-start(bf16[1024,3,128]{2,0,1:T(8,128)(2,1)} %param.12) | copy-start | bytes 2359300
  58.2 2.7 %copy-start.5 = (f32[1024]{0:T(1024)S(1)}, f32[1024]{0:T(1024)}, u32[]{:S(2)}) copy-start(f32[1024]{0:T(1024)} %param.11) | copy-start | bytes 12292
  58.3 20.6 %collective-permute-start.13 = (bf16[2048,128]{1,0:T(8,128)(2,1)S(1)}, bf16[2048,128]{1,0:T(8,128)(2,1)S(1)}, u32[]{:S(2)}, u32[]{:S(2)}) collective-permute-start(bf16[2048,128]{1,0:T(8,128)(2,1)S(1)} %bitcast.18), channel_id=1, source_target_pairs={{0,16},{1,17},{2,18},{3,19},{4,20},{5,21},{6,22},{7,23},{8,24},{9,... | collective-permute-start | bytes 1572872 | tf_op jit(solution)/shard_map/ppermute | solution.py:35
  64.6 20.4 %collective-permute-start.12 = (bf16[512,128]{1,0:T(8,128)(2,1)S(1)}, bf16[512,128]{1,0:T(8,128)(2,1)S(1)}, u32[]{:S(2)}, u32[]{:S(2)}) collective-permute-start(bf16[512,128]{1,0:T(8,128)(2,1)S(1)} %get-tuple-element.11.refs_0_), channel_id=1, source_target_pairs={{0,4},{1,5},{2,6},{3,7},{4,0},{5,1},{6,2},{7,3},{8,12},{9,13},{10,... | collective-permute-start | bytes 393224 | tf_op jit(solution)/shard_map/ppermute | solution.py:35
  71.7 15.4 %collective-permute-start.11 = (bf16[512,128]{1,0:T(8,128)(2,1)S(1)}, bf16[512,128]{1,0:T(8,128)(2,1)S(1)}, u32[]{:S(2)}, u32[]{:S(2)}) collective-permute-start(bf16[512,128]{1,0:T(8,128)(2,1)S(1)} %get-tuple-element.11.refs_0_), channel_id=1, source_target_pairs={{0,3},{1,2},{2,1},{3,0},{4,7},{5,6},{6,5},{7,4},{8,11},{9,10},{10,... | collective-permute-start | bytes 393224 | tf_op jit(solution)/shard_map/ppermute | solution.py:35
  74.7 12.4 %collective-permute-start.10 = (bf16[512,128]{1,0:T(8,128)(2,1)S(1)}, bf16[512,128]{1,0:T(8,128)(2,1)S(1)}, u32[]{:S(2)}, u32[]{:S(2)}) collective-permute-start(bf16[512,128]{1,0:T(8,128)(2,1)S(1)} %get-tuple-element.11.refs_0_), channel_id=1, source_target_pairs={{0,2},{1,3},{2,0},{3,1},{4,6},{5,7},{6,4},{7,5},{8,10},{9,11},{10,... | collective-permute-start | bytes 393224 | tf_op jit(solution)/shard_map/ppermute | solution.py:35
  78.9 8.2 %collective-permute-start.9 = (bf16[512,128]{1,0:T(8,128)(2,1)S(1)}, bf16[512,128]{1,0:T(8,128)(2,1)S(1)}, u32[]{:S(2)}, u32[]{:S(2)}) collective-permute-start(bf16[512,128]{1,0:T(8,128)(2,1)S(1)} %get-tuple-element.11.refs_0_), channel_id=1, source_target_pairs={{0,1},{1,0},{2,3},{3,2},{4,5},{5,4},{6,7},{7,6},{8,9},{9,8},{10,11... | collective-permute-start | bytes 393224 | tf_op jit(solution)/shard_map/ppermute | solution.py:35
  85.0 14.9 %copy-start.3 = (bf16[128,128]{1,0:T(8,128)(2,1)S(1)}, bf16[128,128]{1,0:T(8,128)(2,1)}, u32[]{:S(2)}) copy-start(bf16[128,128]{1,0:T(8,128)(2,1)} %constant.8.clone.refs_11_) | copy-start | bytes 98308
  85.0 14.9 %copy-start.4 = (f32[4096]{0:T(1024)S(1)}, f32[4096]{0:T(1024)}, u32[]{:S(2)}) copy-start(f32[4096]{0:T(1024)} %param.15) | copy-start | bytes 49156
  85.0 14.9 %collective-permute-start.14 = (bf16[4096,128]{1,0:T(8,128)(2,1)S(1)}, bf16[4096,128]{1,0:T(8,128)(2,1)S(1)}, u32[]{:S(2)}, u32[]{:S(2)}) collective-permute-start(bf16[4096,128]{1,0:T(8,128)(2,1)S(1)} %bitcast.14), channel_id=1, source_target_pairs={{0,8},{1,9},{2,10},{3,11},{4,12},{5,13},{6,14},{7,15},{8,0},{9,1},... | collective-permute-start | bytes 3145736 | tf_op jit(solution)/shard_map/ppermute | solution.py:35
  102.3 8.6 %collective-permute-start.16 = (bf16[64,256]{1,0:T(8,128)(2,1)S(1)}, bf16[64,256]{1,0:T(8,128)(2,1)S(1)}, u32[]{:S(2)}, u32[]{:S(2)}) collective-permute-start(bf16[64,256]{1,0:T(8,128)(2,1)S(1)} %get-tuple-element.13), channel_id=1, source_target_pairs={{0,8},{1,9},{2,10},{3,11},{4,12},{5,13},{6,14},{7,15},{8,16},{9,17... | collective-permute-start | bytes 98312 | tf_op jit(solution)/shard_map/ppermute | solution.py:64

commit v9 on v8

--- a/solution.py
+++ b/solution.py
@@ -180,14 +180,13 @@
 
 
 def merged_order():
-    o = np.arange(128)
-    half, i, lon, level = o >> 6, (o >> 5) & 1, (o >> 1) & 15, o & 1
+    o = np.arange(256)
+    half, i, lon, side, level = o >> 7, (o >> 6) & 1, (o >> 2) & 15, (o >> 1) & 1, o & 1
     back = (lon - 2) % 16
-    return half * 64 + (back >> 2) * 16 + i * 8 + (back & 3) * 2 + level
-
-
-def one_hot(order, dtype):
-    return jnp.asarray(np.eye(len(order), dtype=np.float32)[order], dtype)
+    source = half * 64 + (back >> 2) * 16 + i * 8 + (back & 3) * 2 + level
+    hot = np.zeros((2, 256, 128), np.float32)
+    hot[side, o, source] = 1
+    return jnp.asarray(hot, jnp.bfloat16)
 
 
 def dot(left, right):
@@ -200,34 +199,34 @@
 
 def attention_kernel(*refs):
     parts = refs[:8]
-    gain_ref, w_ref, bias_ref, out_ref, stream_ref, qkv_ref = refs[8:]
+    gain_ref, w_ref, bias_ref, out_ref, stream_ref, qkv_ref, normed_ref = refs[8:]
     head_place = lax.axis_index("head")
     last_band = (lax.axis_index("space") == 63).astype(jnp.int32)
-    for start in range(0, TOKENS, 128):
-        swap = 0 if start < HALF else last_band
+    for half in range(0, TOKENS, HALF):
+        swap = 0 if half == 0 else last_band
         blocks = [head_place ^ k ^ (swap * 4) for k in range(8)]
-        total = jnp.zeros((128, BLOCK), jnp.float32)
-        squares = jnp.zeros((128, BLOCK), jnp.float32)
-        for k, ref in enumerate(parts):
-            rounded = ref[start : start + 128, :]
-            stream_ref[k ^ (swap * 4), start : start + 128, :] = rounded
-            value = rounded.astype(jnp.float32)
-            total += value
-            squares += value * value
-        mean = jnp.sum(total, -1, keepdims=True) * (1.0 / D)
-        spread = jnp.sum(squares, -1, keepdims=True) * (1.0 / D) - mean * mean
-        scale = lax.rsqrt(spread + EPS)
-        product = jnp.zeros((128, 3 * BLOCK), jnp.float32)
+        for start in range(half, half + HALF, 128):
+            total = jnp.zeros((128, BLOCK), jnp.float32)
+            squares = jnp.zeros((128, BLOCK), jnp.float32)
+            for k, ref in enumerate(parts):
+                rounded = ref[start : start + 128, :]
+                stream_ref[k ^ (swap * 4), start : start + 128, :] = rounded
+                value = rounded.astype(jnp.float32)
+                total += value
+                squares += value * value
+            mean = jnp.sum(total, -1, keepdims=True) * (1.0 / D)
+            spread = jnp.sum(squares, -1, keepdims=True) * (1.0 / D) - mean * mean
+            scale = lax.rsqrt(spread + EPS)
+            for k, ref in enumerate(parts):
+                value = (ref[start : start + 128, :].astype(jnp.float32) - mean) * scale * gain_ref[blocks[k]]
+                normed_ref[start - half : start - half + 128, k * BLOCK : (k + 1) * BLOCK] = value.astype(jnp.bfloat16)
+        product = jnp.zeros((HALF, 3 * BLOCK), jnp.float32)
         for k in range(0, 8, 2):
-            normed = []
-            for n in (k, k + 1):
-                value = parts[n][start : start + 128, :].astype(jnp.float32)
-                normed.append(((value - mean) * scale * gain_ref[blocks[n]]).astype(jnp.bfloat16))
             weights = jnp.concatenate(
                 [jnp.concatenate([w_ref[part, blocks[n]] for part in range(3)], axis=1) for n in (k, k + 1)], axis=0
             )
-            product += dot(jnp.concatenate(normed, axis=1), weights)
-        qkv_ref[start : start + 128, :] = product.astype(jnp.bfloat16)
+            product += dot(normed_ref[:, k * BLOCK : (k + 2) * BLOCK], weights)
+        qkv_ref[half : half + HALF, :] = product.astype(jnp.bfloat16)
     for window in range(WINDOWS):
         starts = window_rows(window)
         cells = jnp.concatenate([qkv_ref[s : s + 16, :] for s in starts], axis=0)
@@ -300,7 +299,9 @@
                 weights = jnp.concatenate([ref[k * 8 + block] for block in blocks], axis=0)
                 merged[n] = merged[n] + dot(normed[n * rows : (n + 1) * rows], weights)
         merged = jnp.concatenate(merged, axis=0)
-        out_ref[...] = dot(order_ref[...], merged.astype(jnp.bfloat16)).astype(jnp.bfloat16)
+        merged = merged.astype(jnp.bfloat16)
+        sides = [dot(order_ref[side], merged[:, side * BLOCK : (side + 1) * BLOCK]) for side in range(2)]
+        out_ref[...] = (sides[0] + sides[1]).astype(jnp.bfloat16)
 
     pl.when(space != 63)(lambda: merge(w_ref))
     pl.when(space == 63)(lambda: merge(w_turned_ref))
@@ -327,7 +328,7 @@
         ),
         in_specs=in_vmem(11),
         out_specs=(vmem, vmem),
-        scratch_shapes=[pltpu.VMEM((TOKENS, 3 * BLOCK), jnp.bfloat16)],
+        scratch_shapes=[pltpu.VMEM((TOKENS, 3 * BLOCK), jnp.bfloat16), pltpu.VMEM((HALF, D), jnp.bfloat16)],
         compiler_params=pltpu.CompilerParams(vmem_limit_bytes=16 * 2**20),
         cost_estimate=pl.CostEstimate(flops=600_000_000, bytes_accessed=3_000_000, transcendentals=131072),
         name="attention",
@@ -343,7 +344,7 @@
     w_shape = (2, 8, 2, BLOCK, BLOCK)
     merged = pl.pallas_call(
         merge_kernel,
-        out_shape=jax.ShapeDtypeStruct((128, 256), jnp.bfloat16),
+        out_shape=jax.ShapeDtypeStruct((256, BLOCK), jnp.bfloat16),
         in_specs=in_vmem(12),
         out_specs=vmem,
         scratch_shapes=[pltpu.VMEM((TOKENS, D), jnp.bfloat16)],
@@ -358,10 +359,11 @@
         merge_gain.reshape(32, 1, BLOCK),
         w_merge.reshape(32, BLOCK, 256),
         other_columns(w_merge).reshape(32, BLOCK, 256),
-        one_hot(merged_order(), jnp.bfloat16),
-    )
-    lower = lower_rows(merged[64:])
-    return jnp.concatenate([lower, merged[:64]], axis=0).reshape(4, 16, 2, 256)
+        merged_order(),
+    )
+    lower = lower_rows(merged[128:])
+    grid = jnp.concatenate([lower, merged[:128]], axis=0).reshape(4, 16, 2, 2, BLOCK)
+    return grid.transpose(0, 1, 3, 2, 4).reshape(4, 16, 2, 256)
 
 
 def solution(mesh):

time: 113 us -> 113 us (level)
  no operation moved by 1% of the time
where the time goes in v9:
time: 113 us; the launch traced here: 112 us
  starting transfers between devices  71.1 us (63%)
  waiting for transfers between devices  17.6 us (16%)
  blocking collectives  12.7 us (11%)
  Pallas kernels  7.3 us (6%)
  local copies, waits for them, and re-layouts  1.9 us (2%)
    ppermute x14, starting transfers between devices, moved(): return lax.ppermute(value, BOTH, pairs)  55.4 us
    ppermute x1, starting transfers between devices, following_rows(): return lax.ppermute(value, BOTH, pairs)  13 us
    all_to_all x1, blocking collectives, on_device(): lax.all_to_all(attended_partner, 'head', 0, 0, axis_index_groups=[[0, 1,...  12.7 us
    ppermute x14, waiting for transfers between devices, moved(): return lax.ppermute(value, BOTH, pairs)  11 us
    ppermute x1, waiting for transfers between devices, lower_rows(): return lax.ppermute(value, BOTH, pairs)  6.63 us
    pallas_call x1, Pallas kernels, on_device(): pl.pallas_call(attention_kernel, out_shape=(jax.ShapeDtypeStruct((TOKENS,...  3.9 us
    pallas_call x1, Pallas kernels, on_device(): pl.pallas_call(merge_kernel, out_shape=jax.ShapeDtypeStruct((256, BLOCK),...  2.39 us
  transfers between devices with their start and end apart: 17, of which 5 were waited for; matrix products, arithmetic and copies ran while one was open for 0% of the time, Pallas kernels for 4%

profile of v9, /device:TPU:24, one launch (start us, length us, event | category | flops | bytes accessed | tf_op | source)
XLA Modules:
  0.0 111.7 jit_solution(18253138345161571003)
XLA Ops:
  0.0 0.9 copy-done.6
  0.9 0.2 order.1
  1.2 13.0 %collective-permute-start = (bf16[256,128]{1,0:T(8,128)(2,1)S(1)}, bf16[256,128]{1,0:T(8,128)(2,1)S(1)}, u32[]{:S(2)}, u32[]{:S(2)}) collective-permute-start(bf16[256,128]{1,0:T(8,128)(2,1)S(1)} %get-tuple-element.10), channel_id=1, source_target_pairs={{0,508},{1,509},{2,510},{3,511},{4,504},{5,505},{6,506},{7,507},{8... | collective-permute-start | bytes 196616 | tf_op jit(solution)/shard_map/ppermute | solution.py:56
  14.2 0.0 copy-start.2
  14.2 0.9 copy-done.2
  15.2 6.3 %collective-permute-start.4 = (bf16[512,128]{1,0:T(8,128)(2,1)S(1)}, bf16[512,128]{1,0:T(8,128)(2,1)S(1)}, u32[]{:S(2)}, u32[]{:S(2)}) collective-permute-start(bf16[512,128]{1,0:T(8,128)(2,1)S(1)} %piece.1.refs_0_.refs_2_), channel_id=1, source_target_pairs={{0,4},{1,5},{2,6},{3,7},{4,0},{5,1},{6,2},{7,3},{8,12},{9,13},{10,... | collective-permute-start | bytes 393224 | tf_op jit(solution)/shard_map/ppermute | solution.py:35
  21.5 0.0 collective-permute-done.refs_1_
  21.5 8.2 %collective-permute-start.5 = (bf16[256,128]{1,0:T(8,128)(2,1)S(1)}, bf16[256,128]{1,0:T(8,128)(2,1)S(1)}, u32[]{:S(2)}, u32[]{:S(2)}) collective-permute-start(bf16[256,128]{1,0:T(8,128)(2,1)S(1)} %collective-permute-done.refs_1_), channel_id=1, source_target_pairs={{0,4},{1,5},{2,6},{3,7},{4,0},{5,1},{6,2},{7,3},{8,12},{9,13},{10,... | collective-permute-start | bytes 196616 | tf_op jit(solution)/shard_map/ppermute | solution.py:35
  29.8 0.0 copy-start
  29.8 2.3 %collective-permute-start.3 = (bf16[768,128]{1,0:T(8,128)(2,1)S(1)}, bf16[768,128]{1,0:T(8,128)(2,1)S(1)}, u32[]{:S(2)}, u32[]{:S(2)}) collective-permute-start(bf16[768,128]{1,0:T(8,128)(2,1)S(1)} %bitcast.25), channel_id=1, source_target_pairs={{0,3},{1,2},{2,1},{3,0},{4,7},{5,6},{6,5},{7,4},{8,11},{9,10},{10,... | collective-permute-start | bytes 589832 | tf_op jit(solution)/shard_map/ppermute | solution.py:35
  32.1 4.5 %collective-permute-start.2 = (bf16[768,128]{1,0:T(8,128)(2,1)S(1)}, bf16[768,128]{1,0:T(8,128)(2,1)S(1)}, u32[]{:S(2)}, u32[]{:S(2)}) collective-permute-start(bf16[768,128]{1,0:T(8,128)(2,1)S(1)} %bitcast.26), channel_id=1, source_target_pairs={{0,2},{1,3},{2,0},{3,1},{4,6},{5,7},{6,4},{7,5},{8,10},{9,11},{10,... | collective-permute-start | bytes 589832 | tf_op jit(solution)/shard_map/ppermute | solution.py:35
  36.6 3.2 %collective-permute-start.1 = (bf16[768,128]{1,0:T(8,128)(2,1)S(1)}, bf16[768,128]{1,0:T(8,128)(2,1)S(1)}, u32[]{:S(2)}, u32[]{:S(2)}) collective-permute-start(bf16[768,128]{1,0:T(8,128)(2,1)S(1)} %bitcast.27), channel_id=1, source_target_pairs={{0,1},{1,0},{2,3},{3,2},{4,5},{5,4},{6,7},{7,6},{8,9},{9,8},{10,11... | collective-permute-start | bytes 589832 | tf_op jit(solution)/shard_map/ppermute | solution.py:35
  39.8 1.7 %collective-permute-done.5.refs_1_ = bf16[256,128]{1,0:T(8,128)(2,1)S(1)} collective-permute-done((bf16[256,128]{1,0:T(8,128)(2,1)S(1)}, bf16[256,128]{1,0:T(8,128)(2,1)S(1)}, u32[]{:S(2)}, u32[]{:S(2)}) %collective-permute-start.5) | collective-permute-done | bytes 65568 | tf_op jit(solution)/shard_map/ppermute | solution.py:35
  41.5 0.0 collective-permute-done.4.refs_0_.refs_2_
  41.5 0.0 copy-start.7
  41.5 0.0 copy-start.8
  41.5 0.0 copy-start.9
  41.5 2.1 %collective-permute-start.8 = (bf16[768,128]{1,0:T(8,128)(2,1)S(1)}, bf16[768,128]{1,0:T(8,128)(2,1)S(1)}, u32[]{:S(2)}, u32[]{:S(2)}) collective-permute-start(bf16[768,128]{1,0:T(8,128)(2,1)S(1)} %bitcast.32), channel_id=1, source_target_pairs={{0,3},{1,2},{2,1},{3,0},{4,7},{5,6},{6,5},{7,4},{8,11},{9,10},{10,... | collective-permute-start | bytes 589832 | tf_op jit(solution)/shard_map/ppermute | solution.py:35
  43.6 4.7 %collective-permute-start.7 = (bf16[768,128]{1,0:T(8,128)(2,1)S(1)}, bf16[768,128]{1,0:T(8,128)(2,1)S(1)}, u32[]{:S(2)}, u32[]{:S(2)}) collective-permute-start(bf16[768,128]{1,0:T(8,128)(2,1)S(1)} %bitcast.33), channel_id=1, source_target_pairs={{0,2},{1,3},{2,0},{3,1},{4,6},{5,7},{6,4},{7,5},{8,10},{9,11},{10,... | collective-permute-start | bytes 589832 | tf_op jit(solution)/shard_map/ppermute | solution.py:35
  48.3 0.0 collective-permute-done.3.refs_3_
  48.3 3.2 %collective-permute-start.6 = (bf16[768,128]{1,0:T(8,128)(2,1)S(1)}, bf16[768,128]{1,0:T(8,128)(2,1)S(1)}, u32[]{:S(2)}, u32[]{:S(2)}) collective-permute-start(bf16[768,128]{1,0:T(8,128)(2,1)S(1)} %bitcast.34), channel_id=1, source_target_pairs={{0,1},{1,0},{2,3},{3,2},{4,5},{5,4},{6,7},{7,6},{8,9},{9,8},{10,11... | collective-permute-start | bytes 589832 | tf_op jit(solution)/shard_map/ppermute | solution.py:35
  51.5 0.0 collective-permute-done.2.refs_2_
  51.5 0.8 collective-permute-start.15
  52.3 3.4 %collective-permute-done.8.refs_7_ = bf16[768,128]{1,0:T(8,128)(2,1)S(1)} collective-permute-done((bf16[768,128]{1,0:T(8,128)(2,1)S(1)}, bf16[768,128]{1,0:T(8,128)(2,1)S(1)}, u32[]{:S(2)}, u32[]{:S(2)}) %collective-permute-start.8) | collective-permute-done | bytes 196640 | tf_op jit(solution)/shard_map/ppermute | solution.py:35
  55.7 0.0 collective-permute-done.7.refs_6_
  55.7 2.5 %collective-permute-done.6.refs_5_ = bf16[768,128]{1,0:T(8,128)(2,1)S(1)} collective-permute-done((bf16[768,128]{1,0:T(8,128)(2,1)S(1)}, bf16[768,128]{1,0:T(8,128)(2,1)S(1)}, u32[]{:S(2)}, u32[]{:S(2)}) %collective-permute-start.6) | collective-permute-done | bytes 196640 | tf_op jit(solution)/shard_map/ppermute | solution.py:35
  58.2 0.0 copy-start.1
  58.2 0.0 copy-start.5
  58.3 2.1 %collective-permute-start.13 = (bf16[2048,128]{1,0:T(8,128)(2,1)S(1)}, bf16[2048,128]{1,0:T(8,128)(2,1)S(1)}, u32[]{:S(2)}, u32[]{:S(2)}) collective-permute-start(bf16[2048,128]{1,0:T(8,128)(2,1)S(1)} %bitcast.23), channel_id=1, source_target_pairs={{0,16},{1,17},{2,18},{3,19},{4,20},{5,21},{6,22},{7,23},{8,24},{9,... | collective-permute-start | bytes 1572872 | tf_op jit(solution)/shard_map/ppermute | solution.py:35
  60.3 0.5 bias.1.refs_10_
  60.9 3.9 %attention.1 = (bf16[512,128]{1,0:T(8,128)(2,1)S(1)}, bf16[8,512,128]{2,1,0:T(8,128)(2,1)S(1)}) custom-call(bf16[768,128]{1,0:T(8,128)(2,1)S(1)} %bitcast.29, bf16[768,128]{1,0:T(8,128)(2,1)S(1)} %collective-permute-done.1.refs_1_, bf16[768,128]{1,0:T(8,128)(2,1)S(1)} %collective-permute-done.2.refs_2_, bf16[768,128]{1,0:T(8,128)(2,1)S(1)} %collective-permute-done.3.refs_3_, ...), custom_call_target="tpu_custom_call" | custom-call | flops 600000000 | bytes 3000000 | tf_op jit(solution)/shard_map/attention/pallas_call | solution.py:323
  64.8 7.0 %collective-permute-start.12 = (bf16[512,128]{1,0:T(8,128)(2,1)S(1)}, bf16[512,128]{1,0:T(8,128)(2,1)S(1)}, u32[]{:S(2)}, u32[]{:S(2)}) collective-permute-start(bf16[512,128]{1,0:T(8,128)(2,1)S(1)} %get-tuple-element.11.refs_0_), channel_id=1, source_target_pairs={{0,4},{1,5},{2,6},{3,7},{4,0},{5,1},{6,2},{7,3},{8,12},{9,13},{10,... | collective-permute-start | bytes 393224 | tf_op jit(solution)/shard_map/ppermute | solution.py:35
  71.8 3.0 %collective-permute-start.11 = (bf16[512,128]{1,0:T(8,128)(2,1)S(1)}, bf16[512,128]{1,0:T(8,128)(2,1)S(1)}, u32[]{:S(2)}, u32[]{:S(2)}) collective-permute-start(bf16[512,128]{1,0:T(8,128)(2,1)S(1)} %get-tuple-element.11.refs_0_), channel_id=1, source_target_pairs={{0,3},{1,2},{2,1},{3,0},{4,7},{5,6},{6,5},{7,4},{8,11},{9,10},{10,... | collective-permute-start | bytes 393224 | tf_op jit(solution)/shard_map/ppermute | solution.py:35
  74.8 4.2 %collective-permute-start.10 = (bf16[512,128]{1,0:T(8,128)(2,1)S(1)}, bf16[512,128]{1,0:T(8,128)(2,1)S(1)}, u32[]{:S(2)}, u32[]{:S(2)}) collective-permute-start(bf16[512,128]{1,0:T(8,128)(2,1)S(1)} %get-tuple-element.11.refs_0_), channel_id=1, source_target_pairs={{0,2},{1,3},{2,0},{3,1},{4,6},{5,7},{6,4},{7,5},{8,10},{9,11},{10,... | collective-permute-start | bytes 393224 | tf_op jit(solution)/shard_map/ppermute | solution.py:35
  79.0 0.0 collective-permute-done.13.refs_1_
  79.0 2.7 %collective-permute-start.9 = (bf16[512,128]{1,0:T(8,128)(2,1)S(1)}, bf16[512,128]{1,0:T(8,128)(2,1)S(1)}, u32[]{:S(2)}, u32[]{:S(2)}) collective-permute-start(bf16[512,128]{1,0:T(8,128)(2,1)S(1)} %get-tuple-element.11.refs_0_), channel_id=1, source_target_pairs={{0,1},{1,0},{2,3},{3,2},{4,5},{5,4},{6,7},{7,6},{8,9},{9,8},{10,11... | collective-permute-start | bytes 393224 | tf_op jit(solution)/shard_map/ppermute | solution.py:35
  81.7 0.1 join.9
  81.8 3.4 %collective-permute-done.12.refs_0_ = bf16[512,128]{1,0:T(8,128)(2,1)S(1)} collective-permute-done((bf16[512,128]{1,0:T(8,128)(2,1)S(1)}, bf16[512,128]{1,0:T(8,128)(2,1)S(1)}, u32[]{:S(2)}, u32[]{:S(2)}) %collective-permute-start.12) | collective-permute-done | bytes 131104 | tf_op jit(solution)/shard_map/ppermute | solution.py:35
  85.2 2.0 %collective-permute-start.14 = (bf16[4096,128]{1,0:T(8,128)(2,1)S(1)}, bf16[4096,128]{1,0:T(8,128)(2,1)S(1)}, u32[]{:S(2)}, u32[]{:S(2)}) collective-permute-start(bf16[4096,128]{1,0:T(8,128)(2,1)S(1)} %bitcast.19), channel_id=1, source_target_pairs={{0,8},{1,9},{2,10},{3,11},{4,12},{5,13},{6,14},{7,15},{8,0},{9,1},... | collective-permute-start | bytes 3145736 | tf_op jit(solution)/shard_map/ppermute | solution.py:35
  87.2 0.0 collective-permute-done.11.refs_3_
  87.2 0.0 collective-permute-done.10.refs_2_
  87.3 0.1 join.7
  87.3 12.7 %all_to_all.5.refs_4_ = bf16[4,512,128]{2,1,0:T(8,128)(2,1)S(1)} all-to-all(bf16[4,512,128]{2,1,0:T(8,128)(2,1)S(1)} %join.7), channel_id=1, replica_groups={{0,1,2,3},{4,5,6,7},{8,9,10,11},{12,13,14,15},{16,17,18,19},{20,21,22,2..., dimensions={0} | all-to-all | bytes 1048576 | tf_op jit(solution)/shard_map/all_to_all | solution.py:340
  100.0 0.0 collective-permute-done.14
  100.1 2.4 %merge.1 = bf16[256,128]{1,0:T(8,128)(2,1)S(1)} custom-call(bf16[512,128]{1,0:T(8,128)(2,1)S(1)} %get-tuple-element.11.refs_0_, bf16[512,128]{1,0:T(8,128)(2,1)S(1)} %collective-permute-done.9.refs_1_, bf16[512,128]{1,0:T(8,128)(2,1)S(1)} %collective-permute-done.10.refs_2_, bf16[512,128]{1,0:T(8,128)(2,1)S(1)} %collective-permute-done.11.refs_3_, ...), custom_call_target="tpu_custom_call" | custom-call | flops 1400000000 | bytes 7000000 | tf_op jit(solution)/shard_map/merge/pallas_call | solution.py:345
  102.5 1.9 %collective-permute-start.16 = (bf16[128,128]{1,0:T(8,128)(2,1)S(1)}, bf16[128,128]{1,0:T(8,128)(2,1)S(1)}, u32[]{:S(2)}, u32[]{:S(2)}) collective-permute-start(bf16[128,128]{1,0:T(8,128)(2,1)S(1)} %get-tuple-element.13), channel_id=1, source_target_pairs={{0,8},{1,9},{2,10},{3,11},{4,12},{5,13},{6,14},{7,15},{8,16},{9,17... | collective-permute-start | bytes 98312 | tf_op jit(solution)/shard_map/ppermute | solution.py:64
  104.4 6.6 %collective-permute-done.16 = bf16[128,128]{1,0:T(8,128)(2,1)S(1)} collective-permute-done((bf16[128,128]{1,0:T(8,128)(2,1)S(1)}, bf16[128,128]{1,0:T(8,128)(2,1)S(1)}, u32[]{:S(2)}, u32[]{:S(2)}) %collective-permute-start.16) | collective-permute-done | bytes 32800 | tf_op jit(solution)/shard_map/ppermute | solution.py:64
  111.0 0.6 pad_maximum_fusion
  (19 shorter events, 0.1 us)
Async XLA Ops:
  0.0 0.9 copy-start.6
  1.2 20.4 %collective-permute-start = (bf16[256,128]{1,0:T(8,128)(2,1)S(1)}, bf16[256,128]{1,0:T(8,128)(2,1)S(1)}, u32[]{:S(2)}, u32[]{:S(2)}) collective-permute-start(bf16[256,128]{1,0:T(8,128)(2,1)S(1)} %get-tuple-element.10), channel_id=1, source_target_pairs={{0,508},{1,509},{2,510},{3,511},{4,504},{5,505},{6,506},{7,507},{8... | collective-permute-start | bytes 196616 | tf_op jit(solution)/shard_map/ppermute | solution.py:56
  14.2 1.0 copy-start.2
  15.2 26.3 %collective-permute-start.4 = (bf16[512,128]{1,0:T(8,128)(2,1)S(1)}, bf16[512,128]{1,0:T(8,128)(2,1)S(1)}, u32[]{:S(2)}, u32[]{:S(2)}) collective-permute-start(bf16[512,128]{1,0:T(8,128)(2,1)S(1)} %piece.1.refs_0_.refs_2_), channel_id=1, source_target_pairs={{0,4},{1,5},{2,6},{3,7},{4,0},{5,1},{6,2},{7,3},{8,12},{9,13},{10,... | collective-permute-start | bytes 393224 | tf_op jit(solution)/shard_map/ppermute | solution.py:35
  21.5 19.9 %collective-permute-start.5 = (bf16[256,128]{1,0:T(8,128)(2,1)S(1)}, bf16[256,128]{1,0:T(8,128)(2,1)S(1)}, u32[]{:S(2)}, u32[]{:S(2)}) collective-permute-start(bf16[256,128]{1,0:T(8,128)(2,1)S(1)} %collective-permute-done.refs_1_), channel_id=1, source_target_pairs={{0,4},{1,5},{2,6},{3,7},{4,0},{5,1},{6,2},{7,3},{8,12},{9,13},{10,... | collective-permute-start | bytes 196616 | tf_op jit(solution)/shard_map/ppermute | solution.py:35
  29.8 21.7 %copy-start = (bf16[4096,256]{1,0:T(8,128)(2,1)S(1)}, bf16[4096,256]{1,0:T(8,128)(2,1)}, u32[]{:S(2)}) copy-start(bf16[4096,256]{1,0:T(8,128)(2,1)} %param.16) | copy-start | bytes 6291460
  29.8 18.5 %collective-permute-start.3 = (bf16[768,128]{1,0:T(8,128)(2,1)S(1)}, bf16[768,128]{1,0:T(8,128)(2,1)S(1)}, u32[]{:S(2)}, u32[]{:S(2)}) collective-permute-start(bf16[768,128]{1,0:T(8,128)(2,1)S(1)} %bitcast.25), channel_id=1, source_target_pairs={{0,3},{1,2},{2,1},{3,0},{4,7},{5,6},{6,5},{7,4},{8,11},{9,10},{10,... | collective-permute-start | bytes 589832 | tf_op jit(solution)/shard_map/ppermute | solution.py:35
  32.1 19.4 %collective-permute-start.2 = (bf16[768,128]{1,0:T(8,128)(2,1)S(1)}, bf16[768,128]{1,0:T(8,128)(2,1)S(1)}, u32[]{:S(2)}, u32[]{:S(2)}) collective-permute-start(bf16[768,128]{1,0:T(8,128)(2,1)S(1)} %bitcast.26), channel_id=1, source_target_pairs={{0,2},{1,3},{2,0},{3,1},{4,6},{5,7},{6,4},{7,5},{8,10},{9,11},{10,... | collective-permute-start | bytes 589832 | tf_op jit(solution)/shard_map/ppermute | solution.py:35
  36.6 15.8 %collective-permute-start.1 = (bf16[768,128]{1,0:T(8,128)(2,1)S(1)}, bf16[768,128]{1,0:T(8,128)(2,1)S(1)}, u32[]{:S(2)}, u32[]{:S(2)}) collective-permute-start(bf16[768,128]{1,0:T(8,128)(2,1)S(1)} %bitcast.27), channel_id=1, source_target_pairs={{0,1},{1,0},{2,3},{3,2},{4,5},{5,4},{6,7},{7,6},{8,9},{9,8},{10,11... | collective-permute-start | bytes 589832 | tf_op jit(solution)/shard_map/ppermute | solution.py:35
  41.5 18.8 %copy-start.7 = (f32[2,128,128]{2,1,0:T(8,128)S(1)}, f32[2,128,128]{2,1,0:T(8,128)}, u32[]{:S(2)}) copy-start(f32[2,128,128]{2,1,0:T(8,128)} %bias_ref.1) | copy-start | bytes 393220
  41.5 18.8 %copy-start.8 = (f32[128,128]{1,0:T(8,128)S(1)}, f32[128,128]{1,0:T(8,128)}, u32[]{:S(2)}) copy-start(f32[128,128]{1,0:T(8,128)} %constant.7.clone.turned_ref) | copy-start | bytes 196612
  41.5 18.8 %copy-start.9 = (f32[128,128]{1,0:T(8,128)S(1)}, f32[128,128]{1,0:T(8,128)}, u32[]{:S(2)}) copy-start(f32[128,128]{1,0:T(8,128)} %constant.6.clone.hot_ref) | copy-start | bytes 196612
  41.5 14.2 %collective-permute-start.8 = (bf16[768,128]{1,0:T(8,128)(2,1)S(1)}, bf16[768,128]{1,0:T(8,128)(2,1)S(1)}, u32[]{:S(2)}, u32[]{:S(2)}) collective-permute-start(bf16[768,128]{1,0:T(8,128)(2,1)S(1)} %bitcast.32), channel_id=1, source_target_pairs={{0,3},{1,2},{2,1},{3,0},{4,7},{5,6},{6,5},{7,4},{8,11},{9,10},{10,... | collective-permute-start | bytes 589832 | tf_op jit(solution)/shard_map/ppermute | solution.py:35
  43.6 12.1 %collective-permute-start.7 = (bf16[768,128]{1,0:T(8,128)(2,1)S(1)}, bf16[768,128]{1,0:T(8,128)(2,1)S(1)}, u32[]{:S(2)}, u32[]{:S(2)}) collective-permute-start(bf16[768,128]{1,0:T(8,128)(2,1)S(1)} %bitcast.33), channel_id=1, source_target_pairs={{0,2},{1,3},{2,0},{3,1},{4,6},{5,7},{6,4},{7,5},{8,10},{9,11},{10,... | collective-permute-start | bytes 589832 | tf_op jit(solution)/shard_map/ppermute | solution.py:35
  48.3 9.9 %collective-permute-start.6 = (bf16[768,128]{1,0:T(8,128)(2,1)S(1)}, bf16[768,128]{1,0:T(8,128)(2,1)S(1)}, u32[]{:S(2)}, u32[]{:S(2)}) collective-permute-start(bf16[768,128]{1,0:T(8,128)(2,1)S(1)} %bitcast.34), channel_id=1, source_target_pairs={{0,1},{1,0},{2,3},{3,2},{4,5},{5,4},{6,7},{7,6},{8,9},{9,8},{10,11... | collective-permute-start | bytes 589832 | tf_op jit(solution)/shard_map/ppermute | solution.py:35
  51.5 48.5 %collective-permute-start.15 = (bf16[4096,256]{1,0:T(8,128)(2,1)S(1)}, bf16[4096,256]{1,0:T(8,128)(2,1)S(1)}, u32[]{:S(2)}, u32[]{:S(2)}) collective-permute-start(bf16[4096,256]{1,0:T(8,128)(2,1)S(1)} %copy-done), channel_id=1, source_target_pairs={{60,504},{61,505},{62,506},{63,507},{56,508},{57,509},{58,510},{59... | collective-permute-start | bytes 6291464 | tf_op jit(solution)/shard_map/ppermute | solution.py:68
  58.2 2.7 %copy-start.1 = (bf16[1024,3,128]{2,0,1:T(8,128)(2,1)S(1)}, bf16[1024,3,128]{2,0,1:T(8,128)(2,1)}, u32[]{:S(2)}) copy-start(bf16[1024,3,128]{2,0,1:T(8,128)(2,1)} %param.12) | copy-start | bytes 2359300
  58.2 2.7 %copy-start.5 = (f32[1024]{0:T(1024)S(1)}, f32[1024]{0:T(1024)}, u32[]{:S(2)}) copy-start(f32[1024]{0:T(1024)} %param.11) | copy-start | bytes 12292
  58.3 20.8 %collective-permute-start.13 = (bf16[2048,128]{1,0:T(8,128)(2,1)S(1)}, bf16[2048,128]{1,0:T(8,128)(2,1)S(1)}, u32[]{:S(2)}, u32[]{:S(2)}) collective-permute-start(bf16[2048,128]{1,0:T(8,128)(2,1)S(1)} %bitcast.23), channel_id=1, source_target_pairs={{0,16},{1,17},{2,18},{3,19},{4,20},{5,21},{6,22},{7,23},{8,24},{9,... | collective-permute-start | bytes 1572872 | tf_op jit(solution)/shard_map/ppermute | solution.py:35
  64.8 20.4 %collective-permute-start.12 = (bf16[512,128]{1,0:T(8,128)(2,1)S(1)}, bf16[512,128]{1,0:T(8,128)(2,1)S(1)}, u32[]{:S(2)}, u32[]{:S(2)}) collective-permute-start(bf16[512,128]{1,0:T(8,128)(2,1)S(1)} %get-tuple-element.11.refs_0_), channel_id=1, source_target_pairs={{0,4},{1,5},{2,6},{3,7},{4,0},{5,1},{6,2},{7,3},{8,12},{9,13},{10,... | collective-permute-start | bytes 393224 | tf_op jit(solution)/shard_map/ppermute | solution.py:35
  71.8 15.4 %collective-permute-start.11 = (bf16[512,128]{1,0:T(8,128)(2,1)S(1)}, bf16[512,128]{1,0:T(8,128)(2,1)S(1)}, u32[]{:S(2)}, u32[]{:S(2)}) collective-permute-start(bf16[512,128]{1,0:T(8,128)(2,1)S(1)} %get-tuple-element.11.refs_0_), channel_id=1, source_target_pairs={{0,3},{1,2},{2,1},{3,0},{4,7},{5,6},{6,5},{7,4},{8,11},{9,10},{10,... | collective-permute-start | bytes 393224 | tf_op jit(solution)/shard_map/ppermute | solution.py:35
  74.8 12.4 %collective-permute-start.10 = (bf16[512,128]{1,0:T(8,128)(2,1)S(1)}, bf16[512,128]{1,0:T(8,128)(2,1)S(1)}, u32[]{:S(2)}, u32[]{:S(2)}) collective-permute-start(bf16[512,128]{1,0:T(8,128)(2,1)S(1)} %get-tuple-element.11.refs_0_), channel_id=1, source_target_pairs={{0,2},{1,3},{2,0},{3,1},{4,6},{5,7},{6,4},{7,5},{8,10},{9,11},{10,... | collective-permute-start | bytes 393224 | tf_op jit(solution)/shard_map/ppermute | solution.py:35
  79.0 8.2 %collective-permute-start.9 = (bf16[512,128]{1,0:T(8,128)(2,1)S(1)}, bf16[512,128]{1,0:T(8,128)(2,1)S(1)}, u32[]{:S(2)}, u32[]{:S(2)}) collective-permute-start(bf16[512,128]{1,0:T(8,128)(2,1)S(1)} %get-tuple-element.11.refs_0_), channel_id=1, source_target_pairs={{0,1},{1,0},{2,3},{3,2},{4,5},{5,4},{6,7},{7,6},{8,9},{9,8},{10,11... | collective-permute-start | bytes 393224 | tf_op jit(solution)/shard_map/ppermute | solution.py:35
  85.2 14.9 %copy-start.3 = (bf16[2,256,128]{2,1,0:T(8,128)(2,1)S(1)}, bf16[2,256,128]{2,1,0:T(8,128)(2,1)}, u32[]{:S(2)}) copy-start(bf16[2,256,128]{2,1,0:T(8,128)(2,1)} %constant.8.clone.refs_11_) | copy-start | bytes 393220
  85.2 14.9 %copy-start.4 = (f32[4096]{0:T(1024)S(1)}, f32[4096]{0:T(1024)}, u32[]{:S(2)}) copy-start(f32[4096]{0:T(1024)} %param.15) | copy-start | bytes 49156
  85.2 14.9 %collective-permute-start.14 = (bf16[4096,128]{1,0:T(8,128)(2,1)S(1)}, bf16[4096,128]{1,0:T(8,128)(2,1)S(1)}, u32[]{:S(2)}, u32[]{:S(2)}) collective-permute-start(bf16[4096,128]{1,0:T(8,128)(2,1)S(1)} %bitcast.19), channel_id=1, source_target_pairs={{0,8},{1,9},{2,10},{3,11},{4,12},{5,13},{6,14},{7,15},{8,0},{9,1},... | collective-permute-start | bytes 3145736 | tf_op jit(solution)/shard_map/ppermute | solution.py:35
  102.5 8.6 %collective-permute-start.16 = (bf16[128,128]{1,0:T(8,128)(2,1)S(1)}, bf16[128,128]{1,0:T(8,128)(2,1)S(1)}, u32[]{:S(2)}, u32[]{:S(2)}) collective-permute-start(bf16[128,128]{1,0:T(8,128)(2,1)S(1)} %get-tuple-element.13), channel_id=1, source_target_pairs={{0,8},{1,9},{2,10},{3,11},{4,12},{5,13},{6,14},{7,15},{8,16},{9,17... | collective-permute-start | bytes 98312 | tf_op jit(solution)/shard_map/ppermute | solution.py:64

commit v10 on v8

--- a/solution.py
+++ b/solution.py
@@ -14,18 +14,17 @@
 TOKENS = 512
 HALF = 256
 CLAIMED = 10_000_000_000
+
 WINDOWS = 4
 WIN_LON = 8
 EPS = 1e-05
 BOTH = ("space", "head")
-
 
 def place(index):
     space, head = divmod(index, 8)
     z_lo, rest = divmod(space, 8)
     x, core = divmod(rest, 2)
     return z_lo, x, core, head
-
 
 def moved(value, move):
     pairs = []
@@ -34,18 +33,14 @@
         pairs.append((source, ((z_lo * 4 + x) * 2 + core) * 8 + head))
     return lax.ppermute(value, BOTH, pairs)
 
-
 def across(value, bits):
     return moved(value, lambda z_lo, x, core, head: (z_lo, x, core, head ^ bits))
 
-
 def across_x(value, bits):
     return moved(value, lambda z_lo, x, core, head: (z_lo, x ^ bits, core, head))
 
-
 def other_core(value):
     return moved(value, lambda z_lo, x, core, head: (z_lo, x, core ^ 1, head))
-
 
 def following_rows(value):
     pairs = []
@@ -55,7 +50,6 @@
             pairs.append((space * 8 + head, target * 8 + (head ^ 4 if space == 0 else head)))
     return lax.ppermute(value, BOTH, pairs)
 
-
 def lower_rows(value):
     pairs = []
     for space in range(64):
@@ -63,14 +57,11 @@
             pairs.append((space * 8 + head, (space + 1) % 64 * 8 + (head ^ 4 if space == 63 else head)))
     return lax.ppermute(value, BOTH, pairs)
 
-
 def other_columns(w_merge):
     return lax.ppermute(w_merge, BOTH, [(7 * 8 + (head ^ 4), 63 * 8 + head) for head in range(8)])
 
-
 def in_vmem(count):
     return [pl.BlockSpec(memory_space=pltpu.VMEM)] * count
-
 
 def join_kernel(spans, copies, *refs):
     at = 0
@@ -79,7 +70,6 @@
         for copy in range(copies):
             refs[-1][copy, at : at + stop - start, :] = rows
         at += stop - start
-
 
 def joined(parts, copies=1, claimed=0, events=()):
     spans = [(start, stop) for _, start, stop in parts]
@@ -95,10 +85,8 @@
     )(*[part for part, _, _ in parts], *events)
     return result if copies > 1 else result[0]
 
-
 def along_y(value):
     return [value] + [across(value, bits) for bits in (1, 2, 3)]
-
 
 def order_kernel(rows_ref, first_ref, behind_ref):
     place = lax.broadcasted_iota(jnp.int32, (HALF, HALF), 0)
@@ -108,7 +96,6 @@
     hot = jnp.where(row * 64 + lon * 2 + (place & 1) == token, 1.0, 0.0).astype(jnp.bfloat16)
     behind_ref[...] = dot(hot, rows_ref[:HALF, :]).astype(jnp.bfloat16)
     first_ref[...] = dot(hot, rows_ref[HALF:, :]).astype(jnp.bfloat16)
-
 
 def ordered(rows):
     half = jax.ShapeDtypeStruct((HALF, BLOCK), jnp.bfloat16)
@@ -122,7 +109,6 @@
         name="order",
     )(rows)
 
-
 def piece_kernel(rows_ref, w_ref, out_ref):
     space = lax.axis_index("space")
     quarter = (space // 2 % 2) * 2 + space % 2
@@ -130,7 +116,6 @@
     for side in range(2):
         column = pl.multiple_of(quarter * 256 + side * BLOCK, BLOCK)
         out_ref[HALF + side * BLOCK : HALF + (side + 1) * BLOCK, :] = w_ref[:, pl.ds(column, BLOCK)]
-
 
 def with_piece(rows, w_out):
     return pl.pallas_call(
@@ -142,7 +127,6 @@
         name="piece",
     )(rows, w_out)
 
-
 def bias_kernel(hot_ref, turned_ref, bias_ref, out_ref):
     for head in range(2):
         rows = jnp.dot(
@@ -151,7 +135,6 @@
         out_ref[head] = jnp.dot(
             rows, turned_ref[...], precision=lax.Precision.HIGHEST, preferred_element_type=jnp.float32
         )
-
 
 def ordered_bias(bias):
     hot = np.eye(BLOCK, dtype=np.float32)[window_order()]
@@ -165,12 +148,10 @@
         name="bias",
     )(jnp.asarray(hot), jnp.asarray(hot.T.copy()), bias)
 
-
 def gathered(value, extra=None):
     partner = joined([across(value, 4)], claimed=CLAIMED)
     own = value if extra is None else jnp.concatenate([value, extra], axis=0)
     return [place if bits == 0 else across(place, bits) for place in (own, partner) for bits in range(4)]
-
 
 def window_order():
     p = np.arange(128)
@@ -178,25 +159,20 @@
     di, dj, half = (p >> 4) & 1, (p >> 5) & 1, (p >> 6) & 1
     return (half * 4 + 2 * i + di) * 16 + (2 * j + dj) * 2 + (1 - level)
 
-
 def merged_order():
-    o = np.arange(128)
-    half, i, lon, level = o >> 6, (o >> 5) & 1, (o >> 1) & 15, o & 1
+    o = np.arange(256)
+    half, i, lon, side, level = o >> 7, (o >> 6) & 1, (o >> 2) & 15, (o >> 1) & 1, o & 1
     back = (lon - 2) % 16
-    return half * 64 + (back >> 2) * 16 + i * 8 + (back & 3) * 2 + level
-
-
-def one_hot(order, dtype):
-    return jnp.asarray(np.eye(len(order), dtype=np.float32)[order], dtype)
-
+    source = half * 64 + (back >> 2) * 16 + i * 8 + (back & 3) * 2 + level
+    hot = np.zeros((2, 256, 128), np.float32)
+    hot[side, o, source] = 1
+    return jnp.asarray(hot, jnp.bfloat16)
 
 def dot(left, right):
     return jnp.dot(left, right, preferred_element_type=jnp.float32)
 
-
 def window_rows(window):
     return [half * HALF + quad * 64 + window * 16 for half in range(2) for quad in range(4)]
-
 
 def attention_kernel(*refs):
     parts = refs[:8]
@@ -240,12 +216,11 @@
             scores = lax.dot_general(queries, keys, (((1,), (1,)), ((), ())), preferred_element_type=jnp.float32)
             scores = scores * HEAD_DIM ** (-0.5) + bias_ref[head]
             exponent = jnp.exp(scores - jnp.max(scores, -1, keepdims=True))
-            weights = (exponent / jnp.sum(exponent, -1, keepdims=True)).astype(jnp.bfloat16)
+            weights = (exponent * (1.0 / jnp.sum(exponent, -1, keepdims=True))).astype(jnp.bfloat16)
             heads.append(dot(weights, values))
         attended = jnp.concatenate(heads, axis=1).astype(jnp.bfloat16)
         for piece, s in enumerate(starts):
             out_ref[s : s + 16, :] = attended[piece * 16 : piece * 16 + 16, :]
-
 
 def merge_kernel(*refs):
     att_refs = refs[:5]
@@ -300,11 +275,12 @@
                 weights = jnp.concatenate([ref[k * 8 + block] for block in blocks], axis=0)
                 merged[n] = merged[n] + dot(normed[n * rows : (n + 1) * rows], weights)
         merged = jnp.concatenate(merged, axis=0)
-        out_ref[...] = dot(order_ref[...], merged.astype(jnp.bfloat16)).astype(jnp.bfloat16)
+        merged = merged.astype(jnp.bfloat16)
+        sides = [dot(order_ref[side], merged[:, side * BLOCK : (side + 1) * BLOCK]) for side in range(2)]
+        out_ref[...] = (sides[0] + sides[1]).astype(jnp.bfloat16)
 
     pl.when(space != 63)(lambda: merge(w_ref))
     pl.when(space == 63)(lambda: merge(w_turned_ref))
-
 
 def on_device(fields, ln_gain, w_qkv, attn_bias, w_out, merge_gain, w_merge):
     first, behind = ordered(fields.reshape(TOKENS, BLOCK))
@@ -343,7 +319,7 @@
     w_shape = (2, 8, 2, BLOCK, BLOCK)
     merged = pl.pallas_call(
         merge_kernel,
-        out_shape=jax.ShapeDtypeStruct((128, 256), jnp.bfloat16),
+        out_shape=jax.ShapeDtypeStruct((256, BLOCK), jnp.bfloat16),
         in_specs=in_vmem(12),
         out_specs=vmem,
         scratch_shapes=[pltpu.VMEM((TOKENS, D), jnp.bfloat16)],
@@ -358,11 +334,11 @@
         merge_gain.reshape(32, 1, BLOCK),
         w_merge.reshape(32, BLOCK, 256),
         other_columns(w_merge).reshape(32, BLOCK, 256),
-        one_hot(merged_order(), jnp.bfloat16),
-    )
-    lower = lower_rows(merged[64:])
-    return jnp.concatenate([lower, merged[:64]], axis=0).reshape(4, 16, 2, 256)
-
+        merged_order(),
+    )
+    lower = lower_rows(merged[128:])
+    grid = jnp.concatenate([lower, merged[:128]], axis=0).reshape(4, 16, 2, 2, BLOCK)
+    return grid.transpose(0, 1, 3, 2, 4).reshape(4, 16, 2, 256)
 
 def solution(mesh):
     placed = (

time: 113 us -> 113 us (level)
  no operation moved by 1% of the time
where the time goes in v10:
time: 113 us; the launch traced here: 111 us
  starting transfers between devices  71.1 us (63%)
  waiting for transfers between devices  17.6 us (16%)
  blocking collectives  12.7 us (11%)
  Pallas kernels  7.13 us (6%)
  local copies, waits for them, and re-layouts  1.9 us (2%)
    ppermute x14, starting transfers between devices, moved(): return lax.ppermute(value, BOTH, pairs)  55.4 us
    ppermute x1, starting transfers between devices, following_rows(): return lax.ppermute(value, BOTH, pairs)  13 us
    all_to_all x1, blocking collectives, on_device(): lax.all_to_all(attended_partner, 'head', 0, 0, axis_index_groups=[[0, 1,...  12.7 us
    ppermute x14, waiting for transfers between devices, moved(): return lax.ppermute(value, BOTH, pairs)  10.9 us
    ppermute x1, waiting for transfers between devices, lower_rows(): return lax.ppermute(value, BOTH, pairs)  6.63 us
    pallas_call x1, Pallas kernels, on_device(): pl.pallas_call(attention_kernel, out_shape=(jax.ShapeDtypeStruct((TOKENS,...  3.73 us
    pallas_call x1, Pallas kernels, on_device(): pl.pallas_call(merge_kernel, out_shape=jax.ShapeDtypeStruct((256, BLOCK),...  2.4 us
  transfers between devices with their start and end apart: 17, of which 5 were waited for; matrix products, arithmetic and copies ran while one was open for 0% of the time, Pallas kernels for 4%

profile of v10, /device:TPU:24, one launch (start us, length us, event | category | flops | bytes accessed | tf_op | source)
XLA Modules:
  0.0 111.5 jit_solution(7297669342053344423)
XLA Ops:
  0.0 0.9 copy-done.6
  0.9 0.2 order.1
  1.2 13.0 %collective-permute-start = (bf16[256,128]{1,0:T(8,128)(2,1)S(1)}, bf16[256,128]{1,0:T(8,128)(2,1)S(1)}, u32[]{:S(2)}, u32[]{:S(2)}) collective-permute-start(bf16[256,128]{1,0:T(8,128)(2,1)S(1)} %get-tuple-element.10), channel_id=1, source_target_pairs={{0,508},{1,509},{2,510},{3,511},{4,504},{5,505},{6,506},{7,507},{8... | collective-permute-start | bytes 196616 | tf_op jit(solution)/shard_map/ppermute | solution.py:51
  14.2 0.0 copy-start.2
  14.2 0.9 copy-done.2
  15.2 6.3 %collective-permute-start.4 = (bf16[512,128]{1,0:T(8,128)(2,1)S(1)}, bf16[512,128]{1,0:T(8,128)(2,1)S(1)}, u32[]{:S(2)}, u32[]{:S(2)}) collective-permute-start(bf16[512,128]{1,0:T(8,128)(2,1)S(1)} %piece.1.refs_0_.refs_2_), channel_id=1, source_target_pairs={{0,4},{1,5},{2,6},{3,7},{4,0},{5,1},{6,2},{7,3},{8,12},{9,13},{10,... | collective-permute-start | bytes 393224 | tf_op jit(solution)/shard_map/ppermute | solution.py:34
  21.5 0.0 collective-permute-done.refs_1_
  21.5 8.2 %collective-permute-start.5 = (bf16[256,128]{1,0:T(8,128)(2,1)S(1)}, bf16[256,128]{1,0:T(8,128)(2,1)S(1)}, u32[]{:S(2)}, u32[]{:S(2)}) collective-permute-start(bf16[256,128]{1,0:T(8,128)(2,1)S(1)} %collective-permute-done.refs_1_), channel_id=1, source_target_pairs={{0,4},{1,5},{2,6},{3,7},{4,0},{5,1},{6,2},{7,3},{8,12},{9,13},{10,... | collective-permute-start | bytes 196616 | tf_op jit(solution)/shard_map/ppermute | solution.py:34
  29.8 0.0 copy-start
  29.8 2.3 %collective-permute-start.3 = (bf16[768,128]{1,0:T(8,128)(2,1)S(1)}, bf16[768,128]{1,0:T(8,128)(2,1)S(1)}, u32[]{:S(2)}, u32[]{:S(2)}) collective-permute-start(bf16[768,128]{1,0:T(8,128)(2,1)S(1)} %bitcast.25), channel_id=1, source_target_pairs={{0,3},{1,2},{2,1},{3,0},{4,7},{5,6},{6,5},{7,4},{8,11},{9,10},{10,... | collective-permute-start | bytes 589832 | tf_op jit(solution)/shard_map/ppermute | solution.py:34
  32.1 4.5 %collective-permute-start.2 = (bf16[768,128]{1,0:T(8,128)(2,1)S(1)}, bf16[768,128]{1,0:T(8,128)(2,1)S(1)}, u32[]{:S(2)}, u32[]{:S(2)}) collective-permute-start(bf16[768,128]{1,0:T(8,128)(2,1)S(1)} %bitcast.26), channel_id=1, source_target_pairs={{0,2},{1,3},{2,0},{3,1},{4,6},{5,7},{6,4},{7,5},{8,10},{9,11},{10,... | collective-permute-start | bytes 589832 | tf_op jit(solution)/shard_map/ppermute | solution.py:34
  36.6 3.2 %collective-permute-start.1 = (bf16[768,128]{1,0:T(8,128)(2,1)S(1)}, bf16[768,128]{1,0:T(8,128)(2,1)S(1)}, u32[]{:S(2)}, u32[]{:S(2)}) collective-permute-start(bf16[768,128]{1,0:T(8,128)(2,1)S(1)} %bitcast.27), channel_id=1, source_target_pairs={{0,1},{1,0},{2,3},{3,2},{4,5},{5,4},{6,7},{7,6},{8,9},{9,8},{10,11... | collective-permute-start | bytes 589832 | tf_op jit(solution)/shard_map/ppermute | solution.py:34
  39.8 1.7 %collective-permute-done.5.refs_1_ = bf16[256,128]{1,0:T(8,128)(2,1)S(1)} collective-permute-done((bf16[256,128]{1,0:T(8,128)(2,1)S(1)}, bf16[256,128]{1,0:T(8,128)(2,1)S(1)}, u32[]{:S(2)}, u32[]{:S(2)}) %collective-permute-start.5) | collective-permute-done | bytes 65568 | tf_op jit(solution)/shard_map/ppermute | solution.py:34
  41.5 0.0 collective-permute-done.4.refs_0_.refs_2_
  41.5 0.0 copy-start.7
  41.5 0.0 copy-start.8
  41.5 0.0 copy-start.9
  41.5 2.1 %collective-permute-start.8 = (bf16[768,128]{1,0:T(8,128)(2,1)S(1)}, bf16[768,128]{1,0:T(8,128)(2,1)S(1)}, u32[]{:S(2)}, u32[]{:S(2)}) collective-permute-start(bf16[768,128]{1,0:T(8,128)(2,1)S(1)} %bitcast.32), channel_id=1, source_target_pairs={{0,3},{1,2},{2,1},{3,0},{4,7},{5,6},{6,5},{7,4},{8,11},{9,10},{10,... | collective-permute-start | bytes 589832 | tf_op jit(solution)/shard_map/ppermute | solution.py:34
  43.6 4.7 %collective-permute-start.7 = (bf16[768,128]{1,0:T(8,128)(2,1)S(1)}, bf16[768,128]{1,0:T(8,128)(2,1)S(1)}, u32[]{:S(2)}, u32[]{:S(2)}) collective-permute-start(bf16[768,128]{1,0:T(8,128)(2,1)S(1)} %bitcast.33), channel_id=1, source_target_pairs={{0,2},{1,3},{2,0},{3,1},{4,6},{5,7},{6,4},{7,5},{8,10},{9,11},{10,... | collective-permute-start | bytes 589832 | tf_op jit(solution)/shard_map/ppermute | solution.py:34
  48.3 0.0 collective-permute-done.3.refs_3_
  48.3 3.2 %collective-permute-start.6 = (bf16[768,128]{1,0:T(8,128)(2,1)S(1)}, bf16[768,128]{1,0:T(8,128)(2,1)S(1)}, u32[]{:S(2)}, u32[]{:S(2)}) collective-permute-start(bf16[768,128]{1,0:T(8,128)(2,1)S(1)} %bitcast.34), channel_id=1, source_target_pairs={{0,1},{1,0},{2,3},{3,2},{4,5},{5,4},{6,7},{7,6},{8,9},{9,8},{10,11... | collective-permute-start | bytes 589832 | tf_op jit(solution)/shard_map/ppermute | solution.py:34
  51.5 0.0 collective-permute-done.2.refs_2_
  51.5 0.8 collective-permute-start.15
  52.3 3.4 %collective-permute-done.8.refs_7_ = bf16[768,128]{1,0:T(8,128)(2,1)S(1)} collective-permute-done((bf16[768,128]{1,0:T(8,128)(2,1)S(1)}, bf16[768,128]{1,0:T(8,128)(2,1)S(1)}, u32[]{:S(2)}, u32[]{:S(2)}) %collective-permute-start.8) | collective-permute-done | bytes 196640 | tf_op jit(solution)/shard_map/ppermute | solution.py:34
  55.7 0.0 collective-permute-done.7.refs_6_
  55.7 2.5 %collective-permute-done.6.refs_5_ = bf16[768,128]{1,0:T(8,128)(2,1)S(1)} collective-permute-done((bf16[768,128]{1,0:T(8,128)(2,1)S(1)}, bf16[768,128]{1,0:T(8,128)(2,1)S(1)}, u32[]{:S(2)}, u32[]{:S(2)}) %collective-permute-start.6) | collective-permute-done | bytes 196640 | tf_op jit(solution)/shard_map/ppermute | solution.py:34
  58.2 0.0 copy-start.1
  58.2 0.0 copy-start.5
  58.3 2.1 %collective-permute-start.13 = (bf16[2048,128]{1,0:T(8,128)(2,1)S(1)}, bf16[2048,128]{1,0:T(8,128)(2,1)S(1)}, u32[]{:S(2)}, u32[]{:S(2)}) collective-permute-start(bf16[2048,128]{1,0:T(8,128)(2,1)S(1)} %bitcast.23), channel_id=1, source_target_pairs={{0,16},{1,17},{2,18},{3,19},{4,20},{5,21},{6,22},{7,23},{8,24},{9,... | collective-permute-start | bytes 1572872 | tf_op jit(solution)/shard_map/ppermute | solution.py:34
  60.3 0.5 bias.1.refs_10_
  60.9 3.7 %attention.1 = (bf16[512,128]{1,0:T(8,128)(2,1)S(1)}, bf16[8,512,128]{2,1,0:T(8,128)(2,1)S(1)}) custom-call(bf16[768,128]{1,0:T(8,128)(2,1)S(1)} %bitcast.29, bf16[768,128]{1,0:T(8,128)(2,1)S(1)} %collective-permute-done.1.refs_1_, bf16[768,128]{1,0:T(8,128)(2,1)S(1)} %collective-permute-done.2.refs_2_, bf16[768,128]{1,0:T(8,128)(2,1)S(1)} %collective-permute-done.3.refs_3_, ...), custom_call_target="tpu_custom_call" | custom-call | flops 600000000 | bytes 3000000 | tf_op jit(solution)/shard_map/attention/pallas_call | solution.py:298
  64.6 7.0 %collective-permute-start.12 = (bf16[512,128]{1,0:T(8,128)(2,1)S(1)}, bf16[512,128]{1,0:T(8,128)(2,1)S(1)}, u32[]{:S(2)}, u32[]{:S(2)}) collective-permute-start(bf16[512,128]{1,0:T(8,128)(2,1)S(1)} %get-tuple-element.11.refs_0_), channel_id=1, source_target_pairs={{0,4},{1,5},{2,6},{3,7},{4,0},{5,1},{6,2},{7,3},{8,12},{9,13},{10,... | collective-permute-start | bytes 393224 | tf_op jit(solution)/shard_map/ppermute | solution.py:34
  71.7 3.0 %collective-permute-start.11 = (bf16[512,128]{1,0:T(8,128)(2,1)S(1)}, bf16[512,128]{1,0:T(8,128)(2,1)S(1)}, u32[]{:S(2)}, u32[]{:S(2)}) collective-permute-start(bf16[512,128]{1,0:T(8,128)(2,1)S(1)} %get-tuple-element.11.refs_0_), channel_id=1, source_target_pairs={{0,3},{1,2},{2,1},{3,0},{4,7},{5,6},{6,5},{7,4},{8,11},{9,10},{10,... | collective-permute-start | bytes 393224 | tf_op jit(solution)/shard_map/ppermute | solution.py:34
  74.7 4.2 %collective-permute-start.10 = (bf16[512,128]{1,0:T(8,128)(2,1)S(1)}, bf16[512,128]{1,0:T(8,128)(2,1)S(1)}, u32[]{:S(2)}, u32[]{:S(2)}) collective-permute-start(bf16[512,128]{1,0:T(8,128)(2,1)S(1)} %get-tuple-element.11.refs_0_), channel_id=1, source_target_pairs={{0,2},{1,3},{2,0},{3,1},{4,6},{5,7},{6,4},{7,5},{8,10},{9,11},{10,... | collective-permute-start | bytes 393224 | tf_op jit(solution)/shard_map/ppermute | solution.py:34
  78.9 2.7 %collective-permute-start.9 = (bf16[512,128]{1,0:T(8,128)(2,1)S(1)}, bf16[512,128]{1,0:T(8,128)(2,1)S(1)}, u32[]{:S(2)}, u32[]{:S(2)}) collective-permute-start(bf16[512,128]{1,0:T(8,128)(2,1)S(1)} %get-tuple-element.11.refs_0_), channel_id=1, source_target_pairs={{0,1},{1,0},{2,3},{3,2},{4,5},{5,4},{6,7},{7,6},{8,9},{9,8},{10,11... | collective-permute-start | bytes 393224 | tf_op jit(solution)/shard_map/ppermute | solution.py:34
  81.5 0.1 join.9
  81.6 3.4 %collective-permute-done.12.refs_0_ = bf16[512,128]{1,0:T(8,128)(2,1)S(1)} collective-permute-done((bf16[512,128]{1,0:T(8,128)(2,1)S(1)}, bf16[512,128]{1,0:T(8,128)(2,1)S(1)}, u32[]{:S(2)}, u32[]{:S(2)}) %collective-permute-start.12) | collective-permute-done | bytes 131104 | tf_op jit(solution)/shard_map/ppermute | solution.py:34
  85.0 2.0 %collective-permute-start.14 = (bf16[4096,128]{1,0:T(8,128)(2,1)S(1)}, bf16[4096,128]{1,0:T(8,128)(2,1)S(1)}, u32[]{:S(2)}, u32[]{:S(2)}) collective-permute-start(bf16[4096,128]{1,0:T(8,128)(2,1)S(1)} %bitcast.19), channel_id=1, source_target_pairs={{0,8},{1,9},{2,10},{3,11},{4,12},{5,13},{6,14},{7,15},{8,0},{9,1},... | collective-permute-start | bytes 3145736 | tf_op jit(solution)/shard_map/ppermute | solution.py:34
  87.0 0.0 collective-permute-done.11.refs_3_
  87.1 0.0 collective-permute-done.10.refs_2_
  87.1 0.1 join.7
  87.2 12.7 %all_to_all.5.refs_4_ = bf16[4,512,128]{2,1,0:T(8,128)(2,1)S(1)} all-to-all(bf16[4,512,128]{2,1,0:T(8,128)(2,1)S(1)} %join.7), channel_id=1, replica_groups={{0,1,2,3},{4,5,6,7},{8,9,10,11},{12,13,14,15},{16,17,18,19},{20,21,22,2..., dimensions={0} | all-to-all | bytes 1048576 | tf_op jit(solution)/shard_map/all_to_all | solution.py:315
  99.9 0.0 collective-permute-done.14
  99.9 0.0 collective-permute-done.15
  99.9 2.4 %merge.1 = bf16[256,128]{1,0:T(8,128)(2,1)S(1)} custom-call(bf16[512,128]{1,0:T(8,128)(2,1)S(1)} %get-tuple-element.11.refs_0_, bf16[512,128]{1,0:T(8,128)(2,1)S(1)} %collective-permute-done.9.refs_1_, bf16[512,128]{1,0:T(8,128)(2,1)S(1)} %collective-permute-done.10.refs_2_, bf16[512,128]{1,0:T(8,128)(2,1)S(1)} %collective-permute-done.11.refs_3_, ...), custom_call_target="tpu_custom_call" | custom-call | flops 1400000000 | bytes 7000000 | tf_op jit(solution)/shard_map/merge/pallas_call | solution.py:320
  102.3 1.9 %collective-permute-start.16 = (bf16[128,128]{1,0:T(8,128)(2,1)S(1)}, bf16[128,128]{1,0:T(8,128)(2,1)S(1)}, u32[]{:S(2)}, u32[]{:S(2)}) collective-permute-start(bf16[128,128]{1,0:T(8,128)(2,1)S(1)} %get-tuple-element.13), channel_id=1, source_target_pairs={{0,8},{1,9},{2,10},{3,11},{4,12},{5,13},{6,14},{7,15},{8,16},{9,17... | collective-permute-start | bytes 98312 | tf_op jit(solution)/shard_map/ppermute | solution.py:58
  104.2 6.6 %collective-permute-done.16 = bf16[128,128]{1,0:T(8,128)(2,1)S(1)} collective-permute-done((bf16[128,128]{1,0:T(8,128)(2,1)S(1)}, bf16[128,128]{1,0:T(8,128)(2,1)S(1)}, u32[]{:S(2)}, u32[]{:S(2)}) %collective-permute-start.16) | collective-permute-done | bytes 32800 | tf_op jit(solution)/shard_map/ppermute | solution.py:58
  110.8 0.6 pad_maximum_fusion
  (19 shorter events, 0.1 us)
Async XLA Ops:
  0.0 0.9 copy-start.6
  1.2 20.4 %collective-permute-start = (bf16[256,128]{1,0:T(8,128)(2,1)S(1)}, bf16[256,128]{1,0:T(8,128)(2,1)S(1)}, u32[]{:S(2)}, u32[]{:S(2)}) collective-permute-start(bf16[256,128]{1,0:T(8,128)(2,1)S(1)} %get-tuple-element.10), channel_id=1, source_target_pairs={{0,508},{1,509},{2,510},{3,511},{4,504},{5,505},{6,506},{7,507},{8... | collective-permute-start | bytes 196616 | tf_op jit(solution)/shard_map/ppermute | solution.py:51
  14.2 1.0 copy-start.2
  15.2 26.3 %collective-permute-start.4 = (bf16[512,128]{1,0:T(8,128)(2,1)S(1)}, bf16[512,128]{1,0:T(8,128)(2,1)S(1)}, u32[]{:S(2)}, u32[]{:S(2)}) collective-permute-start(bf16[512,128]{1,0:T(8,128)(2,1)S(1)} %piece.1.refs_0_.refs_2_), channel_id=1, source_target_pairs={{0,4},{1,5},{2,6},{3,7},{4,0},{5,1},{6,2},{7,3},{8,12},{9,13},{10,... | collective-permute-start | bytes 393224 | tf_op jit(solution)/shard_map/ppermute | solution.py:34
  21.5 19.9 %collective-permute-start.5 = (bf16[256,128]{1,0:T(8,128)(2,1)S(1)}, bf16[256,128]{1,0:T(8,128)(2,1)S(1)}, u32[]{:S(2)}, u32[]{:S(2)}) collective-permute-start(bf16[256,128]{1,0:T(8,128)(2,1)S(1)} %collective-permute-done.refs_1_), channel_id=1, source_target_pairs={{0,4},{1,5},{2,6},{3,7},{4,0},{5,1},{6,2},{7,3},{8,12},{9,13},{10,... | collective-permute-start | bytes 196616 | tf_op jit(solution)/shard_map/ppermute | solution.py:34
  29.8 21.7 %copy-start = (bf16[4096,256]{1,0:T(8,128)(2,1)S(1)}, bf16[4096,256]{1,0:T(8,128)(2,1)}, u32[]{:S(2)}) copy-start(bf16[4096,256]{1,0:T(8,128)(2,1)} %param.16) | copy-start | bytes 6291460
  29.8 18.5 %collective-permute-start.3 = (bf16[768,128]{1,0:T(8,128)(2,1)S(1)}, bf16[768,128]{1,0:T(8,128)(2,1)S(1)}, u32[]{:S(2)}, u32[]{:S(2)}) collective-permute-start(bf16[768,128]{1,0:T(8,128)(2,1)S(1)} %bitcast.25), channel_id=1, source_target_pairs={{0,3},{1,2},{2,1},{3,0},{4,7},{5,6},{6,5},{7,4},{8,11},{9,10},{10,... | collective-permute-start | bytes 589832 | tf_op jit(solution)/shard_map/ppermute | solution.py:34
  32.1 19.4 %collective-permute-start.2 = (bf16[768,128]{1,0:T(8,128)(2,1)S(1)}, bf16[768,128]{1,0:T(8,128)(2,1)S(1)}, u32[]{:S(2)}, u32[]{:S(2)}) collective-permute-start(bf16[768,128]{1,0:T(8,128)(2,1)S(1)} %bitcast.26), channel_id=1, source_target_pairs={{0,2},{1,3},{2,0},{3,1},{4,6},{5,7},{6,4},{7,5},{8,10},{9,11},{10,... | collective-permute-start | bytes 589832 | tf_op jit(solution)/shard_map/ppermute | solution.py:34
  36.6 15.8 %collective-permute-start.1 = (bf16[768,128]{1,0:T(8,128)(2,1)S(1)}, bf16[768,128]{1,0:T(8,128)(2,1)S(1)}, u32[]{:S(2)}, u32[]{:S(2)}) collective-permute-start(bf16[768,128]{1,0:T(8,128)(2,1)S(1)} %bitcast.27), channel_id=1, source_target_pairs={{0,1},{1,0},{2,3},{3,2},{4,5},{5,4},{6,7},{7,6},{8,9},{9,8},{10,11... | collective-permute-start | bytes 589832 | tf_op jit(solution)/shard_map/ppermute | solution.py:34
  41.5 18.8 %copy-start.7 = (f32[2,128,128]{2,1,0:T(8,128)S(1)}, f32[2,128,128]{2,1,0:T(8,128)}, u32[]{:S(2)}) copy-start(f32[2,128,128]{2,1,0:T(8,128)} %bias_ref.1) | copy-start | bytes 393220
  41.5 18.8 %copy-start.8 = (f32[128,128]{1,0:T(8,128)S(1)}, f32[128,128]{1,0:T(8,128)}, u32[]{:S(2)}) copy-start(f32[128,128]{1,0:T(8,128)} %constant.7.clone.turned_ref) | copy-start | bytes 196612
  41.5 18.8 %copy-start.9 = (f32[128,128]{1,0:T(8,128)S(1)}, f32[128,128]{1,0:T(8,128)}, u32[]{:S(2)}) copy-start(f32[128,128]{1,0:T(8,128)} %constant.6.clone.hot_ref) | copy-start | bytes 196612
  41.5 14.2 %collective-permute-start.8 = (bf16[768,128]{1,0:T(8,128)(2,1)S(1)}, bf16[768,128]{1,0:T(8,128)(2,1)S(1)}, u32[]{:S(2)}, u32[]{:S(2)}) collective-permute-start(bf16[768,128]{1,0:T(8,128)(2,1)S(1)} %bitcast.32), channel_id=1, source_target_pairs={{0,3},{1,2},{2,1},{3,0},{4,7},{5,6},{6,5},{7,4},{8,11},{9,10},{10,... | collective-permute-start | bytes 589832 | tf_op jit(solution)/shard_map/ppermute | solution.py:34
  43.6 12.1 %collective-permute-start.7 = (bf16[768,128]{1,0:T(8,128)(2,1)S(1)}, bf16[768,128]{1,0:T(8,128)(2,1)S(1)}, u32[]{:S(2)}, u32[]{:S(2)}) collective-permute-start(bf16[768,128]{1,0:T(8,128)(2,1)S(1)} %bitcast.33), channel_id=1, source_target_pairs={{0,2},{1,3},{2,0},{3,1},{4,6},{5,7},{6,4},{7,5},{8,10},{9,11},{10,... | collective-permute-start | bytes 589832 | tf_op jit(solution)/shard_map/ppermute | solution.py:34
  48.3 9.9 %collective-permute-start.6 = (bf16[768,128]{1,0:T(8,128)(2,1)S(1)}, bf16[768,128]{1,0:T(8,128)(2,1)S(1)}, u32[]{:S(2)}, u32[]{:S(2)}) collective-permute-start(bf16[768,128]{1,0:T(8,128)(2,1)S(1)} %bitcast.34), channel_id=1, source_target_pairs={{0,1},{1,0},{2,3},{3,2},{4,5},{5,4},{6,7},{7,6},{8,9},{9,8},{10,11... | collective-permute-start | bytes 589832 | tf_op jit(solution)/shard_map/ppermute | solution.py:34
  51.5 48.3 %collective-permute-start.15 = (bf16[4096,256]{1,0:T(8,128)(2,1)S(1)}, bf16[4096,256]{1,0:T(8,128)(2,1)S(1)}, u32[]{:S(2)}, u32[]{:S(2)}) collective-permute-start(bf16[4096,256]{1,0:T(8,128)(2,1)S(1)} %copy-done), channel_id=1, source_target_pairs={{60,504},{61,505},{62,506},{63,507},{56,508},{57,509},{58,510},{59... | collective-permute-start | bytes 6291464 | tf_op jit(solution)/shard_map/ppermute | solution.py:61
  58.2 2.7 %copy-start.1 = (bf16[1024,3,128]{2,0,1:T(8,128)(2,1)S(1)}, bf16[1024,3,128]{2,0,1:T(8,128)(2,1)}, u32[]{:S(2)}) copy-start(bf16[1024,3,128]{2,0,1:T(8,128)(2,1)} %param.12) | copy-start | bytes 2359300
  58.2 2.7 %copy-start.5 = (f32[1024]{0:T(1024)S(1)}, f32[1024]{0:T(1024)}, u32[]{:S(2)}) copy-start(f32[1024]{0:T(1024)} %param.11) | copy-start | bytes 12292
  58.3 20.6 %collective-permute-start.13 = (bf16[2048,128]{1,0:T(8,128)(2,1)S(1)}, bf16[2048,128]{1,0:T(8,128)(2,1)S(1)}, u32[]{:S(2)}, u32[]{:S(2)}) collective-permute-start(bf16[2048,128]{1,0:T(8,128)(2,1)S(1)} %bitcast.23), channel_id=1, source_target_pairs={{0,16},{1,17},{2,18},{3,19},{4,20},{5,21},{6,22},{7,23},{8,24},{9,... | collective-permute-start | bytes 1572872 | tf_op jit(solution)/shard_map/ppermute | solution.py:34
  64.6 20.3 %collective-permute-start.12 = (bf16[512,128]{1,0:T(8,128)(2,1)S(1)}, bf16[512,128]{1,0:T(8,128)(2,1)S(1)}, u32[]{:S(2)}, u32[]{:S(2)}) collective-permute-start(bf16[512,128]{1,0:T(8,128)(2,1)S(1)} %get-tuple-element.11.refs_0_), channel_id=1, source_target_pairs={{0,4},{1,5},{2,6},{3,7},{4,0},{5,1},{6,2},{7,3},{8,12},{9,13},{10,... | collective-permute-start | bytes 393224 | tf_op jit(solution)/shard_map/ppermute | solution.py:34
  71.7 15.4 %collective-permute-start.11 = (bf16[512,128]{1,0:T(8,128)(2,1)S(1)}, bf16[512,128]{1,0:T(8,128)(2,1)S(1)}, u32[]{:S(2)}, u32[]{:S(2)}) collective-permute-start(bf16[512,128]{1,0:T(8,128)(2,1)S(1)} %get-tuple-element.11.refs_0_), channel_id=1, source_target_pairs={{0,3},{1,2},{2,1},{3,0},{4,7},{5,6},{6,5},{7,4},{8,11},{9,10},{10,... | collective-permute-start | bytes 393224 | tf_op jit(solution)/shard_map/ppermute | solution.py:34
  74.7 12.4 %collective-permute-start.10 = (bf16[512,128]{1,0:T(8,128)(2,1)S(1)}, bf16[512,128]{1,0:T(8,128)(2,1)S(1)}, u32[]{:S(2)}, u32[]{:S(2)}) collective-permute-start(bf16[512,128]{1,0:T(8,128)(2,1)S(1)} %get-tuple-element.11.refs_0_), channel_id=1, source_target_pairs={{0,2},{1,3},{2,0},{3,1},{4,6},{5,7},{6,4},{7,5},{8,10},{9,11},{10,... | collective-permute-start | bytes 393224 | tf_op jit(solution)/shard_map/ppermute | solution.py:34
  78.9 8.2 %collective-permute-start.9 = (bf16[512,128]{1,0:T(8,128)(2,1)S(1)}, bf16[512,128]{1,0:T(8,128)(2,1)S(1)}, u32[]{:S(2)}, u32[]{:S(2)}) collective-permute-start(bf16[512,128]{1,0:T(8,128)(2,1)S(1)} %get-tuple-element.11.refs_0_), channel_id=1, source_target_pairs={{0,1},{1,0},{2,3},{3,2},{4,5},{5,4},{6,7},{7,6},{8,9},{9,8},{10,11... | collective-permute-start | bytes 393224 | tf_op jit(solution)/shard_map/ppermute | solution.py:34
  85.0 14.9 %copy-start.3 = (bf16[2,256,128]{2,1,0:T(8,128)(2,1)S(1)}, bf16[2,256,128]{2,1,0:T(8,128)(2,1)}, u32[]{:S(2)}) copy-start(bf16[2,256,128]{2,1,0:T(8,128)(2,1)} %constant.8.clone.refs_11_) | copy-start | bytes 393220
  85.0 14.9 %copy-start.4 = (f32[4096]{0:T(1024)S(1)}, f32[4096]{0:T(1024)}, u32[]{:S(2)}) copy-start(f32[4096]{0:T(1024)} %param.15) | copy-start | bytes 49156
  85.0 14.9 %collective-permute-start.14 = (bf16[4096,128]{1,0:T(8,128)(2,1)S(1)}, bf16[4096,128]{1,0:T(8,128)(2,1)S(1)}, u32[]{:S(2)}, u32[]{:S(2)}) collective-permute-start(bf16[4096,128]{1,0:T(8,128)(2,1)S(1)} %bitcast.19), channel_id=1, source_target_pairs={{0,8},{1,9},{2,10},{3,11},{4,12},{5,13},{6,14},{7,15},{8,0},{9,1},... | collective-permute-start | bytes 3145736 | tf_op jit(solution)/shard_map/ppermute | solution.py:34
  102.3 8.6 %collective-permute-start.16 = (bf16[128,128]{1,0:T(8,128)(2,1)S(1)}, bf16[128,128]{1,0:T(8,128)(2,1)S(1)}, u32[]{:S(2)}, u32[]{:S(2)}) collective-permute-start(bf16[128,128]{1,0:T(8,128)(2,1)S(1)} %get-tuple-element.13), channel_id=1, source_target_pairs={{0,8},{1,9},{2,10},{3,11},{4,12},{5,13},{6,14},{7,15},{8,16},{9,17... | collective-permute-start | bytes 98312 | tf_op jit(solution)/shard_map/ppermute | solution.py:58

commit v11 on v10

--- a/solution.py
+++ b/solution.py
@@ -160,13 +160,13 @@
     return (half * 4 + 2 * i + di) * 16 + (2 * j + dj) * 2 + (1 - level)
 
 def merged_order():
-    o = np.arange(256)
-    half, i, lon, side, level = o >> 7, (o >> 6) & 1, (o >> 2) & 15, (o >> 1) & 1, o & 1
+    o = np.arange(128)
+    i, lon, side, level = o >> 6, (o >> 2) & 15, (o >> 1) & 1, o & 1
     back = (lon - 2) % 16
-    source = half * 64 + (back >> 2) * 16 + i * 8 + (back & 3) * 2 + level
-    hot = np.zeros((2, 256, 128), np.float32)
-    hot[side, o, source] = 1
+    hot = np.zeros((2, 128, 64), np.float32)
+    hot[side, o, (back >> 2) * 16 + i * 8 + (back & 3) * 2 + level] = 1
     return jnp.asarray(hot, jnp.bfloat16)
+
 
 def dot(left, right):
     return jnp.dot(left, right, preferred_element_type=jnp.float32)
@@ -222,18 +222,21 @@
         for piece, s in enumerate(starts):
             out_ref[s : s + 16, :] = attended[piece * 16 : piece * 16 + 16, :]
 
-def merge_kernel(*refs):
+def merge_kernel(half, *refs):
     att_refs = refs[:5]
-    stream_ref, w_same_ref, w_other_ref, gain_ref, w_ref, w_turned_ref, order_ref, out_ref, updated_ref = refs[5:]
+    stream_ref, w_same_ref, w_other_ref, gain_ref, order_ref = refs[5:10]
+    w_refs, out_ref, updated_ref = refs[10:-2], refs[-2], refs[-1]
     head_place = lax.axis_index("head")
     space = lax.axis_index("space")
     blocks = [head_place ^ k for k in range(8)]
     my_x = (space // 2) % 2
     parity = (head_place // 2 + space) % 2
+    rows = slice(half * HALF, (half + 1) * HALF)
 
     def project(odd):
         attended = jnp.concatenate(
-            [ref[...] for ref in att_refs[:4]] + [att_refs[4][head_place % 4 ^ bits] for bits in range(4)], axis=1
+            [ref[rows, :] for ref in att_refs[:4]] + [att_refs[4][head_place % 4 ^ bits, rows, :] for bits in range(4)],
+            axis=1,
         )
         for k in range(0, 8, 2):
             w_from = w_same_ref if (k // 2 + odd) % 2 == 0 else w_other_ref
@@ -242,21 +245,18 @@
                 jnp.concatenate([w_from[x_rel, row, block % 2] for row in range(8)], axis=0)
                 for block in (blocks[k], blocks[k + 1])
             ]
-            w_block = jnp.concatenate(w_blocks, axis=1)
-            stream = jnp.concatenate([stream_ref[n] for n in (k, k + 1)], axis=1)
-            value = stream.astype(jnp.float32) + dot(attended, w_block)
+            stream = jnp.concatenate([stream_ref[n, rows, :] for n in (k, k + 1)], axis=1)
+            value = stream.astype(jnp.float32) + dot(attended, jnp.concatenate(w_blocks, axis=1))
             updated_ref[:, k * BLOCK : (k + 2) * BLOCK] = value.astype(jnp.bfloat16)
 
     for odd in range(2):
         pl.when(parity == odd)(lambda odd=odd: project(odd))
 
     def quad(k):
-        return jnp.concatenate(
-            [updated_ref[half * HALF + k * 64 : half * HALF + k * 64 + 64, :] for half in range(2)], axis=0
-        ).astype(jnp.float32)
-
-    total = jnp.zeros((128, 1), jnp.float32)
-    squares = jnp.zeros((128, 1), jnp.float32)
+        return updated_ref[k * 64 : k * 64 + 64, :].astype(jnp.float32)
+
+    total = jnp.zeros((64, 1), jnp.float32)
+    squares = jnp.zeros((64, 1), jnp.float32)
     for k in range(4):
         value = quad(k)
         total += jnp.sum(value, -1, keepdims=True)
@@ -264,23 +264,22 @@
     mean = total * (1.0 / (4 * D))
     scale = lax.rsqrt(squares * (1.0 / (4 * D)) - mean * mean + EPS)
 
-    def merge(lower_w_ref):
-        merged = [jnp.zeros((128 if lower_w_ref is w_ref else 64, 256), jnp.float32)] * (1 if lower_w_ref is w_ref else 2)
+    def merge(w_ref):
+        merged = jnp.zeros((64, 256), jnp.float32)
         for k in range(4):
-            value = (quad(k) - mean) * scale
             gain = jnp.concatenate([gain_ref[k * 8 + block] for block in blocks], axis=1)
-            normed = (value * gain).astype(jnp.bfloat16)
-            rows = len(normed) // len(merged)
-            for n, ref in enumerate((w_ref, lower_w_ref)[: len(merged)]):
-                weights = jnp.concatenate([ref[k * 8 + block] for block in blocks], axis=0)
-                merged[n] = merged[n] + dot(normed[n * rows : (n + 1) * rows], weights)
-        merged = jnp.concatenate(merged, axis=0)
+            weights = jnp.concatenate([w_ref[k * 8 + block] for block in blocks], axis=0)
+            merged += dot(((quad(k) - mean) * scale * gain).astype(jnp.bfloat16), weights)
         merged = merged.astype(jnp.bfloat16)
         sides = [dot(order_ref[side], merged[:, side * BLOCK : (side + 1) * BLOCK]) for side in range(2)]
         out_ref[...] = (sides[0] + sides[1]).astype(jnp.bfloat16)
 
-    pl.when(space != 63)(lambda: merge(w_ref))
-    pl.when(space == 63)(lambda: merge(w_turned_ref))
+    if len(w_refs) == 1:
+        merge(w_refs[0])
+    else:
+        pl.when(space != 63)(lambda: merge(w_refs[0]))
+        pl.when(space == 63)(lambda: merge(w_refs[1]))
+
 
 def on_device(fields, ln_gain, w_qkv, attn_bias, w_out, merge_gain, w_merge):
     first, behind = ordered(fields.reshape(TOKENS, BLOCK))
@@ -309,36 +308,43 @@
         name="attention",
     )(*around, ln_gain.reshape(8, 1, BLOCK), w_qkv.transpose(1, 0, 2).reshape(3, 8, BLOCK, BLOCK), bias)
 
+    attended_across = across(jnp.concatenate([attended, attended[:16]], axis=0), 4)
     attended_around = along_y(attended)
-    attended_partner = joined([(across(attended, 4), 0, TOKENS)], 4, CLAIMED, attended_around[1:])
+    attended_partner = joined([(attended_across, 0, TOKENS)], 4, CLAIMED, attended_around[1:])
     attended_around.append(
         lax.all_to_all(attended_partner, "head", 0, 0, axis_index_groups=[[0, 1, 2, 3], [4, 5, 6, 7]])
     )
     w_quarter = joined([(place, TOKENS, TOKENS + 256) for place in around])
     w_core = joined([(w_quarter, 0, 2048), (across_x(w_quarter, 1), 0, 2048)])
     w_shape = (2, 8, 2, BLOCK, BLOCK)
-    merged = pl.pallas_call(
-        merge_kernel,
-        out_shape=jax.ShapeDtypeStruct((256, BLOCK), jnp.bfloat16),
-        in_specs=in_vmem(12),
-        out_specs=vmem,
-        scratch_shapes=[pltpu.VMEM((TOKENS, D), jnp.bfloat16)],
-        compiler_params=pltpu.CompilerParams(vmem_limit_bytes=16 * 2**20),
-        cost_estimate=pl.CostEstimate(flops=1_400_000_000, bytes_accessed=7_000_000, transcendentals=0),
-        name="merge",
-    )(
-        *attended_around,
-        stream,
-        w_core.reshape(w_shape),
-        other_core(w_core).reshape(w_shape),
-        merge_gain.reshape(32, 1, BLOCK),
-        w_merge.reshape(32, BLOCK, 256),
-        other_columns(w_merge).reshape(32, BLOCK, 256),
-        merged_order(),
-    )
-    lower = lower_rows(merged[128:])
-    grid = jnp.concatenate([lower, merged[:128]], axis=0).reshape(4, 16, 2, 2, BLOCK)
+    w_other = other_core(w_core).reshape(w_shape)
+    columns = w_merge.reshape(32, BLOCK, 256)
+    turned_columns = other_columns(w_merge).reshape(32, BLOCK, 256)
+
+    def merged(half, weights):
+        return pl.pallas_call(
+            functools.partial(merge_kernel, half),
+            out_shape=jax.ShapeDtypeStruct((128, BLOCK), jnp.bfloat16),
+            in_specs=in_vmem(10 + len(weights)),
+            out_specs=vmem,
+            scratch_shapes=[pltpu.VMEM((HALF, D), jnp.bfloat16)],
+            compiler_params=pltpu.CompilerParams(vmem_limit_bytes=16 * 2**20),
+            cost_estimate=pl.CostEstimate(flops=700_000_000, bytes_accessed=5_000_000, transcendentals=0),
+            name="merge",
+        )(
+            *attended_around,
+            stream,
+            w_core.reshape(w_shape),
+            w_other,
+            merge_gain.reshape(32, 1, BLOCK),
+            merged_order(),
+            *weights,
+        )
+
+    lower = lower_rows(merged(1, [columns, turned_columns]))
+    grid = jnp.concatenate([lower, merged(0, [columns])], axis=0).reshape(4, 16, 2, 2, BLOCK)
     return grid.transpose(0, 1, 3, 2, 4).reshape(4, 16, 2, 256)
+
 
 def solution(mesh):
     placed = (

time: 113 us -> 116 us (1.027)
  waiting for transfers between devices: 17.6 us -> 23.8 us
  starting transfers between devices: 71.1 us -> 68.9 us
  blocking collectives: 12.7 us -> 11.1 us
    ppermute x1, waiting for transfers between devices: 0.01 us -> 11.1 us  [following_rows(): return lax.ppermute(value, BOTH, pairs)]
    ppermute x1, starting transfers between devices: 13 us -> 3.37 us  [following_rows(): return lax.ppermute(value, BOTH, pairs)]
    ppermute x14, starting transfers between devices: 55.4 us -> 62.8 us  [moved(): return lax.ppermute(value, BOTH, pairs)]
    ppermute x14, waiting for transfers between devices: 10.9 us -> 7.71 us  [moved(): return lax.ppermute(value, BOTH, pairs)]
    ppermute x1, waiting for transfers between devices: 6.63 us -> 5.02 us  [lower_rows(): return lax.ppermute(value, BOTH, pairs)]
    all_to_all x1, blocking collectives: 12.7 us -> 11.1 us  [on_device(): lax.all_to_all(attended_partner, 'head', 0, 0, axis_index_groups=[[0, 1,...]
    pallas_call x1 -> x2, Pallas kernels: 2.4 us -> 3.25 us  [merged(): pl.pallas_call(functools.partial(merge_kernel, half), out_shape=jax.Shape...]
  transfers between devices with their start and end apart: 17 -> 17, of which waited for: 5 -> 6; matrix products, arithmetic and copies ran while one was open for 0% -> 0% of each run, Pallas kernels for 4% -> 5%
where the time goes in v11:
time: 116 us; the launch traced here: 115 us
  starting transfers between devices  68.9 us (59%)
  waiting for transfers between devices  23.8 us (21%)
  blocking collectives  11.1 us (10%)
  Pallas kernels  7.98 us (7%)
  local copies, waits for them, and re-layouts  1.91 us (2%)
    ppermute x14, starting transfers between devices, moved(): return lax.ppermute(value, BOTH, pairs)  62.8 us
    all_to_all x1, blocking collectives, on_device(): lax.all_to_all(attended_partner, 'head', 0, 0, axis_index_groups=[[0, 1,...  11.1 us
    ppermute x1, waiting for transfers between devices, following_rows(): return lax.ppermute(value, BOTH, pairs)  11.1 us
    ppermute x14, waiting for transfers between devices, moved(): return lax.ppermute(value, BOTH, pairs)  7.71 us
    ppermute x1, waiting for transfers between devices, lower_rows(): return lax.ppermute(value, BOTH, pairs)  5.02 us
    pallas_call x1, Pallas kernels, on_device(): pl.pallas_call(attention_kernel, out_shape=(jax.ShapeDtypeStruct((TOKENS,...  3.73 us
    ppermute x1, starting transfers between devices, following_rows(): return lax.ppermute(value, BOTH, pairs)  3.37 us
    pallas_call x2, Pallas kernels, merged(): pl.pallas_call(functools.partial(merge_kernel, half), out_shape=jax.Shape...  3.25 us
  transfers between devices with their start and end apart: 17, of which 6 were waited for; matrix products, arithmetic and copies ran while one was open for 0% of the time, Pallas kernels for 5%

profile of v11, /device:TPU:24, one launch (start us, length us, event | category | flops | bytes accessed | tf_op | source)
XLA Modules:
  0.0 114.7 jit_solution(10971994416437206967)
XLA Ops:
  0.0 0.9 copy-done.6
  0.9 0.2 order.1
  1.2 0.0 copy-start.3
  1.2 0.9 copy-done.3
  2.1 15.7 %collective-permute-start.4 = (bf16[512,128]{1,0:T(8,128)(2,1)S(1)}, bf16[512,128]{1,0:T(8,128)(2,1)S(1)}, u32[]{:S(2)}, u32[]{:S(2)}) collective-permute-start(bf16[512,128]{1,0:T(8,128)(2,1)S(1)} %piece.1.refs_0_.refs_2_), channel_id=1, source_target_pairs={{0,4},{1,5},{2,6},{3,7},{4,0},{5,1},{6,2},{7,3},{8,12},{9,13},{10,... | collective-permute-start | bytes 393224 | tf_op jit(solution)/shard_map/ppermute | solution.py:34
  17.9 3.4 %collective-permute-start = (bf16[256,128]{1,0:T(8,128)(2,1)S(1)}, bf16[256,128]{1,0:T(8,128)(2,1)S(1)}, u32[]{:S(2)}, u32[]{:S(2)}) collective-permute-start(bf16[256,128]{1,0:T(8,128)(2,1)S(1)} %get-tuple-element.10), channel_id=1, source_target_pairs={{0,508},{1,509},{2,510},{3,511},{4,504},{5,505},{6,506},{7,507},{8... | collective-permute-start | bytes 196616 | tf_op jit(solution)/shard_map/ppermute | solution.py:51
  21.2 11.1 %collective-permute-done.refs_1_ = bf16[256,128]{1,0:T(8,128)(2,1)S(1)} collective-permute-done((bf16[256,128]{1,0:T(8,128)(2,1)S(1)}, bf16[256,128]{1,0:T(8,128)(2,1)S(1)}, u32[]{:S(2)}, u32[]{:S(2)}) %collective-permute-start) | collective-permute-done | bytes 65568 | tf_op jit(solution)/shard_map/ppermute | solution.py:51
  32.3 1.9 %collective-permute-start.5 = (bf16[256,128]{1,0:T(8,128)(2,1)S(1)}, bf16[256,128]{1,0:T(8,128)(2,1)S(1)}, u32[]{:S(2)}, u32[]{:S(2)}) collective-permute-start(bf16[256,128]{1,0:T(8,128)(2,1)S(1)} %collective-permute-done.refs_1_), channel_id=1, source_target_pairs={{0,4},{1,5},{2,6},{3,7},{4,0},{5,1},{6,2},{7,3},{8,12},{9,13},{10,... | collective-permute-start | bytes 196616 | tf_op jit(solution)/shard_map/ppermute | solution.py:34
  34.3 0.0 copy-start
  34.3 2.8 %collective-permute-start.1 = (bf16[768,128]{1,0:T(8,128)(2,1)S(1)}, bf16[768,128]{1,0:T(8,128)(2,1)S(1)}, u32[]{:S(2)}, u32[]{:S(2)}) collective-permute-start(bf16[768,128]{1,0:T(8,128)(2,1)S(1)} %bitcast.29), channel_id=1, source_target_pairs={{0,1},{1,0},{2,3},{3,2},{4,5},{5,4},{6,7},{7,6},{8,9},{9,8},{10,11... | collective-permute-start | bytes 589832 | tf_op jit(solution)/shard_map/ppermute | solution.py:34
  37.1 2.8 %collective-permute-start.2 = (bf16[768,128]{1,0:T(8,128)(2,1)S(1)}, bf16[768,128]{1,0:T(8,128)(2,1)S(1)}, u32[]{:S(2)}, u32[]{:S(2)}) collective-permute-start(bf16[768,128]{1,0:T(8,128)(2,1)S(1)} %bitcast.30), channel_id=1, source_target_pairs={{0,2},{1,3},{2,0},{3,1},{4,6},{5,7},{6,4},{7,5},{8,10},{9,11},{10,... | collective-permute-start | bytes 589832 | tf_op jit(solution)/shard_map/ppermute | solution.py:34
  39.9 4.9 %collective-permute-start.3 = (bf16[768,128]{1,0:T(8,128)(2,1)S(1)}, bf16[768,128]{1,0:T(8,128)(2,1)S(1)}, u32[]{:S(2)}, u32[]{:S(2)}) collective-permute-start(bf16[768,128]{1,0:T(8,128)(2,1)S(1)} %bitcast.31), channel_id=1, source_target_pairs={{0,3},{1,2},{2,1},{3,0},{4,7},{5,6},{6,5},{7,4},{8,11},{9,10},{10,... | collective-permute-start | bytes 589832 | tf_op jit(solution)/shard_map/ppermute | solution.py:34
  44.9 2.3 %collective-permute-done.5.refs_1_ = bf16[256,128]{1,0:T(8,128)(2,1)S(1)} collective-permute-done((bf16[256,128]{1,0:T(8,128)(2,1)S(1)}, bf16[256,128]{1,0:T(8,128)(2,1)S(1)}, u32[]{:S(2)}, u32[]{:S(2)}) %collective-permute-start.5) | collective-permute-done | bytes 65568 | tf_op jit(solution)/shard_map/ppermute | solution.py:34
  47.2 0.0 copy-start.7
  47.2 0.0 copy-start.8
  47.2 0.0 copy-start.9
  47.2 2.8 %collective-permute-start.6 = (bf16[768,128]{1,0:T(8,128)(2,1)S(1)}, bf16[768,128]{1,0:T(8,128)(2,1)S(1)}, u32[]{:S(2)}, u32[]{:S(2)}) collective-permute-start(bf16[768,128]{1,0:T(8,128)(2,1)S(1)} %bitcast.35), channel_id=1, source_target_pairs={{0,1},{1,0},{2,3},{3,2},{4,5},{5,4},{6,7},{7,6},{8,9},{9,8},{10,11... | collective-permute-start | bytes 589832 | tf_op jit(solution)/shard_map/ppermute | solution.py:34
  50.0 2.8 %collective-permute-start.7 = (bf16[768,128]{1,0:T(8,128)(2,1)S(1)}, bf16[768,128]{1,0:T(8,128)(2,1)S(1)}, u32[]{:S(2)}, u32[]{:S(2)}) collective-permute-start(bf16[768,128]{1,0:T(8,128)(2,1)S(1)} %bitcast.36), channel_id=1, source_target_pairs={{0,2},{1,3},{2,0},{3,1},{4,6},{5,7},{6,4},{7,5},{8,10},{9,11},{10,... | collective-permute-start | bytes 589832 | tf_op jit(solution)/shard_map/ppermute | solution.py:34
  52.9 0.0 collective-permute-done.1.refs_1_
  52.9 4.9 %collective-permute-start.8 = (bf16[768,128]{1,0:T(8,128)(2,1)S(1)}, bf16[768,128]{1,0:T(8,128)(2,1)S(1)}, u32[]{:S(2)}, u32[]{:S(2)}) collective-permute-start(bf16[768,128]{1,0:T(8,128)(2,1)S(1)} %bitcast.37), channel_id=1, source_target_pairs={{0,3},{1,2},{2,1},{3,0},{4,7},{5,6},{6,5},{7,4},{8,11},{9,10},{10,... | collective-permute-start | bytes 589832 | tf_op jit(solution)/shard_map/ppermute | solution.py:34
  57.8 0.8 collective-permute-start.15
  58.7 0.0 collective-permute-done.3.refs_3_
  58.7 0.0 collective-permute-done.6.refs_5_
  58.7 0.4 collective-permute-done.7.refs_6_
  59.1 2.6 %collective-permute-done.8.refs_7_ = bf16[768,128]{1,0:T(8,128)(2,1)S(1)} collective-permute-done((bf16[768,128]{1,0:T(8,128)(2,1)S(1)}, bf16[768,128]{1,0:T(8,128)(2,1)S(1)}, u32[]{:S(2)}, u32[]{:S(2)}) %collective-permute-start.8) | collective-permute-done | bytes 196640 | tf_op jit(solution)/shard_map/ppermute | solution.py:34
  61.7 0.0 copy-start.1
  61.7 0.0 copy-start.5
  61.7 2.1 %collective-permute-start.13 = (bf16[2048,128]{1,0:T(8,128)(2,1)S(1)}, bf16[2048,128]{1,0:T(8,128)(2,1)S(1)}, u32[]{:S(2)}, u32[]{:S(2)}) collective-permute-start(bf16[2048,128]{1,0:T(8,128)(2,1)S(1)} %bitcast.27), channel_id=1, source_target_pairs={{0,16},{1,17},{2,18},{3,19},{4,20},{5,21},{6,22},{7,23},{8,24},{9,... | collective-permute-start | bytes 1572872 | tf_op jit(solution)/shard_map/ppermute | solution.py:34
  63.8 0.5 bias.1.refs_10_
  64.4 3.7 %attention.1 = (bf16[512,128]{1,0:T(8,128)(2,1)S(1)}, bf16[8,512,128]{2,1,0:T(8,128)(2,1)S(1)}) custom-call(bf16[768,128]{1,0:T(8,128)(2,1)S(1)} %bitcast.33, bf16[768,128]{1,0:T(8,128)(2,1)S(1)} %collective-permute-done.1.refs_1_, bf16[768,128]{1,0:T(8,128)(2,1)S(1)} %collective-permute-done.2.refs_2_, bf16[768,128]{1,0:T(8,128)(2,1)S(1)} %collective-permute-done.3.refs_3_, ...), custom_call_target="tpu_custom_call" | custom-call | flops 600000000 | bytes 3000000 | tf_op jit(solution)/shard_map/attention/pallas_call | solution.py:297
  68.2 10.3 %collective-permute-start.12 = (bf16[528,128]{1,0:T(8,128)(2,1)S(1)}, bf16[528,128]{1,0:T(8,128)(2,1)S(1)}, u32[]{:S(2)}, u32[]{:S(2)}) collective-permute-start(bf16[528,128]{1,0:T(8,128)(2,1)S(1)} %pad_maximum_fusion), channel_id=1, source_target_pairs={{0,4},{1,5},{2,6},{3,7},{4,0},{5,1},{6,2},{7,3},{8,12},{9,13},{10,... | collective-permute-start | bytes 405512 | tf_op jit(solution)/shard_map/ppermute | solution.py:34
  78.5 2.6 %collective-permute-start.10 = (bf16[512,128]{1,0:T(8,128)(2,1)S(1)}, bf16[512,128]{1,0:T(8,128)(2,1)S(1)}, u32[]{:S(2)}, u32[]{:S(2)}) collective-permute-start(bf16[512,128]{1,0:T(8,128)(2,1)S(1)} %get-tuple-element.11.refs_0_), channel_id=1, source_target_pairs={{0,2},{1,3},{2,0},{3,1},{4,6},{5,7},{6,4},{7,5},{8,10},{9,11},{10,... | collective-permute-start | bytes 393224 | tf_op jit(solution)/shard_map/ppermute | solution.py:34
  81.1 4.8 %collective-permute-start.11 = (bf16[512,128]{1,0:T(8,128)(2,1)S(1)}, bf16[512,128]{1,0:T(8,128)(2,1)S(1)}, u32[]{:S(2)}, u32[]{:S(2)}) collective-permute-start(bf16[512,128]{1,0:T(8,128)(2,1)S(1)} %get-tuple-element.11.refs_0_), channel_id=1, source_target_pairs={{0,3},{1,2},{2,1},{3,0},{4,7},{5,6},{6,5},{7,4},{8,11},{9,10},{10,... | collective-permute-start | bytes 393224 | tf_op jit(solution)/shard_map/ppermute | solution.py:34
  85.8 2.3 %collective-permute-start.9 = (bf16[512,128]{1,0:T(8,128)(2,1)S(1)}, bf16[512,128]{1,0:T(8,128)(2,1)S(1)}, u32[]{:S(2)}, u32[]{:S(2)}) collective-permute-start(bf16[512,128]{1,0:T(8,128)(2,1)S(1)} %get-tuple-element.11.refs_0_), channel_id=1, source_target_pairs={{0,1},{1,0},{2,3},{3,2},{4,5},{5,4},{6,7},{7,6},{8,9},{9,8},{10,11... | collective-permute-start | bytes 393224 | tf_op jit(solution)/shard_map/ppermute | solution.py:34
  88.1 0.1 join.9
  88.2 0.0 collective-permute-done.10.refs_2_
  88.2 0.0 copy-start.2
  88.2 0.0 copy-start.4
  88.3 2.1 %collective-permute-start.14 = (bf16[4096,128]{1,0:T(8,128)(2,1)S(1)}, bf16[4096,128]{1,0:T(8,128)(2,1)S(1)}, u32[]{:S(2)}, u32[]{:S(2)}) collective-permute-start(bf16[4096,128]{1,0:T(8,128)(2,1)S(1)} %bitcast.19), channel_id=1, source_target_pairs={{0,8},{1,9},{2,10},{3,11},{4,12},{5,13},{6,14},{7,15},{8,0},{9,1},... | collective-permute-start | bytes 3145736 | tf_op jit(solution)/shard_map/ppermute | solution.py:34
  90.3 0.0 collective-permute-done.11.refs_3_
  90.3 2.4 %collective-permute-done.9.refs_1_ = bf16[512,128]{1,0:T(8,128)(2,1)S(1)} collective-permute-done((bf16[512,128]{1,0:T(8,128)(2,1)S(1)}, bf16[512,128]{1,0:T(8,128)(2,1)S(1)}, u32[]{:S(2)}, u32[]{:S(2)}) %collective-permute-start.9) | collective-permute-done | bytes 131104 | tf_op jit(solution)/shard_map/ppermute | solution.py:34
  92.7 0.1 join.7
  92.8 11.1 %all_to_all.5.refs_4_ = bf16[4,512,128]{2,1,0:T(8,128)(2,1)S(1)} all-to-all(bf16[4,512,128]{2,1,0:T(8,128)(2,1)S(1)} %join.7), channel_id=1, replica_groups={{0,1,2,3},{4,5,6,7},{8,9,10,11},{12,13,14,15},{16,17,18,19},{20,21,22,2..., dimensions={0} | all-to-all | bytes 1048576 | tf_op jit(solution)/shard_map/all_to_all | solution.py:315
  103.9 1.7 %merge.2 = bf16[128,128]{1,0:T(8,128)(2,1)S(1)} custom-call(bf16[512,128]{1,0:T(8,128)(2,1)S(1)} %get-tuple-element.11.refs_0_, bf16[512,128]{1,0:T(8,128)(2,1)S(1)} %collective-permute-done.9.refs_1_, bf16[512,128]{1,0:T(8,128)(2,1)S(1)} %collective-permute-done.10.refs_2_, bf16[512,128]{1,0:T(8,128)(2,1)S(1)} %collective-permute-done.11.refs_3_, ...), custom_call_target="tpu_custom_call" | custom-call | flops 700000000 | bytes 5000000 | tf_op jit(solution)/shard_map/merge/pallas_call | solution.py:325
  105.6 1.9 %collective-permute-start.16 = (bf16[128,128]{1,0:T(8,128)(2,1)S(1)}, bf16[128,128]{1,0:T(8,128)(2,1)S(1)}, u32[]{:S(2)}, u32[]{:S(2)}) collective-permute-start(bf16[128,128]{1,0:T(8,128)(2,1)S(1)} %merge.2), channel_id=1, source_target_pairs={{0,8},{1,9},{2,10},{3,11},{4,12},{5,13},{6,14},{7,15},{8,16},{9,17... | collective-permute-start | bytes 98312 | tf_op jit(solution)/shard_map/ppermute | solution.py:58
  107.5 1.6 %merge.3 = bf16[128,128]{1,0:T(8,128)(2,1)S(1)} custom-call(bf16[512,128]{1,0:T(8,128)(2,1)S(1)} %get-tuple-element.11.refs_0_, bf16[512,128]{1,0:T(8,128)(2,1)S(1)} %collective-permute-done.9.refs_1_, bf16[512,128]{1,0:T(8,128)(2,1)S(1)} %collective-permute-done.10.refs_2_, bf16[512,128]{1,0:T(8,128)(2,1)S(1)} %collective-permute-done.11.refs_3_, ...), custom_call_target="tpu_custom_call" | custom-call | flops 700000000 | bytes 5000000 | tf_op jit(solution)/shard_map/merge/pallas_call | solution.py:325
  109.1 5.0 %collective-permute-done.16 = bf16[128,128]{1,0:T(8,128)(2,1)S(1)} collective-permute-done((bf16[128,128]{1,0:T(8,128)(2,1)S(1)}, bf16[128,128]{1,0:T(8,128)(2,1)S(1)}, u32[]{:S(2)}, u32[]{:S(2)}) %collective-permute-start.16) | collective-permute-done | bytes 32800 | tf_op jit(solution)/shard_map/ppermute | solution.py:58
  114.1 0.6 pad_maximum_fusion.1
  (21 shorter events, 0.1 us)
Async XLA Ops:
  0.0 0.9 copy-start.6
  1.2 1.0 copy-start.3
  2.1 42.7 %collective-permute-start.4 = (bf16[512,128]{1,0:T(8,128)(2,1)S(1)}, bf16[512,128]{1,0:T(8,128)(2,1)S(1)}, u32[]{:S(2)}, u32[]{:S(2)}) collective-permute-start(bf16[512,128]{1,0:T(8,128)(2,1)S(1)} %piece.1.refs_0_.refs_2_), channel_id=1, source_target_pairs={{0,4},{1,5},{2,6},{3,7},{4,0},{5,1},{6,2},{7,3},{8,12},{9,13},{10,... | collective-permute-start | bytes 393224 | tf_op jit(solution)/shard_map/ppermute | solution.py:34
  17.9 14.5 %collective-permute-start = (bf16[256,128]{1,0:T(8,128)(2,1)S(1)}, bf16[256,128]{1,0:T(8,128)(2,1)S(1)}, u32[]{:S(2)}, u32[]{:S(2)}) collective-permute-start(bf16[256,128]{1,0:T(8,128)(2,1)S(1)} %get-tuple-element.10), channel_id=1, source_target_pairs={{0,508},{1,509},{2,510},{3,511},{4,504},{5,505},{6,506},{7,507},{8... | collective-permute-start | bytes 196616 | tf_op jit(solution)/shard_map/ppermute | solution.py:51
  32.3 14.9 %collective-permute-start.5 = (bf16[256,128]{1,0:T(8,128)(2,1)S(1)}, bf16[256,128]{1,0:T(8,128)(2,1)S(1)}, u32[]{:S(2)}, u32[]{:S(2)}) collective-permute-start(bf16[256,128]{1,0:T(8,128)(2,1)S(1)} %collective-permute-done.refs_1_), channel_id=1, source_target_pairs={{0,4},{1,5},{2,6},{3,7},{4,0},{5,1},{6,2},{7,3},{8,12},{9,13},{10,... | collective-permute-start | bytes 196616 | tf_op jit(solution)/shard_map/ppermute | solution.py:34
  34.3 23.6 %copy-start = (bf16[4096,256]{1,0:T(8,128)(2,1)S(1)}, bf16[4096,256]{1,0:T(8,128)(2,1)}, u32[]{:S(2)}) copy-start(bf16[4096,256]{1,0:T(8,128)(2,1)} %param.17) | copy-start | bytes 6291460
  34.3 18.6 %collective-permute-start.1 = (bf16[768,128]{1,0:T(8,128)(2,1)S(1)}, bf16[768,128]{1,0:T(8,128)(2,1)S(1)}, u32[]{:S(2)}, u32[]{:S(2)}) collective-permute-start(bf16[768,128]{1,0:T(8,128)(2,1)S(1)} %bitcast.29), channel_id=1, source_target_pairs={{0,1},{1,0},{2,3},{3,2},{4,5},{5,4},{6,7},{7,6},{8,9},{9,8},{10,11... | collective-permute-start | bytes 589832 | tf_op jit(solution)/shard_map/ppermute | solution.py:34
  37.1 20.8 %collective-permute-start.2 = (bf16[768,128]{1,0:T(8,128)(2,1)S(1)}, bf16[768,128]{1,0:T(8,128)(2,1)S(1)}, u32[]{:S(2)}, u32[]{:S(2)}) collective-permute-start(bf16[768,128]{1,0:T(8,128)(2,1)S(1)} %bitcast.30), channel_id=1, source_target_pairs={{0,2},{1,3},{2,0},{3,1},{4,6},{5,7},{6,4},{7,5},{8,10},{9,11},{10,... | collective-permute-start | bytes 589832 | tf_op jit(solution)/shard_map/ppermute | solution.py:34
  39.9 18.7 %collective-permute-start.3 = (bf16[768,128]{1,0:T(8,128)(2,1)S(1)}, bf16[768,128]{1,0:T(8,128)(2,1)S(1)}, u32[]{:S(2)}, u32[]{:S(2)}) collective-permute-start(bf16[768,128]{1,0:T(8,128)(2,1)S(1)} %bitcast.31), channel_id=1, source_target_pairs={{0,3},{1,2},{2,1},{3,0},{4,7},{5,6},{6,5},{7,4},{8,11},{9,10},{10,... | collective-permute-start | bytes 589832 | tf_op jit(solution)/shard_map/ppermute | solution.py:34
  47.2 16.6 %copy-start.7 = (f32[2,128,128]{2,1,0:T(8,128)S(1)}, f32[2,128,128]{2,1,0:T(8,128)}, u32[]{:S(2)}) copy-start(f32[2,128,128]{2,1,0:T(8,128)} %bias_ref.1) | copy-start | bytes 393220
  47.2 16.6 %copy-start.8 = (f32[128,128]{1,0:T(8,128)S(1)}, f32[128,128]{1,0:T(8,128)}, u32[]{:S(2)}) copy-start(f32[128,128]{1,0:T(8,128)} %constant.6.clone.hot_ref) | copy-start | bytes 196612
  47.2 16.6 %copy-start.9 = (f32[128,128]{1,0:T(8,128)S(1)}, f32[128,128]{1,0:T(8,128)}, u32[]{:S(2)}) copy-start(f32[128,128]{1,0:T(8,128)} %constant.7.clone.turned_ref) | copy-start | bytes 196612
  47.2 11.4 %collective-permute-start.6 = (bf16[768,128]{1,0:T(8,128)(2,1)S(1)}, bf16[768,128]{1,0:T(8,128)(2,1)S(1)}, u32[]{:S(2)}, u32[]{:S(2)}) collective-permute-start(bf16[768,128]{1,0:T(8,128)(2,1)S(1)} %bitcast.35), channel_id=1, source_target_pairs={{0,1},{1,0},{2,3},{3,2},{4,5},{5,4},{6,7},{7,6},{8,9},{9,8},{10,11... | collective-permute-start | bytes 589832 | tf_op jit(solution)/shard_map/ppermute | solution.py:34
  50.0 9.1 %collective-permute-start.7 = (bf16[768,128]{1,0:T(8,128)(2,1)S(1)}, bf16[768,128]{1,0:T(8,128)(2,1)S(1)}, u32[]{:S(2)}, u32[]{:S(2)}) collective-permute-start(bf16[768,128]{1,0:T(8,128)(2,1)S(1)} %bitcast.36), channel_id=1, source_target_pairs={{0,2},{1,3},{2,0},{3,1},{4,6},{5,7},{6,4},{7,5},{8,10},{9,11},{10,... | collective-permute-start | bytes 589832 | tf_op jit(solution)/shard_map/ppermute | solution.py:34
  52.9 8.8 %collective-permute-start.8 = (bf16[768,128]{1,0:T(8,128)(2,1)S(1)}, bf16[768,128]{1,0:T(8,128)(2,1)S(1)}, u32[]{:S(2)}, u32[]{:S(2)}) collective-permute-start(bf16[768,128]{1,0:T(8,128)(2,1)S(1)} %bitcast.37), channel_id=1, source_target_pairs={{0,3},{1,2},{2,1},{3,0},{4,7},{5,6},{6,5},{7,4},{8,11},{9,10},{10,... | collective-permute-start | bytes 589832 | tf_op jit(solution)/shard_map/ppermute | solution.py:34
  57.8 46.0 %collective-permute-start.15 = (bf16[4096,256]{1,0:T(8,128)(2,1)S(1)}, bf16[4096,256]{1,0:T(8,128)(2,1)S(1)}, u32[]{:S(2)}, u32[]{:S(2)}) collective-permute-start(bf16[4096,256]{1,0:T(8,128)(2,1)S(1)} %copy-done), channel_id=1, source_target_pairs={{60,504},{61,505},{62,506},{63,507},{56,508},{57,509},{58,510},{59... | collective-permute-start | bytes 6291464 | tf_op jit(solution)/shard_map/ppermute | solution.py:61
  61.7 2.7 %copy-start.1 = (bf16[1024,3,128]{2,0,1:T(8,128)(2,1)S(1)}, bf16[1024,3,128]{2,0,1:T(8,128)(2,1)}, u32[]{:S(2)}) copy-start(bf16[1024,3,128]{2,0,1:T(8,128)(2,1)} %param.13) | copy-start | bytes 2359300
  61.7 2.7 %copy-start.5 = (f32[1024]{0:T(1024)S(1)}, f32[1024]{0:T(1024)}, u32[]{:S(2)}) copy-start(f32[1024]{0:T(1024)} %param.12) | copy-start | bytes 12292
  61.7 24.1 %collective-permute-start.13 = (bf16[2048,128]{1,0:T(8,128)(2,1)S(1)}, bf16[2048,128]{1,0:T(8,128)(2,1)S(1)}, u32[]{:S(2)}, u32[]{:S(2)}) collective-permute-start(bf16[2048,128]{1,0:T(8,128)(2,1)S(1)} %bitcast.27), channel_id=1, source_target_pairs={{0,16},{1,17},{2,18},{3,19},{4,20},{5,21},{6,22},{7,23},{8,24},{9,... | collective-permute-start | bytes 1572872 | tf_op jit(solution)/shard_map/ppermute | solution.py:34
  68.2 24.5 %collective-permute-start.12 = (bf16[528,128]{1,0:T(8,128)(2,1)S(1)}, bf16[528,128]{1,0:T(8,128)(2,1)S(1)}, u32[]{:S(2)}, u32[]{:S(2)}) collective-permute-start(bf16[528,128]{1,0:T(8,128)(2,1)S(1)} %pad_maximum_fusion), channel_id=1, source_target_pairs={{0,4},{1,5},{2,6},{3,7},{4,0},{5,1},{6,2},{7,3},{8,12},{9,13},{10,... | collective-permute-start | bytes 405512 | tf_op jit(solution)/shard_map/ppermute | solution.py:34
  78.5 9.7 %collective-permute-start.10 = (bf16[512,128]{1,0:T(8,128)(2,1)S(1)}, bf16[512,128]{1,0:T(8,128)(2,1)S(1)}, u32[]{:S(2)}, u32[]{:S(2)}) collective-permute-start(bf16[512,128]{1,0:T(8,128)(2,1)S(1)} %get-tuple-element.11.refs_0_), channel_id=1, source_target_pairs={{0,2},{1,3},{2,0},{3,1},{4,6},{5,7},{6,4},{7,5},{8,10},{9,11},{10,... | collective-permute-start | bytes 393224 | tf_op jit(solution)/shard_map/ppermute | solution.py:34
  81.1 9.3 %collective-permute-start.11 = (bf16[512,128]{1,0:T(8,128)(2,1)S(1)}, bf16[512,128]{1,0:T(8,128)(2,1)S(1)}, u32[]{:S(2)}, u32[]{:S(2)}) collective-permute-start(bf16[512,128]{1,0:T(8,128)(2,1)S(1)} %get-tuple-element.11.refs_0_), channel_id=1, source_target_pairs={{0,3},{1,2},{2,1},{3,0},{4,7},{5,6},{6,5},{7,4},{8,11},{9,10},{10,... | collective-permute-start | bytes 393224 | tf_op jit(solution)/shard_map/ppermute | solution.py:34
  85.8 6.9 %collective-permute-start.9 = (bf16[512,128]{1,0:T(8,128)(2,1)S(1)}, bf16[512,128]{1,0:T(8,128)(2,1)S(1)}, u32[]{:S(2)}, u32[]{:S(2)}) collective-permute-start(bf16[512,128]{1,0:T(8,128)(2,1)S(1)} %get-tuple-element.11.refs_0_), channel_id=1, source_target_pairs={{0,1},{1,0},{2,3},{3,2},{4,5},{5,4},{6,7},{7,6},{8,9},{9,8},{10,11... | collective-permute-start | bytes 393224 | tf_op jit(solution)/shard_map/ppermute | solution.py:34
  88.2 15.7 %copy-start.2 = (bf16[2,128,64]{2,1,0:T(8,128)(2,1)S(1)}, bf16[2,128,64]{2,1,0:T(8,128)(2,1)}, u32[]{:S(2)}) copy-start(bf16[2,128,64]{2,1,0:T(8,128)(2,1)} %constant.8.clone.refs_9_) | copy-start | bytes 98308
  88.2 15.6 %copy-start.4 = (f32[4096]{0:T(1024)S(1)}, f32[4096]{0:T(1024)}, u32[]{:S(2)}) copy-start(f32[4096]{0:T(1024)} %param.16) | copy-start | bytes 49156
  88.3 15.6 %collective-permute-start.14 = (bf16[4096,128]{1,0:T(8,128)(2,1)S(1)}, bf16[4096,128]{1,0:T(8,128)(2,1)S(1)}, u32[]{:S(2)}, u32[]{:S(2)}) collective-permute-start(bf16[4096,128]{1,0:T(8,128)(2,1)S(1)} %bitcast.19), channel_id=1, source_target_pairs={{0,8},{1,9},{2,10},{3,11},{4,12},{5,13},{6,14},{7,15},{8,0},{9,1},... | collective-permute-start | bytes 3145736 | tf_op jit(solution)/shard_map/ppermute | solution.py:34
  105.6 8.6 %collective-permute-start.16 = (bf16[128,128]{1,0:T(8,128)(2,1)S(1)}, bf16[128,128]{1,0:T(8,128)(2,1)S(1)}, u32[]{:S(2)}, u32[]{:S(2)}) collective-permute-start(bf16[128,128]{1,0:T(8,128)(2,1)S(1)} %merge.2), channel_id=1, source_target_pairs={{0,8},{1,9},{2,10},{3,11},{4,12},{5,13},{6,14},{7,15},{8,16},{9,17... | collective-permute-start | bytes 98312 | tf_op jit(solution)/shard_map/ppermute | solution.py:58

commit v12 on v10

--- a/solution.py
+++ b/solution.py
@@ -310,7 +310,7 @@
     )(*around, ln_gain.reshape(8, 1, BLOCK), w_qkv.transpose(1, 0, 2).reshape(3, 8, BLOCK, BLOCK), bias)
 
     attended_around = along_y(attended)
-    attended_partner = joined([(across(attended, 4), 0, TOKENS)], 4, CLAIMED, attended_around[1:])
+    attended_partner = joined([(across(jnp.concatenate([attended, attended[:16]], axis=0), 4), 0, TOKENS)], 4, CLAIMED, attended_around[1:])
     attended_around.append(
         lax.all_to_all(attended_partner, "head", 0, 0, axis_index_groups=[[0, 1, 2, 3], [4, 5, 6, 7]])
     )

time: 113 us -> 110 us (0.973)
  blocking collectives: 12.7 us -> 11.1 us
  waiting for transfers between devices: 17.6 us -> 16.2 us
    all_to_all x1, blocking collectives: 12.7 us -> 11.1 us  [on_device(): lax.all_to_all(attended_partner, 'head', 0, 0, axis_index_groups=[[0, 1,...]
    ppermute x14, waiting for transfers between devices: 10.9 us -> 9.58 us  [moved(): return lax.ppermute(value, BOTH, pairs)]
where the time goes in v12:
time: 110 us; the launch traced here: 109 us
  starting transfers between devices  71.2 us (65%)
  waiting for transfers between devices  16.2 us (15%)
  blocking collectives  11.1 us (10%)
  Pallas kernels  7.12 us (6%)
  local copies, waits for them, and re-layouts  1.91 us (2%)
    ppermute x14, starting transfers between devices, moved(): return lax.ppermute(value, BOTH, pairs)  55.4 us
    ppermute x1, starting transfers between devices, following_rows(): return lax.ppermute(value, BOTH, pairs)  13 us
    all_to_all x1, blocking collectives, on_device(): lax.all_to_all(attended_partner, 'head', 0, 0, axis_index_groups=[[0, 1,...  11.1 us
    ppermute x14, waiting for transfers between devices, moved(): return lax.ppermute(value, BOTH, pairs)  9.58 us
    ppermute x1, waiting for transfers between devices, lower_rows(): return lax.ppermute(value, BOTH, pairs)  6.63 us
    pallas_call x1, Pallas kernels, on_device(): pl.pallas_call(attention_kernel, out_shape=(jax.ShapeDtypeStruct((TOKENS,...  3.73 us
    pallas_call x1, Pallas kernels, on_device(): pl.pallas_call(merge_kernel, out_shape=jax.ShapeDtypeStruct((256, BLOCK),...  2.39 us
  transfers between devices with their start and end apart: 17, of which 5 were waited for; matrix products, arithmetic and copies ran while one was open for 0% of the time, Pallas kernels for 4%

profile of v12, /device:TPU:24, one launch (start us, length us, event | category | flops | bytes accessed | tf_op | source)
XLA Modules:
  0.0 108.6 jit_solution(10221436070429347820)
XLA Ops:
  0.0 0.9 copy-done.6
  0.9 0.2 order.1
  1.2 13.0 %collective-permute-start = (bf16[256,128]{1,0:T(8,128)(2,1)S(1)}, bf16[256,128]{1,0:T(8,128)(2,1)S(1)}, u32[]{:S(2)}, u32[]{:S(2)}) collective-permute-start(bf16[256,128]{1,0:T(8,128)(2,1)S(1)} %get-tuple-element.10), channel_id=1, source_target_pairs={{0,508},{1,509},{2,510},{3,511},{4,504},{5,505},{6,506},{7,507},{8... | collective-permute-start | bytes 196616 | tf_op jit(solution)/shard_map/ppermute | solution.py:51
  14.2 0.0 copy-start.2
  14.2 0.9 copy-done.2
  15.2 6.3 %collective-permute-start.4 = (bf16[512,128]{1,0:T(8,128)(2,1)S(1)}, bf16[512,128]{1,0:T(8,128)(2,1)S(1)}, u32[]{:S(2)}, u32[]{:S(2)}) collective-permute-start(bf16[512,128]{1,0:T(8,128)(2,1)S(1)} %piece.1.refs_0_.refs_2_), channel_id=1, source_target_pairs={{0,4},{1,5},{2,6},{3,7},{4,0},{5,1},{6,2},{7,3},{8,12},{9,13},{10,... | collective-permute-start | bytes 393224 | tf_op jit(solution)/shard_map/ppermute | solution.py:34
  21.5 0.0 collective-permute-done.refs_1_
  21.5 8.2 %collective-permute-start.5 = (bf16[256,128]{1,0:T(8,128)(2,1)S(1)}, bf16[256,128]{1,0:T(8,128)(2,1)S(1)}, u32[]{:S(2)}, u32[]{:S(2)}) collective-permute-start(bf16[256,128]{1,0:T(8,128)(2,1)S(1)} %collective-permute-done.refs_1_), channel_id=1, source_target_pairs={{0,4},{1,5},{2,6},{3,7},{4,0},{5,1},{6,2},{7,3},{8,12},{9,13},{10,... | collective-permute-start | bytes 196616 | tf_op jit(solution)/shard_map/ppermute | solution.py:34
  29.8 0.0 copy-start
  29.8 2.3 %collective-permute-start.3 = (bf16[768,128]{1,0:T(8,128)(2,1)S(1)}, bf16[768,128]{1,0:T(8,128)(2,1)S(1)}, u32[]{:S(2)}, u32[]{:S(2)}) collective-permute-start(bf16[768,128]{1,0:T(8,128)(2,1)S(1)} %bitcast.25), channel_id=1, source_target_pairs={{0,3},{1,2},{2,1},{3,0},{4,7},{5,6},{6,5},{7,4},{8,11},{9,10},{10,... | collective-permute-start | bytes 589832 | tf_op jit(solution)/shard_map/ppermute | solution.py:34
  32.1 4.5 %collective-permute-start.2 = (bf16[768,128]{1,0:T(8,128)(2,1)S(1)}, bf16[768,128]{1,0:T(8,128)(2,1)S(1)}, u32[]{:S(2)}, u32[]{:S(2)}) collective-permute-start(bf16[768,128]{1,0:T(8,128)(2,1)S(1)} %bitcast.26), channel_id=1, source_target_pairs={{0,2},{1,3},{2,0},{3,1},{4,6},{5,7},{6,4},{7,5},{8,10},{9,11},{10,... | collective-permute-start | bytes 589832 | tf_op jit(solution)/shard_map/ppermute | solution.py:34
  36.6 3.2 %collective-permute-start.1 = (bf16[768,128]{1,0:T(8,128)(2,1)S(1)}, bf16[768,128]{1,0:T(8,128)(2,1)S(1)}, u32[]{:S(2)}, u32[]{:S(2)}) collective-permute-start(bf16[768,128]{1,0:T(8,128)(2,1)S(1)} %bitcast.27), channel_id=1, source_target_pairs={{0,1},{1,0},{2,3},{3,2},{4,5},{5,4},{6,7},{7,6},{8,9},{9,8},{10,11... | collective-permute-start | bytes 589832 | tf_op jit(solution)/shard_map/ppermute | solution.py:34
  39.8 1.7 %collective-permute-done.5.refs_1_ = bf16[256,128]{1,0:T(8,128)(2,1)S(1)} collective-permute-done((bf16[256,128]{1,0:T(8,128)(2,1)S(1)}, bf16[256,128]{1,0:T(8,128)(2,1)S(1)}, u32[]{:S(2)}, u32[]{:S(2)}) %collective-permute-start.5) | collective-permute-done | bytes 65568 | tf_op jit(solution)/shard_map/ppermute | solution.py:34
  41.5 0.0 collective-permute-done.4.refs_0_.refs_2_
  41.5 0.0 copy-start.7
  41.5 0.0 copy-start.8
  41.5 0.0 copy-start.9
  41.5 2.1 %collective-permute-start.8 = (bf16[768,128]{1,0:T(8,128)(2,1)S(1)}, bf16[768,128]{1,0:T(8,128)(2,1)S(1)}, u32[]{:S(2)}, u32[]{:S(2)}) collective-permute-start(bf16[768,128]{1,0:T(8,128)(2,1)S(1)} %bitcast.32), channel_id=1, source_target_pairs={{0,3},{1,2},{2,1},{3,0},{4,7},{5,6},{6,5},{7,4},{8,11},{9,10},{10,... | collective-permute-start | bytes 589832 | tf_op jit(solution)/shard_map/ppermute | solution.py:34
  43.6 4.7 %collective-permute-start.7 = (bf16[768,128]{1,0:T(8,128)(2,1)S(1)}, bf16[768,128]{1,0:T(8,128)(2,1)S(1)}, u32[]{:S(2)}, u32[]{:S(2)}) collective-permute-start(bf16[768,128]{1,0:T(8,128)(2,1)S(1)} %bitcast.33), channel_id=1, source_target_pairs={{0,2},{1,3},{2,0},{3,1},{4,6},{5,7},{6,4},{7,5},{8,10},{9,11},{10,... | collective-permute-start | bytes 589832 | tf_op jit(solution)/shard_map/ppermute | solution.py:34
  48.3 0.0 collective-permute-done.3.refs_3_
  48.3 3.2 %collective-permute-start.6 = (bf16[768,128]{1,0:T(8,128)(2,1)S(1)}, bf16[768,128]{1,0:T(8,128)(2,1)S(1)}, u32[]{:S(2)}, u32[]{:S(2)}) collective-permute-start(bf16[768,128]{1,0:T(8,128)(2,1)S(1)} %bitcast.34), channel_id=1, source_target_pairs={{0,1},{1,0},{2,3},{3,2},{4,5},{5,4},{6,7},{7,6},{8,9},{9,8},{10,11... | collective-permute-start | bytes 589832 | tf_op jit(solution)/shard_map/ppermute | solution.py:34
  51.5 0.8 collective-permute-start.15
  52.3 0.0 collective-permute-done.1.refs_1_
  52.3 3.4 %collective-permute-done.8.refs_7_ = bf16[768,128]{1,0:T(8,128)(2,1)S(1)} collective-permute-done((bf16[768,128]{1,0:T(8,128)(2,1)S(1)}, bf16[768,128]{1,0:T(8,128)(2,1)S(1)}, u32[]{:S(2)}, u32[]{:S(2)}) %collective-permute-start.8) | collective-permute-done | bytes 196640 | tf_op jit(solution)/shard_map/ppermute | solution.py:34
  55.7 2.5 %collective-permute-done.6.refs_5_ = bf16[768,128]{1,0:T(8,128)(2,1)S(1)} collective-permute-done((bf16[768,128]{1,0:T(8,128)(2,1)S(1)}, bf16[768,128]{1,0:T(8,128)(2,1)S(1)}, u32[]{:S(2)}, u32[]{:S(2)}) %collective-permute-start.6) | collective-permute-done | bytes 196640 | tf_op jit(solution)/shard_map/ppermute | solution.py:34
  58.2 0.0 copy-start.1
  58.2 0.0 copy-start.5
  58.3 2.1 %collective-permute-start.13 = (bf16[2048,128]{1,0:T(8,128)(2,1)S(1)}, bf16[2048,128]{1,0:T(8,128)(2,1)S(1)}, u32[]{:S(2)}, u32[]{:S(2)}) collective-permute-start(bf16[2048,128]{1,0:T(8,128)(2,1)S(1)} %bitcast.23), channel_id=1, source_target_pairs={{0,16},{1,17},{2,18},{3,19},{4,20},{5,21},{6,22},{7,23},{8,24},{9,... | collective-permute-start | bytes 1572872 | tf_op jit(solution)/shard_map/ppermute | solution.py:34
  60.3 0.5 bias.1.refs_10_
  60.9 3.7 %attention.1 = (bf16[512,128]{1,0:T(8,128)(2,1)S(1)}, bf16[8,512,128]{2,1,0:T(8,128)(2,1)S(1)}) custom-call(bf16[768,128]{1,0:T(8,128)(2,1)S(1)} %bitcast.29, bf16[768,128]{1,0:T(8,128)(2,1)S(1)} %collective-permute-done.1.refs_1_, bf16[768,128]{1,0:T(8,128)(2,1)S(1)} %collective-permute-done.2.refs_2_, bf16[768,128]{1,0:T(8,128)(2,1)S(1)} %collective-permute-done.3.refs_3_, ...), custom_call_target="tpu_custom_call" | custom-call | flops 600000000 | bytes 3000000 | tf_op jit(solution)/shard_map/attention/pallas_call | solution.py:298
  64.7 7.0 %collective-permute-start.12 = (bf16[528,128]{1,0:T(8,128)(2,1)S(1)}, bf16[528,128]{1,0:T(8,128)(2,1)S(1)}, u32[]{:S(2)}, u32[]{:S(2)}) collective-permute-start(bf16[528,128]{1,0:T(8,128)(2,1)S(1)} %pad_maximum_fusion), channel_id=1, source_target_pairs={{0,4},{1,5},{2,6},{3,7},{4,0},{5,1},{6,2},{7,3},{8,12},{9,13},{10,... | collective-permute-start | bytes 405512 | tf_op jit(solution)/shard_map/ppermute | solution.py:34
  71.7 3.0 %collective-permute-start.11 = (bf16[512,128]{1,0:T(8,128)(2,1)S(1)}, bf16[512,128]{1,0:T(8,128)(2,1)S(1)}, u32[]{:S(2)}, u32[]{:S(2)}) collective-permute-start(bf16[512,128]{1,0:T(8,128)(2,1)S(1)} %get-tuple-element.11.refs_0_), channel_id=1, source_target_pairs={{0,3},{1,2},{2,1},{3,0},{4,7},{5,6},{6,5},{7,4},{8,11},{9,10},{10,... | collective-permute-start | bytes 393224 | tf_op jit(solution)/shard_map/ppermute | solution.py:34
  74.7 4.2 %collective-permute-start.10 = (bf16[512,128]{1,0:T(8,128)(2,1)S(1)}, bf16[512,128]{1,0:T(8,128)(2,1)S(1)}, u32[]{:S(2)}, u32[]{:S(2)}) collective-permute-start(bf16[512,128]{1,0:T(8,128)(2,1)S(1)} %get-tuple-element.11.refs_0_), channel_id=1, source_target_pairs={{0,2},{1,3},{2,0},{3,1},{4,6},{5,7},{6,4},{7,5},{8,10},{9,11},{10,... | collective-permute-start | bytes 393224 | tf_op jit(solution)/shard_map/ppermute | solution.py:34
  78.9 2.7 %collective-permute-start.9 = (bf16[512,128]{1,0:T(8,128)(2,1)S(1)}, bf16[512,128]{1,0:T(8,128)(2,1)S(1)}, u32[]{:S(2)}, u32[]{:S(2)}) collective-permute-start(bf16[512,128]{1,0:T(8,128)(2,1)S(1)} %get-tuple-element.11.refs_0_), channel_id=1, source_target_pairs={{0,1},{1,0},{2,3},{3,2},{4,5},{5,4},{6,7},{7,6},{8,9},{9,8},{10,11... | collective-permute-start | bytes 393224 | tf_op jit(solution)/shard_map/ppermute | solution.py:34
  81.6 0.1 join.9
  81.6 0.0 collective-permute-done.11.refs_3_
  81.7 0.0 copy-start.3
  81.7 0.0 copy-start.4
  81.7 2.1 %collective-permute-start.14 = (bf16[4096,128]{1,0:T(8,128)(2,1)S(1)}, bf16[4096,128]{1,0:T(8,128)(2,1)S(1)}, u32[]{:S(2)}, u32[]{:S(2)}) collective-permute-start(bf16[4096,128]{1,0:T(8,128)(2,1)S(1)} %bitcast.19), channel_id=1, source_target_pairs={{0,8},{1,9},{2,10},{3,11},{4,12},{5,13},{6,14},{7,15},{8,0},{9,1},... | collective-permute-start | bytes 3145736 | tf_op jit(solution)/shard_map/ppermute | solution.py:34
  83.7 2.0 %collective-permute-done.9.refs_1_ = bf16[512,128]{1,0:T(8,128)(2,1)S(1)} collective-permute-done((bf16[512,128]{1,0:T(8,128)(2,1)S(1)}, bf16[512,128]{1,0:T(8,128)(2,1)S(1)}, u32[]{:S(2)}, u32[]{:S(2)}) %collective-permute-start.9) | collective-permute-done | bytes 131104 | tf_op jit(solution)/shard_map/ppermute | solution.py:34
  85.8 0.0 collective-permute-done.12.refs_0_
  85.8 0.1 join.7
  85.8 11.1 %all_to_all.5.refs_4_ = bf16[4,512,128]{2,1,0:T(8,128)(2,1)S(1)} all-to-all(bf16[4,512,128]{2,1,0:T(8,128)(2,1)S(1)} %join.7), channel_id=1, replica_groups={{0,1,2,3},{4,5,6,7},{8,9,10,11},{12,13,14,15},{16,17,18,19},{20,21,22,2..., dimensions={0} | all-to-all | bytes 1048576 | tf_op jit(solution)/shard_map/all_to_all | solution.py:315
  96.9 0.0 collective-permute-done.15
  97.0 2.4 %merge.1 = bf16[256,128]{1,0:T(8,128)(2,1)S(1)} custom-call(bf16[512,128]{1,0:T(8,128)(2,1)S(1)} %get-tuple-element.11.refs_0_, bf16[512,128]{1,0:T(8,128)(2,1)S(1)} %collective-permute-done.9.refs_1_, bf16[512,128]{1,0:T(8,128)(2,1)S(1)} %collective-permute-done.10.refs_2_, bf16[512,128]{1,0:T(8,128)(2,1)S(1)} %collective-permute-done.11.refs_3_, ...), custom_call_target="tpu_custom_call" | custom-call | flops 1400000000 | bytes 7000000 | tf_op jit(solution)/shard_map/merge/pallas_call | solution.py:320
  99.4 1.9 %collective-permute-start.16 = (bf16[128,128]{1,0:T(8,128)(2,1)S(1)}, bf16[128,128]{1,0:T(8,128)(2,1)S(1)}, u32[]{:S(2)}, u32[]{:S(2)}) collective-permute-start(bf16[128,128]{1,0:T(8,128)(2,1)S(1)} %get-tuple-element.13), channel_id=1, source_target_pairs={{0,8},{1,9},{2,10},{3,11},{4,12},{5,13},{6,14},{7,15},{8,16},{9,17... | collective-permute-start | bytes 98312 | tf_op jit(solution)/shard_map/ppermute | solution.py:58
  101.3 6.6 %collective-permute-done.16 = bf16[128,128]{1,0:T(8,128)(2,1)S(1)} collective-permute-done((bf16[128,128]{1,0:T(8,128)(2,1)S(1)}, bf16[128,128]{1,0:T(8,128)(2,1)S(1)}, u32[]{:S(2)}, u32[]{:S(2)}) %collective-permute-start.16) | collective-permute-done | bytes 32800 | tf_op jit(solution)/shard_map/ppermute | solution.py:58
  107.9 0.6 pad_maximum_fusion.1
  (21 shorter events, 0.1 us)
Async XLA Ops:
  0.0 0.9 copy-start.6
  1.2 20.4 %collective-permute-start = (bf16[256,128]{1,0:T(8,128)(2,1)S(1)}, bf16[256,128]{1,0:T(8,128)(2,1)S(1)}, u32[]{:S(2)}, u32[]{:S(2)}) collective-permute-start(bf16[256,128]{1,0:T(8,128)(2,1)S(1)} %get-tuple-element.10), channel_id=1, source_target_pairs={{0,508},{1,509},{2,510},{3,511},{4,504},{5,505},{6,506},{7,507},{8... | collective-permute-start | bytes 196616 | tf_op jit(solution)/shard_map/ppermute | solution.py:51
  14.2 1.0 copy-start.2
  15.2 26.3 %collective-permute-start.4 = (bf16[512,128]{1,0:T(8,128)(2,1)S(1)}, bf16[512,128]{1,0:T(8,128)(2,1)S(1)}, u32[]{:S(2)}, u32[]{:S(2)}) collective-permute-start(bf16[512,128]{1,0:T(8,128)(2,1)S(1)} %piece.1.refs_0_.refs_2_), channel_id=1, source_target_pairs={{0,4},{1,5},{2,6},{3,7},{4,0},{5,1},{6,2},{7,3},{8,12},{9,13},{10,... | collective-permute-start | bytes 393224 | tf_op jit(solution)/shard_map/ppermute | solution.py:34
  21.5 19.9 %collective-permute-start.5 = (bf16[256,128]{1,0:T(8,128)(2,1)S(1)}, bf16[256,128]{1,0:T(8,128)(2,1)S(1)}, u32[]{:S(2)}, u32[]{:S(2)}) collective-permute-start(bf16[256,128]{1,0:T(8,128)(2,1)S(1)} %collective-permute-done.refs_1_), channel_id=1, source_target_pairs={{0,4},{1,5},{2,6},{3,7},{4,0},{5,1},{6,2},{7,3},{8,12},{9,13},{10,... | collective-permute-start | bytes 196616 | tf_op jit(solution)/shard_map/ppermute | solution.py:34
  29.8 21.7 %copy-start = (bf16[4096,256]{1,0:T(8,128)(2,1)S(1)}, bf16[4096,256]{1,0:T(8,128)(2,1)}, u32[]{:S(2)}) copy-start(bf16[4096,256]{1,0:T(8,128)(2,1)} %param.16) | copy-start | bytes 6291460
  29.8 18.5 %collective-permute-start.3 = (bf16[768,128]{1,0:T(8,128)(2,1)S(1)}, bf16[768,128]{1,0:T(8,128)(2,1)S(1)}, u32[]{:S(2)}, u32[]{:S(2)}) collective-permute-start(bf16[768,128]{1,0:T(8,128)(2,1)S(1)} %bitcast.25), channel_id=1, source_target_pairs={{0,3},{1,2},{2,1},{3,0},{4,7},{5,6},{6,5},{7,4},{8,11},{9,10},{10,... | collective-permute-start | bytes 589832 | tf_op jit(solution)/shard_map/ppermute | solution.py:34
  32.1 19.4 %collective-permute-start.2 = (bf16[768,128]{1,0:T(8,128)(2,1)S(1)}, bf16[768,128]{1,0:T(8,128)(2,1)S(1)}, u32[]{:S(2)}, u32[]{:S(2)}) collective-permute-start(bf16[768,128]{1,0:T(8,128)(2,1)S(1)} %bitcast.26), channel_id=1, source_target_pairs={{0,2},{1,3},{2,0},{3,1},{4,6},{5,7},{6,4},{7,5},{8,10},{9,11},{10,... | collective-permute-start | bytes 589832 | tf_op jit(solution)/shard_map/ppermute | solution.py:34
  36.6 15.8 %collective-permute-start.1 = (bf16[768,128]{1,0:T(8,128)(2,1)S(1)}, bf16[768,128]{1,0:T(8,128)(2,1)S(1)}, u32[]{:S(2)}, u32[]{:S(2)}) collective-permute-start(bf16[768,128]{1,0:T(8,128)(2,1)S(1)} %bitcast.27), channel_id=1, source_target_pairs={{0,1},{1,0},{2,3},{3,2},{4,5},{5,4},{6,7},{7,6},{8,9},{9,8},{10,11... | collective-permute-start | bytes 589832 | tf_op jit(solution)/shard_map/ppermute | solution.py:34
  41.5 18.8 %copy-start.7 = (f32[2,128,128]{2,1,0:T(8,128)S(1)}, f32[2,128,128]{2,1,0:T(8,128)}, u32[]{:S(2)}) copy-start(f32[2,128,128]{2,1,0:T(8,128)} %bias_ref.1) | copy-start | bytes 393220
  41.5 18.8 %copy-start.8 = (f32[128,128]{1,0:T(8,128)S(1)}, f32[128,128]{1,0:T(8,128)}, u32[]{:S(2)}) copy-start(f32[128,128]{1,0:T(8,128)} %constant.7.clone.turned_ref) | copy-start | bytes 196612
  41.5 18.8 %copy-start.9 = (f32[128,128]{1,0:T(8,128)S(1)}, f32[128,128]{1,0:T(8,128)}, u32[]{:S(2)}) copy-start(f32[128,128]{1,0:T(8,128)} %constant.6.clone.hot_ref) | copy-start | bytes 196612
  41.5 14.2 %collective-permute-start.8 = (bf16[768,128]{1,0:T(8,128)(2,1)S(1)}, bf16[768,128]{1,0:T(8,128)(2,1)S(1)}, u32[]{:S(2)}, u32[]{:S(2)}) collective-permute-start(bf16[768,128]{1,0:T(8,128)(2,1)S(1)} %bitcast.32), channel_id=1, source_target_pairs={{0,3},{1,2},{2,1},{3,0},{4,7},{5,6},{6,5},{7,4},{8,11},{9,10},{10,... | collective-permute-start | bytes 589832 | tf_op jit(solution)/shard_map/ppermute | solution.py:34
  43.6 12.1 %collective-permute-start.7 = (bf16[768,128]{1,0:T(8,128)(2,1)S(1)}, bf16[768,128]{1,0:T(8,128)(2,1)S(1)}, u32[]{:S(2)}, u32[]{:S(2)}) collective-permute-start(bf16[768,128]{1,0:T(8,128)(2,1)S(1)} %bitcast.33), channel_id=1, source_target_pairs={{0,2},{1,3},{2,0},{3,1},{4,6},{5,7},{6,4},{7,5},{8,10},{9,11},{10,... | collective-permute-start | bytes 589832 | tf_op jit(solution)/shard_map/ppermute | solution.py:34
  48.3 9.9 %collective-permute-start.6 = (bf16[768,128]{1,0:T(8,128)(2,1)S(1)}, bf16[768,128]{1,0:T(8,128)(2,1)S(1)}, u32[]{:S(2)}, u32[]{:S(2)}) collective-permute-start(bf16[768,128]{1,0:T(8,128)(2,1)S(1)} %bitcast.34), channel_id=1, source_target_pairs={{0,1},{1,0},{2,3},{3,2},{4,5},{5,4},{6,7},{7,6},{8,9},{9,8},{10,11... | collective-permute-start | bytes 589832 | tf_op jit(solution)/shard_map/ppermute | solution.py:34
  51.5 45.4 %collective-permute-start.15 = (bf16[4096,256]{1,0:T(8,128)(2,1)S(1)}, bf16[4096,256]{1,0:T(8,128)(2,1)S(1)}, u32[]{:S(2)}, u32[]{:S(2)}) collective-permute-start(bf16[4096,256]{1,0:T(8,128)(2,1)S(1)} %copy-done), channel_id=1, source_target_pairs={{60,504},{61,505},{62,506},{63,507},{56,508},{57,509},{58,510},{59... | collective-permute-start | bytes 6291464 | tf_op jit(solution)/shard_map/ppermute | solution.py:61
  58.2 2.7 %copy-start.1 = (bf16[1024,3,128]{2,0,1:T(8,128)(2,1)S(1)}, bf16[1024,3,128]{2,0,1:T(8,128)(2,1)}, u32[]{:S(2)}) copy-start(bf16[1024,3,128]{2,0,1:T(8,128)(2,1)} %param.12) | copy-start | bytes 2359300
  58.2 2.7 %copy-start.5 = (f32[1024]{0:T(1024)S(1)}, f32[1024]{0:T(1024)}, u32[]{:S(2)}) copy-start(f32[1024]{0:T(1024)} %param.11) | copy-start | bytes 12292
  58.3 20.6 %collective-permute-start.13 = (bf16[2048,128]{1,0:T(8,128)(2,1)S(1)}, bf16[2048,128]{1,0:T(8,128)(2,1)S(1)}, u32[]{:S(2)}, u32[]{:S(2)}) collective-permute-start(bf16[2048,128]{1,0:T(8,128)(2,1)S(1)} %bitcast.23), channel_id=1, source_target_pairs={{0,16},{1,17},{2,18},{3,19},{4,20},{5,21},{6,22},{7,23},{8,24},{9,... | collective-permute-start | bytes 1572872 | tf_op jit(solution)/shard_map/ppermute | solution.py:34
  64.7 21.1 %collective-permute-start.12 = (bf16[528,128]{1,0:T(8,128)(2,1)S(1)}, bf16[528,128]{1,0:T(8,128)(2,1)S(1)}, u32[]{:S(2)}, u32[]{:S(2)}) collective-permute-start(bf16[528,128]{1,0:T(8,128)(2,1)S(1)} %pad_maximum_fusion), channel_id=1, source_target_pairs={{0,4},{1,5},{2,6},{3,7},{4,0},{5,1},{6,2},{7,3},{8,12},{9,13},{10,... | collective-permute-start | bytes 405512 | tf_op jit(solution)/shard_map/ppermute | solution.py:34
  71.7 9.9 %collective-permute-start.11 = (bf16[512,128]{1,0:T(8,128)(2,1)S(1)}, bf16[512,128]{1,0:T(8,128)(2,1)S(1)}, u32[]{:S(2)}, u32[]{:S(2)}) collective-permute-start(bf16[512,128]{1,0:T(8,128)(2,1)S(1)} %get-tuple-element.11.refs_0_), channel_id=1, source_target_pairs={{0,3},{1,2},{2,1},{3,0},{4,7},{5,6},{6,5},{7,4},{8,11},{9,10},{10,... | collective-permute-start | bytes 393224 | tf_op jit(solution)/shard_map/ppermute | solution.py:34
  74.7 9.1 %collective-permute-start.10 = (bf16[512,128]{1,0:T(8,128)(2,1)S(1)}, bf16[512,128]{1,0:T(8,128)(2,1)S(1)}, u32[]{:S(2)}, u32[]{:S(2)}) collective-permute-start(bf16[512,128]{1,0:T(8,128)(2,1)S(1)} %get-tuple-element.11.refs_0_), channel_id=1, source_target_pairs={{0,2},{1,3},{2,0},{3,1},{4,6},{5,7},{6,4},{7,5},{8,10},{9,11},{10,... | collective-permute-start | bytes 393224 | tf_op jit(solution)/shard_map/ppermute | solution.py:34
  78.9 6.9 %collective-permute-start.9 = (bf16[512,128]{1,0:T(8,128)(2,1)S(1)}, bf16[512,128]{1,0:T(8,128)(2,1)S(1)}, u32[]{:S(2)}, u32[]{:S(2)}) collective-permute-start(bf16[512,128]{1,0:T(8,128)(2,1)S(1)} %get-tuple-element.11.refs_0_), channel_id=1, source_target_pairs={{0,1},{1,0},{2,3},{3,2},{4,5},{5,4},{6,7},{7,6},{8,9},{9,8},{10,11... | collective-permute-start | bytes 393224 | tf_op jit(solution)/shard_map/ppermute | solution.py:34
  81.7 15.3 %copy-start.3 = (bf16[2,256,128]{2,1,0:T(8,128)(2,1)S(1)}, bf16[2,256,128]{2,1,0:T(8,128)(2,1)}, u32[]{:S(2)}) copy-start(bf16[2,256,128]{2,1,0:T(8,128)(2,1)} %constant.8.clone.refs_11_) | copy-start | bytes 393220
  81.7 15.3 %copy-start.4 = (f32[4096]{0:T(1024)S(1)}, f32[4096]{0:T(1024)}, u32[]{:S(2)}) copy-start(f32[4096]{0:T(1024)} %param.15) | copy-start | bytes 49156
  81.7 15.3 %collective-permute-start.14 = (bf16[4096,128]{1,0:T(8,128)(2,1)S(1)}, bf16[4096,128]{1,0:T(8,128)(2,1)S(1)}, u32[]{:S(2)}, u32[]{:S(2)}) collective-permute-start(bf16[4096,128]{1,0:T(8,128)(2,1)S(1)} %bitcast.19), channel_id=1, source_target_pairs={{0,8},{1,9},{2,10},{3,11},{4,12},{5,13},{6,14},{7,15},{8,0},{9,1},... | collective-permute-start | bytes 3145736 | tf_op jit(solution)/shard_map/ppermute | solution.py:34
  99.4 8.6 %collective-permute-start.16 = (bf16[128,128]{1,0:T(8,128)(2,1)S(1)}, bf16[128,128]{1,0:T(8,128)(2,1)S(1)}, u32[]{:S(2)}, u32[]{:S(2)}) collective-permute-start(bf16[128,128]{1,0:T(8,128)(2,1)S(1)} %get-tuple-element.13), channel_id=1, source_target_pairs={{0,8},{1,9},{2,10},{3,11},{4,12},{5,13},{6,14},{7,15},{8,16},{9,17... | collective-permute-start | bytes 98312 | tf_op jit(solution)/shard_map/ppermute | solution.py:58

commit v13 on v12

--- a/solution.py
+++ b/solution.py
@@ -314,7 +314,7 @@
     attended_around.append(
         lax.all_to_all(attended_partner, "head", 0, 0, axis_index_groups=[[0, 1, 2, 3], [4, 5, 6, 7]])
     )
-    w_quarter = joined([(place, TOKENS, TOKENS + 256) for place in around])
+    w_quarter = joined([(place, TOKENS, TOKENS + 256) for place in around], events=[bias])
     w_core = joined([(w_quarter, 0, 2048), (across_x(w_quarter, 1), 0, 2048)])
     w_shape = (2, 8, 2, BLOCK, BLOCK)
     merged = pl.pallas_call(

time: 110 us -> 112 us (1.018)
  waiting for transfers between devices: 16.2 us -> 18 us
    ppermute x14, waiting for transfers between devices: 9.58 us -> 11.4 us  [moved(): return lax.ppermute(value, BOTH, pairs)]
  transfers between devices with their start and end apart: 17 -> 17, of which waited for: 5 -> 6; matrix products, arithmetic and copies ran while one was open for 0% -> 0% of each run, Pallas kernels for 4% -> 4%
where the time goes in v13:
time: 112 us; the launch traced here: 110 us
  starting transfers between devices  70.9 us (63%)
  waiting for transfers between devices  18 us (16%)
  blocking collectives  11.2 us (10%)
  Pallas kernels  7.12 us (6%)
  local copies, waits for them, and re-layouts  1.91 us (2%)
    ppermute x14, starting transfers between devices, moved(): return lax.ppermute(value, BOTH, pairs)  55.1 us
    ppermute x1, starting transfers between devices, following_rows(): return lax.ppermute(value, BOTH, pairs)  13 us
    ppermute x14, waiting for transfers between devices, moved(): return lax.ppermute(value, BOTH, pairs)  11.4 us
    all_to_all x1, blocking collectives, on_device(): lax.all_to_all(attended_partner, 'head', 0, 0, axis_index_groups=[[0, 1,...  11.2 us
    ppermute x1, waiting for transfers between devices, lower_rows(): return lax.ppermute(value, BOTH, pairs)  6.63 us
    pallas_call x1, Pallas kernels, on_device(): pl.pallas_call(attention_kernel, out_shape=(jax.ShapeDtypeStruct((TOKENS,...  3.72 us
    pallas_call x1, Pallas kernels, on_device(): pl.pallas_call(merge_kernel, out_shape=jax.ShapeDtypeStruct((256, BLOCK),...  2.4 us
  transfers between devices with their start and end apart: 17, of which 6 were waited for; matrix products, arithmetic and copies ran while one was open for 0% of the time, Pallas kernels for 4%

profile of v13, /device:TPU:24, one launch (start us, length us, event | category | flops | bytes accessed | tf_op | source)
XLA Modules:
  0.0 110.2 jit_solution(14335045601350485964)
XLA Ops:
  0.0 0.9 copy-done.6
  0.9 0.2 order.1
  1.2 13.0 %collective-permute-start = (bf16[256,128]{1,0:T(8,128)(2,1)S(1)}, bf16[256,128]{1,0:T(8,128)(2,1)S(1)}, u32[]{:S(2)}, u32[]{:S(2)}) collective-permute-start(bf16[256,128]{1,0:T(8,128)(2,1)S(1)} %get-tuple-element.10), channel_id=1, source_target_pairs={{0,508},{1,509},{2,510},{3,511},{4,504},{5,505},{6,506},{7,507},{8... | collective-permute-start | bytes 196616 | tf_op jit(solution)/shard_map/ppermute | solution.py:51
  14.2 0.0 copy-start.2
  14.2 0.9 copy-done.2
  15.2 6.3 %collective-permute-start.4 = (bf16[512,128]{1,0:T(8,128)(2,1)S(1)}, bf16[512,128]{1,0:T(8,128)(2,1)S(1)}, u32[]{:S(2)}, u32[]{:S(2)}) collective-permute-start(bf16[512,128]{1,0:T(8,128)(2,1)S(1)} %piece.1.refs_0_.refs_2_), channel_id=1, source_target_pairs={{0,4},{1,5},{2,6},{3,7},{4,0},{5,1},{6,2},{7,3},{8,12},{9,13},{10,... | collective-permute-start | bytes 393224 | tf_op jit(solution)/shard_map/ppermute | solution.py:34
  21.5 0.0 collective-permute-done.refs_1_
  21.5 8.2 %collective-permute-start.5 = (bf16[256,128]{1,0:T(8,128)(2,1)S(1)}, bf16[256,128]{1,0:T(8,128)(2,1)S(1)}, u32[]{:S(2)}, u32[]{:S(2)}) collective-permute-start(bf16[256,128]{1,0:T(8,128)(2,1)S(1)} %collective-permute-done.refs_1_), channel_id=1, source_target_pairs={{0,4},{1,5},{2,6},{3,7},{4,0},{5,1},{6,2},{7,3},{8,12},{9,13},{10,... | collective-permute-start | bytes 196616 | tf_op jit(solution)/shard_map/ppermute | solution.py:34
  29.8 0.8 collective-permute-start.15
  30.6 0.0 copy-start.7
  30.6 0.0 copy-start.8
  30.6 0.0 copy-start.9
  30.6 2.3 %collective-permute-start.3 = (bf16[768,128]{1,0:T(8,128)(2,1)S(1)}, bf16[768,128]{1,0:T(8,128)(2,1)S(1)}, u32[]{:S(2)}, u32[]{:S(2)}) collective-permute-start(bf16[768,128]{1,0:T(8,128)(2,1)S(1)} %bitcast.25), channel_id=1, source_target_pairs={{0,3},{1,2},{2,1},{3,0},{4,7},{5,6},{6,5},{7,4},{8,11},{9,10},{10,... | collective-permute-start | bytes 589832 | tf_op jit(solution)/shard_map/ppermute | solution.py:34
  32.9 4.5 %collective-permute-start.2 = (bf16[768,128]{1,0:T(8,128)(2,1)S(1)}, bf16[768,128]{1,0:T(8,128)(2,1)S(1)}, u32[]{:S(2)}, u32[]{:S(2)}) collective-permute-start(bf16[768,128]{1,0:T(8,128)(2,1)S(1)} %bitcast.26), channel_id=1, source_target_pairs={{0,2},{1,3},{2,0},{3,1},{4,6},{5,7},{6,4},{7,5},{8,10},{9,11},{10,... | collective-permute-start | bytes 589832 | tf_op jit(solution)/shard_map/ppermute | solution.py:34
  37.4 4.1 %collective-permute-done.5.refs_1_ = bf16[256,128]{1,0:T(8,128)(2,1)S(1)} collective-permute-done((bf16[256,128]{1,0:T(8,128)(2,1)S(1)}, bf16[256,128]{1,0:T(8,128)(2,1)S(1)}, u32[]{:S(2)}, u32[]{:S(2)}) %collective-permute-start.5) | collective-permute-done | bytes 65568 | tf_op jit(solution)/shard_map/ppermute | solution.py:34
  41.5 2.6 %collective-permute-start.1 = (bf16[768,128]{1,0:T(8,128)(2,1)S(1)}, bf16[768,128]{1,0:T(8,128)(2,1)S(1)}, u32[]{:S(2)}, u32[]{:S(2)}) collective-permute-start(bf16[768,128]{1,0:T(8,128)(2,1)S(1)} %bitcast.27), channel_id=1, source_target_pairs={{0,1},{1,0},{2,3},{3,2},{4,5},{5,4},{6,7},{7,6},{8,9},{9,8},{10,11... | collective-permute-start | bytes 589832 | tf_op jit(solution)/shard_map/ppermute | solution.py:34
  44.1 0.0 collective-permute-done.4.refs_0_.refs_2_
  44.1 3.0 %collective-permute-start.8 = (bf16[768,128]{1,0:T(8,128)(2,1)S(1)}, bf16[768,128]{1,0:T(8,128)(2,1)S(1)}, u32[]{:S(2)}, u32[]{:S(2)}) collective-permute-start(bf16[768,128]{1,0:T(8,128)(2,1)S(1)} %bitcast.32), channel_id=1, source_target_pairs={{0,3},{1,2},{2,1},{3,0},{4,7},{5,6},{6,5},{7,4},{8,11},{9,10},{10,... | collective-permute-start | bytes 589832 | tf_op jit(solution)/shard_map/ppermute | solution.py:34
  47.1 0.0 collective-permute-done.3.refs_3_
  47.1 4.2 %collective-permute-start.7 = (bf16[768,128]{1,0:T(8,128)(2,1)S(1)}, bf16[768,128]{1,0:T(8,128)(2,1)S(1)}, u32[]{:S(2)}, u32[]{:S(2)}) collective-permute-start(bf16[768,128]{1,0:T(8,128)(2,1)S(1)} %bitcast.33), channel_id=1, source_target_pairs={{0,2},{1,3},{2,0},{3,1},{4,6},{5,7},{6,4},{7,5},{8,10},{9,11},{10,... | collective-permute-start | bytes 589832 | tf_op jit(solution)/shard_map/ppermute | solution.py:34
  51.3 2.7 %collective-permute-start.6 = (bf16[768,128]{1,0:T(8,128)(2,1)S(1)}, bf16[768,128]{1,0:T(8,128)(2,1)S(1)}, u32[]{:S(2)}, u32[]{:S(2)}) collective-permute-start(bf16[768,128]{1,0:T(8,128)(2,1)S(1)} %bitcast.34), channel_id=1, source_target_pairs={{0,1},{1,0},{2,3},{3,2},{4,5},{5,4},{6,7},{7,6},{8,9},{9,8},{10,11... | collective-permute-start | bytes 589832 | tf_op jit(solution)/shard_map/ppermute | solution.py:34
  54.0 0.5 bias.1.refs_10_.refs_8_
  54.6 0.0 copy-start.1
  54.6 0.0 copy-start.5
  54.6 0.0 collective-permute-done.1.refs_1_
  54.6 3.0 %collective-permute-done.8.refs_7_ = bf16[768,128]{1,0:T(8,128)(2,1)S(1)} collective-permute-done((bf16[768,128]{1,0:T(8,128)(2,1)S(1)}, bf16[768,128]{1,0:T(8,128)(2,1)S(1)}, u32[]{:S(2)}, u32[]{:S(2)}) %collective-permute-start.8) | collective-permute-done | bytes 196640 | tf_op jit(solution)/shard_map/ppermute | solution.py:34
  57.6 0.6 collective-permute-done.7.refs_6_
  58.2 2.3 %collective-permute-done.6.refs_5_ = bf16[768,128]{1,0:T(8,128)(2,1)S(1)} collective-permute-done((bf16[768,128]{1,0:T(8,128)(2,1)S(1)}, bf16[768,128]{1,0:T(8,128)(2,1)S(1)}, u32[]{:S(2)}, u32[]{:S(2)}) %collective-permute-start.6) | collective-permute-done | bytes 196640 | tf_op jit(solution)/shard_map/ppermute | solution.py:34
  60.5 2.1 %collective-permute-start.13 = (bf16[2048,128]{1,0:T(8,128)(2,1)S(1)}, bf16[2048,128]{1,0:T(8,128)(2,1)S(1)}, u32[]{:S(2)}, u32[]{:S(2)}) collective-permute-start(bf16[2048,128]{1,0:T(8,128)(2,1)S(1)} %bitcast.21), channel_id=1, source_target_pairs={{0,16},{1,17},{2,18},{3,19},{4,20},{5,21},{6,22},{7,23},{8,24},{9,... | collective-permute-start | bytes 1572872 | tf_op jit(solution)/shard_map/ppermute | solution.py:34
  62.6 3.7 %attention.1 = (bf16[512,128]{1,0:T(8,128)(2,1)S(1)}, bf16[8,512,128]{2,1,0:T(8,128)(2,1)S(1)}) custom-call(bf16[768,128]{1,0:T(8,128)(2,1)S(1)} %bitcast.29, bf16[768,128]{1,0:T(8,128)(2,1)S(1)} %collective-permute-done.1.refs_1_, bf16[768,128]{1,0:T(8,128)(2,1)S(1)} %collective-permute-done.2.refs_2_, bf16[768,128]{1,0:T(8,128)(2,1)S(1)} %collective-permute-done.3.refs_3_, ...), custom_call_target="tpu_custom_call" | custom-call | flops 600000000 | bytes 3000000 | tf_op jit(solution)/shard_map/attention/pallas_call | solution.py:298
  66.4 7.3 %collective-permute-start.12 = (bf16[528,128]{1,0:T(8,128)(2,1)S(1)}, bf16[528,128]{1,0:T(8,128)(2,1)S(1)}, u32[]{:S(2)}, u32[]{:S(2)}) collective-permute-start(bf16[528,128]{1,0:T(8,128)(2,1)S(1)} %pad_maximum_fusion), channel_id=1, source_target_pairs={{0,4},{1,5},{2,6},{3,7},{4,0},{5,1},{6,2},{7,3},{8,12},{9,13},{10,... | collective-permute-start | bytes 405512 | tf_op jit(solution)/shard_map/ppermute | solution.py:34
  73.7 2.8 %collective-permute-start.11 = (bf16[512,128]{1,0:T(8,128)(2,1)S(1)}, bf16[512,128]{1,0:T(8,128)(2,1)S(1)}, u32[]{:S(2)}, u32[]{:S(2)}) collective-permute-start(bf16[512,128]{1,0:T(8,128)(2,1)S(1)} %get-tuple-element.11.refs_0_), channel_id=1, source_target_pairs={{0,3},{1,2},{2,1},{3,0},{4,7},{5,6},{6,5},{7,4},{8,11},{9,10},{10,... | collective-permute-start | bytes 393224 | tf_op jit(solution)/shard_map/ppermute | solution.py:34
  76.6 3.8 %collective-permute-start.10 = (bf16[512,128]{1,0:T(8,128)(2,1)S(1)}, bf16[512,128]{1,0:T(8,128)(2,1)S(1)}, u32[]{:S(2)}, u32[]{:S(2)}) collective-permute-start(bf16[512,128]{1,0:T(8,128)(2,1)S(1)} %get-tuple-element.11.refs_0_), channel_id=1, source_target_pairs={{0,2},{1,3},{2,0},{3,1},{4,6},{5,7},{6,4},{7,5},{8,10},{9,11},{10,... | collective-permute-start | bytes 393224 | tf_op jit(solution)/shard_map/ppermute | solution.py:34
  80.4 0.0 collective-permute-done.13.refs_1_
  80.4 3.2 %collective-permute-start.9 = (bf16[512,128]{1,0:T(8,128)(2,1)S(1)}, bf16[512,128]{1,0:T(8,128)(2,1)S(1)}, u32[]{:S(2)}, u32[]{:S(2)}) collective-permute-start(bf16[512,128]{1,0:T(8,128)(2,1)S(1)} %get-tuple-element.11.refs_0_), channel_id=1, source_target_pairs={{0,1},{1,0},{2,3},{3,2},{4,5},{5,4},{6,7},{7,6},{8,9},{9,8},{10,11... | collective-permute-start | bytes 393224 | tf_op jit(solution)/shard_map/ppermute | solution.py:34
  83.6 0.1 join.9
  83.7 0.0 copy-start.3
  83.7 0.0 copy-start.4
  83.7 2.1 %collective-permute-start.14 = (bf16[4096,128]{1,0:T(8,128)(2,1)S(1)}, bf16[4096,128]{1,0:T(8,128)(2,1)S(1)}, u32[]{:S(2)}, u32[]{:S(2)}) collective-permute-start(bf16[4096,128]{1,0:T(8,128)(2,1)S(1)} %bitcast.19), channel_id=1, source_target_pairs={{0,8},{1,9},{2,10},{3,11},{4,12},{5,13},{6,14},{7,15},{8,0},{9,1},... | collective-permute-start | bytes 3145736 | tf_op jit(solution)/shard_map/ppermute | solution.py:34
  85.8 1.5 %collective-permute-done.9.refs_1_ = bf16[512,128]{1,0:T(8,128)(2,1)S(1)} collective-permute-done((bf16[512,128]{1,0:T(8,128)(2,1)S(1)}, bf16[512,128]{1,0:T(8,128)(2,1)S(1)}, u32[]{:S(2)}, u32[]{:S(2)}) %collective-permute-start.9) | collective-permute-done | bytes 131104 | tf_op jit(solution)/shard_map/ppermute | solution.py:34
  87.3 0.0 collective-permute-done.12.refs_0_
  87.3 0.1 join.7
  87.3 11.2 %all_to_all.5.refs_4_ = bf16[4,512,128]{2,1,0:T(8,128)(2,1)S(1)} all-to-all(bf16[4,512,128]{2,1,0:T(8,128)(2,1)S(1)} %join.7), channel_id=1, replica_groups={{0,1,2,3},{4,5,6,7},{8,9,10,11},{12,13,14,15},{16,17,18,19},{20,21,22,2..., dimensions={0} | all-to-all | bytes 1048576 | tf_op jit(solution)/shard_map/all_to_all | solution.py:315
  98.6 0.0 collective-permute-done.15
  98.6 2.4 %merge.1 = bf16[256,128]{1,0:T(8,128)(2,1)S(1)} custom-call(bf16[512,128]{1,0:T(8,128)(2,1)S(1)} %get-tuple-element.11.refs_0_, bf16[512,128]{1,0:T(8,128)(2,1)S(1)} %collective-permute-done.9.refs_1_, bf16[512,128]{1,0:T(8,128)(2,1)S(1)} %collective-permute-done.10.refs_2_, bf16[512,128]{1,0:T(8,128)(2,1)S(1)} %collective-permute-done.11.refs_3_, ...), custom_call_target="tpu_custom_call" | custom-call | flops 1400000000 | bytes 7000000 | tf_op jit(solution)/shard_map/merge/pallas_call | solution.py:320
  101.0 1.9 %collective-permute-start.16 = (bf16[128,128]{1,0:T(8,128)(2,1)S(1)}, bf16[128,128]{1,0:T(8,128)(2,1)S(1)}, u32[]{:S(2)}, u32[]{:S(2)}) collective-permute-start(bf16[128,128]{1,0:T(8,128)(2,1)S(1)} %get-tuple-element.13), channel_id=1, source_target_pairs={{0,8},{1,9},{2,10},{3,11},{4,12},{5,13},{6,14},{7,15},{8,16},{9,17... | collective-permute-start | bytes 98312 | tf_op jit(solution)/shard_map/ppermute | solution.py:58
  103.0 6.6 %collective-permute-done.16 = bf16[128,128]{1,0:T(8,128)(2,1)S(1)} collective-permute-done((bf16[128,128]{1,0:T(8,128)(2,1)S(1)}, bf16[128,128]{1,0:T(8,128)(2,1)S(1)}, u32[]{:S(2)}, u32[]{:S(2)}) %collective-permute-start.16) | collective-permute-done | bytes 32800 | tf_op jit(solution)/shard_map/ppermute | solution.py:58
  109.6 0.6 pad_maximum_fusion.1
  (21 shorter events, 0.1 us)
Async XLA Ops:
  0.0 0.9 copy-start.6
  1.2 20.4 %collective-permute-start = (bf16[256,128]{1,0:T(8,128)(2,1)S(1)}, bf16[256,128]{1,0:T(8,128)(2,1)S(1)}, u32[]{:S(2)}, u32[]{:S(2)}) collective-permute-start(bf16[256,128]{1,0:T(8,128)(2,1)S(1)} %get-tuple-element.10), channel_id=1, source_target_pairs={{0,508},{1,509},{2,510},{3,511},{4,504},{5,505},{6,506},{7,507},{8... | collective-permute-start | bytes 196616 | tf_op jit(solution)/shard_map/ppermute | solution.py:51
  14.2 1.0 copy-start.2
  15.2 28.9 %collective-permute-start.4 = (bf16[512,128]{1,0:T(8,128)(2,1)S(1)}, bf16[512,128]{1,0:T(8,128)(2,1)S(1)}, u32[]{:S(2)}, u32[]{:S(2)}) collective-permute-start(bf16[512,128]{1,0:T(8,128)(2,1)S(1)} %piece.1.refs_0_.refs_2_), channel_id=1, source_target_pairs={{0,4},{1,5},{2,6},{3,7},{4,0},{5,1},{6,2},{7,3},{8,12},{9,13},{10,... | collective-permute-start | bytes 393224 | tf_op jit(solution)/shard_map/ppermute | solution.py:34
  21.5 19.9 %collective-permute-start.5 = (bf16[256,128]{1,0:T(8,128)(2,1)S(1)}, bf16[256,128]{1,0:T(8,128)(2,1)S(1)}, u32[]{:S(2)}, u32[]{:S(2)}) collective-permute-start(bf16[256,128]{1,0:T(8,128)(2,1)S(1)} %collective-permute-done.refs_1_), channel_id=1, source_target_pairs={{0,4},{1,5},{2,6},{3,7},{4,0},{5,1},{6,2},{7,3},{8,12},{9,13},{10,... | collective-permute-start | bytes 196616 | tf_op jit(solution)/shard_map/ppermute | solution.py:34
  29.8 68.8 %collective-permute-start.15 = (bf16[4096,256]{1,0:T(8,128)(2,1)}, bf16[4096,256]{1,0:T(8,128)(2,1)S(1)}, u32[]{:S(2)}, u32[]{:S(2)}) collective-permute-start(bf16[4096,256]{1,0:T(8,128)(2,1)} %param.16), channel_id=1, source_target_pairs={{60,504},{61,505},{62,506},{63,507},{56,508},{57,509},{58,510},{59... | collective-permute-start | bytes 6291464 | tf_op jit(solution)/shard_map/ppermute | solution.py:61
  30.6 23.4 %copy-start.7 = (f32[2,128,128]{2,1,0:T(8,128)S(1)}, f32[2,128,128]{2,1,0:T(8,128)}, u32[]{:S(2)}) copy-start(f32[2,128,128]{2,1,0:T(8,128)} %bias_ref.1) | copy-start | bytes 393220
  30.6 23.4 %copy-start.8 = (f32[128,128]{1,0:T(8,128)S(1)}, f32[128,128]{1,0:T(8,128)}, u32[]{:S(2)}) copy-start(f32[128,128]{1,0:T(8,128)} %constant.7.clone.turned_ref) | copy-start | bytes 196612
  30.6 23.4 %copy-start.9 = (f32[128,128]{1,0:T(8,128)S(1)}, f32[128,128]{1,0:T(8,128)}, u32[]{:S(2)}) copy-start(f32[128,128]{1,0:T(8,128)} %constant.6.clone.hot_ref) | copy-start | bytes 196612
  30.6 16.5 %collective-permute-start.3 = (bf16[768,128]{1,0:T(8,128)(2,1)S(1)}, bf16[768,128]{1,0:T(8,128)(2,1)S(1)}, u32[]{:S(2)}, u32[]{:S(2)}) collective-permute-start(bf16[768,128]{1,0:T(8,128)(2,1)S(1)} %bitcast.25), channel_id=1, source_target_pairs={{0,3},{1,2},{2,1},{3,0},{4,7},{5,6},{6,5},{7,4},{8,11},{9,10},{10,... | collective-permute-start | bytes 589832 | tf_op jit(solution)/shard_map/ppermute | solution.py:34
  32.9 18.4 %collective-permute-start.2 = (bf16[768,128]{1,0:T(8,128)(2,1)S(1)}, bf16[768,128]{1,0:T(8,128)(2,1)S(1)}, u32[]{:S(2)}, u32[]{:S(2)}) collective-permute-start(bf16[768,128]{1,0:T(8,128)(2,1)S(1)} %bitcast.26), channel_id=1, source_target_pairs={{0,2},{1,3},{2,0},{3,1},{4,6},{5,7},{6,4},{7,5},{8,10},{9,11},{10,... | collective-permute-start | bytes 589832 | tf_op jit(solution)/shard_map/ppermute | solution.py:34
  41.5 13.1 %collective-permute-start.1 = (bf16[768,128]{1,0:T(8,128)(2,1)S(1)}, bf16[768,128]{1,0:T(8,128)(2,1)S(1)}, u32[]{:S(2)}, u32[]{:S(2)}) collective-permute-start(bf16[768,128]{1,0:T(8,128)(2,1)S(1)} %bitcast.27), channel_id=1, source_target_pairs={{0,1},{1,0},{2,3},{3,2},{4,5},{5,4},{6,7},{7,6},{8,9},{9,8},{10,11... | collective-permute-start | bytes 589832 | tf_op jit(solution)/shard_map/ppermute | solution.py:34
  44.1 13.5 %collective-permute-start.8 = (bf16[768,128]{1,0:T(8,128)(2,1)S(1)}, bf16[768,128]{1,0:T(8,128)(2,1)S(1)}, u32[]{:S(2)}, u32[]{:S(2)}) collective-permute-start(bf16[768,128]{1,0:T(8,128)(2,1)S(1)} %bitcast.32), channel_id=1, source_target_pairs={{0,3},{1,2},{2,1},{3,0},{4,7},{5,6},{6,5},{7,4},{8,11},{9,10},{10,... | collective-permute-start | bytes 589832 | tf_op jit(solution)/shard_map/ppermute | solution.py:34
  47.1 11.1 %collective-permute-start.7 = (bf16[768,128]{1,0:T(8,128)(2,1)S(1)}, bf16[768,128]{1,0:T(8,128)(2,1)S(1)}, u32[]{:S(2)}, u32[]{:S(2)}) collective-permute-start(bf16[768,128]{1,0:T(8,128)(2,1)S(1)} %bitcast.33), channel_id=1, source_target_pairs={{0,2},{1,3},{2,0},{3,1},{4,6},{5,7},{6,4},{7,5},{8,10},{9,11},{10,... | collective-permute-start | bytes 589832 | tf_op jit(solution)/shard_map/ppermute | solution.py:34
  51.3 9.1 %collective-permute-start.6 = (bf16[768,128]{1,0:T(8,128)(2,1)S(1)}, bf16[768,128]{1,0:T(8,128)(2,1)S(1)}, u32[]{:S(2)}, u32[]{:S(2)}) collective-permute-start(bf16[768,128]{1,0:T(8,128)(2,1)S(1)} %bitcast.34), channel_id=1, source_target_pairs={{0,1},{1,0},{2,3},{3,2},{4,5},{5,4},{6,7},{7,6},{8,9},{9,8},{10,11... | collective-permute-start | bytes 589832 | tf_op jit(solution)/shard_map/ppermute | solution.py:34
  54.6 8.1 %copy-start.1 = (bf16[1024,3,128]{2,0,1:T(8,128)(2,1)S(1)}, bf16[1024,3,128]{2,0,1:T(8,128)(2,1)}, u32[]{:S(2)}) copy-start(bf16[1024,3,128]{2,0,1:T(8,128)(2,1)} %param.12) | copy-start | bytes 2359300
  54.6 8.1 %copy-start.5 = (f32[1024]{0:T(1024)S(1)}, f32[1024]{0:T(1024)}, u32[]{:S(2)}) copy-start(f32[1024]{0:T(1024)} %param.11) | copy-start | bytes 12292
  60.5 19.9 %collective-permute-start.13 = (bf16[2048,128]{1,0:T(8,128)(2,1)S(1)}, bf16[2048,128]{1,0:T(8,128)(2,1)S(1)}, u32[]{:S(2)}, u32[]{:S(2)}) collective-permute-start(bf16[2048,128]{1,0:T(8,128)(2,1)S(1)} %bitcast.21), channel_id=1, source_target_pairs={{0,16},{1,17},{2,18},{3,19},{4,20},{5,21},{6,22},{7,23},{8,24},{9,... | collective-permute-start | bytes 1572872 | tf_op jit(solution)/shard_map/ppermute | solution.py:34
  66.4 20.8 %collective-permute-start.12 = (bf16[528,128]{1,0:T(8,128)(2,1)S(1)}, bf16[528,128]{1,0:T(8,128)(2,1)S(1)}, u32[]{:S(2)}, u32[]{:S(2)}) collective-permute-start(bf16[528,128]{1,0:T(8,128)(2,1)S(1)} %pad_maximum_fusion), channel_id=1, source_target_pairs={{0,4},{1,5},{2,6},{3,7},{4,0},{5,1},{6,2},{7,3},{8,12},{9,13},{10,... | collective-permute-start | bytes 405512 | tf_op jit(solution)/shard_map/ppermute | solution.py:34
  73.7 9.9 %collective-permute-start.11 = (bf16[512,128]{1,0:T(8,128)(2,1)S(1)}, bf16[512,128]{1,0:T(8,128)(2,1)S(1)}, u32[]{:S(2)}, u32[]{:S(2)}) collective-permute-start(bf16[512,128]{1,0:T(8,128)(2,1)S(1)} %get-tuple-element.11.refs_0_), channel_id=1, source_target_pairs={{0,3},{1,2},{2,1},{3,0},{4,7},{5,6},{6,5},{7,4},{8,11},{9,10},{10,... | collective-permute-start | bytes 393224 | tf_op jit(solution)/shard_map/ppermute | solution.py:34
  76.6 9.2 %collective-permute-start.10 = (bf16[512,128]{1,0:T(8,128)(2,1)S(1)}, bf16[512,128]{1,0:T(8,128)(2,1)S(1)}, u32[]{:S(2)}, u32[]{:S(2)}) collective-permute-start(bf16[512,128]{1,0:T(8,128)(2,1)S(1)} %get-tuple-element.11.refs_0_), channel_id=1, source_target_pairs={{0,2},{1,3},{2,0},{3,1},{4,6},{5,7},{6,4},{7,5},{8,10},{9,11},{10,... | collective-permute-start | bytes 393224 | tf_op jit(solution)/shard_map/ppermute | solution.py:34
  80.4 6.9 %collective-permute-start.9 = (bf16[512,128]{1,0:T(8,128)(2,1)S(1)}, bf16[512,128]{1,0:T(8,128)(2,1)S(1)}, u32[]{:S(2)}, u32[]{:S(2)}) collective-permute-start(bf16[512,128]{1,0:T(8,128)(2,1)S(1)} %get-tuple-element.11.refs_0_), channel_id=1, source_target_pairs={{0,1},{1,0},{2,3},{3,2},{4,5},{5,4},{6,7},{7,6},{8,9},{9,8},{10,11... | collective-permute-start | bytes 393224 | tf_op jit(solution)/shard_map/ppermute | solution.py:34
  83.7 14.9 %copy-start.3 = (bf16[2,256,128]{2,1,0:T(8,128)(2,1)S(1)}, bf16[2,256,128]{2,1,0:T(8,128)(2,1)}, u32[]{:S(2)}) copy-start(bf16[2,256,128]{2,1,0:T(8,128)(2,1)} %constant.8.clone.refs_11_) | copy-start | bytes 393220
  83.7 14.9 %copy-start.4 = (f32[4096]{0:T(1024)S(1)}, f32[4096]{0:T(1024)}, u32[]{:S(2)}) copy-start(f32[4096]{0:T(1024)} %param.15) | copy-start | bytes 49156
  83.7 14.9 %collective-permute-start.14 = (bf16[4096,128]{1,0:T(8,128)(2,1)S(1)}, bf16[4096,128]{1,0:T(8,128)(2,1)S(1)}, u32[]{:S(2)}, u32[]{:S(2)}) collective-permute-start(bf16[4096,128]{1,0:T(8,128)(2,1)S(1)} %bitcast.19), channel_id=1, source_target_pairs={{0,8},{1,9},{2,10},{3,11},{4,12},{5,13},{6,14},{7,15},{8,0},{9,1},... | collective-permute-start | bytes 3145736 | tf_op jit(solution)/shard_map/ppermute | solution.py:34
  87.3 11.3 %copy-start = (bf16[4096,256]{1,0:T(8,128)(2,1)S(1)}, bf16[4096,256]{1,0:T(8,128)(2,1)}, u32[]{:S(2)}) copy-start(bf16[4096,256]{1,0:T(8,128)(2,1)} %param.16) | copy-start | bytes 6291460
  101.0 8.6 %collective-permute-start.16 = (bf16[128,128]{1,0:T(8,128)(2,1)S(1)}, bf16[128,128]{1,0:T(8,128)(2,1)S(1)}, u32[]{:S(2)}, u32[]{:S(2)}) collective-permute-start(bf16[128,128]{1,0:T(8,128)(2,1)S(1)} %get-tuple-element.13), channel_id=1, source_target_pairs={{0,8},{1,9},{2,10},{3,11},{4,12},{5,13},{6,14},{7,15},{8,16},{9,17... | collective-permute-start | bytes 98312 | tf_op jit(solution)/shard_map/ppermute | solution.py:58

commit v14 on v12

--- a/solution.py
+++ b/solution.py
@@ -86,7 +86,8 @@
     return result if copies > 1 else result[0]
 
 def along_y(value):
-    return [value] + [across(value, bits) for bits in (1, 2, 3)]
+    near, far_side, two_away = [across(value, bits) for bits in (1, 3, 2)]
+    return [value, near, two_away, far_side]
 
 def order_kernel(rows_ref, first_ref, behind_ref):
     place = lax.broadcasted_iota(jnp.int32, (HALF, HALF), 0)

time: 110 us -> 110 us (level)
  no operation moved by 1% of the time
where the time goes in v14:
time: 110 us; the launch traced here: 109 us
  starting transfers between devices  71.2 us (65%)
  waiting for transfers between devices  16.2 us (15%)
  blocking collectives  11.1 us (10%)
  Pallas kernels  7.12 us (6%)
  local copies, waits for them, and re-layouts  1.91 us (2%)
    ppermute x14, starting transfers between devices, moved(): return lax.ppermute(value, BOTH, pairs)  55.4 us
    ppermute x1, starting transfers between devices, following_rows(): return lax.ppermute(value, BOTH, pairs)  13 us
    all_to_all x1, blocking collectives, on_device(): lax.all_to_all(attended_partner, 'head', 0, 0, axis_index_groups=[[0, 1,...  11.1 us
    ppermute x14, waiting for transfers between devices, moved(): return lax.ppermute(value, BOTH, pairs)  9.58 us
    ppermute x1, waiting for transfers between devices, lower_rows(): return lax.ppermute(value, BOTH, pairs)  6.63 us
    pallas_call x1, Pallas kernels, on_device(): pl.pallas_call(attention_kernel, out_shape=(jax.ShapeDtypeStruct((TOKENS,...  3.73 us
    pallas_call x1, Pallas kernels, on_device(): pl.pallas_call(merge_kernel, out_shape=jax.ShapeDtypeStruct((256, BLOCK),...  2.39 us
  transfers between devices with their start and end apart: 17, of which 5 were waited for; matrix products, arithmetic and copies ran while one was open for 0% of the time, Pallas kernels for 4%

profile of v14, /device:TPU:24, one launch (start us, length us, event | category | flops | bytes accessed | tf_op | source)
XLA Modules:
  0.0 108.6 jit_solution(10221436070429347820)
XLA Ops:
  0.0 0.9 copy-done.6
  0.9 0.2 order.1
  1.2 13.0 %collective-permute-start = (bf16[256,128]{1,0:T(8,128)(2,1)S(1)}, bf16[256,128]{1,0:T(8,128)(2,1)S(1)}, u32[]{:S(2)}, u32[]{:S(2)}) collective-permute-start(bf16[256,128]{1,0:T(8,128)(2,1)S(1)} %get-tuple-element.10), channel_id=1, source_target_pairs={{0,508},{1,509},{2,510},{3,511},{4,504},{5,505},{6,506},{7,507},{8... | collective-permute-start | bytes 196616 | tf_op jit(solution)/shard_map/ppermute | solution.py:51
  14.2 0.0 copy-start.2
  14.2 0.9 copy-done.2
  15.2 6.3 %collective-permute-start.4 = (bf16[512,128]{1,0:T(8,128)(2,1)S(1)}, bf16[512,128]{1,0:T(8,128)(2,1)S(1)}, u32[]{:S(2)}, u32[]{:S(2)}) collective-permute-start(bf16[512,128]{1,0:T(8,128)(2,1)S(1)} %piece.1.refs_0_.refs_2_), channel_id=1, source_target_pairs={{0,4},{1,5},{2,6},{3,7},{4,0},{5,1},{6,2},{7,3},{8,12},{9,13},{10,... | collective-permute-start | bytes 393224 | tf_op jit(solution)/shard_map/ppermute | solution.py:34
  21.5 0.0 collective-permute-done.refs_1_
  21.5 8.2 %collective-permute-start.5 = (bf16[256,128]{1,0:T(8,128)(2,1)S(1)}, bf16[256,128]{1,0:T(8,128)(2,1)S(1)}, u32[]{:S(2)}, u32[]{:S(2)}) collective-permute-start(bf16[256,128]{1,0:T(8,128)(2,1)S(1)} %collective-permute-done.refs_1_), channel_id=1, source_target_pairs={{0,4},{1,5},{2,6},{3,7},{4,0},{5,1},{6,2},{7,3},{8,12},{9,13},{10,... | collective-permute-start | bytes 196616 | tf_op jit(solution)/shard_map/ppermute | solution.py:34
  29.8 0.0 copy-start
  29.8 2.3 %collective-permute-start.3 = (bf16[768,128]{1,0:T(8,128)(2,1)S(1)}, bf16[768,128]{1,0:T(8,128)(2,1)S(1)}, u32[]{:S(2)}, u32[]{:S(2)}) collective-permute-start(bf16[768,128]{1,0:T(8,128)(2,1)S(1)} %bitcast.25), channel_id=1, source_target_pairs={{0,3},{1,2},{2,1},{3,0},{4,7},{5,6},{6,5},{7,4},{8,11},{9,10},{10,... | collective-permute-start | bytes 589832 | tf_op jit(solution)/shard_map/ppermute | solution.py:34
  32.1 4.5 %collective-permute-start.2 = (bf16[768,128]{1,0:T(8,128)(2,1)S(1)}, bf16[768,128]{1,0:T(8,128)(2,1)S(1)}, u32[]{:S(2)}, u32[]{:S(2)}) collective-permute-start(bf16[768,128]{1,0:T(8,128)(2,1)S(1)} %bitcast.26), channel_id=1, source_target_pairs={{0,2},{1,3},{2,0},{3,1},{4,6},{5,7},{6,4},{7,5},{8,10},{9,11},{10,... | collective-permute-start | bytes 589832 | tf_op jit(solution)/shard_map/ppermute | solution.py:34
  36.6 3.2 %collective-permute-start.1 = (bf16[768,128]{1,0:T(8,128)(2,1)S(1)}, bf16[768,128]{1,0:T(8,128)(2,1)S(1)}, u32[]{:S(2)}, u32[]{:S(2)}) collective-permute-start(bf16[768,128]{1,0:T(8,128)(2,1)S(1)} %bitcast.27), channel_id=1, source_target_pairs={{0,1},{1,0},{2,3},{3,2},{4,5},{5,4},{6,7},{7,6},{8,9},{9,8},{10,11... | collective-permute-start | bytes 589832 | tf_op jit(solution)/shard_map/ppermute | solution.py:34
  39.8 1.7 %collective-permute-done.5.refs_1_ = bf16[256,128]{1,0:T(8,128)(2,1)S(1)} collective-permute-done((bf16[256,128]{1,0:T(8,128)(2,1)S(1)}, bf16[256,128]{1,0:T(8,128)(2,1)S(1)}, u32[]{:S(2)}, u32[]{:S(2)}) %collective-permute-start.5) | collective-permute-done | bytes 65568 | tf_op jit(solution)/shard_map/ppermute | solution.py:34
  41.5 0.0 collective-permute-done.4.refs_0_.refs_2_
  41.5 0.0 copy-start.7
  41.5 0.0 copy-start.8
  41.5 0.0 copy-start.9
  41.5 2.1 %collective-permute-start.8 = (bf16[768,128]{1,0:T(8,128)(2,1)S(1)}, bf16[768,128]{1,0:T(8,128)(2,1)S(1)}, u32[]{:S(2)}, u32[]{:S(2)}) collective-permute-start(bf16[768,128]{1,0:T(8,128)(2,1)S(1)} %bitcast.32), channel_id=1, source_target_pairs={{0,3},{1,2},{2,1},{3,0},{4,7},{5,6},{6,5},{7,4},{8,11},{9,10},{10,... | collective-permute-start | bytes 589832 | tf_op jit(solution)/shard_map/ppermute | solution.py:34
  43.6 4.7 %collective-permute-start.7 = (bf16[768,128]{1,0:T(8,128)(2,1)S(1)}, bf16[768,128]{1,0:T(8,128)(2,1)S(1)}, u32[]{:S(2)}, u32[]{:S(2)}) collective-permute-start(bf16[768,128]{1,0:T(8,128)(2,1)S(1)} %bitcast.33), channel_id=1, source_target_pairs={{0,2},{1,3},{2,0},{3,1},{4,6},{5,7},{6,4},{7,5},{8,10},{9,11},{10,... | collective-permute-start | bytes 589832 | tf_op jit(solution)/shard_map/ppermute | solution.py:34
  48.3 0.0 collective-permute-done.3.refs_3_
  48.3 3.2 %collective-permute-start.6 = (bf16[768,128]{1,0:T(8,128)(2,1)S(1)}, bf16[768,128]{1,0:T(8,128)(2,1)S(1)}, u32[]{:S(2)}, u32[]{:S(2)}) collective-permute-start(bf16[768,128]{1,0:T(8,128)(2,1)S(1)} %bitcast.34), channel_id=1, source_target_pairs={{0,1},{1,0},{2,3},{3,2},{4,5},{5,4},{6,7},{7,6},{8,9},{9,8},{10,11... | collective-permute-start | bytes 589832 | tf_op jit(solution)/shard_map/ppermute | solution.py:34
  51.5 0.8 collective-permute-start.15
  52.3 0.0 collective-permute-done.1.refs_1_
  52.3 3.4 %collective-permute-done.8.refs_7_ = bf16[768,128]{1,0:T(8,128)(2,1)S(1)} collective-permute-done((bf16[768,128]{1,0:T(8,128)(2,1)S(1)}, bf16[768,128]{1,0:T(8,128)(2,1)S(1)}, u32[]{:S(2)}, u32[]{:S(2)}) %collective-permute-start.8) | collective-permute-done | bytes 196640 | tf_op jit(solution)/shard_map/ppermute | solution.py:34
  55.7 2.5 %collective-permute-done.6.refs_5_ = bf16[768,128]{1,0:T(8,128)(2,1)S(1)} collective-permute-done((bf16[768,128]{1,0:T(8,128)(2,1)S(1)}, bf16[768,128]{1,0:T(8,128)(2,1)S(1)}, u32[]{:S(2)}, u32[]{:S(2)}) %collective-permute-start.6) | collective-permute-done | bytes 196640 | tf_op jit(solution)/shard_map/ppermute | solution.py:34
  58.2 0.0 copy-start.1
  58.2 0.0 copy-start.5
  58.3 2.1 %collective-permute-start.13 = (bf16[2048,128]{1,0:T(8,128)(2,1)S(1)}, bf16[2048,128]{1,0:T(8,128)(2,1)S(1)}, u32[]{:S(2)}, u32[]{:S(2)}) collective-permute-start(bf16[2048,128]{1,0:T(8,128)(2,1)S(1)} %bitcast.23), channel_id=1, source_target_pairs={{0,16},{1,17},{2,18},{3,19},{4,20},{5,21},{6,22},{7,23},{8,24},{9,... | collective-permute-start | bytes 1572872 | tf_op jit(solution)/shard_map/ppermute | solution.py:34
  60.3 0.5 bias.1.refs_10_
  60.9 3.7 %attention.1 = (bf16[512,128]{1,0:T(8,128)(2,1)S(1)}, bf16[8,512,128]{2,1,0:T(8,128)(2,1)S(1)}) custom-call(bf16[768,128]{1,0:T(8,128)(2,1)S(1)} %bitcast.29, bf16[768,128]{1,0:T(8,128)(2,1)S(1)} %collective-permute-done.1.refs_1_, bf16[768,128]{1,0:T(8,128)(2,1)S(1)} %collective-permute-done.2.refs_2_, bf16[768,128]{1,0:T(8,128)(2,1)S(1)} %collective-permute-done.3.refs_3_, ...), custom_call_target="tpu_custom_call" | custom-call | flops 600000000 | bytes 3000000 | tf_op jit(solution)/shard_map/attention/pallas_call | solution.py:299
  64.7 7.0 %collective-permute-start.12 = (bf16[528,128]{1,0:T(8,128)(2,1)S(1)}, bf16[528,128]{1,0:T(8,128)(2,1)S(1)}, u32[]{:S(2)}, u32[]{:S(2)}) collective-permute-start(bf16[528,128]{1,0:T(8,128)(2,1)S(1)} %pad_maximum_fusion), channel_id=1, source_target_pairs={{0,4},{1,5},{2,6},{3,7},{4,0},{5,1},{6,2},{7,3},{8,12},{9,13},{10,... | collective-permute-start | bytes 405512 | tf_op jit(solution)/shard_map/ppermute | solution.py:34
  71.7 3.0 %collective-permute-start.11 = (bf16[512,128]{1,0:T(8,128)(2,1)S(1)}, bf16[512,128]{1,0:T(8,128)(2,1)S(1)}, u32[]{:S(2)}, u32[]{:S(2)}) collective-permute-start(bf16[512,128]{1,0:T(8,128)(2,1)S(1)} %get-tuple-element.11.refs_0_), channel_id=1, source_target_pairs={{0,3},{1,2},{2,1},{3,0},{4,7},{5,6},{6,5},{7,4},{8,11},{9,10},{10,... | collective-permute-start | bytes 393224 | tf_op jit(solution)/shard_map/ppermute | solution.py:34
  74.7 4.2 %collective-permute-start.10 = (bf16[512,128]{1,0:T(8,128)(2,1)S(1)}, bf16[512,128]{1,0:T(8,128)(2,1)S(1)}, u32[]{:S(2)}, u32[]{:S(2)}) collective-permute-start(bf16[512,128]{1,0:T(8,128)(2,1)S(1)} %get-tuple-element.11.refs_0_), channel_id=1, source_target_pairs={{0,2},{1,3},{2,0},{3,1},{4,6},{5,7},{6,4},{7,5},{8,10},{9,11},{10,... | collective-permute-start | bytes 393224 | tf_op jit(solution)/shard_map/ppermute | solution.py:34
  78.9 2.7 %collective-permute-start.9 = (bf16[512,128]{1,0:T(8,128)(2,1)S(1)}, bf16[512,128]{1,0:T(8,128)(2,1)S(1)}, u32[]{:S(2)}, u32[]{:S(2)}) collective-permute-start(bf16[512,128]{1,0:T(8,128)(2,1)S(1)} %get-tuple-element.11.refs_0_), channel_id=1, source_target_pairs={{0,1},{1,0},{2,3},{3,2},{4,5},{5,4},{6,7},{7,6},{8,9},{9,8},{10,11... | collective-permute-start | bytes 393224 | tf_op jit(solution)/shard_map/ppermute | solution.py:34
  81.6 0.1 join.9
  81.6 0.0 collective-permute-done.11.refs_3_
  81.7 0.0 copy-start.3
  81.7 0.0 copy-start.4
  81.7 2.1 %collective-permute-start.14 = (bf16[4096,128]{1,0:T(8,128)(2,1)S(1)}, bf16[4096,128]{1,0:T(8,128)(2,1)S(1)}, u32[]{:S(2)}, u32[]{:S(2)}) collective-permute-start(bf16[4096,128]{1,0:T(8,128)(2,1)S(1)} %bitcast.19), channel_id=1, source_target_pairs={{0,8},{1,9},{2,10},{3,11},{4,12},{5,13},{6,14},{7,15},{8,0},{9,1},... | collective-permute-start | bytes 3145736 | tf_op jit(solution)/shard_map/ppermute | solution.py:34
  83.7 2.0 %collective-permute-done.9.refs_1_ = bf16[512,128]{1,0:T(8,128)(2,1)S(1)} collective-permute-done((bf16[512,128]{1,0:T(8,128)(2,1)S(1)}, bf16[512,128]{1,0:T(8,128)(2,1)S(1)}, u32[]{:S(2)}, u32[]{:S(2)}) %collective-permute-start.9) | collective-permute-done | bytes 131104 | tf_op jit(solution)/shard_map/ppermute | solution.py:34
  85.8 0.0 collective-permute-done.12.refs_0_
  85.8 0.1 join.7
  85.8 11.1 %all_to_all.5.refs_4_ = bf16[4,512,128]{2,1,0:T(8,128)(2,1)S(1)} all-to-all(bf16[4,512,128]{2,1,0:T(8,128)(2,1)S(1)} %join.7), channel_id=1, replica_groups={{0,1,2,3},{4,5,6,7},{8,9,10,11},{12,13,14,15},{16,17,18,19},{20,21,22,2..., dimensions={0} | all-to-all | bytes 1048576 | tf_op jit(solution)/shard_map/all_to_all | solution.py:316
  96.9 0.0 collective-permute-done.15
  97.0 2.4 %merge.1 = bf16[256,128]{1,0:T(8,128)(2,1)S(1)} custom-call(bf16[512,128]{1,0:T(8,128)(2,1)S(1)} %get-tuple-element.11.refs_0_, bf16[512,128]{1,0:T(8,128)(2,1)S(1)} %collective-permute-done.9.refs_1_, bf16[512,128]{1,0:T(8,128)(2,1)S(1)} %collective-permute-done.10.refs_2_, bf16[512,128]{1,0:T(8,128)(2,1)S(1)} %collective-permute-done.11.refs_3_, ...), custom_call_target="tpu_custom_call" | custom-call | flops 1400000000 | bytes 7000000 | tf_op jit(solution)/shard_map/merge/pallas_call | solution.py:321
  99.4 1.9 %collective-permute-start.16 = (bf16[128,128]{1,0:T(8,128)(2,1)S(1)}, bf16[128,128]{1,0:T(8,128)(2,1)S(1)}, u32[]{:S(2)}, u32[]{:S(2)}) collective-permute-start(bf16[128,128]{1,0:T(8,128)(2,1)S(1)} %get-tuple-element.13), channel_id=1, source_target_pairs={{0,8},{1,9},{2,10},{3,11},{4,12},{5,13},{6,14},{7,15},{8,16},{9,17... | collective-permute-start | bytes 98312 | tf_op jit(solution)/shard_map/ppermute | solution.py:58
  101.3 6.6 %collective-permute-done.16 = bf16[128,128]{1,0:T(8,128)(2,1)S(1)} collective-permute-done((bf16[128,128]{1,0:T(8,128)(2,1)S(1)}, bf16[128,128]{1,0:T(8,128)(2,1)S(1)}, u32[]{:S(2)}, u32[]{:S(2)}) %collective-permute-start.16) | collective-permute-done | bytes 32800 | tf_op jit(solution)/shard_map/ppermute | solution.py:58
  107.9 0.6 pad_maximum_fusion.1
  (21 shorter events, 0.1 us)
Async XLA Ops:
  0.0 0.9 copy-start.6
  1.2 20.4 %collective-permute-start = (bf16[256,128]{1,0:T(8,128)(2,1)S(1)}, bf16[256,128]{1,0:T(8,128)(2,1)S(1)}, u32[]{:S(2)}, u32[]{:S(2)}) collective-permute-start(bf16[256,128]{1,0:T(8,128)(2,1)S(1)} %get-tuple-element.10), channel_id=1, source_target_pairs={{0,508},{1,509},{2,510},{3,511},{4,504},{5,505},{6,506},{7,507},{8... | collective-permute-start | bytes 196616 | tf_op jit(solution)/shard_map/ppermute | solution.py:51
  14.2 1.0 copy-start.2
  15.2 26.3 %collective-permute-start.4 = (bf16[512,128]{1,0:T(8,128)(2,1)S(1)}, bf16[512,128]{1,0:T(8,128)(2,1)S(1)}, u32[]{:S(2)}, u32[]{:S(2)}) collective-permute-start(bf16[512,128]{1,0:T(8,128)(2,1)S(1)} %piece.1.refs_0_.refs_2_), channel_id=1, source_target_pairs={{0,4},{1,5},{2,6},{3,7},{4,0},{5,1},{6,2},{7,3},{8,12},{9,13},{10,... | collective-permute-start | bytes 393224 | tf_op jit(solution)/shard_map/ppermute | solution.py:34
  21.5 19.9 %collective-permute-start.5 = (bf16[256,128]{1,0:T(8,128)(2,1)S(1)}, bf16[256,128]{1,0:T(8,128)(2,1)S(1)}, u32[]{:S(2)}, u32[]{:S(2)}) collective-permute-start(bf16[256,128]{1,0:T(8,128)(2,1)S(1)} %collective-permute-done.refs_1_), channel_id=1, source_target_pairs={{0,4},{1,5},{2,6},{3,7},{4,0},{5,1},{6,2},{7,3},{8,12},{9,13},{10,... | collective-permute-start | bytes 196616 | tf_op jit(solution)/shard_map/ppermute | solution.py:34
  29.8 21.7 %copy-start = (bf16[4096,256]{1,0:T(8,128)(2,1)S(1)}, bf16[4096,256]{1,0:T(8,128)(2,1)}, u32[]{:S(2)}) copy-start(bf16[4096,256]{1,0:T(8,128)(2,1)} %param.16) | copy-start | bytes 6291460
  29.8 18.5 %collective-permute-start.3 = (bf16[768,128]{1,0:T(8,128)(2,1)S(1)}, bf16[768,128]{1,0:T(8,128)(2,1)S(1)}, u32[]{:S(2)}, u32[]{:S(2)}) collective-permute-start(bf16[768,128]{1,0:T(8,128)(2,1)S(1)} %bitcast.25), channel_id=1, source_target_pairs={{0,3},{1,2},{2,1},{3,0},{4,7},{5,6},{6,5},{7,4},{8,11},{9,10},{10,... | collective-permute-start | bytes 589832 | tf_op jit(solution)/shard_map/ppermute | solution.py:34
  32.1 19.4 %collective-permute-start.2 = (bf16[768,128]{1,0:T(8,128)(2,1)S(1)}, bf16[768,128]{1,0:T(8,128)(2,1)S(1)}, u32[]{:S(2)}, u32[]{:S(2)}) collective-permute-start(bf16[768,128]{1,0:T(8,128)(2,1)S(1)} %bitcast.26), channel_id=1, source_target_pairs={{0,2},{1,3},{2,0},{3,1},{4,6},{5,7},{6,4},{7,5},{8,10},{9,11},{10,... | collective-permute-start | bytes 589832 | tf_op jit(solution)/shard_map/ppermute | solution.py:34
  36.6 15.8 %collective-permute-start.1 = (bf16[768,128]{1,0:T(8,128)(2,1)S(1)}, bf16[768,128]{1,0:T(8,128)(2,1)S(1)}, u32[]{:S(2)}, u32[]{:S(2)}) collective-permute-start(bf16[768,128]{1,0:T(8,128)(2,1)S(1)} %bitcast.27), channel_id=1, source_target_pairs={{0,1},{1,0},{2,3},{3,2},{4,5},{5,4},{6,7},{7,6},{8,9},{9,8},{10,11... | collective-permute-start | bytes 589832 | tf_op jit(solution)/shard_map/ppermute | solution.py:34
  41.5 18.8 %copy-start.7 = (f32[2,128,128]{2,1,0:T(8,128)S(1)}, f32[2,128,128]{2,1,0:T(8,128)}, u32[]{:S(2)}) copy-start(f32[2,128,128]{2,1,0:T(8,128)} %bias_ref.1) | copy-start | bytes 393220
  41.5 18.8 %copy-start.8 = (f32[128,128]{1,0:T(8,128)S(1)}, f32[128,128]{1,0:T(8,128)}, u32[]{:S(2)}) copy-start(f32[128,128]{1,0:T(8,128)} %constant.7.clone.turned_ref) | copy-start | bytes 196612
  41.5 18.8 %copy-start.9 = (f32[128,128]{1,0:T(8,128)S(1)}, f32[128,128]{1,0:T(8,128)}, u32[]{:S(2)}) copy-start(f32[128,128]{1,0:T(8,128)} %constant.6.clone.hot_ref) | copy-start | bytes 196612
  41.5 14.2 %collective-permute-start.8 = (bf16[768,128]{1,0:T(8,128)(2,1)S(1)}, bf16[768,128]{1,0:T(8,128)(2,1)S(1)}, u32[]{:S(2)}, u32[]{:S(2)}) collective-permute-start(bf16[768,128]{1,0:T(8,128)(2,1)S(1)} %bitcast.32), channel_id=1, source_target_pairs={{0,3},{1,2},{2,1},{3,0},{4,7},{5,6},{6,5},{7,4},{8,11},{9,10},{10,... | collective-permute-start | bytes 589832 | tf_op jit(solution)/shard_map/ppermute | solution.py:34
  43.6 12.1 %collective-permute-start.7 = (bf16[768,128]{1,0:T(8,128)(2,1)S(1)}, bf16[768,128]{1,0:T(8,128)(2,1)S(1)}, u32[]{:S(2)}, u32[]{:S(2)}) collective-permute-start(bf16[768,128]{1,0:T(8,128)(2,1)S(1)} %bitcast.33), channel_id=1, source_target_pairs={{0,2},{1,3},{2,0},{3,1},{4,6},{5,7},{6,4},{7,5},{8,10},{9,11},{10,... | collective-permute-start | bytes 589832 | tf_op jit(solution)/shard_map/ppermute | solution.py:34
  48.3 9.9 %collective-permute-start.6 = (bf16[768,128]{1,0:T(8,128)(2,1)S(1)}, bf16[768,128]{1,0:T(8,128)(2,1)S(1)}, u32[]{:S(2)}, u32[]{:S(2)}) collective-permute-start(bf16[768,128]{1,0:T(8,128)(2,1)S(1)} %bitcast.34), channel_id=1, source_target_pairs={{0,1},{1,0},{2,3},{3,2},{4,5},{5,4},{6,7},{7,6},{8,9},{9,8},{10,11... | collective-permute-start | bytes 589832 | tf_op jit(solution)/shard_map/ppermute | solution.py:34
  51.5 45.4 %collective-permute-start.15 = (bf16[4096,256]{1,0:T(8,128)(2,1)S(1)}, bf16[4096,256]{1,0:T(8,128)(2,1)S(1)}, u32[]{:S(2)}, u32[]{:S(2)}) collective-permute-start(bf16[4096,256]{1,0:T(8,128)(2,1)S(1)} %copy-done), channel_id=1, source_target_pairs={{60,504},{61,505},{62,506},{63,507},{56,508},{57,509},{58,510},{59... | collective-permute-start | bytes 6291464 | tf_op jit(solution)/shard_map/ppermute | solution.py:61
  58.2 2.7 %copy-start.1 = (bf16[1024,3,128]{2,0,1:T(8,128)(2,1)S(1)}, bf16[1024,3,128]{2,0,1:T(8,128)(2,1)}, u32[]{:S(2)}) copy-start(bf16[1024,3,128]{2,0,1:T(8,128)(2,1)} %param.12) | copy-start | bytes 2359300
  58.2 2.7 %copy-start.5 = (f32[1024]{0:T(1024)S(1)}, f32[1024]{0:T(1024)}, u32[]{:S(2)}) copy-start(f32[1024]{0:T(1024)} %param.11) | copy-start | bytes 12292
  58.3 20.6 %collective-permute-start.13 = (bf16[2048,128]{1,0:T(8,128)(2,1)S(1)}, bf16[2048,128]{1,0:T(8,128)(2,1)S(1)}, u32[]{:S(2)}, u32[]{:S(2)}) collective-permute-start(bf16[2048,128]{1,0:T(8,128)(2,1)S(1)} %bitcast.23), channel_id=1, source_target_pairs={{0,16},{1,17},{2,18},{3,19},{4,20},{5,21},{6,22},{7,23},{8,24},{9,... | collective-permute-start | bytes 1572872 | tf_op jit(solution)/shard_map/ppermute | solution.py:34
  64.7 21.1 %collective-permute-start.12 = (bf16[528,128]{1,0:T(8,128)(2,1)S(1)}, bf16[528,128]{1,0:T(8,128)(2,1)S(1)}, u32[]{:S(2)}, u32[]{:S(2)}) collective-permute-start(bf16[528,128]{1,0:T(8,128)(2,1)S(1)} %pad_maximum_fusion), channel_id=1, source_target_pairs={{0,4},{1,5},{2,6},{3,7},{4,0},{5,1},{6,2},{7,3},{8,12},{9,13},{10,... | collective-permute-start | bytes 405512 | tf_op jit(solution)/shard_map/ppermute | solution.py:34
  71.7 9.9 %collective-permute-start.11 = (bf16[512,128]{1,0:T(8,128)(2,1)S(1)}, bf16[512,128]{1,0:T(8,128)(2,1)S(1)}, u32[]{:S(2)}, u32[]{:S(2)}) collective-permute-start(bf16[512,128]{1,0:T(8,128)(2,1)S(1)} %get-tuple-element.11.refs_0_), channel_id=1, source_target_pairs={{0,3},{1,2},{2,1},{3,0},{4,7},{5,6},{6,5},{7,4},{8,11},{9,10},{10,... | collective-permute-start | bytes 393224 | tf_op jit(solution)/shard_map/ppermute | solution.py:34
  74.7 9.1 %collective-permute-start.10 = (bf16[512,128]{1,0:T(8,128)(2,1)S(1)}, bf16[512,128]{1,0:T(8,128)(2,1)S(1)}, u32[]{:S(2)}, u32[]{:S(2)}) collective-permute-start(bf16[512,128]{1,0:T(8,128)(2,1)S(1)} %get-tuple-element.11.refs_0_), channel_id=1, source_target_pairs={{0,2},{1,3},{2,0},{3,1},{4,6},{5,7},{6,4},{7,5},{8,10},{9,11},{10,... | collective-permute-start | bytes 393224 | tf_op jit(solution)/shard_map/ppermute | solution.py:34
  78.9 6.9 %collective-permute-start.9 = (bf16[512,128]{1,0:T(8,128)(2,1)S(1)}, bf16[512,128]{1,0:T(8,128)(2,1)S(1)}, u32[]{:S(2)}, u32[]{:S(2)}) collective-permute-start(bf16[512,128]{1,0:T(8,128)(2,1)S(1)} %get-tuple-element.11.refs_0_), channel_id=1, source_target_pairs={{0,1},{1,0},{2,3},{3,2},{4,5},{5,4},{6,7},{7,6},{8,9},{9,8},{10,11... | collective-permute-start | bytes 393224 | tf_op jit(solution)/shard_map/ppermute | solution.py:34
  81.7 15.3 %copy-start.3 = (bf16[2,256,128]{2,1,0:T(8,128)(2,1)S(1)}, bf16[2,256,128]{2,1,0:T(8,128)(2,1)}, u32[]{:S(2)}) copy-start(bf16[2,256,128]{2,1,0:T(8,128)(2,1)} %constant.8.clone.refs_11_) | copy-start | bytes 393220
  81.7 15.3 %copy-start.4 = (f32[4096]{0:T(1024)S(1)}, f32[4096]{0:T(1024)}, u32[]{:S(2)}) copy-start(f32[4096]{0:T(1024)} %param.15) | copy-start | bytes 49156
  81.7 15.3 %collective-permute-start.14 = (bf16[4096,128]{1,0:T(8,128)(2,1)S(1)}, bf16[4096,128]{1,0:T(8,128)(2,1)S(1)}, u32[]{:S(2)}, u32[]{:S(2)}) collective-permute-start(bf16[4096,128]{1,0:T(8,128)(2,1)S(1)} %bitcast.19), channel_id=1, source_target_pairs={{0,8},{1,9},{2,10},{3,11},{4,12},{5,13},{6,14},{7,15},{8,0},{9,1},... | collective-permute-start | bytes 3145736 | tf_op jit(solution)/shard_map/ppermute | solution.py:34
  99.4 8.6 %collective-permute-start.16 = (bf16[128,128]{1,0:T(8,128)(2,1)S(1)}, bf16[128,128]{1,0:T(8,128)(2,1)S(1)}, u32[]{:S(2)}, u32[]{:S(2)}) collective-permute-start(bf16[128,128]{1,0:T(8,128)(2,1)S(1)} %get-tuple-element.13), channel_id=1, source_target_pairs={{0,8},{1,9},{2,10},{3,11},{4,12},{5,13},{6,14},{7,15},{8,16},{9,17... | collective-permute-start | bytes 98312 | tf_op jit(solution)/shard_map/ppermute | solution.py:58
